TPU v7x, 32 devices: a whole 2x2x4 slice. The times are simulated.
32 devices in a mesh: dp: 4 (over z), tensor: 4 (over y, core), section: 2 (over x).
Axes of the slice: x: 2, y: 2, z: 4, core: 2. Of those that a mesh axis runs over, the one named last changes fastest.
Arguments:
- section_inputs: bfloat16 [2, 8, 256, 1152], P('section', 'dp', 'tensor'), may hold values from -6 to 6
- condition: float32 [8, 1152], P('dp'), may hold values from -6 to 6
- timesteps: int32 [8], P('dp'), may hold values from 0 to 999
- ada_weight: bfloat16 [2, 1152, 6912], P('section', 'dp', 'tensor'), may hold values from -0.1875 to 0.1875
- ada_bias: bfloat16 [2, 6912], P('section', 'tensor'), may hold values from -3 to 3
- in_weight: bfloat16 [2, 4, 1152, 1152], P('section', None, 'dp', 'tensor'), may hold values from -0.1875 to 0.1875
- gate_weight: bfloat16 [2, 1152, 16], P('section', 'dp', 'tensor'), may hold values from -0.1875 to 0.1875
- gate_bias: bfloat16 [2, 16], P('section', 'tensor'), may hold values from -6 to 1
- conv_taps: bfloat16 [2, 9, 1152], P('section', None, 'tensor'), may hold values from -1.5 to 1.5
- out_weight: bfloat16 [2, 1152, 1152], P('section', 'tensor', 'dp'), may hold values from -0.1875 to 0.1875
- up_weight: bfloat16 [2, 1152, 4608], P('section', 'dp', 'tensor'), may hold values from -0.1875 to 0.1875
- up_bias: bfloat16 [2, 4608], P('section', 'tensor'), may hold values from -3 to 3
- down_weight: bfloat16 [2, 4608, 1152], P('section', 'tensor', 'dp'), may hold values from -0.09375 to 0.09375
Outputs:
- section_ends: bfloat16 [2, 8, 256, 1152], P('section', 'dp', 'tensor')
- cond_grad: float32 [8, 1152], P('dp')
- grad_ada_weight: float32 [2, 1152, 6912], P('section', 'dp', 'tensor')
- grad_ada_bias: float32 [2, 6912], P('section', 'tensor')
- grad_in_weight: float32 [2, 4, 1152, 1152], P('section', None, 'dp', 'tensor')
- grad_gate_weight: float32 [2, 1152, 16], P('section', 'dp', 'tensor')
- grad_gate_bias: float32 [2, 16], P('section', 'tensor')
- grad_conv_taps: float32 [2, 9, 1152], P('section', None, 'tensor')
- grad_out_weight: float32 [2, 1152, 1152], P('section', 'tensor', 'dp')
- grad_up_weight: float32 [2, 1152, 4608], P('section', 'dp', 'tensor')
- grad_up_bias: float32 [2, 4608], P('section', 'tensor')
- grad_down_weight: float32 [2, 4608, 1152], P('section', 'tensor', 'dp')
All inputs are finite; a program needn't handle non-finite values.
Results may differ from a plain program's by a relative error of at most 0.03.
Values may be sent and summed in bfloat16 or wider, within the bound.
No kernel may reach another device: no remote copies, remote signals or barrier semaphores. Data moves between devices by JAX's collectives and lax.ppermute only.
A program may use at most 128 MiB of HBM per device.

v0:
```python
import math

import jax
import jax.numpy as jnp
from jax import lax
from jax.sharding import PartitionSpec as P

SIDE = 16


HIGHEST = lax.Precision.HIGHEST


def from_behind(block, axis, distance):
    devices = range(lax.axis_size(axis))
    route = [(i - distance, i) for i in devices if i - distance in devices]
    return lax.ppermute(block, axis, route)


def sinusoid(time_steps, channels):
    half_width = channels // 2
    frequency = jnp.exp(
        jnp.arange(half_width, dtype=jnp.float32) * (-math.log(10000.0) / half_width)
    )
    angles = time_steps.astype(jnp.float32)[:, None] * frequency[None, :]
    return jnp.concatenate([jnp.cos(angles), jnp.sin(angles)], axis=1)


def layer_norm(values):
    row_mean = jnp.mean(values, axis=-1, keepdims=True)
    centered = values - row_mean
    variance = jnp.mean(centered * centered, axis=-1, keepdims=True)
    return centered * lax.rsqrt(variance + 1e-06)


def modulate(values, shift_vec, scale_vec):
    return layer_norm(values) * (1.0 + scale_vec) + shift_vec


def reorient(values, flip, side):
    lead_shape = values.shape[:-2]
    channels = values.shape[-1]
    grid_view = values.reshape(lead_shape + (side, side, channels))
    turned = jnp.swapaxes(grid_view, -3, -2).reshape(values.shape)
    return jnp.where(flip, turned, values)


def middle(projected, logits, taps, flip, side):
    length = projected.shape[1]
    channels = projected.shape[2]
    head_count = logits.shape[1]
    head_width = channels // head_count
    scan_proj = reorient(projected[:3], flip, side)
    scan_logit = reorient(logits, flip, side)
    split_parts = scan_proj.reshape(3, length, head_count, head_width).transpose(0, 2, 1, 3)
    query_rows = split_parts[0].astype(jnp.bfloat16)
    key_rows = split_parts[1].astype(jnp.bfloat16)
    value_rows = split_parts[2]
    decay_rates = -jax.nn.softplus(scan_logit)
    totals = jnp.cumsum(decay_rates, axis=0).T
    positions = jnp.arange(length)
    causal = positions[:, None] >= positions[None, :]
    log_spans = jnp.where(causal[None], totals[:, :, None] - totals[:, None, :], -1e30)
    decays = jnp.exp(log_spans)
    raw_scores = jnp.einsum(
        "htc,hsc->hts", query_rows, key_rows, preferred_element_type=jnp.float32
    ) * head_width ** (-0.5)
    scores = raw_scores * decays
    mixed_out = jnp.einsum("hts,hsc->htc", scores, value_rows, precision=HIGHEST)
    decay_mass = jnp.sum(decays, axis=2)
    normed = mixed_out * lax.rsqrt(decay_mass)[:, :, None]
    flat_out = reorient(normed.transpose(1, 0, 2).reshape(length, channels), flip, side)
    grid_out = flat_out.reshape(side, side, channels)
    padded = jnp.pad(grid_out, ((1, 1), (1, 1), (0, 0)))
    spread = grid_out
    for tap_row in range(3):
        for tap_col in range(3):
            spread = (
                spread
                + padded[tap_row : tap_row + side, tap_col : tap_col + side]
                * taps[3 * tap_row + tap_col]
            )
    return spread.reshape(length, channels) * jax.nn.silu(projected[3])


def weight_products(factors):
    (
        whole_one,
        grad_proj,
        grad_logit,
        mixed_rows,
        grad_attn,
        whole_two,
        grad_pre,
        hidden,
        grad_mlp,
    ) = factors
    grad_inw = jnp.einsum("nld,njle->jde", whole_one, grad_proj, preferred_element_type=jnp.float32)
    grad_gatew = jnp.einsum(
        "nld,nlh->dh", whole_one, grad_logit, preferred_element_type=jnp.float32
    )
    grad_outw = jnp.einsum("nlc,nld->cd", mixed_rows, grad_attn, preferred_element_type=jnp.float32)
    grad_up = jnp.einsum("nld,nlf->df", whole_two, grad_pre, preferred_element_type=jnp.float32)
    grad_down = jnp.einsum("nlf,nld->fd", hidden, grad_mlp, preferred_element_type=jnp.float32)
    return (grad_inw, grad_gatew, grad_outw, grad_up, grad_down)


def per_device(
    section_inputs,
    condition,
    timesteps,
    ada_weight,
    ada_bias,
    in_weight,
    gate_weight,
    gate_bias,
    conv_taps,
    out_weight,
    up_weight,
    up_bias,
    down_weight,
):
    gathered = (
        lax.all_gather(ada_weight, "dp", axis=1, tiled=True),
        lax.all_gather(in_weight, "dp", axis=2, tiled=True),
        lax.all_gather(gate_weight, "dp", axis=1, tiled=True),
        lax.all_gather(out_weight, "dp", axis=2, tiled=True),
        lax.all_gather(up_weight, "dp", axis=1, tiled=True),
        lax.all_gather(down_weight, "dp", axis=2, tiled=True),
    )
    ada_full = gathered[0][0]
    in_full = gathered[1][0]
    gate_full = gathered[2][0]
    out_full = gathered[3][0]
    up_full = gathered[4][0]
    down_full = gathered[5][0]
    ada_row = ada_bias[0].astype(jnp.float32)
    gate_row = gate_bias[0].astype(jnp.float32)
    taps = conv_taps[0].astype(jnp.float32)
    up_row = up_bias[0].astype(jnp.float32)
    section_index = lax.axis_index("section")
    first_section = section_index == 0
    flipped = section_index == 1
    images = condition.shape[0]
    local_rows = section_inputs.shape[2]
    model_width = section_inputs.shape[3]
    cond_vec = condition + sinusoid(timesteps, model_width)
    activated = jax.nn.silu(cond_vec).astype(jnp.bfloat16)
    mod_part = jnp.dot(activated, ada_full, preferred_element_type=jnp.float32) + ada_row
    modulation = lax.all_gather(mod_part, "tensor", axis=1, tiled=True)

    def gather_rows(values):
        return lax.all_gather(values, "tensor", axis=0, tiled=True)

    def sum_rows(term):
        return lax.psum_scatter(
            term(jnp.int32(0), local_rows * lax.axis_size("tensor")).astype(jnp.bfloat16),
            "tensor",
            scatter_dimension=0,
            tiled=True,
        ).astype(jnp.float32)

    def gather_grads(values):
        return lax.all_gather(values, "tensor", axis=0, tiled=True)

    def sum_grads(term):
        return lax.psum_scatter(
            term(jnp.int32(0), local_rows * lax.axis_size("tensor")).astype(jnp.bfloat16),
            "tensor",
            scatter_dimension=0,
            tiled=True,
        ).astype(jnp.float32)

    def forward_block(block_in, mod_vec):
        pieces = jnp.split(mod_vec, 6)
        whole_one = gather_rows(modulate(block_in, pieces[0], pieces[1]).astype(jnp.bfloat16))
        projected = jnp.einsum(
            "ld,jde->jle", whole_one, in_full, preferred_element_type=jnp.float32
        ).astype(jnp.bfloat16)
        logits = jnp.dot(whole_one, gate_full, preferred_element_type=jnp.float32) + gate_row
        mixed_rows = middle(projected.astype(jnp.float32), logits, taps, flipped, SIDE).astype(
            jnp.bfloat16
        )

        def attn_term(row_start, row_count):
            return jnp.dot(mixed_rows, out_full, preferred_element_type=jnp.float32)

        attended = sum_rows(attn_term)
        after_attn = block_in + pieces[2] * attended
        whole_two = gather_rows(modulate(after_attn, pieces[3], pieces[4]).astype(jnp.bfloat16))
        pre_act = jnp.dot(whole_two, up_full, preferred_element_type=jnp.float32) + up_row
        hidden = jax.nn.gelu(pre_act).astype(jnp.bfloat16)

        def mlp_term(row_start, row_count):
            return jnp.dot(hidden, down_full, preferred_element_type=jnp.float32)

        mlp_out = sum_rows(mlp_term)
        block_out = after_attn + pieces[5] * mlp_out
        return (
            block_out,
            (
                whole_one,
                projected,
                logits,
                mixed_rows,
                attended,
                after_attn,
                whole_two,
                pre_act,
                hidden,
                mlp_out,
            ),
        )

    def backward_inputs(block_in, mod_vec, grad_out):
        unused_out, saved = forward_block(block_in, mod_vec)
        (
            whole_one,
            projected,
            logits,
            mixed_rows,
            attended,
            after_attn,
            whole_two,
            pre_act,
            hidden,
            mlp_out,
        ) = saved
        pieces = jnp.split(mod_vec, 6)
        grad_gate_two = jnp.sum(grad_out * mlp_out, axis=0)
        grad_mlp = gather_grads((pieces[5] * grad_out).astype(jnp.bfloat16))
        grad_hidden = jnp.einsum(
            "ld,fd->lf", grad_mlp, down_full, preferred_element_type=jnp.float32
        )
        grad_pre = jax.vjp(jax.nn.gelu, pre_act)[1](grad_hidden)[0].astype(jnp.bfloat16)
        grad_up_bias = jnp.sum(grad_pre.astype(jnp.float32), axis=0)

        def mlp_back(row_start, row_count):
            return jnp.einsum("lf,df->ld", grad_pre, up_full, preferred_element_type=jnp.float32)

        grad_normed_two = sum_grads(mlp_back)
        grad_after, grad_shift_two, grad_scale_two = jax.vjp(
            modulate, after_attn, pieces[3], pieces[4]
        )[1](grad_normed_two)
        grad_after = grad_after + grad_out
        grad_gate_one = jnp.sum(grad_after * attended, axis=0)
        grad_attn = gather_grads((pieces[2] * grad_after).astype(jnp.bfloat16))
        grad_mixed = jnp.einsum(
            "ld,cd->lc", grad_attn, out_full, preferred_element_type=jnp.float32
        )

        def local_middle(proj_in, logit_in, tap_in):
            return middle(proj_in, logit_in, tap_in, flipped, SIDE)

        grad_proj, grad_logit, grad_taps = jax.vjp(
            local_middle, projected.astype(jnp.float32), logits, taps
        )[1](grad_mixed)
        grad_proj = grad_proj.astype(jnp.bfloat16)
        grad_logit = grad_logit.astype(jnp.bfloat16)
        grad_gateb = jnp.sum(grad_logit.astype(jnp.float32), axis=0)

        def attn_back(row_start, row_count):
            return jnp.einsum(
                "jle,jde->ld", grad_proj, in_full, preferred_element_type=jnp.float32
            ) + jnp.einsum("lh,dh->ld", grad_logit, gate_full, preferred_element_type=jnp.float32)

        grad_normed_one = sum_grads(attn_back)
        grad_in, grad_shift_one, grad_scale_one = jax.vjp(modulate, block_in, pieces[0], pieces[1])[
            1
        ](grad_normed_one)
        grad_in = grad_in + grad_after
        grad_mod = jnp.concatenate(
            [
                grad_shift_one,
                grad_scale_one,
                grad_gate_one,
                grad_shift_two,
                grad_scale_two,
                grad_gate_two,
            ]
        )
        factors = (
            whole_one,
            grad_proj,
            grad_logit,
            mixed_rows,
            grad_attn,
            whole_two,
            grad_pre,
            hidden,
            grad_mlp,
        )
        return (grad_in, grad_mod, (grad_gateb, grad_taps, grad_up_bias), factors)

    local_inputs = section_inputs[0]
    zero_rows = jnp.zeros((local_rows, model_width), jnp.bfloat16)

    def forward_step(state_carry, step_index):
        received, kept_inputs, forward_out = state_carry
        slot_index = jnp.clip(step_index - section_index, 0, images - 1)
        own_rows = lax.dynamic_index_in_dim(
            local_inputs, jnp.minimum(step_index, images - 1), 0, keepdims=False
        )
        block_in = jnp.where(first_section, own_rows, received)
        mod_vec = lax.dynamic_index_in_dim(modulation, slot_index, 0, keepdims=False)
        block_out = forward_block(block_in.astype(jnp.float32), mod_vec)[0].astype(jnp.bfloat16)
        kept_inputs = lax.dynamic_update_index_in_dim(kept_inputs, block_in, slot_index, 0)
        forward_out = lax.dynamic_update_index_in_dim(forward_out, block_out, slot_index, 0)
        received = from_behind(block_out, "section", 1)
        return ((received, kept_inputs, forward_out), None)

    forward_state, unused_steps = lax.scan(
        forward_step, (zero_rows, local_inputs, local_inputs), jnp.arange(images + 1)
    )
    kept_inputs = forward_state[1]
    forward_out = forward_state[2]
    zero_small = tuple((jnp.zeros(piece.shape, jnp.float32) for piece in (gate_row, taps, up_row)))
    zero_matrices = tuple(
        (
            jnp.zeros(piece.shape, jnp.float32)
            for piece in (in_full, gate_full, out_full, up_full, down_full)
        )
    )
    zero_mods = jnp.zeros((images, modulation.shape[1]), jnp.float32)

    def backward_step(state_carry, step_index):
        received, input_grads, mod_grads, small_totals, matrix_totals = state_carry
        position = step_index - (1 - section_index)
        slot_index = jnp.clip(position, 0, images - 1)
        live = ((position >= 0) & (position < images)).astype(jnp.float32)
        own_rows = lax.dynamic_index_in_dim(
            local_inputs, jnp.minimum(step_index, images - 1), 0, keepdims=False
        )
        grad_out = jnp.where(first_section, received, own_rows).astype(jnp.float32) * live
        block_in = lax.dynamic_index_in_dim(kept_inputs, slot_index, 0, keepdims=False).astype(
            jnp.float32
        )
        mod_vec = lax.dynamic_index_in_dim(modulation, slot_index, 0, keepdims=False)
        grad_in, grad_mod, small_terms, factors = backward_inputs(block_in, mod_vec, grad_out)
        grad_low = grad_in.astype(jnp.bfloat16)
        input_grads = lax.dynamic_update_index_in_dim(input_grads, grad_low, slot_index, 0)
        mod_before = lax.dynamic_index_in_dim(mod_grads, slot_index, 0, keepdims=False)
        mod_grads = lax.dynamic_update_index_in_dim(mod_grads, mod_before + grad_mod, slot_index, 0)
        small_totals = jax.tree.map(
            lambda total_sum, term_sum: total_sum + term_sum, small_totals, small_terms
        )
        received = from_behind(grad_low, "section", -1)
        return ((received, input_grads, mod_grads, small_totals, matrix_totals), factors)

    backward_state, step_factors = lax.scan(
        backward_step,
        (zero_rows, local_inputs, zero_mods, zero_small, zero_matrices),
        jnp.arange(images + 1),
    )
    input_grads = backward_state[1]
    mod_grads = backward_state[2]
    grad_gateb, grad_taps, grad_up_bias = backward_state[3]
    live_factors = tuple(
        (lax.dynamic_slice_in_dim(piece, 1 - section_index, images, 0) for piece in step_factors)
    )
    matrix_grads = weight_products(live_factors)
    grad_inw, grad_gatew, grad_outw, grad_up, grad_down = matrix_grads
    section_ends = jnp.where(first_section, input_grads, forward_out)[None]
    mod_share = lax.psum_scatter(
        mod_grads.astype(jnp.bfloat16), "tensor", scatter_dimension=1, tiled=True
    )
    grad_ada_bias = jnp.sum(mod_share.astype(jnp.float32), axis=0)
    act_grad = jnp.einsum("me,de->md", mod_share, ada_full, preferred_element_type=jnp.float32)
    cond_term = jax.vjp(jax.nn.silu, cond_vec)[1](act_grad)[0]
    cond_grad = lax.psum(cond_term, ("tensor", "section"))
    grad_ada = jnp.einsum("md,me->de", activated, mod_share, preferred_element_type=jnp.float32)
    shares = (
        lax.psum_scatter(
            grad_ada.astype(jnp.bfloat16), "dp", scatter_dimension=0, tiled=True
        ).astype(jnp.float32),
        lax.psum_scatter(
            grad_inw.astype(jnp.bfloat16), "dp", scatter_dimension=1, tiled=True
        ).astype(jnp.float32),
        lax.psum_scatter(
            grad_gatew.astype(jnp.bfloat16), "dp", scatter_dimension=0, tiled=True
        ).astype(jnp.float32),
        lax.psum_scatter(
            grad_outw.astype(jnp.bfloat16), "dp", scatter_dimension=1, tiled=True
        ).astype(jnp.float32),
        lax.psum_scatter(
            grad_up.astype(jnp.bfloat16), "dp", scatter_dimension=0, tiled=True
        ).astype(jnp.float32),
        lax.psum_scatter(
            grad_down.astype(jnp.bfloat16), "dp", scatter_dimension=1, tiled=True
        ).astype(jnp.float32),
    )
    ada_share = shares[0]
    other_shares = shares[1:]
    small_sums = lax.psum((grad_ada_bias, grad_gateb, grad_taps, grad_up_bias), "dp")
    return (
        section_ends,
        cond_grad,
        ada_share[None],
        small_sums[0][None],
        other_shares[0][None],
        other_shares[1][None],
        small_sums[1][None],
        small_sums[2][None],
        other_shares[2][None],
        other_shares[3][None],
        small_sums[3][None],
        other_shares[4][None],
    )


def solution(mesh):
    in_specs = (
        P("section", "dp", "tensor", None),
        P("dp", None),
        P("dp"),
        P("section", "dp", "tensor"),
        P("section", "tensor"),
        P("section", None, "dp", "tensor"),
        P("section", "dp", "tensor"),
        P("section", "tensor"),
        P("section", None, "tensor"),
        P("section", "tensor", "dp"),
        P("section", "dp", "tensor"),
        P("section", "tensor"),
        P("section", "tensor", "dp"),
    )
    out_specs = (
        P("section", "dp", "tensor", None),
        P("dp", None),
        P("section", "dp", "tensor"),
        P("section", "tensor"),
        P("section", None, "dp", "tensor"),
        P("section", "dp", "tensor"),
        P("section", "tensor"),
        P("section", None, "tensor"),
        P("section", "tensor", "dp"),
        P("section", "dp", "tensor"),
        P("section", "tensor"),
        P("section", "tensor", "dp"),
    )
    return jax.shard_map(
        per_device, mesh=mesh, in_specs=in_specs, out_specs=out_specs, check_vma=False
    )
```

profile of v0, /device:TPU:0, one launch (start us, length us, event | category | flops | bytes accessed | tf_op | source)
XLA Modules:
  0.0 1576.2 jit_solution(11858616285197163486)
XLA Ops:
  13.7 25.6 %all_gather.60 = bf16[1,1152,4]{2,0,1:T(2,128)(2,1)S(1)} all-gather(bf16[1,288,4]{2,0,1:T(2,128)(2,1)S(1)} %copy.200), channel_id=1, replica_groups=mesh['dp'=4,'tensor'=4,'section'=2] {'dp'}, dimensions={1}, use_global_device_ids=true | all-gather | bytes 11520 | tf_op jit(solution)/shard_map/all_gather | solution.py:126
  41.2 59.5 %all_gather.61 = bf16[1,288,1152]{1,0,2:T(2,128)(2,1)S(1)} all-gather(bf16[1,288,288]{1,0,2:T(2,128)(2,1)S(1)} %copy.202), channel_id=1, replica_groups=mesh['dp'=4,'tensor'=4,'section'=2] {'dp'}, dimensions={2}, use_global_device_ids=true | all-gather | bytes 829440 | tf_op jit(solution)/shard_map/all_gather | solution.py:127
  111.8 61.2 %all-gather.8.cloned.1.call-done = bf16[1,4,1152,288]{3,1,0,2:T(4,128)(2,1)} async-done(((bf16[1,4,288,288]{3,1,0,2:T(4,128)(2,1)}), bf16[1,4,1152,288]{3,1,0,2:T(4,128)(2,1)}) %all-gather.8.cloned.1.call-update) | async-done | bytes 2654224 | tf_op jit(solution)/shard_map/all_gather | solution.py:125
  173.0 7.3 copy.204
  180.3 72.6 %all-gather.6.cloned.1.call-done = bf16[1,1152,1728]{2,1,0:T(8,128)(2,1)} async-done(((bf16[1,288,1728]{2,1,0:T(8,128)(2,1)}), bf16[1,1152,1728]{2,1,0:T(8,128)(2,1)}) %all-gather.6.cloned.1.call-update) | async-done | bytes 3981328 | tf_op jit(solution)/shard_map/all_gather | solution.py:124
  262.2 46.1 %all-gather.10.cloned.1.call-done = bf16[1,1152,1152]{2,1,0:T(8,128)(2,1)} async-done(((bf16[1,288,1152]{2,1,0:T(8,128)(2,1)}), bf16[1,1152,1152]{2,1,0:T(8,128)(2,1)}) %all-gather.10.cloned.1.call-update) | async-done | bytes 2654224 | tf_op jit(solution)/shard_map/all_gather | solution.py:128
  308.3 288.6 %while.57 = (s32[]{:T(128)}, bf16[64,1152]{1,0:T(8,128)(2,1)S(1)}, bf16[2,64,1152]{2,1,0:T(8,128)(2,1)S(1)}, bf16[2,64,1152]{2,1,0:T(8,128)(2,1)}, pred[]{:T(512...) while((s32[]{:T(128)}, bf16[64,1152]{1,0:T(8,128)(2,1)S(1)}, ...), condition=%wide.region_10.11_spmd, body=%wide.region_0.10_spmd.sunk | while | flops 2486528512 | bytes 45829020 | solution.py:312
  312.8 7.5 all_gather.74
  336.4 20.7 %reduce-scatter.36.cloned.1.call-done = bf16[64,1152]{1,0:T(8,128)(2,1)} async-done(((bf16[256,1152]{1,0:T(8,128)(2,1)}), bf16[64,1152]{1,0:T(8,128)(2,1)}) %reduce-scatter.36.cloned.1.call-update) | async-done | bytes 147472 | tf_op jit(solution)/shard_map/while/body/eval_jaxpr/reduce_scatter | solution.py:156
  360.3 7.1 all_gather.75
  372.8 22.6 %reduce-scatter.38.cloned.1.call-done = bf16[64,1152]{1,0:T(8,128)(2,1)} async-done(((bf16[256,1152]{1,0:T(8,128)(2,1)}), bf16[64,1152]{1,0:T(8,128)(2,1)}) %reduce-scatter.38.cloned.1.call-update) | async-done | bytes 147472 | tf_op jit(solution)/shard_map/while/body/eval_jaxpr/reduce_scatter | solution.py:156
  407.3 6.7 all_gather.74
  430.1 24.0 %reduce-scatter.36.cloned.1.call-done = bf16[64,1152]{1,0:T(8,128)(2,1)} async-done(((bf16[256,1152]{1,0:T(8,128)(2,1)}), bf16[64,1152]{1,0:T(8,128)(2,1)}) %reduce-scatter.36.cloned.1.call-update) | async-done | bytes 147472 | tf_op jit(solution)/shard_map/while/body/eval_jaxpr/reduce_scatter | solution.py:156
  457.3 7.2 all_gather.75
  469.8 22.6 %reduce-scatter.38.cloned.1.call-done = bf16[64,1152]{1,0:T(8,128)(2,1)} async-done(((bf16[256,1152]{1,0:T(8,128)(2,1)}), bf16[64,1152]{1,0:T(8,128)(2,1)}) %reduce-scatter.38.cloned.1.call-update) | async-done | bytes 147472 | tf_op jit(solution)/shard_map/while/body/eval_jaxpr/reduce_scatter | solution.py:156
  504.3 6.7 all_gather.74
  527.1 24.0 %reduce-scatter.36.cloned.1.call-done = bf16[64,1152]{1,0:T(8,128)(2,1)} async-done(((bf16[256,1152]{1,0:T(8,128)(2,1)}), bf16[64,1152]{1,0:T(8,128)(2,1)}) %reduce-scatter.36.cloned.1.call-update) | async-done | bytes 147472 | tf_op jit(solution)/shard_map/while/body/eval_jaxpr/reduce_scatter | solution.py:156
  554.3 7.1 all_gather.75
  566.8 22.6 %reduce-scatter.38.cloned.1.call-done = bf16[64,1152]{1,0:T(8,128)(2,1)} async-done(((bf16[256,1152]{1,0:T(8,128)(2,1)}), bf16[64,1152]{1,0:T(8,128)(2,1)}) %reduce-scatter.38.cloned.1.call-update) | async-done | bytes 147472 | tf_op jit(solution)/shard_map/while/body/eval_jaxpr/reduce_scatter | solution.py:156
  598.8 646.1 %while.58 = (s32[]{:T(128)}, bf16[64,1152]{1,0:T(8,128)(2,1)}, bf16[2,64,1152]{2,1,0:T(8,128)(2,1)}, f32[2,6912]{1,0:T(2,128)}, f32[4]{0:T(128)}, /*index=5*/f32...) while((s32[]{:T(128)}, bf16[64,1152]{1,0:T(8,128)(2,1)}, ...), condition=%wide.region_49.50_spmd.clone, body=%wide.region_11.49_spmd.clone.sunk | while | flops 5251735552 | bytes 176957456 | solution.py:350
  646.4 24.0 %reduce-scatter.40.cloned.1.call-done = bf16[64,1152]{1,0:T(8,128)(2,1)} async-done(((bf16[256,1152]{1,0:T(8,128)(2,1)}), bf16[64,1152]{1,0:T(8,128)(2,1)}) %reduce-scatter.40.cloned.1.call-update) | async-done | bytes 147472 | tf_op jit(solution)/shard_map/while/body/eval_jaxpr/reduce_scatter | solution.py:156
  673.7 7.2 all_gather.77
  688.3 21.9 %reduce-scatter.42.cloned.1.call-done = bf16[64,1152]{1,0:T(8,128)(2,1)} async-done(((bf16[256,1152]{1,0:T(8,128)(2,1)}), bf16[64,1152]{1,0:T(8,128)(2,1)}) %reduce-scatter.42.cloned.1.call-update) | async-done | bytes 147472 | tf_op jit(solution)/shard_map/while/body/eval_jaxpr/reduce_scatter | solution.py:156
  711.9 7.2 all_gather.78
  739.6 9.4 reduce-scatter.44.cloned.1.call-done
  753.9 7.1 all_gather.79
  794.1 20.5 %reduce-scatter.46.cloned.1.call-done = bf16[64,1152]{1,0:T(8,128)(2,1)} async-done(((bf16[256,1152]{1,0:T(8,128)(2,1)}), bf16[64,1152]{1,0:T(8,128)(2,1)}) %reduce-scatter.46.cloned.1.call-update) | async-done | bytes 147472 | tf_op jit(solution)/shard_map/while/body/eval_jaxpr/reduce_scatter | solution.py:167
  857.4 22.1 %reduce-scatter.40.cloned.1.call-done = bf16[64,1152]{1,0:T(8,128)(2,1)} async-done(((bf16[256,1152]{1,0:T(8,128)(2,1)}), bf16[64,1152]{1,0:T(8,128)(2,1)}) %reduce-scatter.40.cloned.1.call-update) | async-done | bytes 147472 | tf_op jit(solution)/shard_map/while/body/eval_jaxpr/reduce_scatter | solution.py:156
  882.9 7.1 all_gather.77
  897.5 21.9 %reduce-scatter.42.cloned.1.call-done = bf16[64,1152]{1,0:T(8,128)(2,1)} async-done(((bf16[256,1152]{1,0:T(8,128)(2,1)}), bf16[64,1152]{1,0:T(8,128)(2,1)}) %reduce-scatter.42.cloned.1.call-update) | async-done | bytes 147472 | tf_op jit(solution)/shard_map/while/body/eval_jaxpr/reduce_scatter | solution.py:156
  921.0 7.1 all_gather.78
  948.8 9.4 reduce-scatter.44.cloned.1.call-done
  963.0 7.1 all_gather.79
  1003.2 20.5 %reduce-scatter.46.cloned.1.call-done = bf16[64,1152]{1,0:T(8,128)(2,1)} async-done(((bf16[256,1152]{1,0:T(8,128)(2,1)}), bf16[64,1152]{1,0:T(8,128)(2,1)}) %reduce-scatter.46.cloned.1.call-update) | async-done | bytes 147472 | tf_op jit(solution)/shard_map/while/body/eval_jaxpr/reduce_scatter | solution.py:167
  1066.5 22.1 %reduce-scatter.40.cloned.1.call-done = bf16[64,1152]{1,0:T(8,128)(2,1)} async-done(((bf16[256,1152]{1,0:T(8,128)(2,1)}), bf16[64,1152]{1,0:T(8,128)(2,1)}) %reduce-scatter.40.cloned.1.call-update) | async-done | bytes 147472 | tf_op jit(solution)/shard_map/while/body/eval_jaxpr/reduce_scatter | solution.py:156
  1091.9 7.1 all_gather.77
  1106.5 21.9 %reduce-scatter.42.cloned.1.call-done = bf16[64,1152]{1,0:T(8,128)(2,1)} async-done(((bf16[256,1152]{1,0:T(8,128)(2,1)}), bf16[64,1152]{1,0:T(8,128)(2,1)}) %reduce-scatter.42.cloned.1.call-update) | async-done | bytes 147472 | tf_op jit(solution)/shard_map/while/body/eval_jaxpr/reduce_scatter | solution.py:156
  1130.1 7.1 all_gather.78
  1157.9 9.4 reduce-scatter.44.cloned.1.call-done
  1172.0 7.1 all_gather.79
  1212.3 20.5 %reduce-scatter.46.cloned.1.call-done = bf16[64,1152]{1,0:T(8,128)(2,1)} async-done(((bf16[256,1152]{1,0:T(8,128)(2,1)}), bf16[64,1152]{1,0:T(8,128)(2,1)}) %reduce-scatter.46.cloned.1.call-update) | async-done | bytes 147472 | tf_op jit(solution)/shard_map/while/body/eval_jaxpr/reduce_scatter | solution.py:167
  1284.0 15.5 reduce-scatter.32.cloned.1.call-done
  1304.7 14.7 psum.35
  1319.4 17.5 %all-reduce.25 = (f32[1,1728]{1,0:T(1,128)}, f32[1,4]{1,0:T(1,128)}, f32[1,9,288]{2,0,1:T(1,128)}, f32[1,1152]{1,0:T(1,128)}) all-reduce(f32[1,1728]{1,0:T(1,128)S(1)} %broadcast_in_dim.382, f32[1,4]{1,0:T(1,128)S(1)} %bitcast.625, f32[1,9,288]{2,0,1:T(1,128)S(1)} %broadcast_in_dim.388, ...), channel_id=1, replica_groups=mesh['dp'=4,'tensor'=4,'section'=2] {'dp'}, use_global_device_ids=true, to_apply=%region_54.55 | all-reduce | flops 5476 | bytes 43808 | tf_op jit(solution)/shard_map/psum | solution.py:394
  1338.8 40.7 %reduce-scatter.30.cloned.1.call-done = bf16[288,1152]{1,0:T(8,128)(2,1)} async-done(((bf16[1152,1152]{1,0:T(8,128)(2,1)}), bf16[288,1152]{1,0:T(8,128)(2,1)}) %reduce-scatter.30.cloned.1.call-update) | async-done | bytes 663568
  1384.9 49.2 %reduce-scatter.24.cloned.1.call-done = bf16[288,1152]{1,0:T(8,128)(2,1)} async-done(((bf16[1152,1152]{1,0:T(8,128)(2,1)}), bf16[288,1152]{1,0:T(8,128)(2,1)}) %reduce-scatter.24.cloned.1.call-update) | async-done | bytes 663568 | tf_op jit(solution)/shard_map/reduce_scatter | solution.py:385
  1436.4 52.5 %reduce-scatter.26.cloned.1.call-done = bf16[1152,288]{0,1:T(8,128)(2,1)} async-done(((bf16[1152,1152]{0,1:T(8,128)(2,1)}), bf16[1152,288]{0,1:T(8,128)(2,1)}) %reduce-scatter.26.cloned.1.call-update) | async-done | bytes 663568 | tf_op jit(solution)/shard_map/reduce_scatter | solution.py:388
  1491.2 75.7 %reduce-scatter.22.cloned.1.call-done = bf16[288,1728]{1,0:T(8,128)(2,1)} async-done(((bf16[1152,1728]{1,0:T(8,128)(2,1)}), bf16[288,1728]{1,0:T(8,128)(2,1)}) %reduce-scatter.22.cloned.1.call-update) | async-done | bytes 995344 | tf_op jit(solution)/shard_map/reduce_scatter | solution.py:373
  (1281 shorter events, 527.7 us)
Async XLA Ops:
  7.2 99.4 %all-gather.12.cloned.1.call-start = ((), (), s32[]{:S(2)}) async-start(), calls=%async_computation.16 | async-start | bytes 3317760 | tf_op jit(solution)/shard_map/all_gather | solution.py:129
  7.9 165.1 %all-gather.8.cloned.1.call-start = ((), (), s32[]{:S(2)}) async-start(), calls=%async_computation.14 | async-start | bytes 4423680 | tf_op jit(solution)/shard_map/all_gather | solution.py:125
  10.6 242.3 %all-gather.6.cloned.1.call-start = ((), (), s32[]{:S(2)}) async-start(), calls=%async_computation.13 | async-start | bytes 5160960 | tf_op jit(solution)/shard_map/all_gather | solution.py:124
  11.3 296.9 %all-gather.10.cloned.1.call-start = ((), (), s32[]{:S(2)}) async-start(), calls=%async_computation.15 | async-start | bytes 3317760 | tf_op jit(solution)/shard_map/all_gather | solution.py:128
  105.9 147.0 %copy-start.97 = (f32[2,576]{1,0:T(2,128)}, f32[2,576]{1,0:T(2,128)S(1)}, u32[]{:S(2)}) copy-start(f32[2,576]{1,0:T(2,128)S(1)} %get-tuple-element.1069) | copy-start | bytes 13828
  105.9 147.0 %copy-start.99 = (f32[2,576]{1,0:T(2,128)}, f32[2,576]{1,0:T(2,128)S(1)}, u32[]{:S(2)}) copy-start(f32[2,576]{1,0:T(2,128)S(1)} %get-tuple-element.1070) | copy-start | bytes 13828
  173.0 79.9 %copy-start.95 = (f32[2,1152]{1,0:T(2,128)S(1)}, f32[2,1152]{1,0:T(2,128)}, u32[]{:S(2)}) copy-start(f32[2,1152]{1,0:T(2,128)} %param.18) | copy-start | bytes 27652
  308.3 48.8 %reduce-scatter.36.cloned.1.call-start = ((), (), s32[]{:S(2)}) async-start(), calls=%async_computation.24 | async-start | bytes 737280 | tf_op jit(solution)/shard_map/while/body/eval_jaxpr/reduce_scatter | solution.py:156
  336.3 59.0 %reduce-scatter.38.cloned.1.call-start = ((), (), s32[]{:S(2)}) async-start(), calls=%async_computation.25 | async-start | bytes 737280 | tf_op jit(solution)/shard_map/while/body/eval_jaxpr/reduce_scatter | solution.py:156
  396.4 6.5 collective-permute-start
  402.8 51.2 %reduce-scatter.36.cloned.1.call-start = ((), (), s32[]{:S(2)}) async-start(), calls=%async_computation.24 | async-start | bytes 737280 | tf_op jit(solution)/shard_map/while/body/eval_jaxpr/reduce_scatter | solution.py:156
  430.0 62.4 %reduce-scatter.38.cloned.1.call-start = ((), (), s32[]{:S(2)}) async-start(), calls=%async_computation.25 | async-start | bytes 737280 | tf_op jit(solution)/shard_map/while/body/eval_jaxpr/reduce_scatter | solution.py:156
  493.4 6.5 collective-permute-start
  499.9 51.2 %reduce-scatter.36.cloned.1.call-start = ((), (), s32[]{:S(2)}) async-start(), calls=%async_computation.24 | async-start | bytes 737280 | tf_op jit(solution)/shard_map/while/body/eval_jaxpr/reduce_scatter | solution.py:156
  527.0 62.3 %reduce-scatter.38.cloned.1.call-start = ((), (), s32[]{:S(2)}) async-start(), calls=%async_computation.25 | async-start | bytes 737280 | tf_op jit(solution)/shard_map/while/body/eval_jaxpr/reduce_scatter | solution.py:156
  590.4 6.5 collective-permute-start
  615.2 55.2 %reduce-scatter.40.cloned.1.call-start = ((), (), s32[]{:S(2)}) async-start(), calls=%async_computation.26 | async-start | bytes 737280 | tf_op jit(solution)/shard_map/while/body/eval_jaxpr/reduce_scatter | solution.py:156
  646.4 63.8 %reduce-scatter.42.cloned.1.call-start = ((), (), s32[]{:S(2)}) async-start(), calls=%async_computation.27 | async-start | bytes 737280 | tf_op jit(solution)/shard_map/while/body/eval_jaxpr/reduce_scatter | solution.py:156
  671.5 78.8 %copy-start.78 = (f32[64]{0:T(128)}, f32[64]{0:T(128)S(1)}, u32[]{:S(2)}) copy-start(f32[64]{0:T(128)S(1)} %broadcast_multiply_fusion.21) | copy-start | bytes 772 | tf_op jit(solution)/shard_map/while
  672.6 77.7 %copy-start.94 = (f32[64]{0:T(128)}, f32[64]{0:T(128)S(1)}, u32[]{:S(2)}) copy-start(f32[64]{0:T(128)S(1)} %fusion.306) | copy-start | bytes 772 | tf_op jit(solution)/shard_map/while
  687.6 61.5 %reduce-scatter.44.cloned.1.call-start = ((), (), s32[]{:S(2)}) async-start(), calls=%async_computation.28 | async-start | bytes 737280 | tf_op jit(solution)/shard_map/while/body/eval_jaxpr/reduce_scatter | solution.py:167
  726.5 88.2 %reduce-scatter.46.cloned.1.call-start = ((), (), s32[]{:S(2)}) async-start(), calls=%async_computation.29 | async-start | bytes 737280 | tf_op jit(solution)/shard_map/while/body/eval_jaxpr/reduce_scatter | solution.py:167
  793.1 33.2 %copy-start.12 = (bf16[2,64,1152]{2,1,0:T(8,128)(2,1)S(1)}, bf16[2,64,1152]{2,1,0:T(8,128)(2,1)}, u32[]{:S(2)}) copy-start(bf16[2,64,1152]{2,1,0:T(8,128)(2,1)} %copy-done.11) | copy-start | bytes 884740 | tf_op jit(solution)/shard_map/while
  818.2 7.5 collective-permute-start.1
  826.3 53.2 %reduce-scatter.40.cloned.1.call-start = ((), (), s32[]{:S(2)}) async-start(), calls=%async_computation.26 | async-start | bytes 737280 | tf_op jit(solution)/shard_map/while/body/eval_jaxpr/reduce_scatter | solution.py:156
  857.4 61.9 %reduce-scatter.42.cloned.1.call-start = ((), (), s32[]{:S(2)}) async-start(), calls=%async_computation.27 | async-start | bytes 737280 | tf_op jit(solution)/shard_map/while/body/eval_jaxpr/reduce_scatter | solution.py:156
  880.6 78.7 %copy-start.78 = (f32[64]{0:T(128)}, f32[64]{0:T(128)S(1)}, u32[]{:S(2)}) copy-start(f32[64]{0:T(128)S(1)} %broadcast_multiply_fusion.21) | copy-start | bytes 772 | tf_op jit(solution)/shard_map/while
  881.8 77.6 %copy-start.94 = (f32[64]{0:T(128)}, f32[64]{0:T(128)S(1)}, u32[]{:S(2)}) copy-start(f32[64]{0:T(128)S(1)} %fusion.306) | copy-start | bytes 772 | tf_op jit(solution)/shard_map/while
  896.7 61.4 %reduce-scatter.44.cloned.1.call-start = ((), (), s32[]{:S(2)}) async-start(), calls=%async_computation.28 | async-start | bytes 737280 | tf_op jit(solution)/shard_map/while/body/eval_jaxpr/reduce_scatter | solution.py:167
  935.5 88.2 %reduce-scatter.46.cloned.1.call-start = ((), (), s32[]{:S(2)}) async-start(), calls=%async_computation.29 | async-start | bytes 737280 | tf_op jit(solution)/shard_map/while/body/eval_jaxpr/reduce_scatter | solution.py:167
  1002.2 33.3 %copy-start.12 = (bf16[2,64,1152]{2,1,0:T(8,128)(2,1)S(1)}, bf16[2,64,1152]{2,1,0:T(8,128)(2,1)}, u32[]{:S(2)}) copy-start(bf16[2,64,1152]{2,1,0:T(8,128)(2,1)} %copy-done.11) | copy-start | bytes 884740 | tf_op jit(solution)/shard_map/while
  1002.2 32.6 %copy-start.102 = (f32[4]{0:T(128)}, f32[4]{0:T(128)S(1)}, u32[]{:S(2)}) copy-start(f32[4]{0:T(128)S(1)} %fusion.320) | copy-start | bytes 52 | tf_op jit(solution)/shard_map/while
  1027.3 7.5 collective-permute-start.1
  1035.4 53.2 %reduce-scatter.40.cloned.1.call-start = ((), (), s32[]{:S(2)}) async-start(), calls=%async_computation.26 | async-start | bytes 737280 | tf_op jit(solution)/shard_map/while/body/eval_jaxpr/reduce_scatter | solution.py:156
  1066.5 61.9 %reduce-scatter.42.cloned.1.call-start = ((), (), s32[]{:S(2)}) async-start(), calls=%async_computation.27 | async-start | bytes 737280 | tf_op jit(solution)/shard_map/while/body/eval_jaxpr/reduce_scatter | solution.py:156
  1089.7 78.8 %copy-start.78 = (f32[64]{0:T(128)}, f32[64]{0:T(128)S(1)}, u32[]{:S(2)}) copy-start(f32[64]{0:T(128)S(1)} %broadcast_multiply_fusion.21) | copy-start | bytes 772 | tf_op jit(solution)/shard_map/while
  1090.9 77.6 %copy-start.94 = (f32[64]{0:T(128)}, f32[64]{0:T(128)S(1)}, u32[]{:S(2)}) copy-start(f32[64]{0:T(128)S(1)} %fusion.306) | copy-start | bytes 772 | tf_op jit(solution)/shard_map/while
  1105.8 61.4 %reduce-scatter.44.cloned.1.call-start = ((), (), s32[]{:S(2)}) async-start(), calls=%async_computation.28 | async-start | bytes 737280 | tf_op jit(solution)/shard_map/while/body/eval_jaxpr/reduce_scatter | solution.py:167
  1144.7 88.1 %reduce-scatter.46.cloned.1.call-start = ((), (), s32[]{:S(2)}) async-start(), calls=%async_computation.29 | async-start | bytes 737280 | tf_op jit(solution)/shard_map/while/body/eval_jaxpr/reduce_scatter | solution.py:167
  1211.3 33.2 %copy-start.12 = (bf16[2,64,1152]{2,1,0:T(8,128)(2,1)S(1)}, bf16[2,64,1152]{2,1,0:T(8,128)(2,1)}, u32[]{:S(2)}) copy-start(bf16[2,64,1152]{2,1,0:T(8,128)(2,1)} %copy-done.11) | copy-start | bytes 884740 | tf_op jit(solution)/shard_map/while
  1236.4 7.5 collective-permute-start.1
  1244.9 32.2 %reduce-scatter.28.cloned.1.call-start = ((), (), s32[]{:S(2)}) async-start(), calls=%async_computation.20 | async-start | bytes 2211840
  1247.5 52.0 %reduce-scatter.32.cloned.1.call-start = ((), (), s32[]{:S(2)}) async-start(), calls=%async_computation.22 | async-start | bytes 368640
  1248.8 88.1 %reduce-scatter.34.cloned.1.call-start = ((), (), s32[]{:S(2)}) async-start(), calls=%async_computation.23 | async-start | bytes 1105920
  1252.0 127.5 %reduce-scatter.30.cloned.1.call-start = ((), (), s32[]{:S(2)}) async-start(), calls=%async_computation.21 | async-start | bytes 3317760
  1266.3 167.9 %reduce-scatter.24.cloned.1.call-start = ((), (), s32[]{:S(2)}) async-start(), calls=%async_computation.18 | async-start | bytes 3317760 | tf_op jit(solution)/shard_map/reduce_scatter | solution.py:385
  1272.4 216.6 %reduce-scatter.26.cloned.1.call-start = ((), (), s32[]{:S(2)}) async-start(), calls=%async_computation.19 | async-start | bytes 3317760 | tf_op jit(solution)/shard_map/reduce_scatter | solution.py:388
  1277.1 289.8 %reduce-scatter.22.cloned.1.call-start = ((), (), s32[]{:S(2)}) async-start(), calls=%async_computation.17 | async-start | bytes 5160960 | tf_op jit(solution)/shard_map/reduce_scatter | solution.py:373
  (289 other events, 2467.7 us)
Sparse Core Ops, SparseCore 0:
  9.6 90.9 all-gather.11
  102.7 70.2 all-gather.7
  174.6 78.2 all-gather.5
  254.3 53.8 all-gather.9
  336.4 20.5 reduce-scatter.35
  372.9 22.4 reduce-scatter.37
  430.1 23.8 reduce-scatter.35
  469.9 22.4 reduce-scatter.37
  527.1 23.8 reduce-scatter.35
  566.9 22.4 reduce-scatter.37
  646.5 23.8 reduce-scatter.39
  687.7 22.4 reduce-scatter.41
  726.6 22.4 reduce-scatter.43
  792.2 22.4 reduce-scatter.45
  857.5 22.0 reduce-scatter.39
  896.9 22.4 reduce-scatter.41
  935.7 22.4 reduce-scatter.43
  1001.2 22.4 reduce-scatter.45
  1066.6 21.9 reduce-scatter.39
  1105.9 22.4 reduce-scatter.41
  1144.8 22.4 reduce-scatter.43
  1210.3 22.4 reduce-scatter.45
  1248.3 28.4 reduce-scatter.27
  1279.6 19.8 reduce-scatter.31
  1302.5 22.8 reduce-scatter.33
  1327.7 51.7 reduce-scatter.29
  1381.8 52.3 reduce-scatter.23
  1436.6 52.3 reduce-scatter.25
  1491.4 75.4 reduce-scatter.21
where the time goes:
time: 1590 us; the launch traced here: 1580 us
  waiting for transfers between devices  802 us (50%)
  blocking collectives  250 us (16%)
  local copies, waits for them, and re-layouts  166 us (10%)
  matrix products  164 us (10%)
  other arithmetic  135 us (8%)
  loops' own time  29.5 us (2%)
    reduce_scatter x12, waiting for transfers between devices, sum_rows(): lax.psum_scatter(term(jnp.int32(0), local_rows * lax.axis_size('tensor'))...  270 us
    reduce_scatter x6, waiting for transfers between devices, sum_grads(): lax.psum_scatter(term(jnp.int32(0), local_rows * lax.axis_size('tensor'))...  89.6 us
    all_gather x12, blocking collectives, gather_rows(): return lax.all_gather(values, 'tensor', axis=0, tiled=True)  83.8 us
    reduce_scatter x1, waiting for transfers between devices, per_device(): lax.psum_scatter(grad_ada.astype(jnp.bfloat16), 'dp', scatter_dimension=0...  75.7 us
    all_gather x1, waiting for transfers between devices, per_device(): lax.all_gather(ada_weight, 'dp', axis=1, tiled=True)  72.6 us
    all_gather x1, waiting for transfers between devices, per_device(): lax.all_gather(in_weight, 'dp', axis=2, tiled=True)  61.2 us
    all_gather x1, blocking collectives, per_device(): lax.all_gather(out_weight, 'dp', axis=2, tiled=True)  59.5 us
    unnamed x15, waiting for transfers between devices  58.2 us
  transfers between devices with their start and end apart: 35, of which 32 were waited for; matrix products, arithmetic and copies ran while one was open for 8% of the time, Pallas kernels for 0%

commit v1 on v0

v1 whole, which is shorter than its diff:
```python
import functools
import math

import jax
import jax.numpy as jnp
from jax import lax
from jax.experimental import pallas as pl
from jax.experimental.pallas import tpu as pltpu
from jax.sharding import PartitionSpec as P

SIDE = 16
PATCHES = SIDE * SIDE
LANES = 128
F32 = jnp.float32
BF16 = jnp.bfloat16
HIGHEST = lax.Precision.HIGHEST
PLANE = ("tensor", "section")


def call(body, outs, *args, scalars=0, flops=0, scratch=(), after=(), saved=()):
    count, waits, many = len(args), len(after), len(outs)

    def kernel(*refs):
        ins, out_refs = refs[:count], list(refs[count + waits : count + waits + many])
        own = refs[count + waits + many : count + waits + many + len(scratch)]
        held = refs[count + waits + many + len(scratch) :]
        copies = []
        for i, at in enumerate(saved):
            copies.append(pltpu.make_async_copy(held[i], out_refs[at], held[-1].at[i]))
            out_refs[at] = held[i]
        started = []

        def flush(*places):
            for at in places:
                copies[saved.index(at)].start()
                started.append(at)

        if saved:
            body(flush, *ins, *out_refs, *own)
        else:
            body(*ins, *out_refs, *own)
        flush(*[at for at in saved if at not in started])
        for copy in copies:
            copy.wait()

    moved = sum(a.size * a.dtype.itemsize for a in args)
    moved += sum(math.prod(o.shape) * o.dtype.itemsize for o in outs)
    specs = [pl.BlockSpec(memory_space=pltpu.SMEM)] * scalars
    specs += [pl.BlockSpec(memory_space=pltpu.VMEM)] * (count - scalars)
    specs += [pl.BlockSpec(memory_space=pl.ANY)] * waits
    spaces = [pltpu.HBM if i in saved else pltpu.VMEM for i in range(many)]
    hold = [pltpu.VMEM(outs[i].shape, outs[i].dtype) for i in saved]
    if saved:
        hold.append(pltpu.SemaphoreType.DMA((len(saved),)))
    return pl.pallas_call(
        kernel,
        out_shape=tuple(outs),
        in_specs=specs,
        out_specs=tuple(pl.BlockSpec(memory_space=space) for space in spaces),
        scratch_shapes=[*scratch, *hold],
        compiler_params=pltpu.CompilerParams(vmem_limit_bytes=6 * 2**20 + moved * 3 // 2),
        cost_estimate=pl.CostEstimate(flops=flops, bytes_accessed=moved, transcendentals=0),
    )(*args, *after)


def out(shape, dtype):
    return jax.ShapeDtypeStruct(shape, dtype)


def mm(a, b):
    return lax.dot_general(a, b, (((1,), (0,)), ((), ())), preferred_element_type=F32)


def mm_nt(a, b):
    return lax.dot_general(a, b, (((1,), (1,)), ((), ())), preferred_element_type=F32)


def mm_tn(a, b):
    return lax.dot_general(a, b, (((0,), (0,)), ((), ())), preferred_element_type=F32)


def normalize(v):
    centered = v - jnp.mean(v, axis=-1, keepdims=True)
    scale = lax.rsqrt(jnp.mean(centered * centered, axis=-1, keepdims=True) + 1e-06)
    return centered * scale, scale


def norm_grad(hat, rstd, grad):
    inner = jnp.mean(grad * hat, axis=-1, keepdims=True)
    return rstd * (grad - jnp.mean(grad, axis=-1, keepdims=True) - hat * inner)


def gather_total(pieces):
    total = pieces[0][...].astype(F32)
    for piece in pieces[1:]:
        total = total + piece[...].astype(F32)
    return total


def rows_sum(v):
    return jnp.sum(v, axis=0, keepdims=True)


def gelu_terms(x):
    k = math.sqrt(2.0 / math.pi)
    th = jnp.tanh(k * (x + 0.044715 * x * x * x))
    value = 0.5 * x * (1.0 + th)
    slope = 0.5 * (1.0 + th) + 0.5 * x * (1.0 - th * th) * k * (1.0 + 3 * 0.044715 * x * x)
    return value, slope


def start_kernel(x_ref, mod_ref, n_ref):
    for m in range(x_ref.shape[0]):
        hat, _ = normalize(x_ref[m].astype(F32))
        n_ref[m] = (hat * (1.0 + mod_ref[m, 1:2]) + mod_ref[m, 0:1]).astype(BF16)


def scale_rows_kernel(g_ref, mod_ref, o_ref):
    for m in range(g_ref.shape[0]):
        o_ref[m] = (mod_ref[m, 5:6] * g_ref[m].astype(F32)).astype(BF16)


def after_attn_kernel(flush, p0, p1, p2, p3, x_ref, mod_ref, att_ref, aft_ref, n_ref):
    for m in range(x_ref.shape[0]):
        att = gather_total([p.at[m] for p in (p0, p1, p2, p3)])
        aft = x_ref[m].astype(F32) + mod_ref[m, 2:3] * att
        hat, _ = normalize(aft)
        att_ref[m] = att
        aft_ref[m] = aft
        n_ref[m] = (hat * (1.0 + mod_ref[m, 4:5]) + mod_ref[m, 3:4]).astype(BF16)


def between_kernel(p0, p1, p2, p3, aft_ref, mod_ref, next_ref, mlp_ref, x_ref, n_ref):
    for m in range(aft_ref.shape[0]):
        mlp = gather_total([p.at[m] for p in (p0, p1, p2, p3)])
        x = (aft_ref[m] + mod_ref[m, 5:6] * mlp).astype(BF16)
        hat, _ = normalize(x.astype(F32))
        mlp_ref[m] = mlp
        x_ref[m] = x
        n_ref[m] = (hat * (1.0 + next_ref[m, 1:2]) + next_ref[m, 0:1]).astype(BF16)


def end_kernel(p0, p1, p2, p3, aft_ref, mod_ref, g_ref, x_ref, gate_ref):
    for m in range(aft_ref.shape[0]):
        mlp = gather_total([p.at[m] for p in (p0, p1, p2, p3)])
        x_ref[m] = (aft_ref[m] + mod_ref[m, 5:6] * mlp).astype(BF16)
        gate_ref[m] = rows_sum(g_ref[m].astype(F32) * mlp)


def back_mlp_rows_kernel(p0, p1, p2, p3, g_ref, aft_ref, att_ref, mod_ref, ga_ref, gt_ref, gm_ref):
    for m in range(aft_ref.shape[0]):
        gn = gather_total([p.at[m] for p in (p0, p1, p2, p3)])
        hat, rstd = normalize(aft_ref[m])
        grad = g_ref[m].astype(F32) + norm_grad(hat, rstd, gn * (1.0 + mod_ref[m, 4:5]))
        ga_ref[m] = grad
        gt_ref[m] = (mod_ref[m, 2:3] * grad).astype(BF16)
        gm_ref[m, 0:1] = rows_sum(grad * att_ref[m])
        gm_ref[m, 1:2] = rows_sum(gn)
        gm_ref[m, 2:3] = rows_sum(gn * hat)


def back_attn_rows(pieces, ga_ref, x_ref, mod_ref, some_ref, gate_ref, gm_ref, m):
    gn = gather_total([p.at[m] for p in pieces])
    hat, rstd = normalize(x_ref[m].astype(F32))
    grad = ga_ref[m] + norm_grad(hat, rstd, gn * (1.0 + mod_ref[m, 1:2]))
    gm_ref[m, 0:1] = rows_sum(gn)
    gm_ref[m, 1:2] = rows_sum(gn * hat)
    gm_ref[m, 2:5] = some_ref[m]
    gm_ref[m, 5:6] = gate_ref[m]
    return grad.astype(BF16)


def back_between_kernel(
    p0, p1, p2, p3, ga_ref, x_ref, mod_ref, some_ref, gate_ref, prev_ref, mlp_ref, g_ref, gmlp_ref, gm_ref, next_ref
):
    for m in range(x_ref.shape[0]):
        grad = back_attn_rows((p0, p1, p2, p3), ga_ref, x_ref, mod_ref, some_ref, gate_ref, gm_ref, m)
        g_ref[m] = grad
        wide = grad.astype(F32)
        gmlp_ref[m] = (prev_ref[m, 5:6] * wide).astype(BF16)
        next_ref[m] = rows_sum(wide * mlp_ref[m])


def back_end_kernel(p0, p1, p2, p3, ga_ref, x_ref, mod_ref, some_ref, gate_ref, g_ref, gm_ref):
    for m in range(x_ref.shape[0]):
        g_ref[m] = back_attn_rows((p0, p1, p2, p3), ga_ref, x_ref, mod_ref, some_ref, gate_ref, gm_ref, m)


def scan_mask(columns_first):
    def place(number):
        if columns_first:
            return (number % SIDE) * SIDE + number // SIDE
        return number

    shape = (PATCHES, PATCHES)
    later = place(lax.broadcasted_iota(jnp.int32, shape, 0))
    return later >= place(lax.broadcasted_iota(jnp.int32, shape, 1))


def grid_column():
    return lax.broadcasted_iota(jnp.int32, (PATCHES, 1), 0) % SIDE


def side_shifts(a, column):
    left = jnp.where(column == 0, 0.0, pltpu.roll(a, 1, 0))
    right = jnp.where(column == SIDE - 1, 0.0, pltpu.roll(a, PATCHES - 1, 0))
    return left, a, right


def convolve(shifted, tap):
    sums = []
    for row in range(3):
        terms = [shifted[col] * tap(3 * row + col) for col in range(3)]
        sums.append(terms[0] + terms[1] + terms[2])
    zeros = jnp.zeros((SIDE, sums[0].shape[1]), F32)
    above = jnp.concatenate([zeros, sums[0][:-SIDE]], axis=0)
    below = jnp.concatenate([sums[2][SIDE:], zeros], axis=0)
    return shifted[1] + sums[1] + above + below


def tap_grads(shifted, grad):
    found = []
    for row in range(3):
        for col in range(3):
            if row == 0:
                product = shifted[col][:-SIDE] * grad[SIDE:]
            elif row == 1:
                product = shifted[col] * grad
            else:
                product = shifted[col][SIDE:] * grad[:-SIDE]
            found.append(rows_sum(product))
    return found


def lane_sets(width, first, head_width, heads):
    lane = lax.broadcasted_iota(jnp.int32, (1, width), 1)
    return [
        (lane >= first + h * head_width) & (lane < first + (h + 1) * head_width)
        for h in range(heads)
    ]


def decay_parts(logits, mask, gate_lane, heads):
    rates = -(jnp.maximum(logits, 0.0) + jnp.log1p(jnp.exp(-jnp.abs(logits))))
    ones = jnp.where(mask, 1.0, 0.0)
    totals = lax.dot_general(
        ones, rates, (((1,), (0,)), ((), ())), precision=HIGHEST, preferred_element_type=F32
    )
    turned = totals.T
    decays = []
    for h in range(heads):
        at = gate_lane + h
        spans = jnp.where(mask, totals[:, at : at + 1] - turned[at : at + 1, :], -1e30)
        w = jnp.exp(spans)
        decays.append((w, jnp.sum(w, axis=1, keepdims=True)))
    return decays, ones


def send_order(k):
    return (0, 1, None, None, 2, 3, None, None)[k], (None, None, 0, 1, None, None, 2, 3)[k]


def write_pieces(me, total_ref, other_ref, own_refs):
    rows = total_ref.shape[1] // 8
    for k in range(8):
        spot = pl.ds(pl.multiple_of(jnp.bitwise_xor(me, k) * rows, rows), rows)
        own, other = send_order(k)
        if own is None:
            other_ref[other] = total_ref[:, spot, :]
        else:
            own_refs[own][...] = total_ref[:, spot, :]


def each_shard(refs):
    own, core, three, crossed = refs
    return (own, three.at[0], core, crossed.at[0], three.at[1], three.at[2], crossed.at[1], crossed.at[2])


def gather_pieces(me, shard_refs, full_ref):
    rows = full_ref.shape[1] // 8
    for k, shard in enumerate(each_shard(shard_refs)):
        spot = pl.ds(pl.multiple_of(jnp.bitwise_xor(me, k) * rows, rows), rows)
        full_ref[:, spot, :] = shard[...]


def tail_spots(heads):
    return (0, 32, 48, 64, 80)


def join_tail(packed, piece, tails, lane):
    tile = packed[:, piece * LANES : (piece + 1) * LANES]
    return jnp.concatenate([tile, pltpu.roll(tails, (LANES - lane) % LANES, 1)], axis=1)


def lanes():
    return lax.broadcasted_iota(jnp.int32, (1, LANES), 1)


def half_tiles(tiles, at):
    if at == 0:
        return tiles[0], tiles[1]
    shift = 2 * LANES - at
    first = jnp.where(lanes() < shift, pltpu.roll(tiles[1], shift, 1), pltpu.roll(tiles[2], shift, 1))
    return first, pltpu.roll(tiles[2], shift, 1)


def pack_attn_kernel(cfg, sec_ref, in_ref, gate_ref, out_ref, keep_ref, send_ref):
    heads, channels = cfg
    spots = tail_spots(heads)
    tail = channels - LANES
    rows = in_ref.shape[1]
    short = jnp.zeros((rows, 3 * LANES - 2 * channels), F32)
    keep_first = sec_ref[0] == 0
    lane = lanes()
    tails = [gate_ref[...], pltpu.roll(gate_ref[...], LANES - heads, 1)]
    tails = [
        jnp.where((lane >= tail) & (lane < tail + heads), pltpu.roll(v, tail, 1), 0.0) for v in tails
    ]
    for j in range(5):
        ref = out_ref if j == 4 else in_ref.at[j]
        tiles = [ref[:, :LANES].astype(F32), ref[:, LANES : 2 * LANES].astype(F32)]
        tiles.append(jnp.concatenate([ref[:, 2 * LANES :].astype(F32), short], axis=1))
        whole = []
        for h in range(2):
            tile, rest = half_tiles(tiles, h * channels)
            whole.append(tile)
            tails[h] = tails[h] + pltpu.roll(jnp.where(lane < tail, rest, 0.0), spots[j], 1)
        cols = slice(j * LANES, (j + 1) * LANES)
        keep_ref[:, cols] = jnp.where(keep_first, whole[0], whole[1]).astype(BF16)
        send_ref[:, cols] = jnp.where(keep_first, whole[1], whole[0]).astype(BF16)
    keep_ref[:, 5 * LANES :] = jnp.where(keep_first, tails[0], tails[1]).astype(BF16)
    send_ref[:, 5 * LANES :] = jnp.where(keep_first, tails[1], tails[0]).astype(BF16)


def unpack_attn_kernel(cfg, sec_ref, mine_ref, recv_ref, in_ref, gate_ref, out_ref):
    heads, channels = cfg
    spots = tail_spots(heads)
    tail = channels - LANES
    mine_first = sec_ref[0] == 0
    lane = lanes()
    shift = channels - LANES

    def both(cols):
        mine, recv = mine_ref[:, cols], recv_ref[:, cols].astype(F32)
        return jnp.where(mine_first, mine, recv), jnp.where(mine_first, recv, mine)

    low_tails, high_tails = both(slice(5 * LANES, 6 * LANES))
    for j in range(5):
        ref = out_ref if j == 4 else in_ref.at[j]
        low, high = both(slice(j * LANES, (j + 1) * LANES))
        ref[:, :LANES] = low
        high = pltpu.roll(high, shift, 1)
        low_tail = pltpu.roll(low_tails, (LANES - spots[j]) % LANES, 1)
        high_tail = pltpu.roll(high_tails, (LANES - spots[j] + shift) % LANES, 1)
        ref[:, LANES : 2 * LANES] = jnp.where(lane < tail, low_tail, high)
        last = jnp.where(lane < shift, high, high_tail)
        ref[:, 2 * LANES :] = last[:, : 2 * channels - 2 * LANES]
    low_gate = pltpu.roll(low_tails, LANES - tail, 1)
    high_gate = pltpu.roll(high_tails, LANES - tail + heads, 1)
    gate_ref[...] = jnp.where(lane < heads, low_gate, high_gate)[:, : 2 * heads]


def attn_forward_kernel(cfg, flush, me_ref, *refs):
    columns_first, heads, head_width = cfg
    shards, (w_ref, gb_ref, tap_ref) = refs[:4], refs[4:7]
    n_ref, proj_ref, log_ref, attn_ref, mix_ref, other_ref = refs[7:13]
    own_refs, total_ref = refs[13:17], refs[17]
    me = me_ref[0]
    wide = 2 * LANES
    gate_lane = heads * head_width - LANES
    spots = tail_spots(heads)
    mask = scan_mask(columns_first)
    column = grid_column()
    sets = lane_sets(wide, 0, head_width, heads)
    gather_pieces(me, shards, n_ref)
    flush(0)
    for m in range(n_ref.shape[0]):
        projected = mm(n_ref[m], w_ref[:, : 4 * LANES])
        tails = mm(n_ref[m], w_ref[:, 5 * LANES :])
        logits = tails + gb_ref[...]
        log_ref[m] = logits
        decays, _ = decay_parts(logits, mask, gate_lane, heads)
        query, key, value, gate = (join_tail(projected, j, tails, spots[j]) for j in range(4))
        in_head = sets[0]
        for own in sets[1:]:
            in_head = in_head | own
        query, key, value = (jnp.where(in_head, v, 0.0).astype(BF16) for v in (query, key, value))
        gate = gate.astype(BF16)
        for j, v in enumerate((query, key, value, gate)):
            proj_ref[m, :, j * wide : (j + 1) * wide] = v
        attn = None
        for h in range(heads):
            w, mass = decays[h]
            raw = mm_nt(jnp.where(sets[h], query, jnp.zeros_like(query)), key)
            scores = (raw * head_width ** (-0.5) * w).astype(BF16)
            normed = mm(scores, value) * lax.rsqrt(mass)
            attn = jnp.where(sets[h], normed, 0.0 if attn is None else attn)
        attn_ref[m] = attn
        spread = convolve(side_shifts(attn, column), lambda i: tap_ref[i : i + 1, :])
        gate = gate.astype(F32)
        mixed = spread * (gate * jax.nn.sigmoid(gate))
        mixed = jnp.where(in_head, mixed, 0.0)
        mixed = jnp.concatenate(
            [mixed[:, :LANES], pltpu.roll(mixed[:, LANES:], spots[4], 1)], axis=1
        ).astype(BF16)
        mix_ref[m] = mixed
        if m == n_ref.shape[0] - 1:
            flush(1, 2, 3, 4)
        total_ref[m] = mm_nt(mixed, w_ref[:, 4 * LANES :]).astype(BF16)
    write_pieces(me, total_ref, other_ref, own_refs)


def attn_backward_kernel(cfg, me_ref, *refs):
    columns_first, heads, head_width = cfg
    shards, (proj_ref, log_ref, attn_ref, w_ref, tap_ref) = refs[:4], refs[4:9]
    g_ref, gproj_ref, gtap_ref, other_ref = refs[9:13]
    own_refs, total_ref = refs[13:17], refs[17]
    me = me_ref[0]
    wide = 2 * LANES
    gate_lane = heads * head_width - LANES
    spots = tail_spots(heads)
    scale = head_width ** (-0.5)
    mask = scan_mask(columns_first)
    column = grid_column()
    sets = lane_sets(wide, 0, head_width, heads)
    gate_sets = lane_sets(LANES, gate_lane, 1, heads)
    sublane = lax.broadcasted_iota(jnp.int32, (LANES, 1), 0)
    in_head = sets[0]
    for own in sets[1:]:
        in_head = in_head | own
    gather_pieces(me, shards, g_ref)
    gtap_ref[...] = jnp.zeros(gtap_ref.shape, F32)
    for m in range(g_ref.shape[0]):
        g_packed = mm(g_ref[m], w_ref[:, 4 * LANES :])
        g_mixed = jnp.where(in_head, join_tail(g_packed, 0, g_packed[:, LANES:], spots[4]), 0.0)
        query, key, value, gate = (proj_ref[m, :, j * wide : (j + 1) * wide] for j in range(4))
        gate = gate.astype(F32)
        sig = jax.nn.sigmoid(gate)
        attn = attn_ref[m]
        shifted = side_shifts(attn, column)
        spread = convolve(shifted, lambda i: tap_ref[i : i + 1, :])
        g_spread = g_mixed * (gate * sig)
        g_gate = g_mixed * spread * (sig * (1.0 + gate * (1.0 - sig)))
        for i, grad in enumerate(tap_grads(shifted, g_spread)):
            gtap_ref[i : i + 1, :] = grad if m == 0 else gtap_ref[i : i + 1, :] + grad
        g_attn = convolve(side_shifts(g_spread, column), lambda i: tap_ref[8 - i : 9 - i, :])
        logits = log_ref[m]
        decays, ones = decay_parts(logits, mask, gate_lane, heads)
        g_query = g_key = g_value = 0.0
        across = jnp.zeros((PATCHES, LANES), F32)
        down = jnp.zeros((LANES, PATCHES), F32)
        for h in range(heads):
            w, mass = decays[h]
            own_query = jnp.where(sets[h], query, jnp.zeros_like(query))
            raw = mm_nt(own_query, key) * scale
            own_grad = jnp.where(sets[h], g_attn, 0.0)
            g_mass = -0.5 * jnp.sum(own_grad * attn, axis=1, keepdims=True) / mass
            g_out = (own_grad * lax.rsqrt(mass)).astype(BF16)
            g_value = g_value + mm_tn((raw * w).astype(BF16), g_out)
            g_scores = mm_nt(g_out, value)
            g_raw = (g_scores * w * scale).astype(BF16)
            g_query = jnp.where(sets[h], mm(g_raw, key), g_query)
            g_key = g_key + mm_tn(g_raw, own_query)
            g_span = (g_scores * raw + g_mass) * w
            across = jnp.where(gate_sets[h], jnp.sum(g_span, axis=1, keepdims=True), across)
            down = jnp.where(sublane == gate_lane + h, rows_sum(g_span), down)
        g_rates = lax.dot_general(
            ones,
            across - down.T,
            (((0,), (0,)), ((), ())),
            precision=HIGHEST,
            preferred_element_type=F32,
        )
        g_logits = (-g_rates * jax.nn.sigmoid(logits)).astype(BF16).astype(F32)
        g_bias = rows_sum(g_logits)
        gtap_ref[9:10, :LANES] = g_bias if m == 0 else gtap_ref[9:10, :LANES] + g_bias
        tails = g_logits
        for j, v in enumerate((g_query, g_key, g_value, g_gate)):
            gproj_ref[m, :, j * LANES : (j + 1) * LANES] = v[:, :LANES].astype(BF16)
            tails = tails + pltpu.roll(v[:, LANES:], spots[j], 1)
        gproj_ref[m, :, 4 * LANES :] = tails.astype(BF16)
        total = mm_nt(gproj_ref[m, :, : 4 * LANES], w_ref[:, : 4 * LANES])
        total = total + mm_nt(gproj_ref[m, :, 4 * LANES :], w_ref[:, 5 * LANES :])
        total_ref[m] = total.astype(BF16)
    write_pieces(me, total_ref, other_ref, own_refs)


def attn_weights_kernel(n_ref, gproj_ref, g_ref, mix_ref, gw_ref):
    for part in range(2):
        cols = slice(part * 2 * LANES, (part + 1) * 2 * LANES)
        total = mm_tn(n_ref[0], gproj_ref[0, :, cols])
        for m in range(1, n_ref.shape[0]):
            total = total + mm_tn(n_ref[m], gproj_ref[m, :, cols])
        gw_ref[:, cols] = total.astype(BF16)
    total = mm_tn(g_ref[0], mix_ref[0])
    tails = mm_tn(n_ref[0], gproj_ref[0, :, 4 * LANES :])
    for m in range(1, n_ref.shape[0]):
        total = total + mm_tn(g_ref[m], mix_ref[m])
        tails = tails + mm_tn(n_ref[m], gproj_ref[m, :, 4 * LANES :])
    gw_ref[:, 4 * LANES : 5 * LANES] = total[:, :LANES].astype(BF16)
    gw_ref[:, 5 * LANES :] = (total[:, LANES:] + tails).astype(BF16)


def stack_shards(shards, full_ref):
    for k, shard in enumerate(each_shard(shards)):
        images, rows, width = shard.shape
        full_ref[k * images * rows : (k + 1) * images * rows, :] = shard[...].reshape(
            images * rows, width
        )


def put_shard(k, value, shape, other_ref, own_refs):
    own, other = send_order(k)
    if own is None:
        other_ref[other] = value.astype(BF16).reshape(shape)
    else:
        own_refs[own][...] = value.astype(BF16).reshape(shape)


def put_shards(total, shape, other_ref, own_refs):
    rows = total.shape[0] // 8
    for k in range(8):
        put_shard(k, total[k * rows : (k + 1) * rows], shape, other_ref, own_refs)


def mlp_forward_kernel(left, flush, *refs):
    shards, (w_ref, ub_ref) = refs[:4], refs[4:6]
    n_ref, pre_ref, hid_ref, other_ref = refs[6:10]
    own_refs = refs[10:14]
    main = (w_ref.shape[1] - LANES) // 2
    stack_shards(shards, n_ref)
    flush(0)
    n = n_ref[...]
    pre = mm(n, w_ref[:, :main]) + ub_ref[:, :main]
    pre_ref[:, :main] = pre
    hidden = gelu_terms(pre)[0].astype(BF16)
    hid_ref[:, :main] = hidden
    last = mm(n, w_ref[:, 2 * main :]) + ub_ref[:, main:]
    pre_ref[:, main:] = last
    lane = lax.broadcasted_iota(jnp.int32, (1, LANES), 1)
    tail = jnp.where(lane < left, gelu_terms(last)[0], 0.0)
    tail = pltpu.roll(tail, LANES - left, 1).astype(BF16)
    hid_ref[:, main:] = tail
    flush(1, 2)
    total = mm_nt(hidden, w_ref[:, main : 2 * main]) + mm_nt(tail, w_ref[:, 2 * main :])
    put_shards(total, shards[0].shape, other_ref, own_refs)


def mlp_backward_kernel(left, *refs):
    shards, (pre_ref, w_ref) = refs[:4], refs[4:6]
    g_ref, gpre_ref, gub_ref, other_ref = refs[6:10]
    own_refs = refs[10:14]
    main = (w_ref.shape[1] - LANES) // 2
    stack_shards(shards, g_ref)
    g = g_ref[...]
    g_pre = mm(g, w_ref[:, main : 2 * main]) * gelu_terms(pre_ref[:, :main])[1]
    g_pre = g_pre.astype(BF16)
    gpre_ref[:, :main] = g_pre
    gub_ref[:, :main] = rows_sum(g_pre.astype(F32))
    lane = lax.broadcasted_iota(jnp.int32, (1, LANES), 1)
    last = pltpu.roll(mm(g, w_ref[:, 2 * main :]), left, 1) * gelu_terms(pre_ref[:, main:])[1]
    last = jnp.where(lane < left, last, 0.0).astype(BF16)
    gpre_ref[:, main:] = last
    gub_ref[:, main:] = rows_sum(last.astype(F32))
    total = mm_nt(g_pre, w_ref[:, :main]) + mm_nt(last, w_ref[:, 2 * main :])
    put_shards(total, shards[0].shape, other_ref, own_refs)


def mlp_weights_kernel(n_ref, gpre_ref, g_ref, hid_ref, gw_ref):
    main = gpre_ref.shape[1] - LANES
    gw_ref[:, :main] = mm_tn(n_ref[...], gpre_ref[:, :main]).astype(BF16)
    gw_ref[:, main : 2 * main] = mm_tn(g_ref[...], hid_ref[:, :main]).astype(BF16)
    last = mm_tn(n_ref[...], gpre_ref[:, main:]) + mm_tn(g_ref[...], hid_ref[:, main:])
    gw_ref[:, 2 * main :] = last.astype(BF16)


def swap(value, tensor_bits, section_bit):
    tensors, sections = lax.axis_size("tensor"), lax.axis_size("section")
    route = [
        (t * sections + s, (t ^ tensor_bits) * sections + (s ^ section_bit))
        for t in range(tensors)
        for s in range(sections)
    ]
    return lax.ppermute(value, PLANE, route)


def gather_plane(own):
    core = swap(own, 1, 0)
    xy, x, y = swap(own, 2, 1), swap(own, 0, 1), swap(own, 2, 0)
    three = jnp.stack([x, y, xy])
    return own, core, three, swap(three, 1, 0)


def scatter_plane(other, own):
    received = swap(other, 1, 0)
    sums = [(o.astype(F32) + received[j].astype(F32)).astype(BF16) for j, o in enumerate(own)]
    return (sums[0], swap(sums[3], 2, 1), swap(sums[1], 0, 1), swap(sums[2], 2, 0)), sums


def spread_over(value, axes):
    count = math.prod(lax.axis_size(a) for a in axes)
    copies = jnp.broadcast_to(value[None], (count,) + value.shape)
    return lax.all_to_all(copies, axes, split_axis=0, concat_axis=0, tiled=True)


def along(value, pairs):
    return lax.ppermute(value, "dp", pairs)


def gather_rows(own, ring=False):
    count = lax.axis_size("dp")
    if count != 4 or not ring:
        return lax.all_gather(own, "dp", axis=0, tiled=True)
    d = lax.axis_index("dp")
    rows = own.shape[0]
    r1 = along(own, [(0, 1), (1, 2), (2, 3)])
    l1 = along(own, [(3, 2), (2, 1), (1, 0)])
    r2 = along(r1, [(1, 2), (2, 3)])
    l2 = along(l1, [(2, 1), (1, 0)])
    r3 = along(r2, [(2, 3)])
    l3 = along(l2, [(1, 0)])
    full = jnp.zeros((count * rows, own.shape[1]), own.dtype)
    full = lax.dynamic_update_slice_in_dim(full, own, d * rows, 0)
    for k, (left, right) in enumerate(((r3, l1), (r2, l2), (r1, l3)), 1):
        piece = jnp.where(d + k < count, right, left)
        full = lax.dynamic_update_slice_in_dim(full, piece, (d + k) % count * rows, 0)
    return full


def scatter_rows(partial, ring=False):
    count = lax.axis_size("dp")
    if count != 4 or not ring:
        return lax.psum_scatter(partial, "dp", scatter_dimension=0, tiled=True).astype(F32)
    d = lax.axis_index("dp")
    parts = partial.reshape(count, partial.shape[0] // count, partial.shape[1])

    def part(at):
        return lax.dynamic_index_in_dim(parts, at % count, 0, keepdims=False)

    def plus(a, b):
        return (a.astype(F32) + b.astype(F32)).astype(BF16)

    l1 = along(part(d + 1), [(3, 2)])
    r1 = along(part(d + 3), [(0, 1)])
    l2 = along(plus(part(d + 2), l1), [(3, 2), (2, 1)])
    r2 = along(plus(part(d + 2), r1), [(0, 1), (1, 2)])
    l3 = along(plus(part(d + 3), l2), [(3, 2), (2, 1), (1, 0)])
    r3 = along(plus(part(d + 1), r2), [(0, 1), (1, 2), (2, 3)])
    return part(d).astype(F32) + l3.astype(F32) + r3.astype(F32)


def sinusoid(time_steps, channels):
    half_width = channels // 2
    frequency = jnp.exp(
        jnp.arange(half_width, dtype=jnp.float32) * (-math.log(10000.0) / half_width)
    )
    angles = time_steps.astype(jnp.float32)[:, None] * frequency[None, :]
    return jnp.concatenate([jnp.cos(angles), jnp.sin(angles)], axis=1)


def per_device(
    section_inputs,
    condition,
    timesteps,
    ada_weight,
    ada_bias,
    in_weight,
    gate_weight,
    gate_bias,
    conv_taps,
    out_weight,
    up_weight,
    up_bias,
    down_weight,
):
    d = lax.axis_index("dp")
    t = lax.axis_index("tensor")
    s = lax.axis_index("section")
    dps, tensors, sections = (lax.axis_size(a) for a in ("dp", "tensor", "section"))
    first = s == 0
    me = (t * sections + s).astype(jnp.int32).reshape(1)
    images = condition.shape[0]
    width = condition.shape[1]
    slab = in_weight.shape[2]
    heads = gate_weight.shape[2] // sections
    channels = in_weight.shape[3] // sections
    head_width = channels // heads
    units = up_weight.shape[2] // sections
    wide = 2 * LANES
    tail = channels - LANES
    rows = section_inputs.shape[2] // sections
    main = units // LANES * LANES
    left = units - main
    spots = tail_spots(heads)

    def cut(value, axis):
        half = value.shape[axis] // 2
        return (
            lax.slice_in_dim(value, 0, half, axis=axis),
            lax.slice_in_dim(value, half, 2 * half, axis=axis),
        )

    def swap_halves(keep, send):
        received = lax.ppermute(send, "section", [(0, 1), (1, 0)])
        return jnp.where(first, keep, received), jnp.where(first, received, keep)

    def choose(pair):
        return jnp.where(first, pair[0], pair[1]), jnp.where(first, pair[1], pair[0])

    shape_a = (slab, 6 * LANES)
    cfg = (heads, channels)
    section = s.astype(jnp.int32).reshape(1)
    def unit_halves(value):
        rest = sections * main
        return tuple(
            (value[:, h * main : (h + 1) * main], value[:, rest + h * left : rest + (h + 1) * left])
            for h in (0, 1)
        )

    def pack_b(up_half, down_half):
        return jnp.concatenate([up_half[0], down_half[0], up_half[1], down_half[1]], axis=1)

    def pack_small(gate_half, taps_half, up_half):
        return jnp.concatenate([gate_half.reshape(-1), taps_half.reshape(-1), up_half.reshape(-1)])

    def pack_halves(pack, *pairs):
        return tuple(pack(*(pair[i] for pair in pairs)) for i in (0, 1))

    x_pair = cut(section_inputs[0], 1)
    x_received = lax.ppermute(
        jnp.where(first, x_pair[1], x_pair[0]), "section", [(0, 1), (1, 0)]
    )
    x0 = jnp.where(first, x_pair[0], x_received)
    g1 = jnp.where(first, x_received, x_pair[1])
    kept_b, sent_b = choose(
        pack_halves(pack_b, unit_halves(up_weight[0]), unit_halves(down_weight[0].T))
    )
    in_own, sent_b = lax.optimization_barrier((in_weight[0], sent_b))
    packs_b = swap_halves(kept_b, sent_b)
    kept_a, sent_a = (
        call(
            functools.partial(pack_attn_kernel, cfg),
            (out(shape_a, BF16),) * 2,
            section,
            in_own,
            jnp.pad(gate_weight[0].astype(F32), ((0, 0), (0, LANES - gate_weight.shape[2]))),
            out_weight[0].T,
            scalars=1,
        )
    )

    kept_a, sent_a, condition = lax.optimization_barrier((kept_a, sent_a, condition))
    packs_a = swap_halves(kept_a, sent_a)
    taps_count = conv_taps.shape[1]
    up_row = up_bias[0].astype(F32)[None]
    small = swap_halves(
        *choose(
            pack_halves(
                pack_small,
                cut(gate_bias[0].astype(F32), 0),
                cut(conv_taps[0].astype(F32), 1),
                tuple(jnp.concatenate(v, axis=1) for v in unit_halves(up_row)),
            )
        )
    )

    def unpack_small(packed):
        gate_row = jnp.pad(packed[:heads][None], ((0, 0), (tail, LANES - heads - tail)))
        taps = packed[heads : heads + taps_count * channels].reshape(taps_count, channels)
        taps = jnp.pad(taps, ((0, 16 - taps_count), (0, wide - channels)))
        up_row = packed[heads + taps_count * channels :][None]
        return gate_row, taps, jnp.pad(up_row, ((0, 0), (0, main + LANES - units)))

    weights = [
        (gather_rows(packs_a[b], b == 0), gather_rows(packs_b[b]), *unpack_small(small[b]))
        for b in (0, 1)
    ]

    cond_vec = condition + sinusoid(timesteps, width)
    activated = jax.nn.silu(cond_vec).astype(BF16)
    slab_active = activated.reshape(images, dps, slab).transpose(1, 0, 2)
    slab_active = lax.all_to_all(slab_active, "dp", split_axis=0, concat_axis=0, tiled=True)
    slab_active = slab_active.reshape(dps * images, slab)
    mod_part = jnp.dot(slab_active, ada_weight[0], preferred_element_type=F32)
    mod_parts = lax.all_to_all(
        mod_part.reshape(dps, images, -1), "dp", split_axis=0, concat_axis=0, tiled=True
    )
    mod_share = jnp.sum(mod_parts, axis=0) + ada_bias[0].astype(F32)
    mod_all = spread_over(mod_share, ("section", "tensor"))
    mod_all = mod_all.reshape(sections, tensors, images, -1).transpose(0, 2, 1, 3)
    mod_all = mod_all.reshape(sections, images, 6, width)
    mods = (mod_all[0], mod_all[1])

    shard = out((images, rows, width), BF16)
    shard_wide = out((images, rows, width), F32)
    vector = out((images, 1, width), F32)
    pieces_out = (out((4, images, rows, width), BF16),) + (shard,) * 4
    full = out((images, PATCHES, width), BF16)
    flat = out((images * PATCHES, width), BF16)
    total_rows = images * PATCHES
    kept = pltpu.VMEM((images, PATCHES, width), BF16)
    middle_flops = 2 * total_rows * PATCHES * wide * heads * 6
    attn_flops = 2 * total_rows * width * wide * 5 + middle_flops
    mlp_flops = 4 * total_rows * width * units

    def attn_forward(b, normed):
        w, _, gate_row, taps, _ = weights[b]
        body = functools.partial(attn_forward_kernel, (b == 1, heads, head_width))
        found = call(
            body,
            (
                full,
                out((images, PATCHES, 4 * wide), BF16),
                out((images, PATCHES, LANES), F32),
                out((images, PATCHES, wide), F32),
                out((images, PATCHES, wide), BF16),
                *pieces_out,
            ),
            me,
            *gather_plane(normed),
            w,
            gate_row,
            taps,
            scalars=1,
            flops=attn_flops,
            scratch=[kept],
            saved=(0, 1, 2, 3, 4),
        )
        return found[:5], scatter_plane(found[5], found[6:])[0]

    def attn_backward(b, grad, saved):
        w, _, _, taps, _ = weights[b]
        body = functools.partial(attn_backward_kernel, (b == 1, heads, head_width))
        found = call(
            body,
            (
                full,
                out((images, PATCHES, 5 * LANES), BF16),
                out((16, wide), F32),
                *pieces_out,
            ),
            me,
            *gather_plane(grad),
            saved[1],
            saved[2],
            saved[3],
            w,
            taps,
            scalars=1,
            flops=2 * attn_flops,
            scratch=[kept],
        )
        terms, sums = scatter_plane(found[3], found[4:])
        (grads,) = call(
            attn_weights_kernel,
            (out((width, 6 * LANES), BF16),),
            saved[0],
            found[1],
            found[0],
            saved[4],
            flops=2 * total_rows * width * wide * 5,
            after=sums,
        )
        return terms, grads, found[2]

    def mlp_forward(b, normed):
        _, w, _, _, up_row = weights[b]
        found = call(
            functools.partial(mlp_forward_kernel, left),
            (
                flat,
                out((total_rows, main + LANES), F32),
                out((total_rows, main + LANES), BF16),
                *pieces_out,
            ),
            *gather_plane(normed),
            w,
            up_row,
            flops=mlp_flops,
            saved=(0, 1, 2),
        )
        return found[:3], scatter_plane(found[3], found[4:])[0]

    def mlp_backward(b, shards, saved):
        _, w, _, _, _ = weights[b]
        found = call(
            functools.partial(mlp_backward_kernel, left),
            (flat, out((total_rows, main + LANES), BF16), out((1, main + LANES), F32), *pieces_out),
            *shards,
            saved[1],
            w,
            flops=mlp_flops,
        )
        terms, sums = scatter_plane(found[3], found[4:])
        (grads,) = call(
            mlp_weights_kernel,
            (out((width, 2 * main + LANES), BF16),),
            saved[0],
            found[1],
            found[0],
            saved[2],
            flops=mlp_flops,
            after=sums,
        )
        return terms, grads, found[2]

    (normed,) = call(start_kernel, (shard,), x0, mods[0])
    attn0, terms = attn_forward(0, normed)
    att0, aft0, normed = call(
        after_attn_kernel,
        (shard_wide, shard_wide, shard),
        *terms,
        x0,
        mods[0],
        saved=(0, 1),
    )
    mlp0, terms = mlp_forward(0, normed)
    mlp_out0, x1, normed = call(
        between_kernel, (shard_wide, shard, shard), *terms, aft0, mods[0], mods[1]
    )
    attn1, terms = attn_forward(1, normed)
    att1, aft1, normed = call(
        after_attn_kernel,
        (shard_wide, shard_wide, shard),
        *terms,
        x1,
        mods[1],
        saved=(0, 1),
    )
    mlp1, end_terms = mlp_forward(1, normed)
    (g_mlp,) = call(scale_rows_kernel, (shard,), g1, mods[1])
    block_out, g_gate_two1 = call(end_kernel, (shard, vector), *end_terms, aft1, mods[1], g1)

    three, six = out((images, 3, width), F32), out((images, 6, width), F32)
    terms, mlp_grads1, g_up_bias1 = mlp_backward(1, gather_plane(g_mlp), mlp1)
    g_after, g_attn, g_some = call(
        back_mlp_rows_kernel,
        (shard_wide, shard, three),
        *terms,
        g1,
        aft1,
        att1,
        mods[1],
        after=(mlp_grads1,),
    )
    sum_b1 = scatter_rows(mlp_grads1)
    terms, attn_grads1, g_taps1 = attn_backward(1, g_attn, attn1)
    g0, g_mlp, g_mods1, g_gate_two0 = call(
        back_between_kernel,
        (shard, shard, six, vector),
        *terms,
        g_after,
        x1,
        mods[1],
        g_some,
        g_gate_two1,
        mods[0],
        mlp_out0,
        after=(attn_grads1,),
    )
    sum_a1 = scatter_rows(attn_grads1)
    terms, mlp_grads0, g_up_bias0 = mlp_backward(0, gather_plane(g_mlp), mlp0)
    g_after, g_attn, g_some = call(
        back_mlp_rows_kernel,
        (shard_wide, shard, three),
        *terms,
        g0,
        aft0,
        att0,
        mods[0],
        after=(mlp_grads0, sum_b1),
    )
    terms, attn_grads0, g_taps0 = attn_backward(0, g_attn, attn0)
    g_in, g_mods0 = call(
        back_end_kernel,
        (shard, six),
        *terms,
        g_after,
        x0,
        mods[0],
        g_some,
        g_gate_two0,
        after=(attn_grads0, sum_a1),
    )

    def finish(sum1, sum0):
        from_first = lax.ppermute(sum1.astype(BF16), "section", [(0, 1)])
        from_second = lax.ppermute(sum0.astype(BF16), "section", [(1, 0)])
        return jnp.where(first, sum0, sum1), jnp.where(first, from_second, from_first)

    mine, received = finish(sum_b1, scatter_rows(mlp_grads0))
    pair_b = choose((mine, received.astype(F32)))
    end = 2 * main + left
    grad_up = [g[:, :main] for g in pair_b] + [g[:, 2 * main : end] for g in pair_b]
    grad_up = jnp.concatenate(grad_up, axis=1)
    grad_down = [g[:, main : 2 * main].T for g in pair_b] + [g[:, end:].T for g in pair_b]
    grad_down = jnp.concatenate(grad_down, axis=0)
    grad_in, grad_gate, grad_out = call(
        functools.partial(unpack_attn_kernel, cfg),
        (
            out(in_weight.shape[1:], F32),
            out(gate_weight.shape[1:], F32),
            out((slab, out_weight.shape[1]), F32),
        ),
        section,
        *finish(sum_a1, scatter_rows(attn_grads0)),
        scalars=1,
    )
    grad_out = grad_out.T

    g_mod = jnp.stack([g_mods0.reshape(images, -1), g_mods1.reshape(images, -1)])
    g_mod = g_mod.reshape(sections, images, tensors, -1).transpose(0, 2, 1, 3)
    columns = g_mod.shape[3]
    g_mod = g_mod.reshape(sections, tensors, images * columns)
    taps_rows = taps_count + 1

    def small_grads(g_taps, g_up_bias):
        return jnp.concatenate([g_taps[:taps_rows].reshape(-1), g_up_bias.reshape(-1)])

    g_small = jnp.stack([small_grads(g_taps0, g_up_bias0), small_grads(g_taps1, g_up_bias1)])
    to_tensor = (jnp.arange(tensors) == t)[None, :, None]
    g_small = jnp.where(to_tensor, g_small[:, None], 0.0)
    g_sent = jnp.concatenate([g_mod, g_small], axis=2).reshape(sections * tensors, -1)
    g_parts = lax.all_to_all(
        g_sent, ("section", "tensor"), split_axis=0, concat_axis=0, tiled=True
    )
    g_share = jnp.sum(g_parts[:, : images * columns], axis=0)
    small_parts = g_parts[:, images * columns :].reshape(sections, tensors, -1).sum(1)
    g_all = spread_over(jnp.concatenate([g_share, small_parts.reshape(-1)]), ("dp",))
    small_own = jnp.sum(g_all[:, images * columns :], axis=0).reshape(sections, -1)
    g_all = g_all[:, : images * columns].reshape(dps * images, columns).astype(BF16)
    grad_ada_bias = jnp.sum(g_all.astype(F32), axis=0)
    grad_ada = jnp.einsum("md,me->de", slab_active, g_all, preferred_element_type=F32)
    act_part = jnp.einsum("me,de->md", g_all, ada_weight[0], preferred_element_type=F32)
    act_all = lax.all_to_all(
        act_part.reshape(dps, images, slab), "dp", split_axis=0, concat_axis=0, tiled=True
    )
    act_all = jnp.sum(spread_over(act_all, ("section", "tensor")), axis=0)
    act_grad = act_all.reshape(dps, images, slab).transpose(1, 0, 2).reshape(images, width)
    cond_grad = jax.vjp(jax.nn.silu, cond_vec)[1](act_grad)[0]

    small_taps = small_own[:, : taps_rows * wide].reshape(sections, taps_rows, wide)
    grad_gateb = small_taps[:, taps_count, tail : tail + heads].reshape(-1)
    grad_taps = small_taps[:, :taps_count, :channels].transpose(1, 0, 2)
    grad_taps = grad_taps.reshape(taps_count, sections * channels)
    up_halves = small_own[:, taps_rows * wide :]
    grad_up_bias = jnp.concatenate(
        [up_halves[:, :main].reshape(-1), up_halves[:, main : main + left].reshape(-1)]
    )

    ends_from_first = lax.ppermute(block_out, "section", [(0, 1)])
    ends_from_second = lax.ppermute(g_in, "section", [(1, 0)])
    mine = jnp.where(first, g_in, block_out)
    received = jnp.where(first, ends_from_second, ends_from_first)
    section_ends = jnp.concatenate(
        [jnp.where(first, mine, received), jnp.where(first, received, mine)], axis=1
    )
    return (
        section_ends[None],
        cond_grad,
        grad_ada[None],
        grad_ada_bias[None],
        grad_in[None],
        grad_gate[None],
        grad_gateb[None],
        grad_taps[None],
        grad_out[None],
        grad_up[None],
        grad_up_bias[None],
        grad_down[None],
    )


def solution(mesh):
    in_specs = (
        P("section", "dp", "tensor", None),
        P("dp", None),
        P("dp"),
        P("section", "dp", "tensor"),
        P("section", "tensor"),
        P("section", None, "dp", "tensor"),
        P("section", "dp", "tensor"),
        P("section", "tensor"),
        P("section", None, "tensor"),
        P("section", "tensor", "dp"),
        P("section", "dp", "tensor"),
        P("section", "tensor"),
        P("section", "tensor", "dp"),
    )
    out_specs = (
        P("section", "dp", "tensor", None),
        P("dp", None),
        P("section", "dp", "tensor"),
        P("section", "tensor"),
        P("section", None, "dp", "tensor"),
        P("section", "dp", "tensor"),
        P("section", "tensor"),
        P("section", None, "tensor"),
        P("section", "tensor", "dp"),
        P("section", "dp", "tensor"),
        P("section", "tensor"),
        P("section", "tensor", "dp"),
    )
    return jax.shard_map(
        per_device, mesh=mesh, in_specs=in_specs, out_specs=out_specs, check_vma=False
    )
```

time: 1590 us -> 538 us (0.34)
  waiting for transfers between devices: 802 us -> 194 us
  blocking collectives: 250 us -> 0 us
  matrix products: 164 us -> 3.67 us
  starting transfers between devices: 15.1 us -> 119 us
  other arithmetic: 135 us -> 38.2 us
  local copies, waits for them, and re-layouts: 166 us -> 89.1 us
  Pallas kernels: 0 us -> 67.1 us
  loops' own time: 29.5 us -> 0 us
    reduce_scatter x21 -> x4, waiting for transfers between devices: 537 us -> 0.04 us  [scatter_rows(): lax.psum_scatter(partial, 'dp', scatter_dimension=0, tiled=True).astype(F32)]
    all_gather x21 -> x0, blocking collectives: 217 us -> none  [the longest x12 83.8 us: gather_rows(): return lax.all_gather(values, 'tensor', axis=0, tiled=True)]
    all_gather x4 -> x3, waiting for transfers between devices: 180 us -> 0.03 us  [gather_rows(): return lax.all_gather(own, 'dp', axis=0, tiled=True)]
    dot_general x74 -> x3, matrix products: 164 us -> 3.67 us  [the longest x1 1.78 us: per_device(): jnp.einsum('md,me->de', slab_active, g_all, preferred_element_type=F32)]
    ppermute x6 -> x88, waiting for transfers between devices: 26.5 us -> 157 us  [the longest x72 89.6 us: swap(): return lax.ppermute(value, PLANE, route)]
    ppermute x6 -> x88, starting transfers between devices: 14 us -> 90.6 us  [the longest x72 63.2 us: swap(): return lax.ppermute(value, PLANE, route)]
    pallas_call x0 -> x24, Pallas kernels: none -> 67.1 us  [call(): pl.pallas_call(kernel, out_shape=tuple(outs), in_specs=specs, out_specs=t...]
    unnamed x15 -> x7, waiting for transfers between devices: 58.2 us -> 0.12 us
  transfers between devices with their start and end apart: 35 -> 102, of which waited for: 32 -> 56; matrix products, arithmetic and copies ran while one was open for 8% -> 12% of each run, Pallas kernels for 0% -> 11%
where the time goes in v1:
time: 538 us; the launch traced here: 528 us
  waiting for transfers between devices  194 us (36%)
  starting transfers between devices  119 us (22%)
  local copies, waits for them, and re-layouts  89.1 us (17%)
  Pallas kernels  67.1 us (12%)
  other arithmetic  38.2 us (7%)
  between operations  16.2 us (3%)
    ppermute x72, waiting for transfers between devices, swap(): return lax.ppermute(value, PLANE, route)  89.6 us
    pallas_call x24, Pallas kernels, call(): pl.pallas_call(kernel, out_shape=tuple(outs), in_specs=specs, out_specs=t...  67.1 us
    ppermute x72, starting transfers between devices, swap(): return lax.ppermute(value, PLANE, route)  63.2 us
    unnamed x282, local copies, waits for them, and re-layouts  62.5 us
    ppermute x6, waiting for transfers between devices, along(): return lax.ppermute(value, 'dp', pairs)  47 us
    all_to_all x3, waiting for transfers between devices, spread_over(): return lax.all_to_all(copies, axes, split_axis=0, concat_axis=0, tiled=True)  19.2 us
    ppermute x3, waiting for transfers between devices, swap_halves(): received = lax.ppermute(send, 'section', [(0, 1), (1, 0)])  12.7 us
    all_to_all x3, starting transfers between devices, spread_over(): return lax.all_to_all(copies, axes, split_axis=0, concat_axis=0, tiled=True)  11.2 us
  transfers between devices with their start and end apart: 102, of which 56 were waited for; matrix products, arithmetic and copies ran while one was open for 12% of the time, Pallas kernels for 11%

profile of v1, /device:TPU:0, one launch (start us, length us, event | category | flops | bytes accessed | tf_op | source)
XLA Modules:
  0.0 527.8 jit_solution(1865853617996041002)
XLA Ops:
  11.3 2.9 collective-permute-start.18
  25.6 12.7 %collective-permute-done.28 = bf16[288,1152]{1,0:T(8,128)(2,1)} collective-permute-done((bf16[288,1152]{1,0:T(8,128)(2,1)}, bf16[288,1152]{1,0:T(8,128)(2,1)}, u32[]{:S(2)}, u32[]{:S(2)}) %collective-permute-start.28) | collective-permute-done | bytes 663584 | tf_op jit(solution)/shard_map/ppermute | solution.py:704
  38.3 2.3 broadcast_select_fusion.1
  41.4 4.9 all-to-all-start
  46.6 5.4 %all-to-all-done = bf16[4,2,288]{2,1,0:T(2,128)(2,1)S(1)} async-done(((bf16[4,2,288]{2,1,0:T(2,128)(2,1)}), bf16[4,2,288]{2,1,0:T(2,128)(2,1)S(1)}, u32[]{:S(2)}, u32[]{:S(2)}) %all-to-all-start) | async-done | bytes 4640 | tf_op jit(solution)/shard_map/all_to_all | solution.py:782
  52.9 3.3 all-to-all-start.1
  58.1 5.8 %all-to-all-done.1 = f32[4,2,1728]{2,1,0:T(2,128)S(1)} async-done(((f32[4,2,1728]{2,1,0:T(2,128)}), f32[4,2,1728]{2,1,0:T(2,128)S(1)}, u32[]{:S(2)}, u32[]{:S(2)}) %all-to-all-start.1) | async-done | bytes 55328 | tf_op jit(solution)/shard_map/all_to_all | solution.py:785
  64.6 4.0 all-to-all-start.2
  71.0 2.6 collective-permute-start.13
  75.8 17.1 %collective-permute-done.13 = bf16[288,768]{1,0:T(8,128)(2,1)} collective-permute-done((bf16[288,768]{1,0:T(8,128)(2,1)}, bf16[288,768]{1,0:T(8,128)(2,1)}, u32[]{:S(2)}, u32[]{:S(2)}) %collective-permute-start.13) | collective-permute-done | bytes 442400 | tf_op jit(solution)/shard_map/ppermute | solution.py:607
  96.2 2.8 collective-permute-start.9
  99.7 4.3 collective-permute-done.12
  108.7 16.7 %collective-permute-done.16 = bf16[288,768]{1,0:T(8,128)(2,1)} collective-permute-done((bf16[288,768]{1,0:T(8,128)(2,1)}, bf16[288,768]{1,0:T(8,128)(2,1)}, u32[]{:S(2)}, u32[]{:S(2)}) %collective-permute-start.16) | collective-permute-done | bytes 442400 | tf_op jit(solution)/shard_map/ppermute | solution.py:607
  128.9 9.0 %collective-permute-done.17 = bf16[288,768]{1,0:T(8,128)(2,1)S(1)} collective-permute-done((bf16[288,768]{1,0:T(8,128)(2,1)}, bf16[288,768]{1,0:T(8,128)(2,1)S(1)}, u32[]{:S(2)}, u32[]{:S(2)}) %collective-permute-start.17) | collective-permute-done | bytes 442400 | tf_op jit(solution)/shard_map/ppermute | solution.py:607
  138.8 5.9 %shard_map.223 = (bf16[2,256,1152]{2,1,0:T(8,128)(2,1)S(1)}, bf16[2,256,1024]{2,1,0:T(8,128)(2,1)S(1)}, f32[2,256,128]{2,1,0:T(8,128)S(1)}, f32[2,256,256]{2,1,0...) custom-call(s32[1]{0:T(128)} %bitcast.refs_0_, ...), custom_call_target="tpu_custom_call" | custom-call | flops 2315255808 | bytes 7422468 | tf_op jit(solution)/shard_map/pallas_call | solution.py:55
  157.3 2.4 collective-permute-done.22.refs_3_
  159.7 2.4 collective-permute-done.21.refs_2_
  165.2 2.5 collective-permute-start.26
  168.7 3.6 collective-permute-done.26
  182.4 5.1 shard_map.225
  214.2 4.2 collective-permute-done.36
  224.2 6.3 %shard_map.227 = (bf16[2,256,1152]{2,1,0:T(8,128)(2,1)S(1)}, bf16[2,256,1024]{2,1,0:T(8,128)(2,1)S(1)}, f32[2,256,128]{2,1,0:T(8,128)S(1)}, f32[2,256,256]{2,1,0...) custom-call(s32[1]{0:T(128)} %bitcast.refs_0_, ...), custom_call_target="tpu_custom_call" | custom-call | flops 2315255808 | bytes 7422468 | tf_op jit(solution)/shard_map/pallas_call | solution.py:55
  237.8 2.4 collective-permute-done.41.refs_3_
  255.8 2.6 collective-permute-done.44
  266.0 6.8 %shard_map.229 = (bf16[512,1152]{1,0:T(8,128)(2,1)S(1)}, f32[512,640]{1,0:T(8,128)S(1)}, bf16[512,640]{1,0:T(8,128)(2,1)S(1)}, bf16[4,2,32,1152]{3,2,1,0:T(8,128...) custom-call(bf16[2,32,1152]{2,1,0:T(8,128)(2,1)} %get-tuple-element., ...), custom_call_target="tpu_custom_call" | custom-call | flops 1358954496 | bytes 8161792 | tf_op jit(solution)/shard_map/pallas_call | solution.py:55
  275.5 4.9 shard_map.230
  290.8 2.6 collective-permute-done.50.refs_3_
  305.2 4.0 collective-permute-done.54
  312.8 6.1 %shard_map.233 = (bf16[2,256,1152]{2,1,0:T(8,128)(2,1)S(1)}, bf16[2,256,640]{2,1,0:T(8,128)(2,1)S(1)}, f32[16,256]{1,0:T(8,128)S(1)}, bf16[4,2,32,1152]{3,2,1,0:...) custom-call(s32[1]{0:T(128)} %bitcast.refs_0_, ...), custom_call_target="tpu_custom_call" | custom-call | flops 4630511616 | bytes 7831556 | tf_op jit(solution)/shard_map/pallas_call | solution.py:55
  321.2 2.7 shard_map.235.refs_11_
  336.4 2.9 collective-permute-done.61.refs_1_
  348.5 3.9 collective-permute-done.67
  356.0 3.7 shard_map.237
  388.9 4.2 collective-permute-done.76
  397.0 4.2 collective-permute-start.83
  405.8 8.0 %shard_map.240 = (bf16[2,256,1152]{2,1,0:T(8,128)(2,1)S(1)}, bf16[2,256,640]{2,1,0:T(8,128)(2,1)S(1)}, f32[16,256]{1,0:T(8,128)S(1)}, bf16[4,2,32,1152]{3,2,1,0:...) custom-call(s32[1]{0:T(128)} %bitcast.refs_0_, ...), custom_call_target="tpu_custom_call" | custom-call | flops 4630511616 | bytes 7831556 | tf_op jit(solution)/shard_map/pallas_call | solution.py:55
  423.8 2.3 fusion.4
  426.9 2.7 collective-permute-start.79
  433.2 2.6 shard_map.241.refs_9_
  437.0 2.8 collective-permute-start.87
  445.5 4.2 all-to-all-start.3
  449.8 5.6 %all-to-all-done.3 = f32[8,1,6656]{2,1,0:T(1,128)S(1)} async-done(((f32[8,1,6656]{2,1,0:T(1,128)}), f32[8,1,6656]{2,1,0:T(1,128)S(1)}, u32[]{:S(2)}, u32[]{:S(2)}) %all-to-all-start.3) | async-done | bytes 213024 | tf_op jit(solution)/shard_map/all_to_all | solution.py:1024
  456.4 3.3 all-to-all-start.4
  460.5 10.8 %all-to-all-done.4 = f32[4,1,9856]{2,1,0:T(1,128)S(1)} async-done(((f32[4,1,9856]{2,1,0:T(1,128)}), f32[4,1,9856]{2,1,0:T(1,128)S(1)}, u32[]{:S(2)}, u32[]{:S(2)}) %all-to-all-start.4) | async-done | bytes 157728 | tf_op jit(solution)/shard_map/all_to_all | solution.py:603
  472.9 4.1 all-to-all-start.5
  483.2 3.9 all-to-all-start.6
  488.9 8.3 %all-to-all-done.6 = f32[8,4,2,288]{3,2,1,0:T(2,128)S(1)} async-done(((f32[8,4,2,288]{3,2,1,0:T(2,128)}), f32[8,4,2,288]{3,2,1,0:T(2,128)S(1)}, u32[]{:S(2)}, u32[]{:S(2)}) %all-to-all-start.6) | async-done | bytes 73760 | tf_op jit(solution)/shard_map/all_to_all | solution.py:603
  508.8 7.2 %collective-permute-done.84 = bf16[288,768]{1,0:T(8,128)(2,1)} collective-permute-done((bf16[288,768]{1,0:T(8,128)(2,1)}, bf16[288,768]{1,0:T(8,128)(2,1)}, u32[]{:S(2)}, u32[]{:S(2)}) %collective-permute-start.84) | collective-permute-done | bytes 442400 | tf_op jit(solution)/shard_map/ppermute | solution.py:988
  (612 shorter events, 268.4 us)
Async XLA Ops:
  7.2 170.6 %all-gather.4.cloned.1.call-start = ((), (), s32[]{:S(2)}) async-start(), calls=%async_computation.11 | async-start | bytes 3317760 | tf_op jit(solution)/shard_map/all_gather | solution.py:613
  11.3 44.9 %collective-permute-start.18 = (f32[1874]{0:T(1024)}, f32[1874]{0:T(1024)}, u32[]{:S(2)}, u32[]{:S(2)}) collective-permute-start(f32[1874]{0:T(1024)} %broadcast_select_fusion.18), channel_id=1, source_target_pairs={{0,1},{1,0},{2,3},{3,2},{4,5},{5,4},{6,7},{7,6},{8,9},{9,8},{10,11... | collective-permute-start | bytes 22496 | tf_op jit(solution)/shard_map/ppermute | solution.py:704
  20.1 18.1 %collective-permute-start.28 = (bf16[288,1152]{1,0:T(8,128)(2,1)}, bf16[288,1152]{1,0:T(8,128)(2,1)}, u32[]{:S(2)}, u32[]{:S(2)}) collective-permute-start(bf16[288,1152]{1,0:T(8,128)(2,1)} %broadcast_select_fusion.4), channel_id=1, source_target_pairs={{0,1},{1,0},{2,3},{3,2},{4,5},{5,4},{6,7},{7,6},{8,9},{9,8},{10,11... | collective-permute-start | bytes 1990664 | tf_op jit(solution)/shard_map/ppermute | solution.py:704
  20.8 52.8 %collective-permute-start = (bf16[2,32,1152]{2,1,0:T(8,128)(2,1)}, bf16[2,32,1152]{2,1,0:T(8,128)(2,1)}, u32[]{:S(2)}, u32[]{:S(2)}) collective-permute-start(bf16[2,32,1152]{2,1,0:T(8,128)(2,1)} %broadcast_select_fusion.14), channel_id=1, source_target_pairs={{0,1},{1,0},{2,3},{3,2},{4,5},{5,4},{6,7},{7,6},{8,9},{9,8},{10,11... | collective-permute-start | bytes 442376 | tf_op jit(solution)/shard_map/ppermute | solution.py:730
  41.4 10.6 %all-to-all-start = ((bf16[4,2,288]{2,1,0:T(2,128)(2,1)}), bf16[4,2,288]{2,1,0:T(2,128)(2,1)S(1)}, u32[]{:S(2)}, u32[]{:S(2)}) async-start(bf16[4,2,288]{2,1,0:T(2,128)(2,1)} %copy.106), calls=%async_computation | async-start | bytes 12288 | tf_op jit(solution)/shard_map/all_to_all | solution.py:782
  46.3 22.4 %collective-permute-start.11 = (bf16[288,768]{1,0:T(8,128)(2,1)S(1)}, bf16[288,768]{1,0:T(8,128)(2,1)}, u32[]{:S(2)}, u32[]{:S(2)}) collective-permute-start(bf16[288,768]{1,0:T(8,128)(2,1)S(1)} %get-tuple-element.118), channel_id=1, source_target_pairs={{0,1},{1,0},{2,3},{3,2},{4,5},{5,4},{6,7},{7,6},{8,9},{9,8},{10,11... | collective-permute-start | bytes 1327112 | tf_op jit(solution)/shard_map/ppermute | solution.py:704
  52.9 11.0 %all-to-all-start.1 = ((f32[4,2,1728]{2,1,0:T(2,128)}), f32[4,2,1728]{2,1,0:T(2,128)S(1)}, u32[]{:S(2)}, u32[]{:S(2)}) async-start(f32[4,2,1728]{2,1,0:T(2,128)} %fusion.2), calls=%async_computation.1 | async-start | bytes 114688 | tf_op jit(solution)/shard_map/all_to_all | solution.py:785
  64.6 29.7 %all-to-all-start.2 = ((f32[8,2,1728]{2,1,0:T(2,128)}), f32[8,2,1728]{2,1,0:T(2,128)}, u32[]{:S(2)}, u32[]{:S(2)}) async-start(f32[8,2,1728]{2,1,0:T(2,128)} %broadcast_in_dim.92), calls=%async_computation.2 | async-start | bytes 229376 | tf_op jit(solution)/shard_map/all_to_all | solution.py:603
  68.6 152.7 %all-gather.6.cloned.1.call-start = ((), (), s32[]{:S(2)}) async-start(), calls=%async_computation.12 | async-start | bytes 2211840 | tf_op jit(solution)/shard_map/all_gather | solution.py:613
  71.0 21.9 %collective-permute-start.13 = (bf16[288,768]{1,0:T(8,128)(2,1)}, bf16[288,768]{1,0:T(8,128)(2,1)}, u32[]{:S(2)}, u32[]{:S(2)}) collective-permute-start(bf16[288,768]{1,0:T(8,128)(2,1)} %get-tuple-element.311), channel_id=1, source_target_pairs={{0,8},{8,16},{16,24},{1,9},{9,17},{17,25},{2,10},{10,18},{18,26},{... | collective-permute-start | bytes 1327112 | tf_op jit(solution)/shard_map/ppermute | solution.py:607
  74.5 29.5 %collective-permute-start.12 = (bf16[288,768]{1,0:T(8,128)(2,1)}, bf16[288,768]{1,0:T(8,128)(2,1)}, u32[]{:S(2)}, u32[]{:S(2)}) collective-permute-start(bf16[288,768]{1,0:T(8,128)(2,1)} %get-tuple-element.311), channel_id=1, source_target_pairs={{24,16},{16,8},{8,0},{25,17},{17,9},{9,1},{26,18},{18,10},{10,2},{... | collective-permute-start | bytes 1327112 | tf_op jit(solution)/shard_map/ppermute | solution.py:607
  92.9 12.4 %collective-permute-start.14 = (bf16[288,768]{1,0:T(8,128)(2,1)}, bf16[288,768]{1,0:T(8,128)(2,1)}, u32[]{:S(2)}, u32[]{:S(2)}) collective-permute-start(bf16[288,768]{1,0:T(8,128)(2,1)} %collective-permute-done.13), channel_id=1, source_target_pairs={{8,16},{16,24},{9,17},{17,25},{10,18},{18,26},{11,19},{19,27},{12,... | collective-permute-start | bytes 1327112 | tf_op jit(solution)/shard_map/ppermute | solution.py:607
  96.2 10.8 %collective-permute-start.9 = (bf16[2,32,1152]{2,1,0:T(8,128)(2,1)S(1)}, bf16[2,32,1152]{2,1,0:T(8,128)(2,1)S(1)}, u32[]{:S(2)}, u32[]{:S(2)}) collective-permute-start(bf16[2,32,1152]{2,1,0:T(8,128)(2,1)S(1)} %shard_map.222.refs_1_), channel_id=1, source_target_pairs={{0,5},{1,4},{2,7},{3,6},{4,1},{5,0},{6,3},{7,2},{8,13},{9,12},{10,... | collective-permute-start | bytes 442376 | tf_op jit(solution)/shard_map/ppermute | solution.py:584
  99.0 8.1 %collective-permute-start.8 = (bf16[2,32,1152]{2,1,0:T(8,128)(2,1)S(1)}, bf16[2,32,1152]{2,1,0:T(8,128)(2,1)}, u32[]{:S(2)}, u32[]{:S(2)}) collective-permute-start(bf16[2,32,1152]{2,1,0:T(8,128)(2,1)S(1)} %shard_map.222.refs_1_), channel_id=1, source_target_pairs={{0,4},{1,5},{2,6},{3,7},{4,0},{5,1},{6,2},{7,3},{8,12},{9,13},{10,... | collective-permute-start | bytes 442376 | tf_op jit(solution)/shard_map/ppermute | solution.py:584
  104.0 21.3 %collective-permute-start.16 = (bf16[288,768]{1,0:T(8,128)(2,1)}, bf16[288,768]{1,0:T(8,128)(2,1)}, u32[]{:S(2)}, u32[]{:S(2)}) collective-permute-start(bf16[288,768]{1,0:T(8,128)(2,1)} %collective-permute-done.12), channel_id=1, source_target_pairs={{16,8},{8,0},{17,9},{9,1},{18,10},{10,2},{19,11},{11,3},{20,12},{1... | collective-permute-start | bytes 1327112 | tf_op jit(solution)/shard_map/ppermute | solution.py:607
  105.3 21.3 %collective-permute-start.15 = (bf16[288,768]{1,0:T(8,128)(2,1)}, bf16[288,768]{1,0:T(8,128)(2,1)}, u32[]{:S(2)}, u32[]{:S(2)}) collective-permute-start(bf16[288,768]{1,0:T(8,128)(2,1)} %collective-permute-done.14), channel_id=1, source_target_pairs={{16,24},{17,25},{18,26},{19,27},{20,28},{21,29},{22,30},{23,31}} | collective-permute-start | bytes 1327112 | tf_op jit(solution)/shard_map/ppermute | solution.py:607
  107.0 31.1 %collective-permute-start.6 = (bf16[2,32,1152]{2,1,0:T(8,128)(2,1)S(1)}, bf16[2,32,1152]{2,1,0:T(8,128)(2,1)S(1)}, u32[]{:S(2)}, u32[]{:S(2)}) collective-permute-start(bf16[2,32,1152]{2,1,0:T(8,128)(2,1)S(1)} %shard_map.222.refs_1_), channel_id=1, source_target_pairs={{0,2},{1,3},{2,0},{3,1},{4,6},{5,7},{6,4},{7,5},{8,10},{9,11},{10,... | collective-permute-start | bytes 442376 | tf_op jit(solution)/shard_map/ppermute | solution.py:584
  108.1 30.0 %collective-permute-start.10 = (bf16[3,2,32,1152]{3,2,1,0:T(8,128)(2,1)S(1)}, bf16[3,2,32,1152]{3,2,1,0:T(8,128)(2,1)S(1)}, u32[]{:S(2)}, u32[]{:S(2)}) collective-permute-start(bf16[3,2,32,1152]{3,2,1,0:T(8,128)(2,1)S(1)} %pad_maximum_fusion.1.refs_3_), channel_id=1, source_target_pairs={{0,2},{1,3},{2,0},{3,1},{4,6},{5,7},{6,4},{7,5},{8,10},{9,11},{10,... | collective-permute-start | bytes 1327112 | tf_op jit(solution)/shard_map/ppermute | solution.py:584
  125.3 12.6 %collective-permute-start.17 = (bf16[288,768]{1,0:T(8,128)(2,1)}, bf16[288,768]{1,0:T(8,128)(2,1)S(1)}, u32[]{:S(2)}, u32[]{:S(2)}) collective-permute-start(bf16[288,768]{1,0:T(8,128)(2,1)} %collective-permute-done.16), channel_id=1, source_target_pairs={{8,0},{9,1},{10,2},{11,3},{12,4},{13,5},{14,6},{15,7}} | collective-permute-start | bytes 1327112 | tf_op jit(solution)/shard_map/ppermute | solution.py:607
  150.4 112.2 %all-gather.8.cloned.1.call-start = ((), (), s32[]{:S(2)}) async-start(), calls=%async_computation.13 | async-start | bytes 3317760 | tf_op jit(solution)/shard_map/all_gather | solution.py:613
  192.2 177.0 %reduce-scatter.5.cloned.1.call-start = ((), (), s32[]{:S(2)}) async-start(), calls=%async_computation.14 | async-start | bytes 3317760 | tf_op jit(solution)/shard_map/reduce_scatter | solution.py:633
  198.9 8.2 %collective-permute-start.30 = (bf16[2,32,1152]{2,1,0:T(8,128)(2,1)}, bf16[2,32,1152]{2,1,0:T(8,128)(2,1)}, u32[]{:S(2)}, u32[]{:S(2)}) collective-permute-start(bf16[2,32,1152]{2,1,0:T(8,128)(2,1)} %get-tuple-element.361), channel_id=1, source_target_pairs={{0,5},{1,4},{2,7},{3,6},{4,1},{5,0},{6,3},{7,2},{8,13},{9,12},{10,... | collective-permute-start | bytes 442376 | tf_op jit(solution)/shard_map/ppermute | solution.py:584
  248.1 10.2 %collective-permute-start.44 = (bf16[2,32,1152]{2,1,0:T(8,128)(2,1)}, bf16[2,32,1152]{2,1,0:T(8,128)(2,1)S(1)}, u32[]{:S(2)}, u32[]{:S(2)}) collective-permute-start(bf16[2,32,1152]{2,1,0:T(8,128)(2,1)} %get-tuple-element.139.refs_0_), channel_id=1, source_target_pairs={{0,4},{1,5},{2,6},{3,7},{4,0},{5,1},{6,2},{7,3},{8,12},{9,13},{10,... | collective-permute-start | bytes 442376 | tf_op jit(solution)/shard_map/ppermute | solution.py:584
  249.3 9.1 %collective-permute-start.43 = (bf16[2,32,1152]{2,1,0:T(8,128)(2,1)}, bf16[2,32,1152]{2,1,0:T(8,128)(2,1)S(1)}, u32[]{:S(2)}, u32[]{:S(2)}) collective-permute-start(bf16[2,32,1152]{2,1,0:T(8,128)(2,1)} %get-tuple-element.139.refs_0_), channel_id=1, source_target_pairs={{0,1},{1,0},{2,3},{3,2},{4,5},{5,4},{6,7},{7,6},{8,9},{9,8},{10,11... | collective-permute-start | bytes 442376 | tf_op jit(solution)/shard_map/ppermute | solution.py:584
  250.5 9.9 %collective-permute-start.4 = (bf16[2,32,1152]{2,1,0:T(8,128)(2,1)}, bf16[2,32,1152]{2,1,0:T(8,128)(2,1)S(1)}, u32[]{:S(2)}, u32[]{:S(2)}) collective-permute-start(bf16[2,32,1152]{2,1,0:T(8,128)(2,1)} %shard_map.221.refs_0_), channel_id=1, source_target_pairs={{0,5},{1,4},{2,7},{3,6},{4,1},{5,0},{6,3},{7,2},{8,13},{9,12},{10,... | collective-permute-start | bytes 442376 | tf_op jit(solution)/shard_map/ppermute | solution.py:584
  252.4 9.4 %collective-permute-start.3 = (bf16[2,32,1152]{2,1,0:T(8,128)(2,1)}, bf16[2,32,1152]{2,1,0:T(8,128)(2,1)S(1)}, u32[]{:S(2)}, u32[]{:S(2)}) collective-permute-start(bf16[2,32,1152]{2,1,0:T(8,128)(2,1)} %shard_map.221.refs_0_), channel_id=1, source_target_pairs={{0,4},{1,5},{2,6},{3,7},{4,0},{5,1},{6,2},{7,3},{8,12},{9,13},{10,... | collective-permute-start | bytes 442376 | tf_op jit(solution)/shard_map/ppermute | solution.py:584
  261.9 13.7 %collective-permute-start.5 = (bf16[3,2,32,1152]{3,2,1,0:T(8,128)(2,1)S(1)}, bf16[3,2,32,1152]{3,2,1,0:T(8,128)(2,1)}, u32[]{:S(2)}, u32[]{:S(2)}) collective-permute-start(bf16[3,2,32,1152]{3,2,1,0:T(8,128)(2,1)S(1)} %pad_maximum_fusion.refs_2_), channel_id=1, source_target_pairs={{0,2},{1,3},{2,0},{3,1},{4,6},{5,7},{6,4},{7,5},{8,10},{9,11},{10,... | collective-permute-start | bytes 1327112 | tf_op jit(solution)/shard_map/ppermute | solution.py:584
  262.4 13.1 %collective-permute-start.1 = (bf16[2,32,1152]{2,1,0:T(8,128)(2,1)}, bf16[2,32,1152]{2,1,0:T(8,128)(2,1)}, u32[]{:S(2)}, u32[]{:S(2)}) collective-permute-start(bf16[2,32,1152]{2,1,0:T(8,128)(2,1)} %shard_map.221.refs_0_), channel_id=1, source_target_pairs={{0,2},{1,3},{2,0},{3,1},{4,6},{5,7},{6,4},{7,5},{8,10},{9,11},{10,... | collective-permute-start | bytes 442376 | tf_op jit(solution)/shard_map/ppermute | solution.py:584
  287.0 132.8 %reduce-scatter.7.cloned.1.call-start = ((), (), s32[]{:S(2)}) async-start(), calls=%async_computation.15 | async-start | bytes 2211840 | tf_op jit(solution)/shard_map/reduce_scatter | solution.py:633
  289.6 8.1 %collective-permute-start.48 = (bf16[2,32,1152]{2,1,0:T(8,128)(2,1)}, bf16[2,32,1152]{2,1,0:T(8,128)(2,1)S(1)}, u32[]{:S(2)}, u32[]{:S(2)}) collective-permute-start(bf16[2,32,1152]{2,1,0:T(8,128)(2,1)} %copy-done.33), channel_id=1, source_target_pairs={{0,5},{1,4},{2,7},{3,6},{4,1},{5,0},{6,3},{7,2},{8,13},{9,12},{10,... | collective-permute-start | bytes 442376 | tf_op jit(solution)/shard_map/ppermute | solution.py:584
  325.8 151.3 %reduce-scatter.11.cloned.1.call-start = ((), (), s32[]{:S(2)}) async-start(), calls=%async_computation.17 | async-start | bytes 3317760 | tf_op jit(solution)/shard_map/reduce_scatter | solution.py:633
  330.2 9.0 %collective-permute-start.61 = (bf16[2,32,1152]{2,1,0:T(8,128)(2,1)S(1)}, bf16[2,32,1152]{2,1,0:T(8,128)(2,1)S(1)}, u32[]{:S(2)}, u32[]{:S(2)}) collective-permute-start(bf16[2,32,1152]{2,1,0:T(8,128)(2,1)S(1)} %get-tuple-element.345), channel_id=1, source_target_pairs={{0,5},{1,4},{2,7},{3,6},{4,1},{5,0},{6,3},{7,2},{8,13},{9,12},{10,... | collective-permute-start | bytes 442376 | tf_op jit(solution)/shard_map/ppermute | solution.py:584
  331.4 8.7 %collective-permute-start.59 = (bf16[2,32,1152]{2,1,0:T(8,128)(2,1)S(1)}, bf16[2,32,1152]{2,1,0:T(8,128)(2,1)S(1)}, u32[]{:S(2)}, u32[]{:S(2)}) collective-permute-start(bf16[2,32,1152]{2,1,0:T(8,128)(2,1)S(1)} %copy-done.30), channel_id=1, source_target_pairs={{0,4},{1,5},{2,6},{3,7},{4,0},{5,1},{6,2},{7,3},{8,12},{9,13},{10,... | collective-permute-start | bytes 442376 | tf_op jit(solution)/shard_map/ppermute | solution.py:584
  332.8 9.6 %collective-permute-start.58 = (bf16[2,32,1152]{2,1,0:T(8,128)(2,1)S(1)}, bf16[2,32,1152]{2,1,0:T(8,128)(2,1)S(1)}, u32[]{:S(2)}, u32[]{:S(2)}) collective-permute-start(bf16[2,32,1152]{2,1,0:T(8,128)(2,1)S(1)} %copy-done.28), channel_id=1, source_target_pairs={{0,1},{1,0},{2,3},{3,2},{4,5},{5,4},{6,7},{7,6},{8,9},{9,8},{10,11... | collective-permute-start | bytes 442376 | tf_op jit(solution)/shard_map/ppermute | solution.py:584
  334.6 9.8 %collective-permute-start.57 = (bf16[2,32,1152]{2,1,0:T(8,128)(2,1)S(1)}, bf16[2,32,1152]{2,1,0:T(8,128)(2,1)S(1)}, u32[]{:S(2)}, u32[]{:S(2)}) collective-permute-start(bf16[2,32,1152]{2,1,0:T(8,128)(2,1)S(1)} %copy-done.26), channel_id=1, source_target_pairs={{0,5},{1,4},{2,7},{3,6},{4,1},{5,0},{6,3},{7,2},{8,13},{9,12},{10,... | collective-permute-start | bytes 442376 | tf_op jit(solution)/shard_map/ppermute | solution.py:584
  365.6 136.4 %reduce-scatter.9.cloned.1.call-start = ((), (), s32[]{:S(2)}) async-start(), calls=%async_computation.16 | async-start | bytes 2211840 | tf_op jit(solution)/shard_map/reduce_scatter | solution.py:633
  397.0 52.7 %collective-permute-start.83 = (bf16[2,32,1152]{2,1,0:T(8,128)(2,1)}, bf16[2,32,1152]{2,1,0:T(8,128)(2,1)}, u32[]{:S(2)}, u32[]{:S(2)}) collective-permute-start(bf16[2,32,1152]{2,1,0:T(8,128)(2,1)} %copy-done.65), channel_id=1, source_target_pairs={{0,1},{2,3},{4,5},{6,7},{8,9},{10,11},{12,13},{14,15},{16,17},{18,... | collective-permute-start | bytes 442376 | tf_op jit(solution)/shard_map/ppermute | solution.py:1051
  419.8 89.0 %collective-permute-start.85 = (bf16[288,768]{1,0:T(8,128)(2,1)}, bf16[288,768]{1,0:T(8,128)(2,1)}, u32[]{:S(2)}, u32[]{:S(2)}) collective-permute-start(bf16[288,768]{1,0:T(8,128)(2,1)} %reduce-scatter.7.cloned.1.call-done), channel_id=1, source_target_pairs={{0,1},{2,3},{4,5},{6,7},{8,9},{10,11},{12,13},{14,15},{16,17},{18,... | collective-permute-start | bytes 1327112 | tf_op jit(solution)/shard_map/ppermute | solution.py:987
  426.1 9.8 %collective-permute-start.81 = (bf16[2,32,1152]{2,1,0:T(8,128)(2,1)}, bf16[2,32,1152]{2,1,0:T(8,128)(2,1)}, u32[]{:S(2)}, u32[]{:S(2)}) collective-permute-start(bf16[2,32,1152]{2,1,0:T(8,128)(2,1)} %get-tuple-element.335.refs_6_), channel_id=1, source_target_pairs={{0,4},{1,5},{2,6},{3,7},{4,0},{5,1},{6,2},{7,3},{8,12},{9,13},{10,... | collective-permute-start | bytes 442376 | tf_op jit(solution)/shard_map/ppermute | solution.py:584
  426.9 12.8 %collective-permute-start.80 = (bf16[2,32,1152]{2,1,0:T(8,128)(2,1)}, bf16[2,32,1152]{2,1,0:T(8,128)(2,1)}, u32[]{:S(2)}, u32[]{:S(2)}) collective-permute-start(bf16[2,32,1152]{2,1,0:T(8,128)(2,1)} %get-tuple-element.336.refs_5_), channel_id=1, source_target_pairs={{0,1},{1,0},{2,3},{3,2},{4,5},{5,4},{6,7},{7,6},{8,9},{9,8},{10,11... | collective-permute-start | bytes 442376 | tf_op jit(solution)/shard_map/ppermute | solution.py:584
  426.9 12.8 %collective-permute-start.79 = (bf16[2,32,1152]{2,1,0:T(8,128)(2,1)}, bf16[2,32,1152]{2,1,0:T(8,128)(2,1)}, u32[]{:S(2)}, u32[]{:S(2)}) collective-permute-start(bf16[2,32,1152]{2,1,0:T(8,128)(2,1)} %get-tuple-element.337.refs_7_), channel_id=1, source_target_pairs={{0,5},{1,4},{2,7},{3,6},{4,1},{5,0},{6,3},{7,2},{8,13},{9,12},{10,... | collective-permute-start | bytes 442376 | tf_op jit(solution)/shard_map/ppermute | solution.py:584
  437.0 61.1 %collective-permute-start.87 = (bf16[288,1152]{1,0:T(8,128)(2,1)S(1)}, bf16[288,1152]{1,0:T(8,128)(2,1)}, u32[]{:S(2)}, u32[]{:S(2)}) collective-permute-start(bf16[288,1152]{1,0:T(8,128)(2,1)S(1)} %copy-done.112), channel_id=1, source_target_pairs={{0,1},{2,3},{4,5},{6,7},{8,9},{10,11},{12,13},{14,15},{16,17},{18,... | collective-permute-start | bytes 1990664 | tf_op jit(solution)/shard_map/ppermute | solution.py:987
  445.5 9.9 %all-to-all-start.3 = ((f32[8,1,6656]{2,1,0:T(1,128)}), f32[8,1,6656]{2,1,0:T(1,128)S(1)}, u32[]{:S(2)}, u32[]{:S(2)}) async-start(f32[8,1,6656]{2,1,0:T(1,128)} %copy.112), calls=%async_computation.5 | async-start | bytes 425984 | tf_op jit(solution)/shard_map/all_to_all | solution.py:1024
  456.4 14.9 %all-to-all-start.4 = ((f32[4,1,9856]{2,1,0:T(1,128)}), f32[4,1,9856]{2,1,0:T(1,128)S(1)}, u32[]{:S(2)}, u32[]{:S(2)}) async-start(f32[4,1,9856]{2,1,0:T(1,128)} %broadcast_in_dim.105), calls=%async_computation.6 | async-start | bytes 315392 | tf_op jit(solution)/shard_map/all_to_all | solution.py:603
  472.9 9.7 %all-to-all-start.5 = ((f32[4,2,288]{2,1,0:T(2,128)}), f32[4,2,288]{2,1,0:T(2,128)S(1)}, u32[]{:S(2)}, u32[]{:S(2)}) async-start(f32[4,2,288]{2,1,0:T(2,128)} %fusion), calls=%async_computation.7 | async-start | bytes 24576 | tf_op jit(solution)/shard_map/all_to_all | solution.py:1035
  477.1 21.0 %collective-permute-start.86 = (bf16[288,1152]{1,0:T(8,128)(2,1)}, bf16[288,1152]{1,0:T(8,128)(2,1)}, u32[]{:S(2)}, u32[]{:S(2)}) collective-permute-start(bf16[288,1152]{1,0:T(8,128)(2,1)} %reduce-scatter.11.cloned.1.call-done), channel_id=1, source_target_pairs={{1,0},{3,2},{5,4},{7,6},{9,8},{11,10},{13,12},{15,14},{17,16},{19,... | collective-permute-start | bytes 1990664 | tf_op jit(solution)/shard_map/ppermute | solution.py:988
  483.2 14.0 %all-to-all-start.6 = ((f32[8,4,2,288]{3,2,1,0:T(2,128)}), f32[8,4,2,288]{3,2,1,0:T(2,128)S(1)}, u32[]{:S(2)}, u32[]{:S(2)}) async-start(f32[8,4,2,288]{3,2,1,0:T(2,128)} %broadcast_in_dim.106), calls=%async_computation.8 | async-start | bytes 196608 | tf_op jit(solution)/shard_map/all_to_all | solution.py:603
  502.0 14.0 %collective-permute-start.84 = (bf16[288,768]{1,0:T(8,128)(2,1)}, bf16[288,768]{1,0:T(8,128)(2,1)}, u32[]{:S(2)}, u32[]{:S(2)}) collective-permute-start(bf16[288,768]{1,0:T(8,128)(2,1)} %reduce-scatter.9.cloned.1.call-done), channel_id=1, source_target_pairs={{1,0},{3,2},{5,4},{7,6},{9,8},{11,10},{13,12},{15,14},{17,16},{19,... | collective-permute-start | bytes 1327112 | tf_op jit(solution)/shard_map/ppermute | solution.py:988
  (191 other events, 1182.6 us)
Sparse Core Ops, SparseCore 0:
  40.7 66.1 all-gather.3
  150.5 38.6 all-gather.5
  192.3 52.9 all-gather.7
  287.1 50.1 reduce-scatter.4
  340.1 38.0 reduce-scatter.6
  380.5 51.7 reduce-scatter.10
  436.0 39.8 reduce-scatter.8

commit v2 on v1

--- a/solution.py
+++ b/solution.py
@@ -17,44 +17,73 @@
 PLANE = ("tensor", "section")
 
 
-def call(body, outs, *args, scalars=0, flops=0, scratch=(), after=(), saved=()):
+class Traffic:
+    def __init__(self, arriving, leaving):
+        self.arriving, self.leaving, self.left = arriving, leaving, set()
+
+    def wait(self, *places):
+        for at in places:
+            self.arriving[at].wait()
+
+    def flush(self, *places):
+        for at in places:
+            self.leaving[at].start()
+            self.left.add(at)
+
+
+def call(body, outs, *args, scalars=0, flops=0, scratch=(), after=(), streamed=(), saved=()):
     count, waits, many = len(args), len(after), len(outs)
+    moving = bool(streamed or saved)
 
     def kernel(*refs):
-        ins, out_refs = refs[:count], list(refs[count + waits : count + waits + many])
-        own = refs[count + waits + many : count + waits + many + len(scratch)]
-        held = refs[count + waits + many + len(scratch) :]
-        copies = []
-        for i, at in enumerate(saved):
-            copies.append(pltpu.make_async_copy(held[i], out_refs[at], held[-1].at[i]))
+        ins, out_refs = list(refs[:count]), list(refs[count + waits : count + waits + many])
+        rest = refs[count + waits + many :]
+        own, held = rest[: len(scratch)], rest[len(scratch) :]
+        arriving, leaving = {}, {}
+        for i, at in enumerate(streamed):
+            arriving[at] = pltpu.make_async_copy(ins[at], held[i], held[-1].at[i])
+            ins[at] = held[i]
+        for i, at in enumerate(saved, len(streamed)):
+            leaving[at] = pltpu.make_async_copy(held[i], out_refs[at], held[-1].at[i])
             out_refs[at] = held[i]
-        started = []
-
-        def flush(*places):
-            for at in places:
-                copies[saved.index(at)].start()
-                started.append(at)
-
-        if saved:
-            body(flush, *ins, *out_refs, *own)
+        traffic = Traffic(arriving, leaving)
+        for copy in arriving.values():
+            copy.start()
+        if moving:
+            body(traffic, *ins, *out_refs, *own)
         else:
             body(*ins, *out_refs, *own)
-        flush(*[at for at in saved if at not in started])
-        for copy in copies:
+        traffic.flush(*[at for at in saved if at not in traffic.left])
+        for copy in leaving.values():
             copy.wait()
 
     moved = sum(a.size * a.dtype.itemsize for a in args)
     moved += sum(math.prod(o.shape) * o.dtype.itemsize for o in outs)
     specs = [pl.BlockSpec(memory_space=pltpu.SMEM)] * scalars
-    specs += [pl.BlockSpec(memory_space=pltpu.VMEM)] * (count - scalars)
-    specs += [pl.BlockSpec(memory_space=pl.ANY)] * waits
+    specs += [
+        pl.BlockSpec(memory_space=pltpu.HBM if i in streamed else pltpu.VMEM)
+        for i in range(scalars, count)
+    ]
+    large = [a.size > 2**17 for a in after]
+    specs += [pl.BlockSpec(memory_space=pltpu.HBM if v else pl.ANY) for v in large]
+    after = [
+        pltpu.with_memory_space_constraint(a, pltpu.HBM) if v else a for a, v in zip(after, large)
+    ]
     spaces = [pltpu.HBM if i in saved else pltpu.VMEM for i in range(many)]
-    hold = [pltpu.VMEM(outs[i].shape, outs[i].dtype) for i in saved]
-    if saved:
-        hold.append(pltpu.SemaphoreType.DMA((len(saved),)))
+    shapes = [
+        pltpu.HBM(o.shape, o.dtype) if i in saved else o for i, o in enumerate(outs)
+    ]
+    args = [
+        pltpu.with_memory_space_constraint(a, pltpu.HBM) if i in streamed else a
+        for i, a in enumerate(args)
+    ]
+    hold = [pltpu.VMEM(args[i].shape, args[i].dtype) for i in streamed]
+    hold += [pltpu.VMEM(outs[i].shape, outs[i].dtype) for i in saved]
+    if moving:
+        hold.append(pltpu.SemaphoreType.DMA((len(hold),)))
     return pl.pallas_call(
         kernel,
-        out_shape=tuple(outs),
+        out_shape=tuple(shapes),
         in_specs=specs,
         out_specs=tuple(pl.BlockSpec(memory_space=space) for space in spaces),
         scratch_shapes=[*scratch, *hold],
@@ -115,12 +144,17 @@
         n_ref[m] = (hat * (1.0 + mod_ref[m, 1:2]) + mod_ref[m, 0:1]).astype(BF16)
 
 
+def add_kernel(a, b, c, d, recv, *outs):
+    for j, own in enumerate((a, b, c, d)):
+        outs[j][...] = (own[...].astype(F32) + recv[j].astype(F32)).astype(BF16)
+
+
 def scale_rows_kernel(g_ref, mod_ref, o_ref):
     for m in range(g_ref.shape[0]):
         o_ref[m] = (mod_ref[m, 5:6] * g_ref[m].astype(F32)).astype(BF16)
 
 
-def after_attn_kernel(flush, p0, p1, p2, p3, x_ref, mod_ref, att_ref, aft_ref, n_ref):
+def after_attn_kernel(traffic, p0, p1, p2, p3, x_ref, mod_ref, att_ref, aft_ref, n_ref):
     for m in range(x_ref.shape[0]):
         att = gather_total([p.at[m] for p in (p0, p1, p2, p3)])
         aft = x_ref[m].astype(F32) + mod_ref[m, 2:3] * att
@@ -130,7 +164,7 @@
         n_ref[m] = (hat * (1.0 + mod_ref[m, 4:5]) + mod_ref[m, 3:4]).astype(BF16)
 
 
-def between_kernel(p0, p1, p2, p3, aft_ref, mod_ref, next_ref, mlp_ref, x_ref, n_ref):
+def between_kernel(traffic, p0, p1, p2, p3, aft_ref, mod_ref, next_ref, mlp_ref, x_ref, n_ref):
     for m in range(aft_ref.shape[0]):
         mlp = gather_total([p.at[m] for p in (p0, p1, p2, p3)])
         x = (aft_ref[m] + mod_ref[m, 5:6] * mlp).astype(BF16)
@@ -140,14 +174,15 @@
         n_ref[m] = (hat * (1.0 + next_ref[m, 1:2]) + next_ref[m, 0:1]).astype(BF16)
 
 
-def end_kernel(p0, p1, p2, p3, aft_ref, mod_ref, g_ref, x_ref, gate_ref):
+def end_kernel(p0, p1, p2, p3, aft_ref, mod_ref, g_ref, more_ref, x_ref, gm_ref):
     for m in range(aft_ref.shape[0]):
         mlp = gather_total([p.at[m] for p in (p0, p1, p2, p3)])
         x_ref[m] = (aft_ref[m] + mod_ref[m, 5:6] * mlp).astype(BF16)
-        gate_ref[m] = rows_sum(g_ref[m].astype(F32) * mlp)
-
-
-def back_mlp_rows_kernel(p0, p1, p2, p3, g_ref, aft_ref, att_ref, mod_ref, ga_ref, gt_ref, gm_ref):
+        gm_ref[m, 0:5] = more_ref[m]
+        gm_ref[m, 5:6] = rows_sum(g_ref[m].astype(F32) * mlp)
+
+
+def back_mlp_rows_kernel(traffic, p0, p1, p2, p3, g_ref, aft_ref, att_ref, mod_ref, ga_ref, gt_ref, gm_ref):
     for m in range(aft_ref.shape[0]):
         gn = gather_total([p.at[m] for p in (p0, p1, p2, p3)])
         hat, rstd = normalize(aft_ref[m])
@@ -159,31 +194,31 @@
         gm_ref[m, 2:3] = rows_sum(gn * hat)
 
 
-def back_attn_rows(pieces, ga_ref, x_ref, mod_ref, some_ref, gate_ref, gm_ref, m):
+def back_attn_rows(pieces, ga_ref, x_ref, mod_ref, some_ref, gm_ref, m):
     gn = gather_total([p.at[m] for p in pieces])
     hat, rstd = normalize(x_ref[m].astype(F32))
     grad = ga_ref[m] + norm_grad(hat, rstd, gn * (1.0 + mod_ref[m, 1:2]))
     gm_ref[m, 0:1] = rows_sum(gn)
     gm_ref[m, 1:2] = rows_sum(gn * hat)
     gm_ref[m, 2:5] = some_ref[m]
-    gm_ref[m, 5:6] = gate_ref[m]
     return grad.astype(BF16)
 
 
 def back_between_kernel(
-    p0, p1, p2, p3, ga_ref, x_ref, mod_ref, some_ref, gate_ref, prev_ref, mlp_ref, g_ref, gmlp_ref, gm_ref, next_ref
+    p0, p1, p2, p3, ga_ref, x_ref, mod_ref, some_ref, prev_ref, mlp_ref, g_ref, gmlp_ref, gm_ref, gate_ref
 ):
     for m in range(x_ref.shape[0]):
-        grad = back_attn_rows((p0, p1, p2, p3), ga_ref, x_ref, mod_ref, some_ref, gate_ref, gm_ref, m)
+        grad = back_attn_rows((p0, p1, p2, p3), ga_ref, x_ref, mod_ref, some_ref, gm_ref, m)
         g_ref[m] = grad
         wide = grad.astype(F32)
         gmlp_ref[m] = (prev_ref[m, 5:6] * wide).astype(BF16)
-        next_ref[m] = rows_sum(wide * mlp_ref[m])
+        gate_ref[m] = rows_sum(wide * mlp_ref[m])
 
 
 def back_end_kernel(p0, p1, p2, p3, ga_ref, x_ref, mod_ref, some_ref, gate_ref, g_ref, gm_ref):
     for m in range(x_ref.shape[0]):
-        g_ref[m] = back_attn_rows((p0, p1, p2, p3), ga_ref, x_ref, mod_ref, some_ref, gate_ref, gm_ref, m)
+        g_ref[m] = back_attn_rows((p0, p1, p2, p3), ga_ref, x_ref, mod_ref, some_ref, gm_ref, m)
+        gm_ref[m, 5:6] = gate_ref[m]
 
 
 def scan_mask(columns_first):
@@ -272,8 +307,8 @@
 
 
 def each_shard(refs):
-    own, core, three, crossed = refs
-    return (own, three.at[0], core, crossed.at[0], three.at[1], three.at[2], crossed.at[1], crossed.at[2])
+    own, x, y, xy, core, core_x, core_y, core_xy = refs
+    return own, x, core, core_x, y, xy, core_y, core_xy
 
 
 def gather_pieces(me, shard_refs, full_ref):
@@ -304,8 +339,8 @@
     return first, pltpu.roll(tiles[2], shift, 1)
 
 
-def pack_attn_kernel(cfg, sec_ref, in_ref, gate_ref, out_ref, keep_ref, send_ref):
-    heads, channels = cfg
+def pack_kernel(cfg, sec_ref, in_ref, gate_ref, out_ref, up_ref, down_ref, keep_ref, send_ref, keep_b_ref, send_b_ref):
+    heads, channels, main, left = cfg
     spots = tail_spots(heads)
     tail = channels - LANES
     rows = in_ref.shape[1]
@@ -328,8 +363,20 @@
         cols = slice(j * LANES, (j + 1) * LANES)
         keep_ref[:, cols] = jnp.where(keep_first, whole[0], whole[1]).astype(BF16)
         send_ref[:, cols] = jnp.where(keep_first, whole[1], whole[0]).astype(BF16)
-    keep_ref[:, 5 * LANES :] = jnp.where(keep_first, tails[0], tails[1]).astype(BF16)
-    send_ref[:, 5 * LANES :] = jnp.where(keep_first, tails[1], tails[0]).astype(BF16)
+    cols = slice(5 * LANES, 6 * LANES)
+    keep_ref[:, cols] = jnp.where(keep_first, tails[0], tails[1]).astype(BF16)
+    send_ref[:, cols] = jnp.where(keep_first, tails[1], tails[0]).astype(BF16)
+    at = 0
+    for ref in (up_ref, down_ref):
+        low, high = ref[:, :main], ref[:, main : 2 * main]
+        keep_b_ref[:, at : at + main] = jnp.where(keep_first, low, high)
+        send_b_ref[:, at : at + main] = jnp.where(keep_first, high, low)
+        at += main
+    up, down = (ref[:, 2 * main :].astype(F32) for ref in (up_ref, down_ref))
+    low = jnp.where(lane < left, up, pltpu.roll(down, left, 1)).astype(BF16)
+    high = jnp.where(lane < left, pltpu.roll(up, left, 1), down).astype(BF16)
+    keep_b_ref[:, at:] = jnp.where(keep_first, low, high)
+    send_b_ref[:, at:] = jnp.where(keep_first, high, low)
 
 
 def unpack_attn_kernel(cfg, sec_ref, mine_ref, recv_ref, in_ref, gate_ref, out_ref):
@@ -341,7 +388,7 @@
     shift = channels - LANES
 
     def both(cols):
-        mine, recv = mine_ref[:, cols], recv_ref[:, cols].astype(F32)
+        mine, recv = mine_ref[:, cols].astype(F32), recv_ref[:, cols].astype(F32)
         return jnp.where(mine_first, mine, recv), jnp.where(mine_first, recv, mine)
 
     low_tails, high_tails = both(slice(5 * LANES, 6 * LANES))
@@ -360,11 +407,11 @@
     gate_ref[...] = jnp.where(lane < heads, low_gate, high_gate)[:, : 2 * heads]
 
 
-def attn_forward_kernel(cfg, flush, me_ref, *refs):
+def attn_forward_kernel(cfg, traffic, me_ref, *refs):
     columns_first, heads, head_width = cfg
-    shards, (w_ref, gb_ref, tap_ref) = refs[:4], refs[4:7]
-    n_ref, proj_ref, log_ref, attn_ref, mix_ref, other_ref = refs[7:13]
-    own_refs, total_ref = refs[13:17], refs[17]
+    shards, (w_ref, gb_ref, tap_ref) = refs[:8], refs[8:11]
+    n_ref, proj_ref, log_ref, attn_ref, mix_ref, other_ref = refs[11:17]
+    own_refs, total_ref = refs[17:21], refs[21]
     me = me_ref[0]
     wide = 2 * LANES
     gate_lane = heads * head_width - LANES
@@ -373,7 +420,8 @@
     column = grid_column()
     sets = lane_sets(wide, 0, head_width, heads)
     gather_pieces(me, shards, n_ref)
-    flush(0)
+    traffic.flush(0)
+    traffic.wait(9)
     for m in range(n_ref.shape[0]):
         projected = mm(n_ref[m], w_ref[:, : 4 * LANES])
         tails = mm(n_ref[m], w_ref[:, 5 * LANES :])
@@ -405,16 +453,16 @@
         ).astype(BF16)
         mix_ref[m] = mixed
         if m == n_ref.shape[0] - 1:
-            flush(1, 2, 3, 4)
+            traffic.flush(1, 2, 3, 4)
         total_ref[m] = mm_nt(mixed, w_ref[:, 4 * LANES :]).astype(BF16)
     write_pieces(me, total_ref, other_ref, own_refs)
 
 
-def attn_backward_kernel(cfg, me_ref, *refs):
+def attn_backward_kernel(cfg, traffic, me_ref, *refs):
     columns_first, heads, head_width = cfg
-    shards, (proj_ref, log_ref, attn_ref, w_ref, tap_ref) = refs[:4], refs[4:9]
-    g_ref, gproj_ref, gtap_ref, other_ref = refs[9:13]
-    own_refs, total_ref = refs[13:17], refs[17]
+    shards, (proj_ref, log_ref, attn_ref, w_ref, tap_ref) = refs[:8], refs[8:13]
+    g_ref, gproj_ref, gtap_ref, other_ref = refs[13:17]
+    own_refs, total_ref = refs[17:21], refs[21]
     me = me_ref[0]
     wide = 2 * LANES
     gate_lane = heads * head_width - LANES
@@ -430,6 +478,7 @@
         in_head = in_head | own
     gather_pieces(me, shards, g_ref)
     gtap_ref[...] = jnp.zeros(gtap_ref.shape, F32)
+    traffic.wait(9, 10, 11, 12)
     for m in range(g_ref.shape[0]):
         g_packed = mm(g_ref[m], w_ref[:, 4 * LANES :])
         g_mixed = jnp.where(in_head, join_tail(g_packed, 0, g_packed[:, LANES:], spots[4]), 0.0)
@@ -485,7 +534,8 @@
     write_pieces(me, total_ref, other_ref, own_refs)
 
 
-def attn_weights_kernel(n_ref, gproj_ref, g_ref, mix_ref, gw_ref):
+def attn_weights_kernel(traffic, n_ref, gproj_ref, g_ref, mix_ref, gw_ref):
+    traffic.wait(0, 3)
     for part in range(2):
         cols = slice(part * 2 * LANES, (part + 1) * 2 * LANES)
         total = mm_tn(n_ref[0], gproj_ref[0, :, cols])
@@ -509,6 +559,10 @@
         )
 
 
+def stack_kernel(traffic, *refs):
+    stack_shards(refs[:8], refs[8])
+
+
 def put_shard(k, value, shape, other_ref, own_refs):
     own, other = send_order(k)
     if own is None:
@@ -523,13 +577,14 @@
         put_shard(k, total[k * rows : (k + 1) * rows], shape, other_ref, own_refs)
 
 
-def mlp_forward_kernel(left, flush, *refs):
-    shards, (w_ref, ub_ref) = refs[:4], refs[4:6]
-    n_ref, pre_ref, hid_ref, other_ref = refs[6:10]
-    own_refs = refs[10:14]
+def mlp_forward_kernel(left, traffic, *refs):
+    shards, (w_ref, ub_ref) = refs[:8], refs[8:10]
+    n_ref, pre_ref, hid_ref, other_ref = refs[10:14]
+    own_refs = refs[14:18]
     main = (w_ref.shape[1] - LANES) // 2
     stack_shards(shards, n_ref)
-    flush(0)
+    traffic.flush(0)
+    traffic.wait(8)
     n = n_ref[...]
     pre = mm(n, w_ref[:, :main]) + ub_ref[:, :main]
     pre_ref[:, :main] = pre
@@ -541,17 +596,25 @@
     tail = jnp.where(lane < left, gelu_terms(last)[0], 0.0)
     tail = pltpu.roll(tail, LANES - left, 1).astype(BF16)
     hid_ref[:, main:] = tail
-    flush(1, 2)
+    traffic.flush(1, 2)
     total = mm_nt(hidden, w_ref[:, main : 2 * main]) + mm_nt(tail, w_ref[:, 2 * main :])
     put_shards(total, shards[0].shape, other_ref, own_refs)
 
 
-def mlp_backward_kernel(left, *refs):
-    shards, (pre_ref, w_ref) = refs[:4], refs[4:6]
-    g_ref, gpre_ref, gub_ref, other_ref = refs[6:10]
-    own_refs = refs[10:14]
+def mlp_backward_kernel(left, traffic, *refs):
+    count = 1 if len(refs) == 10 else 8
+    given, (pre_ref, w_ref) = refs[:count], refs[count : count + 2]
+    rest = refs[count + 2 :]
+    if count == 8:
+        g_ref, rest = rest[0], rest[1:]
+        stack_shards(given, g_ref)
+        traffic.wait(8, 9)
+    else:
+        g_ref = given[0]
+        traffic.wait(0, 1, 2)
+    gpre_ref, gub_ref, other_ref = rest[:3]
+    own_refs = rest[3:]
     main = (w_ref.shape[1] - LANES) // 2
-    stack_shards(shards, g_ref)
     g = g_ref[...]
     g_pre = mm(g, w_ref[:, main : 2 * main]) * gelu_terms(pre_ref[:, :main])[1]
     g_pre = g_pre.astype(BF16)
@@ -563,11 +626,12 @@
     gpre_ref[:, main:] = last
     gub_ref[:, main:] = rows_sum(last.astype(F32))
     total = mm_nt(g_pre, w_ref[:, :main]) + mm_nt(last, w_ref[:, 2 * main :])
-    put_shards(total, shards[0].shape, other_ref, own_refs)
-
-
-def mlp_weights_kernel(n_ref, gpre_ref, g_ref, hid_ref, gw_ref):
+    put_shards(total, own_refs[0].shape, other_ref, own_refs)
+
+
+def mlp_weights_kernel(traffic, n_ref, gpre_ref, g_ref, hid_ref, gw_ref):
     main = gpre_ref.shape[1] - LANES
+    traffic.wait(0, 3)
     gw_ref[:, :main] = mm_tn(n_ref[...], gpre_ref[:, :main]).astype(BF16)
     gw_ref[:, main : 2 * main] = mm_tn(g_ref[...], hid_ref[:, :main]).astype(BF16)
     last = mm_tn(n_ref[...], gpre_ref[:, main:]) + mm_tn(g_ref[...], hid_ref[:, main:])
@@ -585,16 +649,14 @@
 
 
 def gather_plane(own):
-    core = swap(own, 1, 0)
     xy, x, y = swap(own, 2, 1), swap(own, 0, 1), swap(own, 2, 0)
-    three = jnp.stack([x, y, xy])
-    return own, core, three, swap(three, 1, 0)
+    return own, x, y, xy, *(swap(v, 1, 0) for v in (own, x, y, xy))
 
 
 def scatter_plane(other, own):
     received = swap(other, 1, 0)
-    sums = [(o.astype(F32) + received[j].astype(F32)).astype(BF16) for j, o in enumerate(own)]
-    return (sums[0], swap(sums[3], 2, 1), swap(sums[1], 0, 1), swap(sums[2], 2, 0)), sums
+    sums = call(add_kernel, (out(own[0].shape, BF16),) * 4, *own, received)
+    return (sums[0], swap(sums[3], 2, 1), swap(sums[1], 0, 1), swap(sums[2], 2, 0))
 
 
 def spread_over(value, axes):
@@ -603,50 +665,12 @@
     return lax.all_to_all(copies, axes, split_axis=0, concat_axis=0, tiled=True)
 
 
-def along(value, pairs):
-    return lax.ppermute(value, "dp", pairs)
-
-
-def gather_rows(own, ring=False):
-    count = lax.axis_size("dp")
-    if count != 4 or not ring:
-        return lax.all_gather(own, "dp", axis=0, tiled=True)
-    d = lax.axis_index("dp")
-    rows = own.shape[0]
-    r1 = along(own, [(0, 1), (1, 2), (2, 3)])
-    l1 = along(own, [(3, 2), (2, 1), (1, 0)])
-    r2 = along(r1, [(1, 2), (2, 3)])
-    l2 = along(l1, [(2, 1), (1, 0)])
-    r3 = along(r2, [(2, 3)])
-    l3 = along(l2, [(1, 0)])
-    full = jnp.zeros((count * rows, own.shape[1]), own.dtype)
-    full = lax.dynamic_update_slice_in_dim(full, own, d * rows, 0)
-    for k, (left, right) in enumerate(((r3, l1), (r2, l2), (r1, l3)), 1):
-        piece = jnp.where(d + k < count, right, left)
-        full = lax.dynamic_update_slice_in_dim(full, piece, (d + k) % count * rows, 0)
-    return full
-
-
-def scatter_rows(partial, ring=False):
-    count = lax.axis_size("dp")
-    if count != 4 or not ring:
-        return lax.psum_scatter(partial, "dp", scatter_dimension=0, tiled=True).astype(F32)
-    d = lax.axis_index("dp")
-    parts = partial.reshape(count, partial.shape[0] // count, partial.shape[1])
-
-    def part(at):
-        return lax.dynamic_index_in_dim(parts, at % count, 0, keepdims=False)
-
-    def plus(a, b):
-        return (a.astype(F32) + b.astype(F32)).astype(BF16)
-
-    l1 = along(part(d + 1), [(3, 2)])
-    r1 = along(part(d + 3), [(0, 1)])
-    l2 = along(plus(part(d + 2), l1), [(3, 2), (2, 1)])
-    r2 = along(plus(part(d + 2), r1), [(0, 1), (1, 2)])
-    l3 = along(plus(part(d + 3), l2), [(3, 2), (2, 1), (1, 0)])
-    r3 = along(plus(part(d + 1), r2), [(0, 1), (1, 2), (2, 3)])
-    return part(d).astype(F32) + l3.astype(F32) + r3.astype(F32)
+def gather_all(own):
+    return lax.all_gather(own, "dp", axis=0, tiled=True)
+
+
+def scatter_rows(partial):
+    return lax.psum_scatter(partial, "dp", scatter_dimension=0, tiled=True)
 
 
 def sinusoid(time_steps, channels):
@@ -707,9 +731,24 @@
     def choose(pair):
         return jnp.where(first, pair[0], pair[1]), jnp.where(first, pair[1], pair[0])
 
-    shape_a = (slab, 6 * LANES)
     cfg = (heads, channels)
     section = s.astype(jnp.int32).reshape(1)
+    shape_a, shape_b = (slab, 6 * LANES), (slab, 2 * main + LANES)
+    kept_a, sent_a, kept_b, sent_b = call(
+        functools.partial(pack_kernel, (*cfg, main, left)),
+        (out(shape_a, BF16),) * 2 + (out(shape_b, BF16),) * 2,
+        section,
+        in_weight[0],
+        jnp.pad(gate_weight[0].astype(F32), ((0, 0), (0, LANES - gate_weight.shape[2]))),
+        out_weight[0].T,
+        up_weight[0],
+        down_weight[0].T,
+        scalars=1,
+    )
+    sent_a, condition = lax.optimization_barrier((sent_a, condition))
+    received_a = lax.ppermute(sent_a, "section", [(0, 1), (1, 0)])
+    received_b = lax.ppermute(sent_b, "section", [(0, 1), (1, 0)])
+
     def unit_halves(value):
         rest = sections * main
         return tuple(
@@ -717,9 +756,6 @@
             for h in (0, 1)
         )
 
-    def pack_b(up_half, down_half):
-        return jnp.concatenate([up_half[0], down_half[0], up_half[1], down_half[1]], axis=1)
-
     def pack_small(gate_half, taps_half, up_half):
         return jnp.concatenate([gate_half.reshape(-1), taps_half.reshape(-1), up_half.reshape(-1)])
 
@@ -732,25 +768,6 @@
     )
     x0 = jnp.where(first, x_pair[0], x_received)
     g1 = jnp.where(first, x_received, x_pair[1])
-    kept_b, sent_b = choose(
-        pack_halves(pack_b, unit_halves(up_weight[0]), unit_halves(down_weight[0].T))
-    )
-    in_own, sent_b = lax.optimization_barrier((in_weight[0], sent_b))
-    packs_b = swap_halves(kept_b, sent_b)
-    kept_a, sent_a = (
-        call(
-            functools.partial(pack_attn_kernel, cfg),
-            (out(shape_a, BF16),) * 2,
-            section,
-            in_own,
-            jnp.pad(gate_weight[0].astype(F32), ((0, 0), (0, LANES - gate_weight.shape[2]))),
-            out_weight[0].T,
-            scalars=1,
-        )
-    )
-
-    kept_a, sent_a, condition = lax.optimization_barrier((kept_a, sent_a, condition))
-    packs_a = swap_halves(kept_a, sent_a)
     taps_count = conv_taps.shape[1]
     up_row = up_bias[0].astype(F32)[None]
     small = swap_halves(
@@ -771,22 +788,19 @@
         up_row = packed[heads + taps_count * channels :][None]
         return gate_row, taps, jnp.pad(up_row, ((0, 0), (0, main + LANES - units)))
 
-    weights = [
-        (gather_rows(packs_a[b], b == 0), gather_rows(packs_b[b]), *unpack_small(small[b]))
-        for b in (0, 1)
-    ]
-
     cond_vec = condition + sinusoid(timesteps, width)
     activated = jax.nn.silu(cond_vec).astype(BF16)
     slab_active = activated.reshape(images, dps, slab).transpose(1, 0, 2)
     slab_active = lax.all_to_all(slab_active, "dp", split_axis=0, concat_axis=0, tiled=True)
     slab_active = slab_active.reshape(dps * images, slab)
+    slab_active, received_a = lax.optimization_barrier((slab_active, received_a))
     mod_part = jnp.dot(slab_active, ada_weight[0], preferred_element_type=F32)
     mod_parts = lax.all_to_all(
         mod_part.reshape(dps, images, -1), "dp", split_axis=0, concat_axis=0, tiled=True
     )
     mod_share = jnp.sum(mod_parts, axis=0) + ada_bias[0].astype(F32)
     mod_all = spread_over(mod_share, ("section", "tensor"))
+    received_b, mod_all = lax.optimization_barrier((received_b, mod_all))
     mod_all = mod_all.reshape(sections, tensors, images, -1).transpose(0, 2, 1, 3)
     mod_all = mod_all.reshape(sections, images, 6, width)
     mods = (mod_all[0], mod_all[1])
@@ -803,7 +817,7 @@
     attn_flops = 2 * total_rows * width * wide * 5 + middle_flops
     mlp_flops = 4 * total_rows * width * units
 
-    def attn_forward(b, normed):
+    def attn_forward(b, shards):
         w, _, gate_row, taps, _ = weights[b]
         body = functools.partial(attn_forward_kernel, (b == 1, heads, head_width))
         found = call(
@@ -817,18 +831,19 @@
                 *pieces_out,
             ),
             me,
-            *gather_plane(normed),
+            *shards,
             w,
             gate_row,
             taps,
             scalars=1,
             flops=attn_flops,
             scratch=[kept],
+            streamed=(9,),
             saved=(0, 1, 2, 3, 4),
         )
-        return found[:5], scatter_plane(found[5], found[6:])[0]
-
-    def attn_backward(b, grad, saved):
+        return found[:5], scatter_plane(found[5], found[6:])
+
+    def attn_backward(b, shards, saved, after=()):
         w, _, _, taps, _ = weights[b]
         body = functools.partial(attn_backward_kernel, (b == 1, heads, head_width))
         found = call(
@@ -840,7 +855,7 @@
                 *pieces_out,
             ),
             me,
-            *gather_plane(grad),
+            *shards,
             saved[1],
             saved[2],
             saved[3],
@@ -849,8 +864,10 @@
             scalars=1,
             flops=2 * attn_flops,
             scratch=[kept],
+            streamed=(9, 10, 11, 12),
+            after=after,
         )
-        terms, sums = scatter_plane(found[3], found[4:])
+        terms = scatter_plane(found[3], found[4:])
         (grads,) = call(
             attn_weights_kernel,
             (out((width, 6 * LANES), BF16),),
@@ -859,11 +876,13 @@
             found[0],
             saved[4],
             flops=2 * total_rows * width * wide * 5,
-            after=sums,
+            after=terms if b else (),
+            streamed=(0, 3),
+            saved=(0,),
         )
         return terms, grads, found[2]
 
-    def mlp_forward(b, normed):
+    def mlp_forward(b, normed, late):
         _, w, _, _, up_row = weights[b]
         found = call(
             functools.partial(mlp_forward_kernel, left),
@@ -877,21 +896,28 @@
             w,
             up_row,
             flops=mlp_flops,
-            saved=(0, 1, 2),
+            streamed=(8,),
+            saved=tuple(range(8)) if late else (0, 1, 2),
         )
-        return found[:3], scatter_plane(found[3], found[4:])[0]
-
-    def mlp_backward(b, shards, saved):
+        return found[:3], found[3:]
+
+    def mlp_backward(b, given, saved, after=()):
         _, w, _, _, _ = weights[b]
+        gathered = len(given) == 1
+        outs = (out((total_rows, main + LANES), BF16), out((1, main + LANES), F32), *pieces_out)
         found = call(
             functools.partial(mlp_backward_kernel, left),
-            (flat, out((total_rows, main + LANES), BF16), out((1, main + LANES), F32), *pieces_out),
-            *shards,
+            outs if gathered else (flat, *outs),
+            *given,
             saved[1],
             w,
             flops=mlp_flops,
+            streamed=(0, 1, 2) if gathered else (8, 9),
+            after=after,
         )
-        terms, sums = scatter_plane(found[3], found[4:])
+        if gathered:
+            found = (given[0], *found)
+        terms = scatter_plane(found[3], found[4:])
         (grads,) = call(
             mlp_weights_kernel,
             (out((width, 2 * main + LANES), BF16),),
@@ -900,39 +926,61 @@
             found[0],
             saved[2],
             flops=mlp_flops,
-            after=sums,
+            after=() if b else terms,
+            streamed=(0, 3),
+            saved=(0,),
         )
         return terms, grads, found[2]
 
+    def of_block(b, kept, received):
+        return jnp.where(first == (b == 0), kept, received)
+
+    full_a0 = gather_all(of_block(0, kept_a, received_a))
+    full_b0 = gather_all(of_block(0, kept_b, received_b))
+    (g_mlp,) = call(scale_rows_kernel, (shard,), g1, mods[1])
+    (g_mlp1,) = call(stack_kernel, (flat,), *gather_plane(g_mlp), saved=(0,))
     (normed,) = call(start_kernel, (shard,), x0, mods[0])
-    attn0, terms = attn_forward(0, normed)
+    shards, g_mlp1, next_a, next_b = lax.optimization_barrier(
+        (
+            gather_plane(normed),
+            g_mlp1,
+            of_block(1, kept_a, received_a),
+            of_block(1, kept_b, received_b),
+        )
+    )
+    weights = [
+        (full_a0, full_b0, *unpack_small(small[0])),
+        (gather_all(next_a), gather_all(next_b), *unpack_small(small[1])),
+    ]
+
+    def to_second(value):
+        return lax.ppermute(value, "section", [(0, 1)])
+
+    def to_first(value):
+        return lax.ppermute(value, "section", [(1, 0)])
+
+    attn0, terms = attn_forward(0, shards)
     att0, aft0, normed = call(
-        after_attn_kernel,
-        (shard_wide, shard_wide, shard),
-        *terms,
-        x0,
+        after_attn_kernel, (shard_wide, shard_wide, shard), *terms, x0, mods[0], saved=(0, 1)
+    )
+    mlp0, pieces = mlp_forward(0, normed, False)
+    mlp_out0, x1, normed = call(
+        between_kernel,
+        (shard_wide, shard, shard),
+        *scatter_plane(pieces[0], pieces[1:]),
+        aft0,
         mods[0],
-        saved=(0, 1),
-    )
-    mlp0, terms = mlp_forward(0, normed)
-    mlp_out0, x1, normed = call(
-        between_kernel, (shard_wide, shard, shard), *terms, aft0, mods[0], mods[1]
-    )
-    attn1, terms = attn_forward(1, normed)
-    att1, aft1, normed = call(
-        after_attn_kernel,
-        (shard_wide, shard_wide, shard),
-        *terms,
-        x1,
         mods[1],
         saved=(0, 1),
     )
-    mlp1, end_terms = mlp_forward(1, normed)
-    (g_mlp,) = call(scale_rows_kernel, (shard,), g1, mods[1])
-    block_out, g_gate_two1 = call(end_kernel, (shard, vector), *end_terms, aft1, mods[1], g1)
-
-    three, six = out((images, 3, width), F32), out((images, 6, width), F32)
-    terms, mlp_grads1, g_up_bias1 = mlp_backward(1, gather_plane(g_mlp), mlp1)
+    attn1, terms = attn_forward(1, gather_plane(normed))
+    att1, aft1, normed = call(
+        after_attn_kernel, (shard_wide, shard_wide, shard), *terms, x1, mods[1], saved=(0, 1)
+    )
+    mlp1, end_pieces = mlp_forward(1, normed, True)
+
+    three, five, six = (out((images, n, width), F32) for n in (3, 5, 6))
+    terms, mlp_grads1, g_up_bias1 = mlp_backward(1, (g_mlp1,), mlp1)
     g_after, g_attn, g_some = call(
         back_mlp_rows_kernel,
         (shard_wide, shard, three),
@@ -942,24 +990,23 @@
         att1,
         mods[1],
         after=(mlp_grads1,),
+        saved=(0,),
     )
     sum_b1 = scatter_rows(mlp_grads1)
-    terms, attn_grads1, g_taps1 = attn_backward(1, g_attn, attn1)
-    g0, g_mlp, g_mods1, g_gate_two0 = call(
+    terms, attn_grads1, g_taps1 = attn_backward(1, gather_plane(g_attn), attn1)
+    g0, g_mlp, g_more, g_gate_two0 = call(
         back_between_kernel,
-        (shard, shard, six, vector),
+        (shard, shard, five, vector),
         *terms,
         g_after,
         x1,
         mods[1],
         g_some,
-        g_gate_two1,
         mods[0],
         mlp_out0,
-        after=(attn_grads1,),
     )
     sum_a1 = scatter_rows(attn_grads1)
-    terms, mlp_grads0, g_up_bias0 = mlp_backward(0, gather_plane(g_mlp), mlp0)
+    terms, mlp_grads0, g_up_bias0 = mlp_backward(0, gather_plane(g_mlp), mlp0, (attn_grads1,))
     g_after, g_attn, g_some = call(
         back_mlp_rows_kernel,
         (shard_wide, shard, three),
@@ -968,9 +1015,12 @@
         aft0,
         att0,
         mods[0],
-        after=(mlp_grads0, sum_b1),
-    )
-    terms, attn_grads0, g_taps0 = attn_backward(0, g_attn, attn0)
+        after=(sum_b1,),
+        saved=(0,),
+    )
+    shards, sum_b1, sum_a1 = lax.optimization_barrier((gather_plane(g_attn), sum_b1, sum_a1))
+    terms, attn_grads0, g_taps0 = attn_backward(0, shards, attn0, (mlp_grads0,))
+    other_b1, other_a1 = to_second(sum_b1), to_second(sum_a1)
     g_in, g_mods0 = call(
         back_end_kernel,
         (shard, six),
@@ -980,16 +1030,68 @@
         mods[0],
         g_some,
         g_gate_two0,
-        after=(attn_grads0, sum_a1),
-    )
-
-    def finish(sum1, sum0):
-        from_first = lax.ppermute(sum1.astype(BF16), "section", [(0, 1)])
-        from_second = lax.ppermute(sum0.astype(BF16), "section", [(1, 0)])
-        return jnp.where(first, sum0, sum1), jnp.where(first, from_second, from_first)
-
-    mine, received = finish(sum_b1, scatter_rows(mlp_grads0))
-    pair_b = choose((mine, received.astype(F32)))
+        after=(attn_grads0, other_b1, other_a1),
+    )
+
+    sum_b0, sum_a0 = scatter_rows(mlp_grads0), scatter_rows(attn_grads0)
+
+    end_pieces, g_mods0 = lax.optimization_barrier((end_pieces, g_mods0))
+    block_out, g_mods1 = call(
+        end_kernel,
+        (shard, six),
+        *scatter_plane(end_pieces[0], end_pieces[1:]),
+        aft1,
+        mods[1],
+        g1,
+        g_more,
+    )
+
+    g_mod = jnp.stack([g_mods0.reshape(images, -1), g_mods1.reshape(images, -1)])
+    g_mod = g_mod.reshape(sections, images, tensors, -1).transpose(0, 2, 1, 3)
+    columns = g_mod.shape[3]
+    g_mod = g_mod.reshape(sections, tensors, images * columns)
+    taps_rows = taps_count + 1
+
+    def small_grads(g_taps, g_up_bias):
+        return jnp.concatenate([g_taps[:taps_rows].reshape(-1), g_up_bias.reshape(-1)])
+
+    g_small = jnp.stack([small_grads(g_taps0, g_up_bias0), small_grads(g_taps1, g_up_bias1)])
+    to_tensor = (jnp.arange(tensors) == t)[None, :, None]
+    g_small = jnp.where(to_tensor, g_small[:, None], 0.0)
+    g_sent = jnp.concatenate([g_mod, g_small], axis=2).reshape(sections * tensors, -1)
+    g_parts = lax.all_to_all(
+        g_sent, ("section", "tensor"), split_axis=0, concat_axis=0, tiled=True
+    )
+    block_out, sum_b0 = lax.optimization_barrier((block_out, sum_b0))
+    other_b0 = to_first(sum_b0)
+    g_share = jnp.sum(g_parts[:, : images * columns], axis=0)
+    small_parts = g_parts[:, images * columns :].reshape(sections, tensors, -1).sum(1)
+    g_all = spread_over(jnp.concatenate([g_share, small_parts.reshape(-1)]), ("dp",))
+    small_own = jnp.sum(g_all[:, images * columns :], axis=0).reshape(sections, -1)
+    g_all = g_all[:, : images * columns].reshape(dps * images, columns).astype(BF16)
+    grad_ada_bias = jnp.sum(g_all.astype(F32), axis=0)
+    grad_ada = jnp.einsum("md,me->de", slab_active, g_all, preferred_element_type=F32)
+    act_part = jnp.einsum("me,de->md", g_all, ada_weight[0], preferred_element_type=F32)
+    act_part, other_b0, sum_a0 = lax.optimization_barrier((act_part, other_b0, sum_a0))
+    act_all = lax.all_to_all(
+        act_part.reshape(dps, images, slab), "dp", split_axis=0, concat_axis=0, tiled=True
+    )
+    act_all = jnp.sum(spread_over(act_all, ("section", "tensor")), axis=0)
+    act_grad = act_all.reshape(dps, images, slab).transpose(1, 0, 2).reshape(images, width)
+    cond_grad = jax.vjp(jax.nn.silu, cond_vec)[1](act_grad)[0]
+
+    small_taps = small_own[:, : taps_rows * wide].reshape(sections, taps_rows, wide)
+    grad_gateb = small_taps[:, taps_count, tail : tail + heads].reshape(-1)
+    grad_taps = small_taps[:, :taps_count, :channels].transpose(1, 0, 2)
+    grad_taps = grad_taps.reshape(taps_count, sections * channels)
+    up_halves = small_own[:, taps_rows * wide :]
+    grad_up_bias = jnp.concatenate(
+        [up_halves[:, :main].reshape(-1), up_halves[:, main : main + left].reshape(-1)]
+    )
+
+    mine_b = jnp.where(first, sum_b0, sum_b1)
+    received = jnp.where(first, other_b0, other_b1)
+    pair_b = choose((mine_b.astype(F32), received.astype(F32)))
     end = 2 * main + left
     grad_up = [g[:, :main] for g in pair_b] + [g[:, 2 * main : end] for g in pair_b]
     grad_up = jnp.concatenate(grad_up, axis=1)
@@ -1003,50 +1105,11 @@
             out((slab, out_weight.shape[1]), F32),
         ),
         section,
-        *finish(sum_a1, scatter_rows(attn_grads0)),
+        jnp.where(first, sum_a0, sum_a1),
+        jnp.where(first, to_first(sum_a0), other_a1),
         scalars=1,
     )
     grad_out = grad_out.T
-
-    g_mod = jnp.stack([g_mods0.reshape(images, -1), g_mods1.reshape(images, -1)])
-    g_mod = g_mod.reshape(sections, images, tensors, -1).transpose(0, 2, 1, 3)
-    columns = g_mod.shape[3]
-    g_mod = g_mod.reshape(sections, tensors, images * columns)
-    taps_rows = taps_count + 1
-
-    def small_grads(g_taps, g_up_bias):
-        return jnp.concatenate([g_taps[:taps_rows].reshape(-1), g_up_bias.reshape(-1)])
-
-    g_small = jnp.stack([small_grads(g_taps0, g_up_bias0), small_grads(g_taps1, g_up_bias1)])
-    to_tensor = (jnp.arange(tensors) == t)[None, :, None]
-    g_small = jnp.where(to_tensor, g_small[:, None], 0.0)
-    g_sent = jnp.concatenate([g_mod, g_small], axis=2).reshape(sections * tensors, -1)
-    g_parts = lax.all_to_all(
-        g_sent, ("section", "tensor"), split_axis=0, concat_axis=0, tiled=True
-    )
-    g_share = jnp.sum(g_parts[:, : images * columns], axis=0)
-    small_parts = g_parts[:, images * columns :].reshape(sections, tensors, -1).sum(1)
-    g_all = spread_over(jnp.concatenate([g_share, small_parts.reshape(-1)]), ("dp",))
-    small_own = jnp.sum(g_all[:, images * columns :], axis=0).reshape(sections, -1)
-    g_all = g_all[:, : images * columns].reshape(dps * images, columns).astype(BF16)
-    grad_ada_bias = jnp.sum(g_all.astype(F32), axis=0)
-    grad_ada = jnp.einsum("md,me->de", slab_active, g_all, preferred_element_type=F32)
-    act_part = jnp.einsum("me,de->md", g_all, ada_weight[0], preferred_element_type=F32)
-    act_all = lax.all_to_all(
-        act_part.reshape(dps, images, slab), "dp", split_axis=0, concat_axis=0, tiled=True
-    )
-    act_all = jnp.sum(spread_over(act_all, ("section", "tensor")), axis=0)
-    act_grad = act_all.reshape(dps, images, slab).transpose(1, 0, 2).reshape(images, width)
-    cond_grad = jax.vjp(jax.nn.silu, cond_vec)[1](act_grad)[0]
-
-    small_taps = small_own[:, : taps_rows * wide].reshape(sections, taps_rows, wide)
-    grad_gateb = small_taps[:, taps_count, tail : tail + heads].reshape(-1)
-    grad_taps = small_taps[:, :taps_count, :channels].transpose(1, 0, 2)
-    grad_taps = grad_taps.reshape(taps_count, sections * channels)
-    up_halves = small_own[:, taps_rows * wide :]
-    grad_up_bias = jnp.concatenate(
-        [up_halves[:, :main].reshape(-1), up_halves[:, main : main + left].reshape(-1)]
-    )
 
     ends_from_first = lax.ppermute(block_out, "section", [(0, 1)])
     ends_from_second = lax.ppermute(g_in, "section", [(1, 0)])

time: 538 us -> 497 us (0.924)
  local copies, waits for them, and re-layouts: 89.1 us -> 32 us
  waiting for transfers between devices: 194 us -> 223 us
  other arithmetic: 38.2 us -> 9.28 us
  Pallas kernels: 67.1 us -> 87.4 us
  blocking collectives: 0 us -> 17.6 us
  starting transfers between devices: 119 us -> 103 us
    all_gather x3 -> x4, waiting for transfers between devices: 0.03 us -> 49.1 us  [gather_all(): return lax.all_gather(own, 'dp', axis=0, tiled=True)]
    unnamed x282 -> x114, local copies, waits for them, and re-layouts: 62.5 us -> 16.7 us
    ppermute x10 -> x6, waiting for transfers between devices: 54.2 us -> 26.9 us  [the longest x2 15 us: to_first(): return lax.ppermute(value, 'section', [(1, 0)])]
    ppermute x72 -> x88, waiting for transfers between devices: 89.6 us -> 116 us  [swap(): return lax.ppermute(value, PLANE, route)]
    pallas_call x24 -> x33, Pallas kernels: 67.1 us -> 87.4 us  [call(): pl.pallas_call(kernel, out_shape=tuple(shapes), in_specs=specs, out_specs...]
    all_to_all x0 -> x2, blocking collectives: none -> 17.6 us  [the longest x1 9.46 us: per_device(): lax.all_to_all(g_sent, ('section', 'tensor'), split_axis=0, concat_axis=0...]
    ppermute x3 -> x1, waiting for transfers between devices: 12.7 us -> 2.21 us  [swap_halves(): received = lax.ppermute(send, 'section', [(0, 1), (1, 0)])]
    convert_element_type x10 -> x0, other arithmetic: 10.1 us -> none  [the longest x8 7.83 us: scatter_plane(): (o.astype(F32) + received[j].astype(F32)).astype(BF16)]
  transfers between devices with their start and end apart: 102 -> 111, of which waited for: 56 -> 67; matrix products, arithmetic and copies ran while one was open for 12% -> 5% of each run, Pallas kernels for 11% -> 13%
where the time goes in v2:
time: 497 us; the launch traced here: 491 us
  waiting for transfers between devices  223 us (45%)
  starting transfers between devices  103 us (21%)
  Pallas kernels  87.4 us (18%)
  local copies, waits for them, and re-layouts  32 us (6%)
  blocking collectives  17.6 us (4%)
  between operations  15.7 us (3%)
  other arithmetic  9.28 us (2%)
    ppermute x88, waiting for transfers between devices, swap(): return lax.ppermute(value, PLANE, route)  116 us
    pallas_call x33, Pallas kernels, call(): pl.pallas_call(kernel, out_shape=tuple(shapes), in_specs=specs, out_specs...  87.4 us
    ppermute x88, starting transfers between devices, swap(): return lax.ppermute(value, PLANE, route)  61.7 us
    all_gather x4, waiting for transfers between devices, gather_all(): return lax.all_gather(own, 'dp', axis=0, tiled=True)  49.1 us
    unnamed x114, local copies, waits for them, and re-layouts  16.7 us
    ppermute x2, waiting for transfers between devices, to_first(): return lax.ppermute(value, 'section', [(1, 0)])  15 us
    ppermute x2, waiting for transfers between devices, to_second(): return lax.ppermute(value, 'section', [(0, 1)])  11.9 us
    all_to_all x2, waiting for transfers between devices, spread_over(): return lax.all_to_all(copies, axes, split_axis=0, concat_axis=0, tiled=True)  11.7 us
  transfers between devices with their start and end apart: 111, of which 67 were waited for; matrix products, arithmetic and copies ran while one was open for 5% of the time, Pallas kernels for 13%

profile of v2, /device:TPU:0, one launch (start us, length us, event | category | flops | bytes accessed | tf_op | source)
XLA Modules:
  0.0 491.1 jit_solution(3422198657498200843)
XLA Ops:
  14.3 2.9 collective-permute-start.2
  18.8 4.9 all-to-all-start
  23.7 5.6 %all-to-all-done = bf16[4,2,288]{2,1,0:T(2,128)(2,1)S(1)} async-done(((bf16[4,2,288]{2,1,0:T(2,128)(2,1)}), bf16[4,2,288]{2,1,0:T(2,128)(2,1)S(1)}, u32[]{:S(2)}, u32[]{:S(2)}) %all-to-all-start) | async-done | bytes 4640 | tf_op jit(solution)/shard_map/all_to_all | solution.py:794
  31.9 4.3 all-to-all-start.1
  36.2 5.8 %all-to-all-done.1 = f32[4,2,1728]{2,1,0:T(2,128)S(1)} async-done(((f32[4,2,1728]{2,1,0:T(2,128)}), f32[4,2,1728]{2,1,0:T(2,128)S(1)}, u32[]{:S(2)}, u32[]{:S(2)}) %all-to-all-start.1) | async-done | bytes 55328 | tf_op jit(solution)/shard_map/all_to_all | solution.py:798
  42.1 8.1 %all_to_all.46 = f32[8,2,1728]{2,1,0:T(2,128)} all-to-all(f32[8,2,1728]{2,1,0:T(2,128)S(1)} %broadcast_in_dim.89), channel_id=1, replica_groups=mesh['dp'=4,'tensor'=4,'section'=2] {'section','tensor'}, dimensions={0} | all-to-all | bytes 221184 | tf_op jit(solution)/shard_map/all_to_all | solution.py:665
  52.5 4.8 collective-permute-done
  81.2 7.3 %shard_map.224 = (bf16[2,256,1152]{2,1,0:T(8,128)(2,1)}, bf16[2,256,1024]{2,1,0:T(8,128)(2,1)}, f32[2,256,128]{2,1,0:T(8,128)}, f32[2,256,256]{2,1,0:T(8,128)}, ...) custom-call(s32[1]{0:T(128)} %bitcast.refs_0_, ...), custom_call_target="tpu_custom_call" | custom-call | flops 2315255808 | bytes 7422468 | tf_op jit(solution)/shard_map/pallas_call | solution.py:84
  94.4 4.1 collective-permute-done.19.refs_1_
  105.3 4.2 collective-permute-done.24.refs_3_
  113.3 13.7 %all-gather.7.cloned.1.call-done.refs_8_.refs_9_ = bf16[1152,1152]{1,0:T(8,128)(2,1)} async-done(((bf16[288,1152]{1,0:T(8,128)(2,1)}), bf16[1152,1152]{1,0:T(8,128)(2,1)}) %all-gather.7.cloned.1.call-update) | async-done | bytes 2654224 | tf_op jit(solution)/shard_map/all_gather | solution.py:669
  127.1 6.4 %shard_map.227 = (bf16[512,1152]{1,0:T(8,128)(2,1)}, f32[512,640]{1,0:T(8,128)}, bf16[512,640]{1,0:T(8,128)(2,1)}, bf16[4,2,32,1152]{3,2,1,0:T(8,128)(2,1)S(1)},...) custom-call(bf16[2,32,1152]{2,1,0:T(8,128)(2,1)S(1)} %get-tuple-elem, ...), custom_call_target="tpu_custom_call" | custom-call | flops 1358954496 | bytes 8161792 | tf_op jit(solution)/shard_map/pallas_call | solution.py:84
  139.3 4.1 collective-permute-done.30.refs_1_
  150.4 3.4 collective-permute-done.35.refs_4_
  153.8 2.7 collective-permute-done.34.refs_3_
  157.2 10.6 %all-gather.9.cloned.1.call-done.refs_9_.refs_12_ = bf16[1152,768]{1,0:T(8,128)(2,1)} async-done(((bf16[288,768]{1,0:T(8,128)(2,1)}), bf16[1152,768]{1,0:T(8,128)(2,1)}) %all-gather.9.cloned.1.call-update) | async-done | bytes 1769488 | tf_op jit(solution)/shard_map/all_gather | solution.py:669
  167.8 7.8 %shard_map.230 = (bf16[2,256,1152]{2,1,0:T(8,128)(2,1)}, bf16[2,256,1024]{2,1,0:T(8,128)(2,1)}, f32[2,256,128]{2,1,0:T(8,128)}, f32[2,256,256]{2,1,0:T(8,128)}, ...) custom-call(s32[1]{0:T(128)} %bitcast.refs_0_, ...), custom_call_target="tpu_custom_call" | custom-call | flops 2315255808 | bytes 7422468 | tf_op jit(solution)/shard_map/pallas_call | solution.py:84
  181.4 4.1 collective-permute-done.41.refs_1_
  192.5 3.6 collective-permute-done.46.refs_3_
  199.3 24.7 %all-gather.11.cloned.1.call-done.refs_8_.refs_2_ = bf16[1152,1152]{1,0:T(8,128)(2,1)} async-done(((bf16[288,1152]{1,0:T(8,128)(2,1)}), bf16[1152,1152]{1,0:T(8,128)(2,1)}) %all-gather.11.cloned.1.call-update) | async-done | bytes 2654224 | tf_op jit(solution)/shard_map/all_gather | solution.py:669
  224.1 6.8 %shard_map.233 = (bf16[512,1152]{1,0:T(8,128)(2,1)}, f32[512,640]{1,0:T(8,128)}, bf16[512,640]{1,0:T(8,128)(2,1)}, bf16[4,2,32,1152]{3,2,1,0:T(8,128)(2,1)}, bf1...) custom-call(bf16[2,32,1152]{2,1,0:T(8,128)(2,1)S(1)} %get-tuple-elem, ...), custom_call_target="tpu_custom_call" | custom-call | flops 1358954496 | bytes 8161792 | tf_op jit(solution)/shard_map/pallas_call | solution.py:84
  230.9 6.4 %shard_map.234 = (bf16[512,640]{1,0:T(8,128)(2,1)S(1)}, f32[1,640]{1,0:T(1,128)S(1)}, bf16[4,2,32,1152]{3,2,1,0:T(8,128)(2,1)S(1)}, bf16[2,32,1152]{2,1,0:T(8,12...) custom-call(bf16[512,1152]{1,0:T(8,128)(2,1)} %shard_map.223.refs_0_, ...), custom_call_target="tpu_custom_call" | custom-call | flops 1358954496 | bytes 6982144 | tf_op jit(solution)/shard_map/pallas_call | solution.py:84
  237.8 5.1 %shard_map.236.refs_8_ = bf16[1152,1152]{1,0:T(8,128)(2,1)} custom-call(bf16[512,1152]{1,0:T(8,128)(2,1)} %get-tuple-element.244.refs_0_, bf16[512,640]{1,0:T(8,128)(2,1)S(1)} %get-tuple-element.245.refs_1_, bf16[512,1152]{1,0:T(8,128)(2,1)S(1)} %copy-done.1, bf16[512,640]{1,0:T(8,128)(2,1)} %get-tuple-element.246.refs_3_), custom_call_target="tpu_custom_call" | custom-call | flops 1358954496 | bytes 6324224 | tf_op jit(solution)/shard_map/pallas_call | solution.py:84
  249.8 4.1 collective-permute-done.52.refs_1_
  261.6 3.6 collective-permute-done.57.refs_4_
  269.4 8.2 %shard_map.238 = (bf16[2,256,1152]{2,1,0:T(8,128)(2,1)S(1)}, bf16[2,256,640]{2,1,0:T(8,128)(2,1)S(1)}, f32[16,256]{1,0:T(8,128)S(1)}, bf16[4,2,32,1152]{3,2,1,0:...) custom-call(s32[1]{0:T(128)} %bitcast.refs_0_, ...), custom_call_target="tpu_custom_call" | custom-call | flops 4630511616 | bytes 7831556 | tf_op jit(solution)/shard_map/pallas_call | solution.py:84
  283.4 4.1 collective-permute-done.63.refs_1_.refs_5_
  287.5 2.7 collective-permute-done.64.refs_2_.refs_6_
  290.2 4.0 shard_map.241.refs_10_
  301.2 4.1 collective-permute-done.68.refs_3_
  309.0 5.9 %shard_map.242 = (bf16[512,1152]{1,0:T(8,128)(2,1)S(1)}, bf16[512,640]{1,0:T(8,128)(2,1)S(1)}, f32[1,640]{1,0:T(1,128)S(1)}, bf16[4,2,32,1152]{3,2,1,0:T(8,128)(...) custom-call(bf16[2,32,1152]{2,1,0:T(8,128)(2,1)S(1)} %get-tuple-elem, ...), custom_call_target="tpu_custom_call" | custom-call | flops 1358954496 | bytes 8161792 | tf_op jit(solution)/shard_map/pallas_call | solution.py:84
  320.7 4.1 collective-permute-done.74.refs_1_.refs_5_
  324.8 2.7 collective-permute-done.75.refs_2_.refs_6_
  327.6 5.1 %shard_map.245.refs_14_ = bf16[1152,1152]{1,0:T(8,128)(2,1)} custom-call(bf16[512,1152]{1,0:T(8,128)(2,1)} %get-tuple-element.292.refs_0_, bf16[512,640]{1,0:T(8,128)(2,1)S(1)} %get-tuple-element.293.refs_1_, bf16[512,1152]{1,0:T(8,128)(2,1)S(1)} %get-tuple-element.294.refs_2_, bf16[512,640]{1,0:T(8,128)(2,1)} %get-tuple-element.295.refs_3_, ...), custom_call_target="tpu_custom_call" | custom-call | flops 1358954496 | bytes 6324224 | tf_op jit(solution)/shard_map/pallas_call | solution.py:84
  338.3 4.0 collective-permute-done.79.refs_4_
  346.1 8.0 %shard_map.246 = (bf16[2,256,1152]{2,1,0:T(8,128)(2,1)S(1)}, bf16[2,256,640]{2,1,0:T(8,128)(2,1)S(1)}, f32[16,256]{1,0:T(8,128)S(1)}, bf16[4,2,32,1152]{3,2,1,0:...) custom-call(s32[1]{0:T(128)} %bitcast.refs_0_, ...), custom_call_target="tpu_custom_call" | custom-call | flops 4630511616 | bytes 7831556 | tf_op jit(solution)/shard_map/pallas_call | solution.py:84
  355.1 4.4 collective-permute-start.88
  367.7 4.0 shard_map.248.refs_9_
  371.7 11.9 %collective-permute-done.89.refs_11_ = bf16[288,768]{1,0:T(8,128)(2,1)} collective-permute-done((bf16[288,768]{1,0:T(8,128)(2,1)}, bf16[288,768]{1,0:T(8,128)(2,1)}, u32[]{:S(2)}, u32[]{:S(2)}) %collective-permute-start.89) | collective-permute-done | bytes 442400 | tf_op jit(solution)/shard_map/ppermute | solution.py:957
  383.7 3.1 collective-permute-done.85.refs_1_
  396.8 3.7 collective-permute-done.91.refs_1_
  403.6 9.5 %all_to_all.47 = f32[8,1,6656]{2,1,0:T(1,128)S(1)} all-to-all(f32[8,1,6656]{2,1,0:T(1,128)S(1)} %copy.99), channel_id=1, replica_groups=mesh['dp'=4,'tensor'=4,'section'=2] {'section','tensor'}, dimensions={0} | all-to-all | bytes 425984 | tf_op jit(solution)/shard_map/all_to_all | solution.py:1062
  414.0 3.3 all-to-all-start.4
  418.7 11.0 %all-to-all-done.4 = f32[4,1,9856]{2,1,0:T(1,128)S(1)} async-done(((f32[4,1,9856]{2,1,0:T(1,128)}), f32[4,1,9856]{2,1,0:T(1,128)S(1)}, u32[]{:S(2)}, u32[]{:S(2)}) %all-to-all-start.4) | async-done | bytes 157728 | tf_op jit(solution)/shard_map/all_to_all | solution.py:665
  430.5 3.6 collective-permute-start.95
  440.7 15.0 %collective-permute-done.96 = bf16[288,1152]{1,0:T(8,128)(2,1)} collective-permute-done((bf16[288,1152]{1,0:T(8,128)(2,1)S(1)}, bf16[288,1152]{1,0:T(8,128)(2,1)}, u32[]{:S(2)}, u32[]{:S(2)}) %collective-permute-start.96) | collective-permute-done | bytes 663584 | tf_op jit(solution)/shard_map/ppermute | solution.py:960
  458.7 3.3 all-to-all-start.5
  468.2 4.7 all-to-all-start.6
  (448 shorter events, 185.8 us)
Async XLA Ops:
  14.3 15.0 %collective-permute-start.2 = (bf16[288,768]{1,0:T(8,128)(2,1)}, bf16[288,768]{1,0:T(8,128)(2,1)S(1)}, u32[]{:S(2)}, u32[]{:S(2)}) collective-permute-start(bf16[288,768]{1,0:T(8,128)(2,1)} %get-tuple-element.182), channel_id=1, source_target_pairs={{0,1},{1,0},{2,3},{3,2},{4,5},{5,4},{6,7},{7,6},{8,9},{9,8},{10,11... | collective-permute-start | bytes 1327112 | tf_op jit(solution)/shard_map/ppermute | solution.py:749
  18.8 10.5 %all-to-all-start = ((bf16[4,2,288]{2,1,0:T(2,128)(2,1)}), bf16[4,2,288]{2,1,0:T(2,128)(2,1)S(1)}, u32[]{:S(2)}, u32[]{:S(2)}) async-start(bf16[4,2,288]{2,1,0:T(2,128)(2,1)} %bitcast.73), calls=%async_computation | async-start | bytes 12288 | tf_op jit(solution)/shard_map/all_to_all | solution.py:794
  23.7 57.6 %all-gather.5.cloned.1.call-start = ((), (), s32[]{:S(2)}) async-start(), calls=%async_computation.11 | async-start | bytes 2211840 | tf_op jit(solution)/shard_map/all_gather | solution.py:669
  30.4 19.9 %collective-permute-start.1 = (bf16[288,1152]{1,0:T(8,128)(2,1)S(1)}, bf16[288,1152]{1,0:T(8,128)(2,1)S(1)}, u32[]{:S(2)}, u32[]{:S(2)}) collective-permute-start(bf16[288,1152]{1,0:T(8,128)(2,1)S(1)} %get-tuple-element.179), channel_id=1, source_target_pairs={{0,1},{1,0},{2,3},{3,2},{4,5},{5,4},{6,7},{7,6},{8,9},{9,8},{10,11... | collective-permute-start | bytes 1990664 | tf_op jit(solution)/shard_map/ppermute | solution.py:750
  31.9 10.2 %all-to-all-start.1 = ((f32[4,2,1728]{2,1,0:T(2,128)}), f32[4,2,1728]{2,1,0:T(2,128)S(1)}, u32[]{:S(2)}, u32[]{:S(2)}) async-start(f32[4,2,1728]{2,1,0:T(2,128)} %fusion), calls=%async_computation.1 | async-start | bytes 114688 | tf_op jit(solution)/shard_map/all_to_all | solution.py:798
  36.2 90.9 %all-gather.7.cloned.1.call-start = ((), (), s32[]{:S(2)}) async-start(), calls=%async_computation.12 | async-start | bytes 3317760 | tf_op jit(solution)/shard_map/all_gather | solution.py:669
  51.5 116.3 %all-gather.9.cloned.1.call-start = ((), (), s32[]{:S(2)}) async-start(), calls=%async_computation.13 | async-start | bytes 2211840 | tf_op jit(solution)/shard_map/all_gather | solution.py:669
  57.7 7.7 %collective-permute-start.12 = (bf16[2,32,1152]{2,1,0:T(8,128)(2,1)S(1)}, bf16[2,32,1152]{2,1,0:T(8,128)(2,1)S(1)}, u32[]{:S(2)}, u32[]{:S(2)}) collective-permute-start(bf16[2,32,1152]{2,1,0:T(8,128)(2,1)S(1)} %shard_map.222.refs_0_), channel_id=1, source_target_pairs={{0,5},{1,4},{2,7},{3,6},{4,1},{5,0},{6,3},{7,2},{8,13},{9,12},{10,... | collective-permute-start | bytes 442376 | tf_op jit(solution)/shard_map/ppermute | solution.py:648
  58.6 9.9 %collective-permute-start.11 = (bf16[2,32,1152]{2,1,0:T(8,128)(2,1)S(1)}, bf16[2,32,1152]{2,1,0:T(8,128)(2,1)S(1)}, u32[]{:S(2)}, u32[]{:S(2)}) collective-permute-start(bf16[2,32,1152]{2,1,0:T(8,128)(2,1)S(1)} %shard_map.222.refs_0_), channel_id=1, source_target_pairs={{0,4},{1,5},{2,6},{3,7},{4,0},{5,1},{6,2},{7,3},{8,12},{9,13},{10,... | collective-permute-start | bytes 442376 | tf_op jit(solution)/shard_map/ppermute | solution.py:648
  60.1 8.5 %collective-permute-start.10 = (bf16[2,32,1152]{2,1,0:T(8,128)(2,1)S(1)}, bf16[2,32,1152]{2,1,0:T(8,128)(2,1)S(1)}, u32[]{:S(2)}, u32[]{:S(2)}) collective-permute-start(bf16[2,32,1152]{2,1,0:T(8,128)(2,1)S(1)} %shard_map.222.refs_0_), channel_id=1, source_target_pairs={{0,1},{1,0},{2,3},{3,2},{4,5},{5,4},{6,7},{7,6},{8,9},{9,8},{10,11... | collective-permute-start | bytes 442376 | tf_op jit(solution)/shard_map/ppermute | solution.py:648
  61.6 10.1 %collective-permute-start.5 = (bf16[2,32,1152]{2,1,0:T(8,128)(2,1)S(1)}, bf16[2,32,1152]{2,1,0:T(8,128)(2,1)S(1)}, u32[]{:S(2)}, u32[]{:S(2)}) collective-permute-start(bf16[2,32,1152]{2,1,0:T(8,128)(2,1)S(1)} %shard_map.221.refs_1_), channel_id=1, source_target_pairs={{0,5},{1,4},{2,7},{3,6},{4,1},{5,0},{6,3},{7,2},{8,13},{9,12},{10,... | collective-permute-start | bytes 442376 | tf_op jit(solution)/shard_map/ppermute | solution.py:648
  62.5 11.4 %collective-permute-start.4 = (bf16[2,32,1152]{2,1,0:T(8,128)(2,1)S(1)}, bf16[2,32,1152]{2,1,0:T(8,128)(2,1)S(1)}, u32[]{:S(2)}, u32[]{:S(2)}) collective-permute-start(bf16[2,32,1152]{2,1,0:T(8,128)(2,1)S(1)} %shard_map.221.refs_1_), channel_id=1, source_target_pairs={{0,4},{1,5},{2,6},{3,7},{4,0},{5,1},{6,2},{7,3},{8,12},{9,13},{10,... | collective-permute-start | bytes 442376 | tf_op jit(solution)/shard_map/ppermute | solution.py:648
  65.3 8.7 %collective-permute-start.3 = (bf16[2,32,1152]{2,1,0:T(8,128)(2,1)S(1)}, bf16[2,32,1152]{2,1,0:T(8,128)(2,1)S(1)}, u32[]{:S(2)}, u32[]{:S(2)}) collective-permute-start(bf16[2,32,1152]{2,1,0:T(8,128)(2,1)S(1)} %shard_map.221.refs_1_), channel_id=1, source_target_pairs={{0,1},{1,0},{2,3},{3,2},{4,5},{5,4},{6,7},{7,6},{8,9},{9,8},{10,11... | collective-permute-start | bytes 442376 | tf_op jit(solution)/shard_map/ppermute | solution.py:648
  76.5 147.5 %all-gather.11.cloned.1.call-start = ((), (), s32[]{:S(2)}) async-start(), calls=%async_computation.14 | async-start | bytes 3317760 | tf_op jit(solution)/shard_map/all_gather | solution.py:669
  78.5 254.5 %reduce-scatter.5.cloned.1.call-start = ((), (), s32[]{:S(2)}) async-start(), calls=%async_computation.15 | async-start | bytes 3317760 | tf_op jit(solution)/shard_map/reduce_scatter | solution.py:673
  90.8 7.7 %collective-permute-start.19 = (bf16[2,32,1152]{2,1,0:T(8,128)(2,1)S(1)}, bf16[2,32,1152]{2,1,0:T(8,128)(2,1)S(1)}, u32[]{:S(2)}, u32[]{:S(2)}) collective-permute-start(bf16[2,32,1152]{2,1,0:T(8,128)(2,1)S(1)} %get-tuple-element.204), channel_id=1, source_target_pairs={{0,5},{1,4},{2,7},{3,6},{4,1},{5,0},{6,3},{7,2},{8,13},{9,12},{10,... | collective-permute-start | bytes 442376 | tf_op jit(solution)/shard_map/ppermute | solution.py:648
  92.2 8.4 %collective-permute-start.20 = (bf16[2,32,1152]{2,1,0:T(8,128)(2,1)S(1)}, bf16[2,32,1152]{2,1,0:T(8,128)(2,1)S(1)}, u32[]{:S(2)}, u32[]{:S(2)}) collective-permute-start(bf16[2,32,1152]{2,1,0:T(8,128)(2,1)S(1)} %get-tuple-element.205), channel_id=1, source_target_pairs={{0,1},{1,0},{2,3},{3,2},{4,5},{5,4},{6,7},{7,6},{8,9},{9,8},{10,11... | collective-permute-start | bytes 442376 | tf_op jit(solution)/shard_map/ppermute | solution.py:648
  101.8 7.7 %collective-permute-start.24 = (bf16[2,32,1152]{2,1,0:T(8,128)(2,1)S(1)}, bf16[2,32,1152]{2,1,0:T(8,128)(2,1)S(1)}, u32[]{:S(2)}, u32[]{:S(2)}) collective-permute-start(bf16[2,32,1152]{2,1,0:T(8,128)(2,1)S(1)} %get-tuple-element.207.refs_0_), channel_id=1, source_target_pairs={{0,5},{1,4},{2,7},{3,6},{4,1},{5,0},{6,3},{7,2},{8,13},{9,12},{10,... | collective-permute-start | bytes 442376 | tf_op jit(solution)/shard_map/ppermute | solution.py:648
  103.1 8.6 %collective-permute-start.23 = (bf16[2,32,1152]{2,1,0:T(8,128)(2,1)S(1)}, bf16[2,32,1152]{2,1,0:T(8,128)(2,1)S(1)}, u32[]{:S(2)}, u32[]{:S(2)}) collective-permute-start(bf16[2,32,1152]{2,1,0:T(8,128)(2,1)S(1)} %get-tuple-element.207.refs_0_), channel_id=1, source_target_pairs={{0,4},{1,5},{2,6},{3,7},{4,0},{5,1},{6,2},{7,3},{8,12},{9,13},{10,... | collective-permute-start | bytes 442376 | tf_op jit(solution)/shard_map/ppermute | solution.py:648
  135.7 7.7 %collective-permute-start.30 = (bf16[2,32,1152]{2,1,0:T(8,128)(2,1)S(1)}, bf16[2,32,1152]{2,1,0:T(8,128)(2,1)S(1)}, u32[]{:S(2)}, u32[]{:S(2)}) collective-permute-start(bf16[2,32,1152]{2,1,0:T(8,128)(2,1)S(1)} %get-tuple-element.214), channel_id=1, source_target_pairs={{0,5},{1,4},{2,7},{3,6},{4,1},{5,0},{6,3},{7,2},{8,13},{9,12},{10,... | collective-permute-start | bytes 442376 | tf_op jit(solution)/shard_map/ppermute | solution.py:648
  150.4 17.4 %collective-permute-start.36 = (bf16[2,32,1152]{2,1,0:T(8,128)(2,1)S(1)}, bf16[2,32,1152]{2,1,0:T(8,128)(2,1)S(1)}, u32[]{:S(2)}, u32[]{:S(2)}) collective-permute-start(bf16[2,32,1152]{2,1,0:T(8,128)(2,1)S(1)} %get-tuple-element.218.refs_1_), channel_id=1, source_target_pairs={{0,2},{1,3},{2,0},{3,1},{4,6},{5,7},{6,4},{7,5},{8,10},{9,11},{10,... | collective-permute-start | bytes 442376 | tf_op jit(solution)/shard_map/ppermute | solution.py:648
  153.8 14.0 %collective-permute-start.39 = (bf16[2,32,1152]{2,1,0:T(8,128)(2,1)S(1)}, bf16[2,32,1152]{2,1,0:T(8,128)(2,1)S(1)}, u32[]{:S(2)}, u32[]{:S(2)}) collective-permute-start(bf16[2,32,1152]{2,1,0:T(8,128)(2,1)S(1)} %collective-permute-done.35.refs_4_), channel_id=1, source_target_pairs={{0,2},{1,3},{2,0},{3,1},{4,6},{5,7},{6,4},{7,5},{8,10},{9,11},{10,... | collective-permute-start | bytes 442376 | tf_op jit(solution)/shard_map/ppermute | solution.py:648
  156.4 11.3 %collective-permute-start.38 = (bf16[2,32,1152]{2,1,0:T(8,128)(2,1)S(1)}, bf16[2,32,1152]{2,1,0:T(8,128)(2,1)S(1)}, u32[]{:S(2)}, u32[]{:S(2)}) collective-permute-start(bf16[2,32,1152]{2,1,0:T(8,128)(2,1)S(1)} %collective-permute-done.34.refs_3_), channel_id=1, source_target_pairs={{0,2},{1,3},{2,0},{3,1},{4,6},{5,7},{6,4},{7,5},{8,10},{9,11},{10,... | collective-permute-start | bytes 442376 | tf_op jit(solution)/shard_map/ppermute | solution.py:648
  156.8 11.0 %collective-permute-start.37 = (bf16[2,32,1152]{2,1,0:T(8,128)(2,1)S(1)}, bf16[2,32,1152]{2,1,0:T(8,128)(2,1)S(1)}, u32[]{:S(2)}, u32[]{:S(2)}) collective-permute-start(bf16[2,32,1152]{2,1,0:T(8,128)(2,1)S(1)} %collective-permute-done.33.refs_2_), channel_id=1, source_target_pairs={{0,2},{1,3},{2,0},{3,1},{4,6},{5,7},{6,4},{7,5},{8,10},{9,11},{10,... | collective-permute-start | bytes 442376 | tf_op jit(solution)/shard_map/ppermute | solution.py:648
  192.5 31.6 %collective-permute-start.47 = (bf16[2,32,1152]{2,1,0:T(8,128)(2,1)S(1)}, bf16[2,32,1152]{2,1,0:T(8,128)(2,1)S(1)}, u32[]{:S(2)}, u32[]{:S(2)}) collective-permute-start(bf16[2,32,1152]{2,1,0:T(8,128)(2,1)S(1)} %get-tuple-element.230.refs_0_), channel_id=1, source_target_pairs={{0,2},{1,3},{2,0},{3,1},{4,6},{5,7},{6,4},{7,5},{8,10},{9,11},{10,... | collective-permute-start | bytes 442376 | tf_op jit(solution)/shard_map/ppermute | solution.py:648
  196.1 28.0 %collective-permute-start.50 = (bf16[2,32,1152]{2,1,0:T(8,128)(2,1)S(1)}, bf16[2,32,1152]{2,1,0:T(8,128)(2,1)S(1)}, u32[]{:S(2)}, u32[]{:S(2)}) collective-permute-start(bf16[2,32,1152]{2,1,0:T(8,128)(2,1)S(1)} %collective-permute-done.46.refs_3_), channel_id=1, source_target_pairs={{0,2},{1,3},{2,0},{3,1},{4,6},{5,7},{6,4},{7,5},{8,10},{9,11},{10,... | collective-permute-start | bytes 442376 | tf_op jit(solution)/shard_map/ppermute | solution.py:648
  198.7 25.4 %collective-permute-start.49 = (bf16[2,32,1152]{2,1,0:T(8,128)(2,1)S(1)}, bf16[2,32,1152]{2,1,0:T(8,128)(2,1)S(1)}, u32[]{:S(2)}, u32[]{:S(2)}) collective-permute-start(bf16[2,32,1152]{2,1,0:T(8,128)(2,1)S(1)} %collective-permute-done.45.refs_2_), channel_id=1, source_target_pairs={{0,2},{1,3},{2,0},{3,1},{4,6},{5,7},{6,4},{7,5},{8,10},{9,11},{10,... | collective-permute-start | bytes 442376 | tf_op jit(solution)/shard_map/ppermute | solution.py:648
  198.9 25.1 %collective-permute-start.48 = (bf16[2,32,1152]{2,1,0:T(8,128)(2,1)S(1)}, bf16[2,32,1152]{2,1,0:T(8,128)(2,1)S(1)}, u32[]{:S(2)}, u32[]{:S(2)}) collective-permute-start(bf16[2,32,1152]{2,1,0:T(8,128)(2,1)S(1)} %collective-permute-done.44.refs_1_), channel_id=1, source_target_pairs={{0,2},{1,3},{2,0},{3,1},{4,6},{5,7},{6,4},{7,5},{8,10},{9,11},{10,... | collective-permute-start | bytes 442376 | tf_op jit(solution)/shard_map/ppermute | solution.py:648
  242.9 101.9 %reduce-scatter.7.cloned.1.call-start = ((), (), s32[]{:S(2)}) async-start(), calls=%async_computation.16 | async-start | bytes 2211840 | tf_op jit(solution)/shard_map/reduce_scatter | solution.py:673
  281.6 8.6 %collective-permute-start.64 = (bf16[2,32,1152]{2,1,0:T(8,128)(2,1)S(1)}, bf16[2,32,1152]{2,1,0:T(8,128)(2,1)S(1)}, u32[]{:S(2)}, u32[]{:S(2)}) collective-permute-start(bf16[2,32,1152]{2,1,0:T(8,128)(2,1)S(1)} %get-tuple-element.258), channel_id=1, source_target_pairs={{0,1},{1,0},{2,3},{3,2},{4,5},{5,4},{6,7},{7,6},{8,9},{9,8},{10,11... | collective-permute-start | bytes 442376 | tf_op jit(solution)/shard_map/ppermute | solution.py:648
  294.3 136.2 %reduce-scatter.9.cloned.1.call-start = ((), (), s32[]{:S(2)}) async-start(), calls=%async_computation.17 | async-start | bytes 3317760 | tf_op jit(solution)/shard_map/reduce_scatter | solution.py:673
  299.2 8.1 %collective-permute-start.67 = (bf16[2,32,1152]{2,1,0:T(8,128)(2,1)S(1)}, bf16[2,32,1152]{2,1,0:T(8,128)(2,1)S(1)}, u32[]{:S(2)}, u32[]{:S(2)}) collective-permute-start(bf16[2,32,1152]{2,1,0:T(8,128)(2,1)S(1)} %get-tuple-element.263.refs_0_), channel_id=1, source_target_pairs={{0,4},{1,5},{2,6},{3,7},{4,0},{5,1},{6,2},{7,3},{8,12},{9,13},{10,... | collective-permute-start | bytes 442376 | tf_op jit(solution)/shard_map/ppermute | solution.py:648
  318.9 8.6 %collective-permute-start.75 = (bf16[2,32,1152]{2,1,0:T(8,128)(2,1)S(1)}, bf16[2,32,1152]{2,1,0:T(8,128)(2,1)S(1)}, u32[]{:S(2)}, u32[]{:S(2)}) collective-permute-start(bf16[2,32,1152]{2,1,0:T(8,128)(2,1)S(1)} %get-tuple-element.276), channel_id=1, source_target_pairs={{0,1},{1,0},{2,3},{3,2},{4,5},{5,4},{6,7},{7,6},{8,9},{9,8},{10,11... | collective-permute-start | bytes 442376 | tf_op jit(solution)/shard_map/ppermute | solution.py:648
  332.7 123.0 %reduce-scatter.11.cloned.1.call-start = ((), (), s32[]{:S(2)}) async-start(), calls=%async_computation.18 | async-start | bytes 2211840 | tf_op jit(solution)/shard_map/reduce_scatter | solution.py:673
  336.3 8.0 %collective-permute-start.78 = (bf16[2,32,1152]{2,1,0:T(8,128)(2,1)S(1)}, bf16[2,32,1152]{2,1,0:T(8,128)(2,1)S(1)}, u32[]{:S(2)}, u32[]{:S(2)}) collective-permute-start(bf16[2,32,1152]{2,1,0:T(8,128)(2,1)S(1)} %get-tuple-element.281.refs_1_), channel_id=1, source_target_pairs={{0,4},{1,5},{2,6},{3,7},{4,0},{5,1},{6,2},{7,3},{8,12},{9,13},{10,... | collective-permute-start | bytes 442376 | tf_op jit(solution)/shard_map/ppermute | solution.py:648
  355.1 28.6 %collective-permute-start.88 = (bf16[288,1152]{1,0:T(8,128)(2,1)}, bf16[288,1152]{1,0:T(8,128)(2,1)}, u32[]{:S(2)}, u32[]{:S(2)}) collective-permute-start(bf16[288,1152]{1,0:T(8,128)(2,1)} %reduce-scatter.5.cloned.1.call-done.refs_8_), channel_id=1, source_target_pairs={{0,1},{2,3},{4,5},{6,7},{8,9},{10,11},{12,13},{14,15},{16,17},{18,... | collective-permute-start | bytes 1990664 | tf_op jit(solution)/shard_map/ppermute | solution.py:957
  359.5 24.2 %collective-permute-start.89 = (bf16[288,768]{1,0:T(8,128)(2,1)}, bf16[288,768]{1,0:T(8,128)(2,1)}, u32[]{:S(2)}, u32[]{:S(2)}) collective-permute-start(bf16[288,768]{1,0:T(8,128)(2,1)} %reduce-scatter.7.cloned.1.call-done), channel_id=1, source_target_pairs={{0,1},{2,3},{4,5},{6,7},{8,9},{10,11},{12,13},{14,15},{16,17},{18,... | collective-permute-start | bytes 1327112 | tf_op jit(solution)/shard_map/ppermute | solution.py:957
  361.6 25.1 %collective-permute-start.85 = (bf16[2,32,1152]{2,1,0:T(8,128)(2,1)S(1)}, bf16[2,32,1152]{2,1,0:T(8,128)(2,1)S(1)}, u32[]{:S(2)}, u32[]{:S(2)}) collective-permute-start(bf16[2,32,1152]{2,1,0:T(8,128)(2,1)S(1)} %get-tuple-element.302), channel_id=1, source_target_pairs={{0,5},{1,4},{2,7},{3,6},{4,1},{5,0},{6,3},{7,2},{8,13},{9,12},{10,... | collective-permute-start | bytes 442376 | tf_op jit(solution)/shard_map/ppermute | solution.py:648
  361.7 27.4 %collective-permute-start.86 = (bf16[2,32,1152]{2,1,0:T(8,128)(2,1)S(1)}, bf16[2,32,1152]{2,1,0:T(8,128)(2,1)S(1)}, u32[]{:S(2)}, u32[]{:S(2)}) collective-permute-start(bf16[2,32,1152]{2,1,0:T(8,128)(2,1)S(1)} %get-tuple-element.303), channel_id=1, source_target_pairs={{0,1},{1,0},{2,3},{3,2},{4,5},{5,4},{6,7},{7,6},{8,9},{9,8},{10,11... | collective-permute-start | bytes 442376 | tf_op jit(solution)/shard_map/ppermute | solution.py:648
  363.9 25.3 %collective-permute-start.87 = (bf16[2,32,1152]{2,1,0:T(8,128)(2,1)S(1)}, bf16[2,32,1152]{2,1,0:T(8,128)(2,1)S(1)}, u32[]{:S(2)}, u32[]{:S(2)}) collective-permute-start(bf16[2,32,1152]{2,1,0:T(8,128)(2,1)S(1)} %get-tuple-element.304), channel_id=1, source_target_pairs={{0,4},{1,5},{2,6},{3,7},{4,0},{5,1},{6,2},{7,3},{8,12},{9,13},{10,... | collective-permute-start | bytes 442376 | tf_op jit(solution)/shard_map/ppermute | solution.py:648
  392.7 7.8 %collective-permute-start.91 = (bf16[2,32,1152]{2,1,0:T(8,128)(2,1)}, bf16[2,32,1152]{2,1,0:T(8,128)(2,1)S(1)}, u32[]{:S(2)}, u32[]{:S(2)}) collective-permute-start(bf16[2,32,1152]{2,1,0:T(8,128)(2,1)} %get-tuple-element.327), channel_id=1, source_target_pairs={{0,5},{1,4},{2,7},{3,6},{4,1},{5,0},{6,3},{7,2},{8,13},{9,12},{10,... | collective-permute-start | bytes 442376 | tf_op jit(solution)/shard_map/ppermute | solution.py:648
  414.0 15.7 %all-to-all-start.4 = ((f32[4,1,9856]{2,1,0:T(1,128)}), f32[4,1,9856]{2,1,0:T(1,128)S(1)}, u32[]{:S(2)}, u32[]{:S(2)}) async-start(f32[4,1,9856]{2,1,0:T(1,128)} %broadcast_in_dim.101), calls=%async_computation.7 | async-start | bytes 315392 | tf_op jit(solution)/shard_map/all_to_all | solution.py:665
  417.4 22.6 %collective-permute-start.94 = (bf16[2,32,1152]{2,1,0:T(8,128)(2,1)S(1)}, bf16[2,32,1152]{2,1,0:T(8,128)(2,1)S(1)}, u32[]{:S(2)}, u32[]{:S(2)}) collective-permute-start(bf16[2,32,1152]{2,1,0:T(8,128)(2,1)S(1)} %get-tuple-element.314), channel_id=1, source_target_pairs={{1,0},{3,2},{5,4},{7,6},{9,8},{11,10},{13,12},{15,14},{17,16},{19,... | collective-permute-start | bytes 442376 | tf_op jit(solution)/shard_map/ppermute | solution.py:1115
  430.5 9.4 %collective-permute-start.95 = (bf16[2,32,1152]{2,1,0:T(8,128)(2,1)S(1)}, bf16[2,32,1152]{2,1,0:T(8,128)(2,1)S(1)}, u32[]{:S(2)}, u32[]{:S(2)}) collective-permute-start(bf16[2,32,1152]{2,1,0:T(8,128)(2,1)S(1)} %get-tuple-element.332), channel_id=1, source_target_pairs={{0,1},{2,3},{4,5},{6,7},{8,9},{10,11},{12,13},{14,15},{16,17},{18,... | collective-permute-start | bytes 442376 | tf_op jit(solution)/shard_map/ppermute | solution.py:1114
  438.4 17.3 %collective-permute-start.96 = (bf16[288,1152]{1,0:T(8,128)(2,1)S(1)}, bf16[288,1152]{1,0:T(8,128)(2,1)}, u32[]{:S(2)}, u32[]{:S(2)}) collective-permute-start(bf16[288,1152]{1,0:T(8,128)(2,1)S(1)} %copy-done.37), channel_id=1, source_target_pairs={{1,0},{3,2},{5,4},{7,6},{9,8},{11,10},{13,12},{15,14},{17,16},{19,... | collective-permute-start | bytes 1990664 | tf_op jit(solution)/shard_map/ppermute | solution.py:960
  456.8 22.9 %collective-permute-start.97 = (bf16[288,768]{1,0:T(8,128)(2,1)}, bf16[288,768]{1,0:T(8,128)(2,1)}, u32[]{:S(2)}, u32[]{:S(2)}) collective-permute-start(bf16[288,768]{1,0:T(8,128)(2,1)} %reduce-scatter.11.cloned.1.call-done), channel_id=1, source_target_pairs={{1,0},{3,2},{5,4},{7,6},{9,8},{11,10},{13,12},{15,14},{17,16},{19,... | collective-permute-start | bytes 1327112 | tf_op jit(solution)/shard_map/ppermute | solution.py:960
  458.7 8.8 %all-to-all-start.5 = ((f32[4,2,288]{2,1,0:T(2,128)}), f32[4,2,288]{2,1,0:T(2,128)S(1)}, u32[]{:S(2)}, u32[]{:S(2)}) async-start(f32[4,2,288]{2,1,0:T(2,128)} %reshape.179), calls=%async_computation.9 | async-start | bytes 24576 | tf_op jit(solution)/shard_map/all_to_all | solution.py:1076
  468.2 9.8 %all-to-all-start.6 = ((f32[8,4,2,288]{3,2,1,0:T(2,128)}), f32[8,4,2,288]{3,2,1,0:T(2,128)}, u32[]{:S(2)}, u32[]{:S(2)}) async-start(f32[8,4,2,288]{3,2,1,0:T(2,128)} %broadcast_in_dim.102), calls=%async_computation.10 | async-start | bytes 196608 | tf_op jit(solution)/shard_map/all_to_all | solution.py:665
  (116 other events, 714.1 us)
Sparse Core Ops, SparseCore 0:
  30.5 40.3 all-gather.4
  73.0 53.9 all-gather.6
  128.6 39.1 all-gather.8
  169.8 54.2 all-gather.10
  243.1 51.3 reduce-scatter.4
  297.2 38.0 reduce-scatter.6
  337.8 51.7 reduce-scatter.8
  392.5 40.5 reduce-scatter.10

commit v3 on v2

--- a/solution.py
+++ b/solution.py
@@ -31,8 +31,19 @@
             self.left.add(at)
 
 
+class Columns:
+    def __init__(self, array, start, width):
+        self.array, self.start = array, start
+        self.shape, self.dtype = (array.shape[0], width), array.dtype
+        self.size = array.shape[0] * width
+
+    def source(self, ref):
+        return ref.at[:, self.start : self.start + self.shape[1]]
+
+
 def call(body, outs, *args, scalars=0, flops=0, scratch=(), after=(), streamed=(), saved=()):
     count, waits, many = len(args), len(after), len(outs)
+    given = args
     moving = bool(streamed or saved)
 
     def kernel(*refs):
@@ -41,7 +52,8 @@
         own, held = rest[: len(scratch)], rest[len(scratch) :]
         arriving, leaving = {}, {}
         for i, at in enumerate(streamed):
-            arriving[at] = pltpu.make_async_copy(ins[at], held[i], held[-1].at[i])
+            source = given[at].source(ins[at]) if isinstance(given[at], Columns) else ins[at]
+            arriving[at] = pltpu.make_async_copy(source, held[i], held[-1].at[i])
             ins[at] = held[i]
         for i, at in enumerate(saved, len(streamed)):
             leaving[at] = pltpu.make_async_copy(held[i], out_refs[at], held[-1].at[i])
@@ -73,11 +85,12 @@
     shapes = [
         pltpu.HBM(o.shape, o.dtype) if i in saved else o for i, o in enumerate(outs)
     ]
+    args = [a.array if isinstance(a, Columns) else a for a in args]
     args = [
         pltpu.with_memory_space_constraint(a, pltpu.HBM) if i in streamed else a
         for i, a in enumerate(args)
     ]
-    hold = [pltpu.VMEM(args[i].shape, args[i].dtype) for i in streamed]
+    hold = [pltpu.VMEM(given[i].shape, given[i].dtype) for i in streamed]
     hold += [pltpu.VMEM(outs[i].shape, outs[i].dtype) for i in saved]
     if moving:
         hold.append(pltpu.SemaphoreType.DMA((len(hold),)))
@@ -149,11 +162,6 @@
         outs[j][...] = (own[...].astype(F32) + recv[j].astype(F32)).astype(BF16)
 
 
-def scale_rows_kernel(g_ref, mod_ref, o_ref):
-    for m in range(g_ref.shape[0]):
-        o_ref[m] = (mod_ref[m, 5:6] * g_ref[m].astype(F32)).astype(BF16)
-
-
 def after_attn_kernel(traffic, p0, p1, p2, p3, x_ref, mod_ref, att_ref, aft_ref, n_ref):
     for m in range(x_ref.shape[0]):
         att = gather_total([p.at[m] for p in (p0, p1, p2, p3)])
@@ -174,12 +182,10 @@
         n_ref[m] = (hat * (1.0 + next_ref[m, 1:2]) + next_ref[m, 0:1]).astype(BF16)
 
 
-def end_kernel(p0, p1, p2, p3, aft_ref, mod_ref, g_ref, more_ref, x_ref, gm_ref):
+def end_kernel(p0, p1, p2, p3, aft_ref, mod_ref, x_ref):
     for m in range(aft_ref.shape[0]):
         mlp = gather_total([p.at[m] for p in (p0, p1, p2, p3)])
         x_ref[m] = (aft_ref[m] + mod_ref[m, 5:6] * mlp).astype(BF16)
-        gm_ref[m, 0:5] = more_ref[m]
-        gm_ref[m, 5:6] = rows_sum(g_ref[m].astype(F32) * mlp)
 
 
 def back_mlp_rows_kernel(traffic, p0, p1, p2, p3, g_ref, aft_ref, att_ref, mod_ref, ga_ref, gt_ref, gm_ref):
@@ -194,31 +200,30 @@
         gm_ref[m, 2:3] = rows_sum(gn * hat)
 
 
-def back_attn_rows(pieces, ga_ref, x_ref, mod_ref, some_ref, gm_ref, m):
+def back_attn_rows(pieces, ga_ref, x_ref, mod_ref, some_ref, gate_ref, gm_ref, m):
     gn = gather_total([p.at[m] for p in pieces])
     hat, rstd = normalize(x_ref[m].astype(F32))
     grad = ga_ref[m] + norm_grad(hat, rstd, gn * (1.0 + mod_ref[m, 1:2]))
     gm_ref[m, 0:1] = rows_sum(gn)
     gm_ref[m, 1:2] = rows_sum(gn * hat)
     gm_ref[m, 2:5] = some_ref[m]
+    gm_ref[m, 5:6] = gate_ref[m]
     return grad.astype(BF16)
 
 
-def back_between_kernel(
-    p0, p1, p2, p3, ga_ref, x_ref, mod_ref, some_ref, prev_ref, mlp_ref, g_ref, gmlp_ref, gm_ref, gate_ref
-):
+def back_between_kernel(p0, p1, p2, p3, ga_ref, x_ref, mod_ref, some_ref, gate_ref, prev_ref, mlp_ref, *outs):
+    g_ref, gmlp_ref, gm_ref, next_ref = outs
     for m in range(x_ref.shape[0]):
-        grad = back_attn_rows((p0, p1, p2, p3), ga_ref, x_ref, mod_ref, some_ref, gm_ref, m)
+        grad = back_attn_rows((p0, p1, p2, p3), ga_ref, x_ref, mod_ref, some_ref, gate_ref, gm_ref, m)
         g_ref[m] = grad
         wide = grad.astype(F32)
         gmlp_ref[m] = (prev_ref[m, 5:6] * wide).astype(BF16)
-        gate_ref[m] = rows_sum(wide * mlp_ref[m])
+        next_ref[m] = rows_sum(wide * mlp_ref[m])
 
 
 def back_end_kernel(p0, p1, p2, p3, ga_ref, x_ref, mod_ref, some_ref, gate_ref, g_ref, gm_ref):
     for m in range(x_ref.shape[0]):
-        g_ref[m] = back_attn_rows((p0, p1, p2, p3), ga_ref, x_ref, mod_ref, some_ref, gm_ref, m)
-        gm_ref[m, 5:6] = gate_ref[m]
+        g_ref[m] = back_attn_rows((p0, p1, p2, p3), ga_ref, x_ref, mod_ref, some_ref, gate_ref, gm_ref, m)
 
 
 def scan_mask(columns_first):
@@ -339,8 +344,9 @@
     return first, pltpu.roll(tiles[2], shift, 1)
 
 
-def pack_kernel(cfg, sec_ref, in_ref, gate_ref, out_ref, up_ref, down_ref, keep_ref, send_ref, keep_b_ref, send_b_ref):
-    heads, channels, main, left = cfg
+def pack_attn_kernel(cfg, traffic, sec_ref, in_ref, gate_ref, out_ref, keep_ref, send_ref):
+    heads, channels = cfg
+    traffic.wait(1)
     spots = tail_spots(heads)
     tail = channels - LANES
     rows = in_ref.shape[1]
@@ -366,6 +372,13 @@
     cols = slice(5 * LANES, 6 * LANES)
     keep_ref[:, cols] = jnp.where(keep_first, tails[0], tails[1]).astype(BF16)
     send_ref[:, cols] = jnp.where(keep_first, tails[1], tails[0]).astype(BF16)
+
+
+def pack_mlp_kernel(left, traffic, sec_ref, up_ref, down_ref, keep_b_ref, send_b_ref):
+    keep_first = sec_ref[0] == 0
+    lane = lanes()
+    main = (keep_b_ref.shape[1] - LANES) // 2
+    traffic.wait(1)
     at = 0
     for ref in (up_ref, down_ref):
         low, high = ref[:, :main], ref[:, main : 2 * main]
@@ -379,17 +392,35 @@
     send_b_ref[:, at:] = jnp.where(keep_first, high, low)
 
 
-def unpack_attn_kernel(cfg, sec_ref, mine_ref, recv_ref, in_ref, gate_ref, out_ref):
+def unpack_mlp_kernel(left, sec_ref, sum0_ref, other0_ref, sum1_ref, other1_ref, up_ref, down_ref):
+    in_first = sec_ref[0] == 0
+    main = (sum0_ref.shape[1] - LANES) // 2
+    lane = lanes()
+
+    def both(cols):
+        low = jnp.where(in_first, sum0_ref[:, cols], other1_ref[:, cols])
+        return low.astype(F32), jnp.where(in_first, other0_ref[:, cols], sum1_ref[:, cols]).astype(F32)
+
+    up_ref[:, :main], up_ref[:, main : 2 * main] = both(slice(0, main))
+    down_ref[:, :main], down_ref[:, main : 2 * main] = both(slice(main, 2 * main))
+    low, high = both(slice(2 * main, 2 * main + LANES))
+    up_ref[:, 2 * main :] = jnp.where(lane < left, low, pltpu.roll(high, left, 1))
+    down_ref[:, 2 * main :] = jnp.where(lane < left, pltpu.roll(low, LANES - left, 1), high)
+
+
+def unpack_attn_kernel(
+    cfg, sec_ref, sum0_ref, other0_ref, sum1_ref, other1_ref, in_ref, gate_ref, out_ref
+):
     heads, channels = cfg
     spots = tail_spots(heads)
     tail = channels - LANES
-    mine_first = sec_ref[0] == 0
+    in_first = sec_ref[0] == 0
     lane = lanes()
     shift = channels - LANES
 
     def both(cols):
-        mine, recv = mine_ref[:, cols].astype(F32), recv_ref[:, cols].astype(F32)
-        return jnp.where(mine_first, mine, recv), jnp.where(mine_first, recv, mine)
+        low = jnp.where(in_first, sum0_ref[:, cols], other1_ref[:, cols])
+        return low.astype(F32), jnp.where(in_first, other0_ref[:, cols], sum1_ref[:, cols]).astype(F32)
 
     low_tails, high_tails = both(slice(5 * LANES, 6 * LANES))
     for j in range(5):
@@ -602,16 +633,10 @@
 
 
 def mlp_backward_kernel(left, traffic, *refs):
-    count = 1 if len(refs) == 10 else 8
-    given, (pre_ref, w_ref) = refs[:count], refs[count : count + 2]
-    rest = refs[count + 2 :]
-    if count == 8:
-        g_ref, rest = rest[0], rest[1:]
-        stack_shards(given, g_ref)
-        traffic.wait(8, 9)
-    else:
-        g_ref = given[0]
-        traffic.wait(0, 1, 2)
+    given, (pre_ref, w_ref) = refs[:8], refs[8:10]
+    g_ref, rest = refs[10], refs[11:]
+    stack_shards(given, g_ref)
+    traffic.wait(8, 9)
     gpre_ref, gub_ref, other_ref = rest[:3]
     own_refs = rest[3:]
     main = (w_ref.shape[1] - LANES) // 2
@@ -625,6 +650,44 @@
     last = jnp.where(lane < left, last, 0.0).astype(BF16)
     gpre_ref[:, main:] = last
     gub_ref[:, main:] = rows_sum(last.astype(F32))
+    total = mm_nt(g_pre, w_ref[:, :main]) + mm_nt(last, w_ref[:, 2 * main :])
+    put_shards(total, own_refs[0].shape, other_ref, own_refs)
+
+
+def mlp_both_kernel(left, traffic, n_ref, raw_ref, w_ref, ub_ref, mod_ref, *refs):
+    gw_ref, gub_ref, gate_ref, other_ref = refs[:4]
+    own_refs, end_ref, end_refs = refs[4:8], refs[8], refs[9:13]
+    g_ref = refs[13]
+    images, rows = own_refs[0].shape[:2]
+    main = (w_ref.shape[1] - LANES) // 2
+    lane = lax.broadcasted_iota(jnp.int32, (1, LANES), 1)
+    spans = [(i % images, slice(i * rows, (i + 1) * rows)) for i in range(8 * images)]
+    traffic.wait(0, 1)
+    for m, span in spans:
+        g_ref[span] = (mod_ref[m, 5:6] * raw_ref[span].astype(F32)).astype(BF16)
+    traffic.wait(2)
+    n, g = n_ref[...], g_ref[...]
+    value, slope = gelu_terms(mm(n, w_ref[:, :main]) + ub_ref[:, :main])
+    hidden = value.astype(BF16)
+    g_pre = (mm(g, w_ref[:, main : 2 * main]) * slope).astype(BF16)
+    value, slope = gelu_terms(mm(n, w_ref[:, 2 * main :]) + ub_ref[:, main:])
+    tail = pltpu.roll(jnp.where(lane < left, value, 0.0), LANES - left, 1).astype(BF16)
+    last = pltpu.roll(mm(g, w_ref[:, 2 * main :]), left, 1) * slope
+    last = jnp.where(lane < left, last, 0.0).astype(BF16)
+    gw_ref[:, :main] = mm_tn(n, g_pre).astype(BF16)
+    gw_ref[:, main : 2 * main] = mm_tn(g, hidden).astype(BF16)
+    gw_ref[:, 2 * main :] = (mm_tn(n, last) + mm_tn(g, tail)).astype(BF16)
+    traffic.flush(0)
+    gub_ref[:, :main] = rows_sum(g_pre.astype(F32))
+    gub_ref[:, main:] = rows_sum(last.astype(F32))
+    total = mm_nt(hidden, w_ref[:, main : 2 * main]) + mm_nt(tail, w_ref[:, 2 * main :])
+    put_shards(total, own_refs[0].shape, end_ref, end_refs)
+    traffic.flush(8, 9, 10, 11, 12)
+    gates = [0.0] * images
+    for m, span in spans:
+        gates[m] = gates[m] + rows_sum(raw_ref[span].astype(F32) * total[span])
+    for m in range(images):
+        gate_ref[m] = gates[m]
     total = mm_nt(g_pre, w_ref[:, :main]) + mm_nt(last, w_ref[:, 2 * main :])
     put_shards(total, own_refs[0].shape, other_ref, own_refs)
 
@@ -734,19 +797,27 @@
     cfg = (heads, channels)
     section = s.astype(jnp.int32).reshape(1)
     shape_a, shape_b = (slab, 6 * LANES), (slab, 2 * main + LANES)
-    kept_a, sent_a, kept_b, sent_b = call(
-        functools.partial(pack_kernel, (*cfg, main, left)),
-        (out(shape_a, BF16),) * 2 + (out(shape_b, BF16),) * 2,
+    kept_a, sent_a = call(
+        functools.partial(pack_attn_kernel, cfg),
+        (out(shape_a, BF16),) * 2,
         section,
         in_weight[0],
         jnp.pad(gate_weight[0].astype(F32), ((0, 0), (0, LANES - gate_weight.shape[2]))),
         out_weight[0].T,
+        scalars=1,
+        streamed=(1,),
+    )
+    sent_a, condition, down_in = lax.optimization_barrier((sent_a, condition, down_weight[0]))
+    received_a = lax.ppermute(sent_a, "section", [(0, 1), (1, 0)])
+    kept_b, sent_b = call(
+        functools.partial(pack_mlp_kernel, left),
+        (out(shape_b, BF16),) * 2,
+        section,
         up_weight[0],
-        down_weight[0].T,
+        down_in.T,
         scalars=1,
-    )
-    sent_a, condition = lax.optimization_barrier((sent_a, condition))
-    received_a = lax.ppermute(sent_a, "section", [(0, 1), (1, 0)])
+        streamed=(1,),
+    )
     received_b = lax.ppermute(sent_b, "section", [(0, 1), (1, 0)])
 
     def unit_halves(value):
@@ -882,7 +953,7 @@
         )
         return terms, grads, found[2]
 
-    def mlp_forward(b, normed, late):
+    def mlp_forward(b, normed):
         _, w, _, _, up_row = weights[b]
         found = call(
             functools.partial(mlp_forward_kernel, left),
@@ -897,36 +968,52 @@
             up_row,
             flops=mlp_flops,
             streamed=(8,),
-            saved=tuple(range(8)) if late else (0, 1, 2),
+            saved=(0, 1, 2),
         )
-        return found[:3], found[3:]
+        return found[:3], scatter_plane(found[3], found[4:])
+
+    shape_gw = out((width, 2 * main + LANES), BF16)
+    shape_gub = out((1, main + LANES), F32)
+
+    def mlp_both(b, gathered, gradient):
+        _, w, _, _, up_row = weights[b]
+        found = call(
+            functools.partial(mlp_both_kernel, left),
+            (shape_gw, shape_gub, vector, *pieces_out, *pieces_out),
+            gathered,
+            gradient,
+            w,
+            up_row,
+            mods[b],
+            flops=3 * mlp_flops,
+            scratch=[pltpu.VMEM(flat.shape, flat.dtype)],
+            streamed=(0, 1, 2),
+            saved=(0, 8, 9, 10, 11, 12),
+        )
+        return scatter_plane(found[3], found[4:8]), found[0], found[1], found[2], found[8:]
 
     def mlp_backward(b, given, saved, after=()):
         _, w, _, _, _ = weights[b]
-        gathered = len(given) == 1
-        outs = (out((total_rows, main + LANES), BF16), out((1, main + LANES), F32), *pieces_out)
         found = call(
             functools.partial(mlp_backward_kernel, left),
-            outs if gathered else (flat, *outs),
+            (flat, out((total_rows, main + LANES), BF16), shape_gub, *pieces_out),
             *given,
             saved[1],
             w,
             flops=mlp_flops,
-            streamed=(0, 1, 2) if gathered else (8, 9),
+            streamed=(8, 9),
             after=after,
         )
-        if gathered:
-            found = (given[0], *found)
         terms = scatter_plane(found[3], found[4:])
         (grads,) = call(
             mlp_weights_kernel,
-            (out((width, 2 * main + LANES), BF16),),
+            (shape_gw,),
             saved[0],
             found[1],
             found[0],
             saved[2],
             flops=mlp_flops,
-            after=() if b else terms,
+            after=terms,
             streamed=(0, 3),
             saved=(0,),
         )
@@ -936,21 +1023,22 @@
         return jnp.where(first == (b == 0), kept, received)
 
     full_a0 = gather_all(of_block(0, kept_a, received_a))
-    full_b0 = gather_all(of_block(0, kept_b, received_b))
-    (g_mlp,) = call(scale_rows_kernel, (shard,), g1, mods[1])
-    (g_mlp1,) = call(stack_kernel, (flat,), *gather_plane(g_mlp), saved=(0,))
+    middle = [of_block(0, kept_b, received_b), of_block(1, kept_a, received_a)]
+    full_middle = gather_all(jnp.concatenate(middle, axis=1))
+    full_b0 = Columns(full_middle, 0, middle[0].shape[1])
+    full_a1 = Columns(full_middle, middle[0].shape[1], middle[1].shape[1])
+    (g1_all,) = call(stack_kernel, (flat,), *gather_plane(g1), saved=(0,))
     (normed,) = call(start_kernel, (shard,), x0, mods[0])
-    shards, g_mlp1, next_a, next_b = lax.optimization_barrier(
+    shards, g1_all, next_b = lax.optimization_barrier(
         (
             gather_plane(normed),
-            g_mlp1,
-            of_block(1, kept_a, received_a),
+            g1_all,
             of_block(1, kept_b, received_b),
         )
     )
     weights = [
         (full_a0, full_b0, *unpack_small(small[0])),
-        (gather_all(next_a), gather_all(next_b), *unpack_small(small[1])),
+        (full_a1, gather_all(next_b), *unpack_small(small[1])),
     ]
 
     def to_second(value):
@@ -963,11 +1051,11 @@
     att0, aft0, normed = call(
         after_attn_kernel, (shard_wide, shard_wide, shard), *terms, x0, mods[0], saved=(0, 1)
     )
-    mlp0, pieces = mlp_forward(0, normed, False)
+    mlp0, terms = mlp_forward(0, normed)
     mlp_out0, x1, normed = call(
         between_kernel,
         (shard_wide, shard, shard),
-        *scatter_plane(pieces[0], pieces[1:]),
+        *terms,
         aft0,
         mods[0],
         mods[1],
@@ -977,10 +1065,10 @@
     att1, aft1, normed = call(
         after_attn_kernel, (shard_wide, shard_wide, shard), *terms, x1, mods[1], saved=(0, 1)
     )
-    mlp1, end_pieces = mlp_forward(1, normed, True)
-
-    three, five, six = (out((images, n, width), F32) for n in (3, 5, 6))
-    terms, mlp_grads1, g_up_bias1 = mlp_backward(1, (g_mlp1,), mlp1)
+
+    three, six = (out((images, n, width), F32) for n in (3, 6))
+    (n_all,) = call(stack_kernel, (flat,), *gather_plane(normed), saved=(0,))
+    terms, mlp_grads1, g_up_bias1, g_gate_two1, end_pieces = mlp_both(1, n_all, g1_all)
     g_after, g_attn, g_some = call(
         back_mlp_rows_kernel,
         (shard_wide, shard, three),
@@ -989,19 +1077,19 @@
         aft1,
         att1,
         mods[1],
-        after=(mlp_grads1,),
         saved=(0,),
     )
     sum_b1 = scatter_rows(mlp_grads1)
     terms, attn_grads1, g_taps1 = attn_backward(1, gather_plane(g_attn), attn1)
-    g0, g_mlp, g_more, g_gate_two0 = call(
+    g0, g_mlp, g_mods1, g_gate_two0 = call(
         back_between_kernel,
-        (shard, shard, five, vector),
+        (shard, shard, six, vector),
         *terms,
         g_after,
         x1,
         mods[1],
         g_some,
+        g_gate_two1,
         mods[0],
         mlp_out0,
     )
@@ -1018,9 +1106,7 @@
         after=(sum_b1,),
         saved=(0,),
     )
-    shards, sum_b1, sum_a1 = lax.optimization_barrier((gather_plane(g_attn), sum_b1, sum_a1))
-    terms, attn_grads0, g_taps0 = attn_backward(0, shards, attn0, (mlp_grads0,))
-    other_b1, other_a1 = to_second(sum_b1), to_second(sum_a1)
+    terms, attn_grads0, g_taps0 = attn_backward(0, gather_plane(g_attn), attn0, (mlp_grads0,))
     g_in, g_mods0 = call(
         back_end_kernel,
         (shard, six),
@@ -1030,21 +1116,10 @@
         mods[0],
         g_some,
         g_gate_two0,
-        after=(attn_grads0, other_b1, other_a1),
+        after=(attn_grads0,),
     )
 
     sum_b0, sum_a0 = scatter_rows(mlp_grads0), scatter_rows(attn_grads0)
-
-    end_pieces, g_mods0 = lax.optimization_barrier((end_pieces, g_mods0))
-    block_out, g_mods1 = call(
-        end_kernel,
-        (shard, six),
-        *scatter_plane(end_pieces[0], end_pieces[1:]),
-        aft1,
-        mods[1],
-        g1,
-        g_more,
-    )
 
     g_mod = jnp.stack([g_mods0.reshape(images, -1), g_mods1.reshape(images, -1)])
     g_mod = g_mod.reshape(sections, images, tensors, -1).transpose(0, 2, 1, 3)
@@ -1062,23 +1137,42 @@
     g_parts = lax.all_to_all(
         g_sent, ("section", "tensor"), split_axis=0, concat_axis=0, tiled=True
     )
-    block_out, sum_b0 = lax.optimization_barrier((block_out, sum_b0))
-    other_b0 = to_first(sum_b0)
+    g_parts, sum_b1, sum_a1 = lax.optimization_barrier((g_parts, sum_b1, sum_a1))
+    other_b1, other_a1 = to_second(sum_b1), to_second(sum_a1)
     g_share = jnp.sum(g_parts[:, : images * columns], axis=0)
     small_parts = g_parts[:, images * columns :].reshape(sections, tensors, -1).sum(1)
     g_all = spread_over(jnp.concatenate([g_share, small_parts.reshape(-1)]), ("dp",))
+    g_all, end_pieces, sum_b0 = lax.optimization_barrier((g_all, end_pieces, sum_b0))
+    others = other_b1, other_a1, to_first(sum_b0)
+    (block_out,) = call(
+        end_kernel, (shard,), *scatter_plane(end_pieces[0], end_pieces[1:]), aft1, mods[1]
+    )
     small_own = jnp.sum(g_all[:, images * columns :], axis=0).reshape(sections, -1)
     g_all = g_all[:, : images * columns].reshape(dps * images, columns).astype(BF16)
     grad_ada_bias = jnp.sum(g_all.astype(F32), axis=0)
-    grad_ada = jnp.einsum("md,me->de", slab_active, g_all, preferred_element_type=F32)
     act_part = jnp.einsum("me,de->md", g_all, ada_weight[0], preferred_element_type=F32)
-    act_part, other_b0, sum_a0 = lax.optimization_barrier((act_part, other_b0, sum_a0))
     act_all = lax.all_to_all(
         act_part.reshape(dps, images, slab), "dp", split_axis=0, concat_axis=0, tiled=True
     )
-    act_all = jnp.sum(spread_over(act_all, ("section", "tensor")), axis=0)
+    act_all, others = lax.optimization_barrier((act_all, others))
+    act_all = spread_over(act_all, ("section", "tensor"))
+    act_all = jnp.sum(act_all, axis=0)
     act_grad = act_all.reshape(dps, images, slab).transpose(1, 0, 2).reshape(images, width)
     cond_grad = jax.vjp(jax.nn.silu, cond_vec)[1](act_grad)[0]
+
+    ends_from_first = lax.ppermute(block_out, "section", [(0, 1)])
+    ends_from_second = lax.ppermute(g_in, "section", [(1, 0)])
+    mine = jnp.where(first, g_in, block_out)
+    received = jnp.where(first, ends_from_second, ends_from_first)
+    section_ends = jnp.concatenate(
+        [jnp.where(first, mine, received), jnp.where(first, received, mine)], axis=1
+    )
+    cond_grad, section_ends, sum_a0, g_all, others = lax.optimization_barrier(
+        (cond_grad, section_ends, sum_a0, g_all, others)
+    )
+    other_b1, other_a1, other_b0 = others
+    other_a0 = to_first(sum_a0)
+    grad_ada = jnp.einsum("md,me->de", slab_active, g_all, preferred_element_type=F32)
 
     small_taps = small_own[:, : taps_rows * wide].reshape(sections, taps_rows, wide)
     grad_gateb = small_taps[:, taps_count, tail : tail + heads].reshape(-1)
@@ -1089,14 +1183,17 @@
         [up_halves[:, :main].reshape(-1), up_halves[:, main : main + left].reshape(-1)]
     )
 
-    mine_b = jnp.where(first, sum_b0, sum_b1)
-    received = jnp.where(first, other_b0, other_b1)
-    pair_b = choose((mine_b.astype(F32), received.astype(F32)))
-    end = 2 * main + left
-    grad_up = [g[:, :main] for g in pair_b] + [g[:, 2 * main : end] for g in pair_b]
-    grad_up = jnp.concatenate(grad_up, axis=1)
-    grad_down = [g[:, main : 2 * main].T for g in pair_b] + [g[:, end:].T for g in pair_b]
-    grad_down = jnp.concatenate(grad_down, axis=0)
+    grad_up, grad_down = call(
+        functools.partial(unpack_mlp_kernel, left),
+        (out(up_weight.shape[1:], F32),) * 2,
+        section,
+        sum_b0,
+        other_b0,
+        sum_b1,
+        other_b1,
+        scalars=1,
+    )
+    grad_down = grad_down.T
     grad_in, grad_gate, grad_out = call(
         functools.partial(unpack_attn_kernel, cfg),
         (
@@ -1105,19 +1202,14 @@
             out((slab, out_weight.shape[1]), F32),
         ),
         section,
-        jnp.where(first, sum_a0, sum_a1),
-        jnp.where(first, to_first(sum_a0), other_a1),
+        sum_a0,
+        other_a0,
+        sum_a1,
+        other_a1,
         scalars=1,
     )
     grad_out = grad_out.T
 
-    ends_from_first = lax.ppermute(block_out, "section", [(0, 1)])
-    ends_from_second = lax.ppermute(g_in, "section", [(1, 0)])
-    mine = jnp.where(first, g_in, block_out)
-    received = jnp.where(first, ends_from_second, ends_from_first)
-    section_ends = jnp.concatenate(
-        [jnp.where(first, mine, received), jnp.where(first, received, mine)], axis=1
-    )
     return (
         section_ends[None],
         cond_grad,

time: 497 us -> 452 us (0.909)
  waiting for transfers between devices: 223 us -> 180 us
    all_gather x4 -> x3, waiting for transfers between devices: 49.1 us -> 36.9 us  [gather_all(): return lax.all_gather(own, 'dp', axis=0, tiled=True)]
    ppermute x2, waiting for transfers between devices: 11.9 us -> 2.53 us  [to_second(): return lax.ppermute(value, 'section', [(0, 1)])]
    ppermute x2, waiting for transfers between devices: 15 us -> 6.29 us  [to_first(): return lax.ppermute(value, 'section', [(1, 0)])]
    ppermute x88, waiting for transfers between devices: 116 us -> 109 us  [swap(): return lax.ppermute(value, PLANE, route)]
    unnamed x114 -> x116, local copies, waits for them, and re-layouts: 16.7 us -> 23.2 us
    all_to_all x2, waiting for transfers between devices: 11.7 us -> 5.38 us  [spread_over(): return lax.all_to_all(copies, axes, split_axis=0, concat_axis=0, tiled=True)]
  transfers between devices with their start and end apart: 111 -> 110, of which waited for: 67 -> 63; matrix products, arithmetic and copies ran while one was open for 5% -> 5% of each run, Pallas kernels for 13% -> 17%
where the time goes in v3:
time: 452 us; the launch traced here: 447 us
  waiting for transfers between devices  180 us (40%)
  starting transfers between devices  101 us (22%)
  Pallas kernels  87.9 us (19%)
  local copies, waits for them, and re-layouts  32.6 us (7%)
  blocking collectives  16.8 us (4%)
  between operations  15.5 us (3%)
  other arithmetic  9.12 us (2%)
    ppermute x88, waiting for transfers between devices, swap(): return lax.ppermute(value, PLANE, route)  109 us
    pallas_call x33, Pallas kernels, call(): pl.pallas_call(kernel, out_shape=tuple(shapes), in_specs=specs, out_specs...  87.9 us
    ppermute x88, starting transfers between devices, swap(): return lax.ppermute(value, PLANE, route)  61.2 us
    all_gather x3, waiting for transfers between devices, gather_all(): return lax.all_gather(own, 'dp', axis=0, tiled=True)  36.9 us
    unnamed x116, local copies, waits for them, and re-layouts  23.2 us
  transfers between devices with their start and end apart: 110, of which 63 were waited for; matrix products, arithmetic and copies ran while one was open for 5% of the time, Pallas kernels for 17%

profile of v3, /device:TPU:0, one launch (start us, length us, event | category | flops | bytes accessed | tf_op | source)
XLA Modules:
  0.0 446.9 jit_solution(12978687869871070643)
XLA Ops:
  11.3 3.0 collective-permute-start.2
  15.9 4.9 %all-to-all-start = ((bf16[4,2,288]{2,1,0:T(2,128)(2,1)}), bf16[4,2,288]{2,1,0:T(2,128)(2,1)S(1)}, u32[]{:S(2)}, u32[]{:S(2)}) async-start(bf16[4,2,288]{2,1,0:T(2,128)(2,1)} %bitcast.65), calls=%async_computation | async-start | bytes 12288 | tf_op jit(solution)/shard_map/all_to_all | solution.py:865
  20.8 5.6 %all-to-all-done = bf16[4,2,288]{2,1,0:T(2,128)(2,1)S(1)} async-done(((bf16[4,2,288]{2,1,0:T(2,128)(2,1)}), bf16[4,2,288]{2,1,0:T(2,128)(2,1)S(1)}, u32[]{:S(2)}, u32[]{:S(2)}) %all-to-all-start) | async-done | bytes 4640 | tf_op jit(solution)/shard_map/all_to_all | solution.py:865
  30.1 4.2 all-to-all-start.1
  34.3 6.8 %all-to-all-done.1 = f32[4,2,1728]{2,1,0:T(2,128)S(1)} async-done(((f32[4,2,1728]{2,1,0:T(2,128)}), f32[4,2,1728]{2,1,0:T(2,128)S(1)}, u32[]{:S(2)}, u32[]{:S(2)}) %all-to-all-start.1) | async-done | bytes 55328 | tf_op jit(solution)/shard_map/all_to_all | solution.py:869
  41.2 8.1 %all_to_all.46 = f32[8,2,1728]{2,1,0:T(2,128)} all-to-all(f32[8,2,1728]{2,1,0:T(2,128)S(1)} %broadcast_in_dim.89), channel_id=1, replica_groups=mesh['dp'=4,'tensor'=4,'section'=2] {'section','tensor'}, dimensions={0} | all-to-all | bytes 221184 | tf_op jit(solution)/shard_map/all_to_all | solution.py:728
  53.8 4.6 %collective-permute-done = bf16[2,32,1152]{2,1,0:T(8,128)(2,1)S(1)} collective-permute-done((bf16[2,32,1152]{2,1,0:T(8,128)(2,1)S(1)}, bf16[2,32,1152]{2,1,0:T(8,128)(2,1)S(1)}, u32[]{:S(2)}, u32[]{:S(2)}) %collective-permute-start) | collective-permute-done | bytes 147488 | tf_op jit(solution)/shard_map/ppermute | solution.py:837
  62.2 2.8 collective-permute-done.12.refs_3_
  72.5 3.3 collective-permute-done.5.refs_4_
  75.8 2.7 collective-permute-done.4.refs_3_
  83.9 8.2 %shard_map.224 = (bf16[2,256,1152]{2,1,0:T(8,128)(2,1)}, bf16[2,256,1024]{2,1,0:T(8,128)(2,1)}, f32[2,256,128]{2,1,0:T(8,128)}, f32[2,256,256]{2,1,0:T(8,128)}, ...) custom-call(s32[1]{0:T(128)} %bitcast.refs_0_, ...), custom_call_target="tpu_custom_call" | custom-call | flops 2315255808 | bytes 7422468 | tf_op jit(solution)/shard_map/pallas_call | solution.py:97
  97.9 4.1 collective-permute-done.19.refs_1_
  108.9 4.2 collective-permute-done.24.refs_3_
  116.7 36.9 %all-gather.6.cloned.1.call-done.refs_8_.refs_9_.refs_12_ = bf16[1152,1920]{1,0:T(8,128)(2,1)} async-done(((bf16[288,1920]{1,0:T(8,128)(2,1)}), bf16[1152,1920]{1,0:T(8,128)(2,1)}) %all-gather.6.cloned.1.call-update) | async-done | bytes 4423696 | tf_op jit(solution)/shard_map/all_gather | solution.py:732
  153.6 6.4 %shard_map.227 = (bf16[512,1152]{1,0:T(8,128)(2,1)}, f32[512,640]{1,0:T(8,128)}, bf16[512,640]{1,0:T(8,128)(2,1)}, bf16[4,2,32,1152]{3,2,1,0:T(8,128)(2,1)S(1)},...) custom-call(bf16[2,32,1152]{2,1,0:T(8,128)(2,1)S(1)} %get-tuple-elem, ...), custom_call_target="tpu_custom_call" | custom-call | flops 1358954496 | bytes 8161792 | tf_op jit(solution)/shard_map/pallas_call | solution.py:97
  166.0 4.0 collective-permute-done.30.refs_1_
  176.9 3.4 collective-permute-done.35.refs_4_
  180.4 2.7 collective-permute-done.34.refs_3_
  184.7 7.7 %shard_map.230 = (bf16[2,256,1152]{2,1,0:T(8,128)(2,1)}, bf16[2,256,1024]{2,1,0:T(8,128)(2,1)}, f32[2,256,128]{2,1,0:T(8,128)}, f32[2,256,256]{2,1,0:T(8,128)}, ...) custom-call(s32[1]{0:T(128)} %bitcast.refs_0_, ...), custom_call_target="tpu_custom_call" | custom-call | flops 2315255808 | bytes 7422468 | tf_op jit(solution)/shard_map/pallas_call | solution.py:97
  198.1 4.1 collective-permute-done.41.refs_1_
  202.2 2.7 collective-permute-done.42.refs_2_
  209.4 4.1 collective-permute-done.46.refs_3_
  218.4 9.3 %shard_map.234 = (bf16[1152,1152]{1,0:T(8,128)(2,1)}, f32[1,640]{1,0:T(1,128)S(1)}, f32[2,1,1152]{2,1,0:T(1,128)S(1)}, bf16[4,2,32,1152]{3,2,1,0:T(8,128)(2,1)S(...) custom-call(bf16[512,1152]{1,0:T(8,128)(2,1)} %shard_map.233.refs_0_, ...), custom_call_target="tpu_custom_call" | custom-call | flops 4076863488 | bytes 10096640 | tf_op jit(solution)/shard_map/pallas_call | solution.py:97
  235.4 4.1 collective-permute-done.52.refs_1_
  239.5 2.7 collective-permute-done.53.refs_2_
  246.9 4.0 collective-permute-done.57.refs_4_
  254.7 8.2 %shard_map.237 = (bf16[2,256,1152]{2,1,0:T(8,128)(2,1)S(1)}, bf16[2,256,640]{2,1,0:T(8,128)(2,1)S(1)}, f32[16,256]{1,0:T(8,128)S(1)}, bf16[4,2,32,1152]{3,2,1,0:...) custom-call(s32[1]{0:T(128)} %bitcast.refs_0_, ...), custom_call_target="tpu_custom_call" | custom-call | flops 4630511616 | bytes 7831556 | tf_op jit(solution)/shard_map/pallas_call | solution.py:97
  268.7 4.1 collective-permute-done.63.refs_1_.refs_5_
  272.8 2.7 collective-permute-done.64.refs_2_.refs_6_
  275.5 4.0 shard_map.240.refs_10_
  285.3 3.9 collective-permute-done.68.refs_3_
  293.1 6.0 %shard_map.241 = (bf16[512,1152]{1,0:T(8,128)(2,1)S(1)}, bf16[512,640]{1,0:T(8,128)(2,1)S(1)}, f32[1,640]{1,0:T(1,128)S(1)}, bf16[4,2,32,1152]{3,2,1,0:T(8,128)(...) custom-call(bf16[2,32,1152]{2,1,0:T(8,128)(2,1)S(1)} %get-tuple-elem, ...), custom_call_target="tpu_custom_call" | custom-call | flops 1358954496 | bytes 8161792 | tf_op jit(solution)/shard_map/pallas_call | solution.py:97
  304.8 4.1 collective-permute-done.74.refs_1_.refs_5_
  308.9 2.7 collective-permute-done.75.refs_2_.refs_6_
  311.7 5.1 %shard_map.244.refs_14_ = bf16[1152,1152]{1,0:T(8,128)(2,1)} custom-call(bf16[512,1152]{1,0:T(8,128)(2,1)} %get-tuple-element.280.refs_0_, bf16[512,640]{1,0:T(8,128)(2,1)S(1)} %get-tuple-element.281.refs_1_, bf16[512,1152]{1,0:T(8,128)(2,1)S(1)} %get-tuple-element.282.refs_2_, bf16[512,640]{1,0:T(8,128)(2,1)} %get-tuple-element.283.refs_3_, ...), custom_call_target="tpu_custom_call" | custom-call | flops 1358954496 | bytes 6324224 | tf_op jit(solution)/shard_map/pallas_call | solution.py:97
  322.4 4.0 collective-permute-done.79.refs_4_
  332.8 8.8 %shard_map.245 = (bf16[2,256,1152]{2,1,0:T(8,128)(2,1)S(1)}, bf16[2,256,640]{2,1,0:T(8,128)(2,1)S(1)}, f32[16,256]{1,0:T(8,128)S(1)}, bf16[4,2,32,1152]{3,2,1,0:...) custom-call(s32[1]{0:T(128)} %bitcast.refs_0_, ...), custom_call_target="tpu_custom_call" | custom-call | flops 4630511616 | bytes 7831556 | tf_op jit(solution)/shard_map/pallas_call | solution.py:97
  351.4 4.0 shard_map.247.refs_9_
  358.1 8.7 %all_to_all.47 = f32[8,1,6656]{2,1,0:T(1,128)S(1)} all-to-all(f32[8,1,6656]{2,1,0:T(1,128)S(1)} %copy.102), channel_id=1, replica_groups=mesh['dp'=4,'tensor'=4,'section'=2] {'section','tensor'}, dimensions={0} | all-to-all | bytes 425984 | tf_op jit(solution)/shard_map/all_to_all | solution.py:1137
  367.8 3.3 all-to-all-start.4
  371.2 3.9 collective-permute-start.89
  381.8 3.9 all-to-all-start.5
  391.9 2.9 collective-permute-start.92
  402.1 4.6 %all-to-all-start.6 = ((f32[8,4,2,288]{3,2,1,0:T(2,128)}), f32[8,4,2,288]{3,2,1,0:T(2,128)S(1)}, u32[]{:S(2)}, u32[]{:S(2)}) async-start(f32[8,4,2,288]{3,2,1,0:T(2,128)} %broadcast_in_dim.101), calls=%async_computation.9 | async-start | bytes 196608 | tf_op jit(solution)/shard_map/all_to_all | solution.py:728
  407.4 4.2 all-to-all-done.6
  414.0 2.7 collective-permute-start.96
  429.1 6.3 %collective-permute-done.97.refs_2_ = bf16[288,768]{1,0:T(8,128)(2,1)} collective-permute-done((bf16[288,768]{1,0:T(8,128)(2,1)}, bf16[288,768]{1,0:T(8,128)(2,1)}, u32[]{:S(2)}, u32[]{:S(2)}) %collective-permute-start.97) | collective-permute-done | bytes 442400 | tf_op jit(solution)/shard_map/ppermute | solution.py:1048
  435.4 2.8 shard_map.251
  (439 shorter events, 175.9 us)
Async XLA Ops:
  11.3 15.1 %collective-permute-start.2 = (bf16[288,768]{1,0:T(8,128)(2,1)S(1)}, bf16[288,768]{1,0:T(8,128)(2,1)S(1)}, u32[]{:S(2)}, u32[]{:S(2)}) collective-permute-start(bf16[288,768]{1,0:T(8,128)(2,1)S(1)} %get-tuple-element.181), channel_id=1, source_target_pairs={{0,1},{1,0},{2,3},{3,2},{4,5},{5,4},{6,7},{7,6},{8,9},{9,8},{10,11... | collective-permute-start | bytes 1327112 | tf_op jit(solution)/shard_map/ppermute | solution.py:811
  15.9 10.5 %all-to-all-start = ((bf16[4,2,288]{2,1,0:T(2,128)(2,1)}), bf16[4,2,288]{2,1,0:T(2,128)(2,1)S(1)}, u32[]{:S(2)}, u32[]{:S(2)}) async-start(bf16[4,2,288]{2,1,0:T(2,128)(2,1)} %bitcast.65), calls=%async_computation | async-start | bytes 12288 | tf_op jit(solution)/shard_map/all_to_all | solution.py:865
  20.8 62.2 %all-gather.4.cloned.1.call-start = ((), (), s32[]{:S(2)}) async-start(), calls=%async_computation.11 | async-start | bytes 2211840 | tf_op jit(solution)/shard_map/all_gather | solution.py:732
  28.6 20.7 %collective-permute-start.1 = (bf16[288,1152]{1,0:T(8,128)(2,1)S(1)}, bf16[288,1152]{1,0:T(8,128)(2,1)}, u32[]{:S(2)}, u32[]{:S(2)}) collective-permute-start(bf16[288,1152]{1,0:T(8,128)(2,1)S(1)} %get-tuple-element.179), channel_id=1, source_target_pairs={{0,1},{1,0},{2,3},{3,2},{4,5},{5,4},{6,7},{7,6},{8,9},{9,8},{10,11... | collective-permute-start | bytes 1990664 | tf_op jit(solution)/shard_map/ppermute | solution.py:821
  30.1 11.0 %all-to-all-start.1 = ((f32[4,2,1728]{2,1,0:T(2,128)}), f32[4,2,1728]{2,1,0:T(2,128)S(1)}, u32[]{:S(2)}, u32[]{:S(2)}) async-start(f32[4,2,1728]{2,1,0:T(2,128)} %fusion.2), calls=%async_computation.1 | async-start | bytes 114688 | tf_op jit(solution)/shard_map/all_to_all | solution.py:869
  34.3 119.4 %all-gather.6.cloned.1.call-start = ((), (), s32[]{:S(2)}) async-start(), calls=%async_computation.12 | async-start | bytes 5529600 | tf_op jit(solution)/shard_map/all_gather | solution.py:732
  52.5 165.9 %all-gather.8.cloned.1.call-start = ((), (), s32[]{:S(2)}) async-start(), calls=%async_computation.13 | async-start | bytes 3317760 | tf_op jit(solution)/shard_map/all_gather | solution.py:732
  59.3 7.8 %collective-permute-start.11 = (bf16[2,32,1152]{2,1,0:T(8,128)(2,1)S(1)}, bf16[2,32,1152]{2,1,0:T(8,128)(2,1)S(1)}, u32[]{:S(2)}, u32[]{:S(2)}) collective-permute-start(bf16[2,32,1152]{2,1,0:T(8,128)(2,1)S(1)} %get-tuple-element.432.refs_0_.refs_4_), channel_id=1, source_target_pairs={{0,4},{1,5},{2,6},{3,7},{4,0},{5,1},{6,2},{7,3},{8,12},{9,13},{10,... | collective-permute-start | bytes 442376 | tf_op jit(solution)/shard_map/ppermute | solution.py:711
  60.9 8.5 %collective-permute-start.13 = (bf16[2,32,1152]{2,1,0:T(8,128)(2,1)S(1)}, bf16[2,32,1152]{2,1,0:T(8,128)(2,1)S(1)}, u32[]{:S(2)}, u32[]{:S(2)}) collective-permute-start(bf16[2,32,1152]{2,1,0:T(8,128)(2,1)S(1)} %get-tuple-element.432.refs_0_.refs_4_), channel_id=1, source_target_pairs={{0,2},{1,3},{2,0},{3,1},{4,6},{5,7},{6,4},{7,5},{8,10},{9,11},{10,... | collective-permute-start | bytes 442376 | tf_op jit(solution)/shard_map/ppermute | solution.py:711
  61.0 9.9 %collective-permute-start.10 = (bf16[2,32,1152]{2,1,0:T(8,128)(2,1)S(1)}, bf16[2,32,1152]{2,1,0:T(8,128)(2,1)S(1)}, u32[]{:S(2)}, u32[]{:S(2)}) collective-permute-start(bf16[2,32,1152]{2,1,0:T(8,128)(2,1)S(1)} %get-tuple-element.432.refs_0_.refs_4_), channel_id=1, source_target_pairs={{0,1},{1,0},{2,3},{3,2},{4,5},{5,4},{6,7},{7,6},{8,9},{9,8},{10,11... | collective-permute-start | bytes 442376 | tf_op jit(solution)/shard_map/ppermute | solution.py:711
  68.2 7.7 %collective-permute-start.5 = (bf16[2,32,1152]{2,1,0:T(8,128)(2,1)S(1)}, bf16[2,32,1152]{2,1,0:T(8,128)(2,1)S(1)}, u32[]{:S(2)}, u32[]{:S(2)}) collective-permute-start(bf16[2,32,1152]{2,1,0:T(8,128)(2,1)S(1)} %shard_map.222.refs_1_), channel_id=1, source_target_pairs={{0,5},{1,4},{2,7},{3,6},{4,1},{5,0},{6,3},{7,2},{8,13},{9,12},{10,... | collective-permute-start | bytes 442376 | tf_op jit(solution)/shard_map/ppermute | solution.py:711
  69.4 9.1 %collective-permute-start.4 = (bf16[2,32,1152]{2,1,0:T(8,128)(2,1)S(1)}, bf16[2,32,1152]{2,1,0:T(8,128)(2,1)S(1)}, u32[]{:S(2)}, u32[]{:S(2)}) collective-permute-start(bf16[2,32,1152]{2,1,0:T(8,128)(2,1)S(1)} %shard_map.222.refs_1_), channel_id=1, source_target_pairs={{0,4},{1,5},{2,6},{3,7},{4,0},{5,1},{6,2},{7,3},{8,12},{9,13},{10,... | collective-permute-start | bytes 442376 | tf_op jit(solution)/shard_map/ppermute | solution.py:711
  70.9 7.7 %collective-permute-start.3 = (bf16[2,32,1152]{2,1,0:T(8,128)(2,1)S(1)}, bf16[2,32,1152]{2,1,0:T(8,128)(2,1)S(1)}, u32[]{:S(2)}, u32[]{:S(2)}) collective-permute-start(bf16[2,32,1152]{2,1,0:T(8,128)(2,1)S(1)} %shard_map.222.refs_1_), channel_id=1, source_target_pairs={{0,1},{1,0},{2,3},{3,2},{4,5},{5,4},{6,7},{7,6},{8,9},{9,8},{10,11... | collective-permute-start | bytes 442376 | tf_op jit(solution)/shard_map/ppermute | solution.py:711
  72.0 9.4 %collective-permute-start.6 = (bf16[2,32,1152]{2,1,0:T(8,128)(2,1)S(1)}, bf16[2,32,1152]{2,1,0:T(8,128)(2,1)S(1)}, u32[]{:S(2)}, u32[]{:S(2)}) collective-permute-start(bf16[2,32,1152]{2,1,0:T(8,128)(2,1)S(1)} %shard_map.222.refs_1_), channel_id=1, source_target_pairs={{0,2},{1,3},{2,0},{3,1},{4,6},{5,7},{6,4},{7,5},{8,10},{9,11},{10,... | collective-permute-start | bytes 442376 | tf_op jit(solution)/shard_map/ppermute | solution.py:711
  81.5 235.5 %reduce-scatter.5.cloned.1.call-start = ((), (), s32[]{:S(2)}) async-start(), calls=%async_computation.14 | async-start | bytes 3317760 | tf_op jit(solution)/shard_map/reduce_scatter | solution.py:736
  94.4 7.7 %collective-permute-start.19 = (bf16[2,32,1152]{2,1,0:T(8,128)(2,1)S(1)}, bf16[2,32,1152]{2,1,0:T(8,128)(2,1)S(1)}, u32[]{:S(2)}, u32[]{:S(2)}) collective-permute-start(bf16[2,32,1152]{2,1,0:T(8,128)(2,1)S(1)} %get-tuple-element.202), channel_id=1, source_target_pairs={{0,5},{1,4},{2,7},{3,6},{4,1},{5,0},{6,3},{7,2},{8,13},{9,12},{10,... | collective-permute-start | bytes 442376 | tf_op jit(solution)/shard_map/ppermute | solution.py:711
  95.6 8.5 %collective-permute-start.20 = (bf16[2,32,1152]{2,1,0:T(8,128)(2,1)S(1)}, bf16[2,32,1152]{2,1,0:T(8,128)(2,1)S(1)}, u32[]{:S(2)}, u32[]{:S(2)}) collective-permute-start(bf16[2,32,1152]{2,1,0:T(8,128)(2,1)S(1)} %get-tuple-element.203), channel_id=1, source_target_pairs={{0,1},{1,0},{2,3},{3,2},{4,5},{5,4},{6,7},{7,6},{8,9},{9,8},{10,11... | collective-permute-start | bytes 442376 | tf_op jit(solution)/shard_map/ppermute | solution.py:711
  105.3 7.7 %collective-permute-start.24 = (bf16[2,32,1152]{2,1,0:T(8,128)(2,1)S(1)}, bf16[2,32,1152]{2,1,0:T(8,128)(2,1)S(1)}, u32[]{:S(2)}, u32[]{:S(2)}) collective-permute-start(bf16[2,32,1152]{2,1,0:T(8,128)(2,1)S(1)} %get-tuple-element.205.refs_0_), channel_id=1, source_target_pairs={{0,5},{1,4},{2,7},{3,6},{4,1},{5,0},{6,3},{7,2},{8,13},{9,12},{10,... | collective-permute-start | bytes 442376 | tf_op jit(solution)/shard_map/ppermute | solution.py:711
  106.7 8.5 %collective-permute-start.23 = (bf16[2,32,1152]{2,1,0:T(8,128)(2,1)S(1)}, bf16[2,32,1152]{2,1,0:T(8,128)(2,1)S(1)}, u32[]{:S(2)}, u32[]{:S(2)}) collective-permute-start(bf16[2,32,1152]{2,1,0:T(8,128)(2,1)S(1)} %get-tuple-element.205.refs_0_), channel_id=1, source_target_pairs={{0,4},{1,5},{2,6},{3,7},{4,0},{5,1},{6,2},{7,3},{8,12},{9,13},{10,... | collective-permute-start | bytes 442376 | tf_op jit(solution)/shard_map/ppermute | solution.py:711
  162.3 7.7 %collective-permute-start.30 = (bf16[2,32,1152]{2,1,0:T(8,128)(2,1)S(1)}, bf16[2,32,1152]{2,1,0:T(8,128)(2,1)S(1)}, u32[]{:S(2)}, u32[]{:S(2)}) collective-permute-start(bf16[2,32,1152]{2,1,0:T(8,128)(2,1)S(1)} %get-tuple-element.212), channel_id=1, source_target_pairs={{0,5},{1,4},{2,7},{3,6},{4,1},{5,0},{6,3},{7,2},{8,13},{9,12},{10,... | collective-permute-start | bytes 442376 | tf_op jit(solution)/shard_map/ppermute | solution.py:711
  196.3 8.6 %collective-permute-start.42 = (bf16[2,32,1152]{2,1,0:T(8,128)(2,1)S(1)}, bf16[2,32,1152]{2,1,0:T(8,128)(2,1)S(1)}, u32[]{:S(2)}, u32[]{:S(2)}) collective-permute-start(bf16[2,32,1152]{2,1,0:T(8,128)(2,1)S(1)} %get-tuple-element.224), channel_id=1, source_target_pairs={{0,1},{1,0},{2,3},{3,2},{4,5},{5,4},{6,7},{7,6},{8,9},{9,8},{10,11... | collective-permute-start | bytes 442376 | tf_op jit(solution)/shard_map/ppermute | solution.py:711
  205.9 7.7 %collective-permute-start.46 = (bf16[2,32,1152]{2,1,0:T(8,128)(2,1)S(1)}, bf16[2,32,1152]{2,1,0:T(8,128)(2,1)S(1)}, u32[]{:S(2)}, u32[]{:S(2)}) collective-permute-start(bf16[2,32,1152]{2,1,0:T(8,128)(2,1)S(1)} %get-tuple-element.227.refs_0_), channel_id=1, source_target_pairs={{0,5},{1,4},{2,7},{3,6},{4,1},{5,0},{6,3},{7,2},{8,13},{9,12},{10,... | collective-permute-start | bytes 442376 | tf_op jit(solution)/shard_map/ppermute | solution.py:711
  207.4 8.0 %collective-permute-start.45 = (bf16[2,32,1152]{2,1,0:T(8,128)(2,1)S(1)}, bf16[2,32,1152]{2,1,0:T(8,128)(2,1)S(1)}, u32[]{:S(2)}, u32[]{:S(2)}) collective-permute-start(bf16[2,32,1152]{2,1,0:T(8,128)(2,1)S(1)} %get-tuple-element.227.refs_0_), channel_id=1, source_target_pairs={{0,4},{1,5},{2,6},{3,7},{4,0},{5,1},{6,2},{7,3},{8,12},{9,13},{10,... | collective-permute-start | bytes 442376 | tf_op jit(solution)/shard_map/ppermute | solution.py:711
  229.1 137.8 %reduce-scatter.7.cloned.1.call-start = ((), (), s32[]{:S(2)}) async-start(), calls=%async_computation.15 | async-start | bytes 2211840 | tf_op jit(solution)/shard_map/reduce_scatter | solution.py:736
  231.8 7.7 %collective-permute-start.52 = (bf16[2,32,1152]{2,1,0:T(8,128)(2,1)S(1)}, bf16[2,32,1152]{2,1,0:T(8,128)(2,1)S(1)}, u32[]{:S(2)}, u32[]{:S(2)}) collective-permute-start(bf16[2,32,1152]{2,1,0:T(8,128)(2,1)S(1)} %get-tuple-element.236), channel_id=1, source_target_pairs={{0,5},{1,4},{2,7},{3,6},{4,1},{5,0},{6,3},{7,2},{8,13},{9,12},{10,... | collective-permute-start | bytes 442376 | tf_op jit(solution)/shard_map/ppermute | solution.py:711
  233.5 8.7 %collective-permute-start.53 = (bf16[2,32,1152]{2,1,0:T(8,128)(2,1)S(1)}, bf16[2,32,1152]{2,1,0:T(8,128)(2,1)S(1)}, u32[]{:S(2)}, u32[]{:S(2)}) collective-permute-start(bf16[2,32,1152]{2,1,0:T(8,128)(2,1)S(1)} %get-tuple-element.237), channel_id=1, source_target_pairs={{0,1},{1,0},{2,3},{3,2},{4,5},{5,4},{6,7},{7,6},{8,9},{9,8},{10,11... | collective-permute-start | bytes 442376 | tf_op jit(solution)/shard_map/ppermute | solution.py:711
  244.8 8.0 %collective-permute-start.56 = (bf16[2,32,1152]{2,1,0:T(8,128)(2,1)S(1)}, bf16[2,32,1152]{2,1,0:T(8,128)(2,1)S(1)}, u32[]{:S(2)}, u32[]{:S(2)}) collective-permute-start(bf16[2,32,1152]{2,1,0:T(8,128)(2,1)S(1)} %get-tuple-element.241.refs_1_), channel_id=1, source_target_pairs={{0,4},{1,5},{2,6},{3,7},{4,0},{5,1},{6,2},{7,3},{8,12},{9,13},{10,... | collective-permute-start | bytes 442376 | tf_op jit(solution)/shard_map/ppermute | solution.py:711
  265.1 7.7 %collective-permute-start.63 = (bf16[2,32,1152]{2,1,0:T(8,128)(2,1)S(1)}, bf16[2,32,1152]{2,1,0:T(8,128)(2,1)S(1)}, u32[]{:S(2)}, u32[]{:S(2)}) collective-permute-start(bf16[2,32,1152]{2,1,0:T(8,128)(2,1)S(1)} %get-tuple-element.251), channel_id=1, source_target_pairs={{0,5},{1,4},{2,7},{3,6},{4,1},{5,0},{6,3},{7,2},{8,13},{9,12},{10,... | collective-permute-start | bytes 442376 | tf_op jit(solution)/shard_map/ppermute | solution.py:711
  266.8 8.7 %collective-permute-start.64 = (bf16[2,32,1152]{2,1,0:T(8,128)(2,1)S(1)}, bf16[2,32,1152]{2,1,0:T(8,128)(2,1)S(1)}, u32[]{:S(2)}, u32[]{:S(2)}) collective-permute-start(bf16[2,32,1152]{2,1,0:T(8,128)(2,1)S(1)} %get-tuple-element.252), channel_id=1, source_target_pairs={{0,1},{1,0},{2,3},{3,2},{4,5},{5,4},{6,7},{7,6},{8,9},{9,8},{10,11... | collective-permute-start | bytes 442376 | tf_op jit(solution)/shard_map/ppermute | solution.py:711
  279.6 98.1 %reduce-scatter.9.cloned.1.call-start = ((), (), s32[]{:S(2)}) async-start(), calls=%async_computation.16 | async-start | bytes 3317760 | tf_op jit(solution)/shard_map/reduce_scatter | solution.py:736
  283.2 8.0 %collective-permute-start.67 = (bf16[2,32,1152]{2,1,0:T(8,128)(2,1)S(1)}, bf16[2,32,1152]{2,1,0:T(8,128)(2,1)S(1)}, u32[]{:S(2)}, u32[]{:S(2)}) collective-permute-start(bf16[2,32,1152]{2,1,0:T(8,128)(2,1)S(1)} %get-tuple-element.258.refs_0_), channel_id=1, source_target_pairs={{0,4},{1,5},{2,6},{3,7},{4,0},{5,1},{6,2},{7,3},{8,12},{9,13},{10,... | collective-permute-start | bytes 442376 | tf_op jit(solution)/shard_map/ppermute | solution.py:711
  301.3 7.7 %collective-permute-start.74 = (bf16[2,32,1152]{2,1,0:T(8,128)(2,1)S(1)}, bf16[2,32,1152]{2,1,0:T(8,128)(2,1)S(1)}, u32[]{:S(2)}, u32[]{:S(2)}) collective-permute-start(bf16[2,32,1152]{2,1,0:T(8,128)(2,1)S(1)} %get-tuple-element.270), channel_id=1, source_target_pairs={{0,5},{1,4},{2,7},{3,6},{4,1},{5,0},{6,3},{7,2},{8,13},{9,12},{10,... | collective-permute-start | bytes 442376 | tf_op jit(solution)/shard_map/ppermute | solution.py:711
  302.9 8.7 %collective-permute-start.75 = (bf16[2,32,1152]{2,1,0:T(8,128)(2,1)S(1)}, bf16[2,32,1152]{2,1,0:T(8,128)(2,1)S(1)}, u32[]{:S(2)}, u32[]{:S(2)}) collective-permute-start(bf16[2,32,1152]{2,1,0:T(8,128)(2,1)S(1)} %get-tuple-element.271), channel_id=1, source_target_pairs={{0,1},{1,0},{2,3},{3,2},{4,5},{5,4},{6,7},{7,6},{8,9},{9,8},{10,11... | collective-permute-start | bytes 442376 | tf_op jit(solution)/shard_map/ppermute | solution.py:711
  316.8 105.1 %reduce-scatter.11.cloned.1.call-start = ((), (), s32[]{:S(2)}) async-start(), calls=%async_computation.17 | async-start | bytes 2211840 | tf_op jit(solution)/shard_map/reduce_scatter | solution.py:736
  320.3 8.0 %collective-permute-start.78 = (bf16[2,32,1152]{2,1,0:T(8,128)(2,1)S(1)}, bf16[2,32,1152]{2,1,0:T(8,128)(2,1)S(1)}, u32[]{:S(2)}, u32[]{:S(2)}) collective-permute-start(bf16[2,32,1152]{2,1,0:T(8,128)(2,1)S(1)} %get-tuple-element.276.refs_1_), channel_id=1, source_target_pairs={{0,4},{1,5},{2,6},{3,7},{4,0},{5,1},{6,2},{7,3},{8,12},{9,13},{10,... | collective-permute-start | bytes 442376 | tf_op jit(solution)/shard_map/ppermute | solution.py:711
  345.8 9.6 %collective-permute-start.85 = (bf16[2,32,1152]{2,1,0:T(8,128)(2,1)S(1)}, bf16[2,32,1152]{2,1,0:T(8,128)(2,1)S(1)}, u32[]{:S(2)}, u32[]{:S(2)}) collective-permute-start(bf16[2,32,1152]{2,1,0:T(8,128)(2,1)S(1)} %get-tuple-element.290), channel_id=1, source_target_pairs={{0,5},{1,4},{2,7},{3,6},{4,1},{5,0},{6,3},{7,2},{8,13},{9,12},{10,... | collective-permute-start | bytes 442376 | tf_op jit(solution)/shard_map/ppermute | solution.py:711
  347.8 8.6 %collective-permute-start.86 = (bf16[2,32,1152]{2,1,0:T(8,128)(2,1)S(1)}, bf16[2,32,1152]{2,1,0:T(8,128)(2,1)S(1)}, u32[]{:S(2)}, u32[]{:S(2)}) collective-permute-start(bf16[2,32,1152]{2,1,0:T(8,128)(2,1)S(1)} %get-tuple-element.291), channel_id=1, source_target_pairs={{0,1},{1,0},{2,3},{3,2},{4,5},{5,4},{6,7},{7,6},{8,9},{9,8},{10,11... | collective-permute-start | bytes 442376 | tf_op jit(solution)/shard_map/ppermute | solution.py:711
  367.8 9.7 %all-to-all-start.4 = ((f32[4,1,9856]{2,1,0:T(1,128)}), f32[4,1,9856]{2,1,0:T(1,128)S(1)}, u32[]{:S(2)}, u32[]{:S(2)}) async-start(f32[4,1,9856]{2,1,0:T(1,128)} %broadcast_in_dim.100), calls=%async_computation.6 | async-start | bytes 315392 | tf_op jit(solution)/shard_map/all_to_all | solution.py:728
  371.2 23.6 %collective-permute-start.89 = (bf16[288,768]{1,0:T(8,128)(2,1)}, bf16[288,768]{1,0:T(8,128)(2,1)}, u32[]{:S(2)}, u32[]{:S(2)}) collective-permute-start(bf16[288,768]{1,0:T(8,128)(2,1)} %reduce-scatter.7.cloned.1.call-done.refs_3_), channel_id=1, source_target_pairs={{0,1},{2,3},{4,5},{6,7},{8,9},{10,11},{12,13},{14,15},{16,17},{18,... | collective-permute-start | bytes 1327112 | tf_op jit(solution)/shard_map/ppermute | solution.py:1045
  375.1 24.2 %collective-permute-start.88 = (bf16[288,1152]{1,0:T(8,128)(2,1)S(1)}, bf16[288,1152]{1,0:T(8,128)(2,1)S(1)}, u32[]{:S(2)}, u32[]{:S(2)}) collective-permute-start(bf16[288,1152]{1,0:T(8,128)(2,1)S(1)} %copy-done.1), channel_id=1, source_target_pairs={{0,1},{2,3},{4,5},{6,7},{8,9},{10,11},{12,13},{14,15},{16,17},{18,... | collective-permute-start | bytes 1990664 | tf_op jit(solution)/shard_map/ppermute | solution.py:1045
  378.3 22.3 %collective-permute-start.90 = (bf16[288,1152]{1,0:T(8,128)(2,1)}, bf16[288,1152]{1,0:T(8,128)(2,1)S(1)}, u32[]{:S(2)}, u32[]{:S(2)}) collective-permute-start(bf16[288,1152]{1,0:T(8,128)(2,1)} %reduce-scatter.9.cloned.1.call-done.refs_1_), channel_id=1, source_target_pairs={{1,0},{3,2},{5,4},{7,6},{9,8},{11,10},{13,12},{15,14},{17,16},{19,... | collective-permute-start | bytes 1990664 | tf_op jit(solution)/shard_map/ppermute | solution.py:1048
  381.8 18.8 %all-to-all-start.5 = ((f32[4,2,288]{2,1,0:T(2,128)}), f32[4,2,288]{2,1,0:T(2,128)S(1)}, u32[]{:S(2)}, u32[]{:S(2)}) async-start(f32[4,2,288]{2,1,0:T(2,128)} %fusion), calls=%async_computation.8 | async-start | bytes 24576 | tf_op jit(solution)/shard_map/all_to_all | solution.py:1154
  391.9 19.9 %collective-permute-start.92 = (bf16[2,32,1152]{2,1,0:T(8,128)(2,1)}, bf16[2,32,1152]{2,1,0:T(8,128)(2,1)}, u32[]{:S(2)}, u32[]{:S(2)}) collective-permute-start(bf16[2,32,1152]{2,1,0:T(8,128)(2,1)} %get-tuple-element.324), channel_id=1, source_target_pairs={{0,5},{1,4},{2,7},{3,6},{4,1},{5,0},{6,3},{7,2},{8,13},{9,12},{10,... | collective-permute-start | bytes 442376 | tf_op jit(solution)/shard_map/ppermute | solution.py:711
  394.8 17.0 %collective-permute-start.93 = (bf16[2,32,1152]{2,1,0:T(8,128)(2,1)}, bf16[2,32,1152]{2,1,0:T(8,128)(2,1)}, u32[]{:S(2)}, u32[]{:S(2)}) collective-permute-start(bf16[2,32,1152]{2,1,0:T(8,128)(2,1)} %get-tuple-element.325), channel_id=1, source_target_pairs={{0,1},{1,0},{2,3},{3,2},{4,5},{5,4},{6,7},{7,6},{8,9},{9,8},{10,11... | collective-permute-start | bytes 442376 | tf_op jit(solution)/shard_map/ppermute | solution.py:711
  394.8 17.0 %collective-permute-start.94 = (bf16[2,32,1152]{2,1,0:T(8,128)(2,1)}, bf16[2,32,1152]{2,1,0:T(8,128)(2,1)}, u32[]{:S(2)}, u32[]{:S(2)}) collective-permute-start(bf16[2,32,1152]{2,1,0:T(8,128)(2,1)} %get-tuple-element.326), channel_id=1, source_target_pairs={{0,4},{1,5},{2,6},{3,7},{4,0},{5,1},{6,2},{7,3},{8,12},{9,13},{10,... | collective-permute-start | bytes 442376 | tf_op jit(solution)/shard_map/ppermute | solution.py:711
  399.3 18.1 %collective-permute-start.95 = (bf16[2,32,1152]{2,1,0:T(8,128)(2,1)}, bf16[2,32,1152]{2,1,0:T(8,128)(2,1)}, u32[]{:S(2)}, u32[]{:S(2)}) collective-permute-start(bf16[2,32,1152]{2,1,0:T(8,128)(2,1)} %copy-done.22), channel_id=1, source_target_pairs={{1,0},{3,2},{5,4},{7,6},{9,8},{11,10},{13,12},{15,14},{17,16},{19,... | collective-permute-start | bytes 442376 | tf_op jit(solution)/shard_map/ppermute | solution.py:1164
  402.1 9.5 %all-to-all-start.6 = ((f32[8,4,2,288]{3,2,1,0:T(2,128)}), f32[8,4,2,288]{3,2,1,0:T(2,128)S(1)}, u32[]{:S(2)}, u32[]{:S(2)}) async-start(f32[8,4,2,288]{3,2,1,0:T(2,128)} %broadcast_in_dim.101), calls=%async_computation.9 | async-start | bytes 196608 | tf_op jit(solution)/shard_map/all_to_all | solution.py:728
  421.8 13.5 %collective-permute-start.97 = (bf16[288,768]{1,0:T(8,128)(2,1)}, bf16[288,768]{1,0:T(8,128)(2,1)}, u32[]{:S(2)}, u32[]{:S(2)}) collective-permute-start(bf16[288,768]{1,0:T(8,128)(2,1)} %reduce-scatter.11.cloned.1.call-done.refs_1_), channel_id=1, source_target_pairs={{1,0},{3,2},{5,4},{7,6},{9,8},{11,10},{13,12},{15,14},{17,16},{19,... | collective-permute-start | bytes 1327112 | tf_op jit(solution)/shard_map/ppermute | solution.py:1048
  (116 other events, 644.4 us)
Sparse Core Ops, SparseCore 0:
  27.3 40.5 all-gather.3
  70.1 83.5 all-gather.5
  155.2 53.8 all-gather.7
  229.2 50.3 reduce-scatter.4
  282.4 38.0 reduce-scatter.6
  322.8 51.7 reduce-scatter.8
  377.5 38.4 reduce-scatter.10

commit v4 on v3

--- a/solution.py
+++ b/solution.py
@@ -160,6 +160,11 @@
 def add_kernel(a, b, c, d, recv, *outs):
     for j, own in enumerate((a, b, c, d)):
         outs[j][...] = (own[...].astype(F32) + recv[j].astype(F32)).astype(BF16)
+
+
+def add_late_kernel(traffic, a, b, c, d, recv, *outs):
+    traffic.wait(0, 1, 2, 3)
+    add_kernel(a, b, c, d, recv, *outs)
 
 
 def after_attn_kernel(traffic, p0, p1, p2, p3, x_ref, mod_ref, att_ref, aft_ref, n_ref):
@@ -716,9 +721,15 @@
     return own, x, y, xy, *(swap(v, 1, 0) for v in (own, x, y, xy))
 
 
-def scatter_plane(other, own):
+def scatter_plane(other, own, late=False):
     received = swap(other, 1, 0)
-    sums = call(add_kernel, (out(own[0].shape, BF16),) * 4, *own, received)
+    sums = call(
+        add_late_kernel if late else add_kernel,
+        (out(own[0].shape, BF16),) * 4,
+        *own,
+        received,
+        streamed=(0, 1, 2, 3) if late else (),
+    )
     return (sums[0], swap(sums[3], 2, 1), swap(sums[1], 0, 1), swap(sums[2], 2, 0))
 
 
@@ -1145,18 +1156,28 @@
     g_all, end_pieces, sum_b0 = lax.optimization_barrier((g_all, end_pieces, sum_b0))
     others = other_b1, other_a1, to_first(sum_b0)
     (block_out,) = call(
-        end_kernel, (shard,), *scatter_plane(end_pieces[0], end_pieces[1:]), aft1, mods[1]
+        end_kernel, (shard,), *scatter_plane(end_pieces[0], end_pieces[1:], True), aft1, mods[1]
     )
     small_own = jnp.sum(g_all[:, images * columns :], axis=0).reshape(sections, -1)
     g_all = g_all[:, : images * columns].reshape(dps * images, columns).astype(BF16)
     grad_ada_bias = jnp.sum(g_all.astype(F32), axis=0)
     act_part = jnp.einsum("me,de->md", g_all, ada_weight[0], preferred_element_type=F32)
+    act_part, other_b1 = lax.optimization_barrier((act_part, others[0]))
+    others = other_b1, *others[1:]
+    plane = sections * tensors
+    act_sent = jnp.broadcast_to(
+        act_part.reshape(dps, 1, images, slab), (dps, plane, images, slab)
+    )
     act_all = lax.all_to_all(
-        act_part.reshape(dps, images, slab), "dp", split_axis=0, concat_axis=0, tiled=True
-    )
-    act_all, others = lax.optimization_barrier((act_all, others))
-    act_all = spread_over(act_all, ("section", "tensor"))
-    act_all = jnp.sum(act_all, axis=0)
+        act_sent.reshape(-1, images, slab),
+        ("dp", "section", "tensor"),
+        split_axis=0,
+        concat_axis=0,
+        tiled=True,
+    )
+    act_all, other_b0 = lax.optimization_barrier((act_all, others[2]))
+    others = *others[:2], other_b0
+    act_all = jnp.sum(act_all.reshape(dps, plane, images, slab), axis=1)
     act_grad = act_all.reshape(dps, images, slab).transpose(1, 0, 2).reshape(images, width)
     cond_grad = jax.vjp(jax.nn.silu, cond_vec)[1](act_grad)[0]
 

time: 452 us -> 448 us (level)
  waiting for transfers between devices: 180 us -> 187 us
  starting transfers between devices: 101 us -> 94.5 us
  local copies, waits for them, and re-layouts: 32.6 us -> 27.6 us
    unnamed x116 -> x104, local copies, waits for them, and re-layouts: 23.2 us -> 18.3 us
    all_to_all x2 -> x1, starting transfers between devices: 7.92 us -> 3.34 us  [spread_over(): return lax.all_to_all(copies, axes, split_axis=0, concat_axis=0, tiled=True)]
  transfers between devices with their start and end apart: 110 -> 109, of which waited for: 63 -> 64; matrix products, arithmetic and copies ran while one was open for 5% -> 5% of each run, Pallas kernels for 17% -> 17%
where the time goes in v4:
time: 448 us; the launch traced here: 443 us
  waiting for transfers between devices  187 us (42%)
  starting transfers between devices  94.5 us (21%)
  Pallas kernels  89.6 us (20%)
  local copies, waits for them, and re-layouts  27.6 us (6%)
  blocking collectives  16.8 us (4%)
  between operations  15.5 us (3%)
  other arithmetic  9.12 us (2%)
    ppermute x88, waiting for transfers between devices, swap(): return lax.ppermute(value, PLANE, route)  111 us
    pallas_call x33, Pallas kernels, call(): pl.pallas_call(kernel, out_shape=tuple(shapes), in_specs=specs, out_specs...  89.6 us
    ppermute x88, starting transfers between devices, swap(): return lax.ppermute(value, PLANE, route)  60.8 us
    all_gather x3, waiting for transfers between devices, gather_all(): return lax.all_gather(own, 'dp', axis=0, tiled=True)  36.9 us
    unnamed x104, local copies, waits for them, and re-layouts  18.3 us
    ppermute x2, waiting for transfers between devices, to_first(): return lax.ppermute(value, 'section', [(1, 0)])  10.1 us
  transfers between devices with their start and end apart: 109, of which 64 were waited for; matrix products, arithmetic and copies ran while one was open for 5% of the time, Pallas kernels for 17%

profile of v4, /device:TPU:0, one launch (start us, length us, event | category | flops | bytes accessed | tf_op | source)
XLA Modules:
  0.0 442.7 jit_solution(2989350555937523247)
XLA Ops:
  11.3 3.0 collective-permute-start.2
  15.9 4.9 %all-to-all-start = ((bf16[4,2,288]{2,1,0:T(2,128)(2,1)}), bf16[4,2,288]{2,1,0:T(2,128)(2,1)S(1)}, u32[]{:S(2)}, u32[]{:S(2)}) async-start(bf16[4,2,288]{2,1,0:T(2,128)(2,1)} %bitcast.68), calls=%async_computation | async-start | bytes 12288 | tf_op jit(solution)/shard_map/all_to_all | solution.py:876
  20.8 5.6 %all-to-all-done = bf16[4,2,288]{2,1,0:T(2,128)(2,1)S(1)} async-done(((bf16[4,2,288]{2,1,0:T(2,128)(2,1)}), bf16[4,2,288]{2,1,0:T(2,128)(2,1)S(1)}, u32[]{:S(2)}, u32[]{:S(2)}) %all-to-all-start) | async-done | bytes 4640 | tf_op jit(solution)/shard_map/all_to_all | solution.py:876
  30.1 4.2 all-to-all-start.1
  34.3 6.8 %all-to-all-done.1 = f32[4,2,1728]{2,1,0:T(2,128)S(1)} async-done(((f32[4,2,1728]{2,1,0:T(2,128)}), f32[4,2,1728]{2,1,0:T(2,128)S(1)}, u32[]{:S(2)}, u32[]{:S(2)}) %all-to-all-start.1) | async-done | bytes 55328 | tf_op jit(solution)/shard_map/all_to_all | solution.py:880
  41.2 8.1 %all_to_all.41 = f32[8,2,1728]{2,1,0:T(2,128)} all-to-all(f32[8,2,1728]{2,1,0:T(2,128)S(1)} %broadcast_in_dim.90), channel_id=1, replica_groups=mesh['dp'=4,'tensor'=4,'section'=2] {'section','tensor'}, dimensions={0} | all-to-all | bytes 221184 | tf_op jit(solution)/shard_map/all_to_all | solution.py:739
  53.8 4.6 %collective-permute-done = bf16[2,32,1152]{2,1,0:T(8,128)(2,1)S(1)} collective-permute-done((bf16[2,32,1152]{2,1,0:T(8,128)(2,1)S(1)}, bf16[2,32,1152]{2,1,0:T(8,128)(2,1)S(1)}, u32[]{:S(2)}, u32[]{:S(2)}) %collective-permute-start) | collective-permute-done | bytes 147488 | tf_op jit(solution)/shard_map/ppermute | solution.py:848
  62.2 2.8 collective-permute-done.12.refs_3_
  72.5 3.3 collective-permute-done.5.refs_4_
  75.8 2.7 collective-permute-done.4.refs_3_
  83.9 8.2 %shard_map.224 = (bf16[2,256,1152]{2,1,0:T(8,128)(2,1)}, bf16[2,256,1024]{2,1,0:T(8,128)(2,1)}, f32[2,256,128]{2,1,0:T(8,128)}, f32[2,256,256]{2,1,0:T(8,128)}, ...) custom-call(s32[1]{0:T(128)} %bitcast.refs_0_, ...), custom_call_target="tpu_custom_call" | custom-call | flops 2315255808 | bytes 7422468 | tf_op jit(solution)/shard_map/pallas_call | solution.py:97
  97.9 4.1 collective-permute-done.19.refs_1_
  108.9 4.2 collective-permute-done.24.refs_3_
  116.7 36.9 %all-gather.6.cloned.1.call-done.refs_8_.refs_9_.refs_12_ = bf16[1152,1920]{1,0:T(8,128)(2,1)} async-done(((bf16[288,1920]{1,0:T(8,128)(2,1)}), bf16[1152,1920]{1,0:T(8,128)(2,1)}) %all-gather.6.cloned.1.call-update) | async-done | bytes 4423696 | tf_op jit(solution)/shard_map/all_gather | solution.py:743
  153.6 6.4 %shard_map.227 = (bf16[512,1152]{1,0:T(8,128)(2,1)}, f32[512,640]{1,0:T(8,128)}, bf16[512,640]{1,0:T(8,128)(2,1)}, bf16[4,2,32,1152]{3,2,1,0:T(8,128)(2,1)S(1)},...) custom-call(bf16[2,32,1152]{2,1,0:T(8,128)(2,1)S(1)} %get-tuple-elem, ...), custom_call_target="tpu_custom_call" | custom-call | flops 1358954496 | bytes 8161792 | tf_op jit(solution)/shard_map/pallas_call | solution.py:97
  166.0 4.0 collective-permute-done.30.refs_1_
  176.9 3.4 collective-permute-done.35.refs_4_
  180.3 2.7 collective-permute-done.34.refs_3_
  184.6 7.7 %shard_map.230 = (bf16[2,256,1152]{2,1,0:T(8,128)(2,1)}, bf16[2,256,1024]{2,1,0:T(8,128)(2,1)}, f32[2,256,128]{2,1,0:T(8,128)}, f32[2,256,256]{2,1,0:T(8,128)}, ...) custom-call(s32[1]{0:T(128)} %bitcast.refs_0_, ...), custom_call_target="tpu_custom_call" | custom-call | flops 2315255808 | bytes 7422468 | tf_op jit(solution)/shard_map/pallas_call | solution.py:97
  198.1 4.1 collective-permute-done.41.refs_1_
  202.2 2.7 collective-permute-done.42.refs_2_
  209.4 4.1 collective-permute-done.46.refs_3_
  218.4 9.3 %shard_map.234 = (bf16[1152,1152]{1,0:T(8,128)(2,1)}, f32[1,640]{1,0:T(1,128)S(1)}, f32[2,1,1152]{2,1,0:T(1,128)S(1)}, bf16[4,2,32,1152]{3,2,1,0:T(8,128)(2,1)S(...) custom-call(bf16[512,1152]{1,0:T(8,128)(2,1)} %shard_map.233.refs_0_, ...), custom_call_target="tpu_custom_call" | custom-call | flops 4076863488 | bytes 10096640 | tf_op jit(solution)/shard_map/pallas_call | solution.py:97
  235.3 4.1 collective-permute-done.52.refs_1_
  239.4 2.7 collective-permute-done.53.refs_2_
  246.9 4.0 collective-permute-done.57.refs_4_
  254.7 8.2 %shard_map.237 = (bf16[2,256,1152]{2,1,0:T(8,128)(2,1)S(1)}, bf16[2,256,640]{2,1,0:T(8,128)(2,1)S(1)}, f32[16,256]{1,0:T(8,128)S(1)}, bf16[4,2,32,1152]{3,2,1,0:...) custom-call(s32[1]{0:T(128)} %bitcast.refs_0_, ...), custom_call_target="tpu_custom_call" | custom-call | flops 4630511616 | bytes 7831556 | tf_op jit(solution)/shard_map/pallas_call | solution.py:97
  268.7 4.1 collective-permute-done.63.refs_1_.refs_5_
  272.8 2.7 collective-permute-done.64.refs_2_.refs_6_
  275.5 4.0 shard_map.240.refs_10_
  285.3 3.9 collective-permute-done.68.refs_3_
  293.1 6.0 %shard_map.241 = (bf16[512,1152]{1,0:T(8,128)(2,1)S(1)}, bf16[512,640]{1,0:T(8,128)(2,1)S(1)}, f32[1,640]{1,0:T(1,128)S(1)}, bf16[4,2,32,1152]{3,2,1,0:T(8,128)(...) custom-call(bf16[2,32,1152]{2,1,0:T(8,128)(2,1)S(1)} %get-tuple-elem, ...), custom_call_target="tpu_custom_call" | custom-call | flops 1358954496 | bytes 8161792 | tf_op jit(solution)/shard_map/pallas_call | solution.py:97
  304.8 4.1 collective-permute-done.74.refs_1_.refs_5_
  308.9 2.7 collective-permute-done.75.refs_2_.refs_6_
  311.6 5.0 %shard_map.244.refs_14_ = bf16[1152,1152]{1,0:T(8,128)(2,1)} custom-call(bf16[512,1152]{1,0:T(8,128)(2,1)} %get-tuple-element.280.refs_0_, bf16[512,640]{1,0:T(8,128)(2,1)S(1)} %get-tuple-element.281.refs_1_, bf16[512,1152]{1,0:T(8,128)(2,1)S(1)} %get-tuple-element.282.refs_2_, bf16[512,640]{1,0:T(8,128)(2,1)} %get-tuple-element.283.refs_3_, ...), custom_call_target="tpu_custom_call" | custom-call | flops 1358954496 | bytes 6324224 | tf_op jit(solution)/shard_map/pallas_call | solution.py:97
  322.4 4.0 collective-permute-done.79.refs_4_
  332.8 8.8 %shard_map.245 = (bf16[2,256,1152]{2,1,0:T(8,128)(2,1)S(1)}, bf16[2,256,640]{2,1,0:T(8,128)(2,1)S(1)}, f32[16,256]{1,0:T(8,128)S(1)}, bf16[4,2,32,1152]{3,2,1,0:...) custom-call(s32[1]{0:T(128)} %bitcast.refs_0_, ...), custom_call_target="tpu_custom_call" | custom-call | flops 4630511616 | bytes 7831556 | tf_op jit(solution)/shard_map/pallas_call | solution.py:97
  351.4 4.0 shard_map.247.refs_9_
  358.1 8.7 %all_to_all.42 = f32[8,1,6656]{2,1,0:T(1,128)S(1)} all-to-all(f32[8,1,6656]{2,1,0:T(1,128)S(1)} %copy.101), channel_id=1, replica_groups=mesh['dp'=4,'tensor'=4,'section'=2] {'section','tensor'}, dimensions={0} | all-to-all | bytes 425984 | tf_op jit(solution)/shard_map/all_to_all | solution.py:1148
  367.0 3.2 collective-permute-start.88
  371.0 3.3 all-to-all-start.4
  375.7 5.0 %all-to-all-done.4 = f32[4,1,9856]{2,1,0:T(1,128)S(1)} async-done(((f32[4,1,9856]{2,1,0:T(1,128)}), f32[4,1,9856]{2,1,0:T(1,128)S(1)}, u32[]{:S(2)}, u32[]{:S(2)}) %all-to-all-start.4) | async-done | bytes 157728 | tf_op jit(solution)/shard_map/all_to_all | solution.py:739
  385.1 3.3 all-to-all-start.5
  388.6 3.0 shard_map.249
  397.2 4.5 %collective-permute-done.89.refs_2_ = bf16[288,1152]{1,0:T(8,128)(2,1)S(1)} collective-permute-done((bf16[288,1152]{1,0:T(8,128)(2,1)}, bf16[288,1152]{1,0:T(8,128)(2,1)S(1)}, u32[]{:S(2)}, u32[]{:S(2)}) %collective-permute-start.89) | collective-permute-done | bytes 663584 | tf_op jit(solution)/shard_map/ppermute | solution.py:1059
  412.3 4.1 collective-permute-done.95
  425.5 5.6 %collective-permute-done.97.refs_2_ = bf16[288,768]{1,0:T(8,128)(2,1)} collective-permute-done((bf16[288,768]{1,0:T(8,128)(2,1)}, bf16[288,768]{1,0:T(8,128)(2,1)}, u32[]{:S(2)}, u32[]{:S(2)}) %collective-permute-start.97) | collective-permute-done | bytes 442400 | tf_op jit(solution)/shard_map/ppermute | solution.py:1059
  431.2 2.8 shard_map.251
  (425 shorter events, 171.6 us)
Async XLA Ops:
  11.3 15.1 %collective-permute-start.2 = (bf16[288,768]{1,0:T(8,128)(2,1)S(1)}, bf16[288,768]{1,0:T(8,128)(2,1)S(1)}, u32[]{:S(2)}, u32[]{:S(2)}) collective-permute-start(bf16[288,768]{1,0:T(8,128)(2,1)S(1)} %get-tuple-element.181), channel_id=1, source_target_pairs={{0,1},{1,0},{2,3},{3,2},{4,5},{5,4},{6,7},{7,6},{8,9},{9,8},{10,11... | collective-permute-start | bytes 1327112 | tf_op jit(solution)/shard_map/ppermute | solution.py:822
  15.9 10.5 %all-to-all-start = ((bf16[4,2,288]{2,1,0:T(2,128)(2,1)}), bf16[4,2,288]{2,1,0:T(2,128)(2,1)S(1)}, u32[]{:S(2)}, u32[]{:S(2)}) async-start(bf16[4,2,288]{2,1,0:T(2,128)(2,1)} %bitcast.68), calls=%async_computation | async-start | bytes 12288 | tf_op jit(solution)/shard_map/all_to_all | solution.py:876
  20.8 62.3 %all-gather.4.cloned.1.call-start = ((), (), s32[]{:S(2)}) async-start(), calls=%async_computation.10 | async-start | bytes 2211840 | tf_op jit(solution)/shard_map/all_gather | solution.py:743
  28.6 20.7 %collective-permute-start.1 = (bf16[288,1152]{1,0:T(8,128)(2,1)S(1)}, bf16[288,1152]{1,0:T(8,128)(2,1)}, u32[]{:S(2)}, u32[]{:S(2)}) collective-permute-start(bf16[288,1152]{1,0:T(8,128)(2,1)S(1)} %get-tuple-element.179), channel_id=1, source_target_pairs={{0,1},{1,0},{2,3},{3,2},{4,5},{5,4},{6,7},{7,6},{8,9},{9,8},{10,11... | collective-permute-start | bytes 1990664 | tf_op jit(solution)/shard_map/ppermute | solution.py:832
  30.1 11.0 %all-to-all-start.1 = ((f32[4,2,1728]{2,1,0:T(2,128)}), f32[4,2,1728]{2,1,0:T(2,128)S(1)}, u32[]{:S(2)}, u32[]{:S(2)}) async-start(f32[4,2,1728]{2,1,0:T(2,128)} %fusion), calls=%async_computation.1 | async-start | bytes 114688 | tf_op jit(solution)/shard_map/all_to_all | solution.py:880
  34.3 119.4 %all-gather.6.cloned.1.call-start = ((), (), s32[]{:S(2)}) async-start(), calls=%async_computation.11 | async-start | bytes 5529600 | tf_op jit(solution)/shard_map/all_gather | solution.py:743
  52.5 165.9 %all-gather.8.cloned.1.call-start = ((), (), s32[]{:S(2)}) async-start(), calls=%async_computation.12 | async-start | bytes 3317760 | tf_op jit(solution)/shard_map/all_gather | solution.py:743
  59.3 7.8 %collective-permute-start.11 = (bf16[2,32,1152]{2,1,0:T(8,128)(2,1)S(1)}, bf16[2,32,1152]{2,1,0:T(8,128)(2,1)S(1)}, u32[]{:S(2)}, u32[]{:S(2)}) collective-permute-start(bf16[2,32,1152]{2,1,0:T(8,128)(2,1)S(1)} %get-tuple-element.432.refs_0_.refs_4_), channel_id=1, source_target_pairs={{0,4},{1,5},{2,6},{3,7},{4,0},{5,1},{6,2},{7,3},{8,12},{9,13},{10,... | collective-permute-start | bytes 442376 | tf_op jit(solution)/shard_map/ppermute | solution.py:716
  60.9 8.5 %collective-permute-start.13 = (bf16[2,32,1152]{2,1,0:T(8,128)(2,1)S(1)}, bf16[2,32,1152]{2,1,0:T(8,128)(2,1)S(1)}, u32[]{:S(2)}, u32[]{:S(2)}) collective-permute-start(bf16[2,32,1152]{2,1,0:T(8,128)(2,1)S(1)} %get-tuple-element.432.refs_0_.refs_4_), channel_id=1, source_target_pairs={{0,2},{1,3},{2,0},{3,1},{4,6},{5,7},{6,4},{7,5},{8,10},{9,11},{10,... | collective-permute-start | bytes 442376 | tf_op jit(solution)/shard_map/ppermute | solution.py:716
  61.0 9.9 %collective-permute-start.10 = (bf16[2,32,1152]{2,1,0:T(8,128)(2,1)S(1)}, bf16[2,32,1152]{2,1,0:T(8,128)(2,1)S(1)}, u32[]{:S(2)}, u32[]{:S(2)}) collective-permute-start(bf16[2,32,1152]{2,1,0:T(8,128)(2,1)S(1)} %get-tuple-element.432.refs_0_.refs_4_), channel_id=1, source_target_pairs={{0,1},{1,0},{2,3},{3,2},{4,5},{5,4},{6,7},{7,6},{8,9},{9,8},{10,11... | collective-permute-start | bytes 442376 | tf_op jit(solution)/shard_map/ppermute | solution.py:716
  68.2 7.7 %collective-permute-start.5 = (bf16[2,32,1152]{2,1,0:T(8,128)(2,1)S(1)}, bf16[2,32,1152]{2,1,0:T(8,128)(2,1)S(1)}, u32[]{:S(2)}, u32[]{:S(2)}) collective-permute-start(bf16[2,32,1152]{2,1,0:T(8,128)(2,1)S(1)} %shard_map.222.refs_1_), channel_id=1, source_target_pairs={{0,5},{1,4},{2,7},{3,6},{4,1},{5,0},{6,3},{7,2},{8,13},{9,12},{10,... | collective-permute-start | bytes 442376 | tf_op jit(solution)/shard_map/ppermute | solution.py:716
  69.4 9.1 %collective-permute-start.4 = (bf16[2,32,1152]{2,1,0:T(8,128)(2,1)S(1)}, bf16[2,32,1152]{2,1,0:T(8,128)(2,1)S(1)}, u32[]{:S(2)}, u32[]{:S(2)}) collective-permute-start(bf16[2,32,1152]{2,1,0:T(8,128)(2,1)S(1)} %shard_map.222.refs_1_), channel_id=1, source_target_pairs={{0,4},{1,5},{2,6},{3,7},{4,0},{5,1},{6,2},{7,3},{8,12},{9,13},{10,... | collective-permute-start | bytes 442376 | tf_op jit(solution)/shard_map/ppermute | solution.py:716
  70.9 7.7 %collective-permute-start.3 = (bf16[2,32,1152]{2,1,0:T(8,128)(2,1)S(1)}, bf16[2,32,1152]{2,1,0:T(8,128)(2,1)S(1)}, u32[]{:S(2)}, u32[]{:S(2)}) collective-permute-start(bf16[2,32,1152]{2,1,0:T(8,128)(2,1)S(1)} %shard_map.222.refs_1_), channel_id=1, source_target_pairs={{0,1},{1,0},{2,3},{3,2},{4,5},{5,4},{6,7},{7,6},{8,9},{9,8},{10,11... | collective-permute-start | bytes 442376 | tf_op jit(solution)/shard_map/ppermute | solution.py:716
  72.1 9.4 %collective-permute-start.6 = (bf16[2,32,1152]{2,1,0:T(8,128)(2,1)S(1)}, bf16[2,32,1152]{2,1,0:T(8,128)(2,1)S(1)}, u32[]{:S(2)}, u32[]{:S(2)}) collective-permute-start(bf16[2,32,1152]{2,1,0:T(8,128)(2,1)S(1)} %shard_map.222.refs_1_), channel_id=1, source_target_pairs={{0,2},{1,3},{2,0},{3,1},{4,6},{5,7},{6,4},{7,5},{8,10},{9,11},{10,... | collective-permute-start | bytes 442376 | tf_op jit(solution)/shard_map/ppermute | solution.py:716
  81.5 235.5 %reduce-scatter.5.cloned.1.call-start = ((), (), s32[]{:S(2)}) async-start(), calls=%async_computation.13 | async-start | bytes 3317760 | tf_op jit(solution)/shard_map/reduce_scatter | solution.py:747
  94.4 7.7 %collective-permute-start.19 = (bf16[2,32,1152]{2,1,0:T(8,128)(2,1)S(1)}, bf16[2,32,1152]{2,1,0:T(8,128)(2,1)S(1)}, u32[]{:S(2)}, u32[]{:S(2)}) collective-permute-start(bf16[2,32,1152]{2,1,0:T(8,128)(2,1)S(1)} %get-tuple-element.202), channel_id=1, source_target_pairs={{0,5},{1,4},{2,7},{3,6},{4,1},{5,0},{6,3},{7,2},{8,13},{9,12},{10,... | collective-permute-start | bytes 442376 | tf_op jit(solution)/shard_map/ppermute | solution.py:716
  95.6 8.5 %collective-permute-start.20 = (bf16[2,32,1152]{2,1,0:T(8,128)(2,1)S(1)}, bf16[2,32,1152]{2,1,0:T(8,128)(2,1)S(1)}, u32[]{:S(2)}, u32[]{:S(2)}) collective-permute-start(bf16[2,32,1152]{2,1,0:T(8,128)(2,1)S(1)} %get-tuple-element.203), channel_id=1, source_target_pairs={{0,1},{1,0},{2,3},{3,2},{4,5},{5,4},{6,7},{7,6},{8,9},{9,8},{10,11... | collective-permute-start | bytes 442376 | tf_op jit(solution)/shard_map/ppermute | solution.py:716
  105.3 7.7 %collective-permute-start.24 = (bf16[2,32,1152]{2,1,0:T(8,128)(2,1)S(1)}, bf16[2,32,1152]{2,1,0:T(8,128)(2,1)S(1)}, u32[]{:S(2)}, u32[]{:S(2)}) collective-permute-start(bf16[2,32,1152]{2,1,0:T(8,128)(2,1)S(1)} %get-tuple-element.205.refs_0_), channel_id=1, source_target_pairs={{0,5},{1,4},{2,7},{3,6},{4,1},{5,0},{6,3},{7,2},{8,13},{9,12},{10,... | collective-permute-start | bytes 442376 | tf_op jit(solution)/shard_map/ppermute | solution.py:716
  106.7 8.5 %collective-permute-start.23 = (bf16[2,32,1152]{2,1,0:T(8,128)(2,1)S(1)}, bf16[2,32,1152]{2,1,0:T(8,128)(2,1)S(1)}, u32[]{:S(2)}, u32[]{:S(2)}) collective-permute-start(bf16[2,32,1152]{2,1,0:T(8,128)(2,1)S(1)} %get-tuple-element.205.refs_0_), channel_id=1, source_target_pairs={{0,4},{1,5},{2,6},{3,7},{4,0},{5,1},{6,2},{7,3},{8,12},{9,13},{10,... | collective-permute-start | bytes 442376 | tf_op jit(solution)/shard_map/ppermute | solution.py:716
  162.3 7.7 %collective-permute-start.30 = (bf16[2,32,1152]{2,1,0:T(8,128)(2,1)S(1)}, bf16[2,32,1152]{2,1,0:T(8,128)(2,1)S(1)}, u32[]{:S(2)}, u32[]{:S(2)}) collective-permute-start(bf16[2,32,1152]{2,1,0:T(8,128)(2,1)S(1)} %get-tuple-element.212), channel_id=1, source_target_pairs={{0,5},{1,4},{2,7},{3,6},{4,1},{5,0},{6,3},{7,2},{8,13},{9,12},{10,... | collective-permute-start | bytes 442376 | tf_op jit(solution)/shard_map/ppermute | solution.py:716
  196.3 8.6 %collective-permute-start.42 = (bf16[2,32,1152]{2,1,0:T(8,128)(2,1)S(1)}, bf16[2,32,1152]{2,1,0:T(8,128)(2,1)S(1)}, u32[]{:S(2)}, u32[]{:S(2)}) collective-permute-start(bf16[2,32,1152]{2,1,0:T(8,128)(2,1)S(1)} %get-tuple-element.224), channel_id=1, source_target_pairs={{0,1},{1,0},{2,3},{3,2},{4,5},{5,4},{6,7},{7,6},{8,9},{9,8},{10,11... | collective-permute-start | bytes 442376 | tf_op jit(solution)/shard_map/ppermute | solution.py:716
  205.9 7.7 %collective-permute-start.46 = (bf16[2,32,1152]{2,1,0:T(8,128)(2,1)S(1)}, bf16[2,32,1152]{2,1,0:T(8,128)(2,1)S(1)}, u32[]{:S(2)}, u32[]{:S(2)}) collective-permute-start(bf16[2,32,1152]{2,1,0:T(8,128)(2,1)S(1)} %get-tuple-element.227.refs_0_), channel_id=1, source_target_pairs={{0,5},{1,4},{2,7},{3,6},{4,1},{5,0},{6,3},{7,2},{8,13},{9,12},{10,... | collective-permute-start | bytes 442376 | tf_op jit(solution)/shard_map/ppermute | solution.py:716
  207.4 8.0 %collective-permute-start.45 = (bf16[2,32,1152]{2,1,0:T(8,128)(2,1)S(1)}, bf16[2,32,1152]{2,1,0:T(8,128)(2,1)S(1)}, u32[]{:S(2)}, u32[]{:S(2)}) collective-permute-start(bf16[2,32,1152]{2,1,0:T(8,128)(2,1)S(1)} %get-tuple-element.227.refs_0_), channel_id=1, source_target_pairs={{0,4},{1,5},{2,6},{3,7},{4,0},{5,1},{6,2},{7,3},{8,12},{9,13},{10,... | collective-permute-start | bytes 442376 | tf_op jit(solution)/shard_map/ppermute | solution.py:716
  229.1 137.8 %reduce-scatter.7.cloned.1.call-start = ((), (), s32[]{:S(2)}) async-start(), calls=%async_computation.14 | async-start | bytes 2211840 | tf_op jit(solution)/shard_map/reduce_scatter | solution.py:747
  231.8 7.7 %collective-permute-start.52 = (bf16[2,32,1152]{2,1,0:T(8,128)(2,1)S(1)}, bf16[2,32,1152]{2,1,0:T(8,128)(2,1)S(1)}, u32[]{:S(2)}, u32[]{:S(2)}) collective-permute-start(bf16[2,32,1152]{2,1,0:T(8,128)(2,1)S(1)} %get-tuple-element.236), channel_id=1, source_target_pairs={{0,5},{1,4},{2,7},{3,6},{4,1},{5,0},{6,3},{7,2},{8,13},{9,12},{10,... | collective-permute-start | bytes 442376 | tf_op jit(solution)/shard_map/ppermute | solution.py:716
  233.5 8.7 %collective-permute-start.53 = (bf16[2,32,1152]{2,1,0:T(8,128)(2,1)S(1)}, bf16[2,32,1152]{2,1,0:T(8,128)(2,1)S(1)}, u32[]{:S(2)}, u32[]{:S(2)}) collective-permute-start(bf16[2,32,1152]{2,1,0:T(8,128)(2,1)S(1)} %get-tuple-element.237), channel_id=1, source_target_pairs={{0,1},{1,0},{2,3},{3,2},{4,5},{5,4},{6,7},{7,6},{8,9},{9,8},{10,11... | collective-permute-start | bytes 442376 | tf_op jit(solution)/shard_map/ppermute | solution.py:716
  244.8 8.0 %collective-permute-start.56 = (bf16[2,32,1152]{2,1,0:T(8,128)(2,1)S(1)}, bf16[2,32,1152]{2,1,0:T(8,128)(2,1)S(1)}, u32[]{:S(2)}, u32[]{:S(2)}) collective-permute-start(bf16[2,32,1152]{2,1,0:T(8,128)(2,1)S(1)} %get-tuple-element.241.refs_1_), channel_id=1, source_target_pairs={{0,4},{1,5},{2,6},{3,7},{4,0},{5,1},{6,2},{7,3},{8,12},{9,13},{10,... | collective-permute-start | bytes 442376 | tf_op jit(solution)/shard_map/ppermute | solution.py:716
  265.1 7.7 %collective-permute-start.63 = (bf16[2,32,1152]{2,1,0:T(8,128)(2,1)S(1)}, bf16[2,32,1152]{2,1,0:T(8,128)(2,1)S(1)}, u32[]{:S(2)}, u32[]{:S(2)}) collective-permute-start(bf16[2,32,1152]{2,1,0:T(8,128)(2,1)S(1)} %get-tuple-element.251), channel_id=1, source_target_pairs={{0,5},{1,4},{2,7},{3,6},{4,1},{5,0},{6,3},{7,2},{8,13},{9,12},{10,... | collective-permute-start | bytes 442376 | tf_op jit(solution)/shard_map/ppermute | solution.py:716
  266.8 8.7 %collective-permute-start.64 = (bf16[2,32,1152]{2,1,0:T(8,128)(2,1)S(1)}, bf16[2,32,1152]{2,1,0:T(8,128)(2,1)S(1)}, u32[]{:S(2)}, u32[]{:S(2)}) collective-permute-start(bf16[2,32,1152]{2,1,0:T(8,128)(2,1)S(1)} %get-tuple-element.252), channel_id=1, source_target_pairs={{0,1},{1,0},{2,3},{3,2},{4,5},{5,4},{6,7},{7,6},{8,9},{9,8},{10,11... | collective-permute-start | bytes 442376 | tf_op jit(solution)/shard_map/ppermute | solution.py:716
  279.5 101.2 %reduce-scatter.9.cloned.1.call-start = ((), (), s32[]{:S(2)}) async-start(), calls=%async_computation.15 | async-start | bytes 3317760 | tf_op jit(solution)/shard_map/reduce_scatter | solution.py:747
  283.2 8.0 %collective-permute-start.67 = (bf16[2,32,1152]{2,1,0:T(8,128)(2,1)S(1)}, bf16[2,32,1152]{2,1,0:T(8,128)(2,1)S(1)}, u32[]{:S(2)}, u32[]{:S(2)}) collective-permute-start(bf16[2,32,1152]{2,1,0:T(8,128)(2,1)S(1)} %get-tuple-element.258.refs_0_), channel_id=1, source_target_pairs={{0,4},{1,5},{2,6},{3,7},{4,0},{5,1},{6,2},{7,3},{8,12},{9,13},{10,... | collective-permute-start | bytes 442376 | tf_op jit(solution)/shard_map/ppermute | solution.py:716
  301.2 7.7 %collective-permute-start.74 = (bf16[2,32,1152]{2,1,0:T(8,128)(2,1)S(1)}, bf16[2,32,1152]{2,1,0:T(8,128)(2,1)S(1)}, u32[]{:S(2)}, u32[]{:S(2)}) collective-permute-start(bf16[2,32,1152]{2,1,0:T(8,128)(2,1)S(1)} %get-tuple-element.270), channel_id=1, source_target_pairs={{0,5},{1,4},{2,7},{3,6},{4,1},{5,0},{6,3},{7,2},{8,13},{9,12},{10,... | collective-permute-start | bytes 442376 | tf_op jit(solution)/shard_map/ppermute | solution.py:716
  302.9 8.7 %collective-permute-start.75 = (bf16[2,32,1152]{2,1,0:T(8,128)(2,1)S(1)}, bf16[2,32,1152]{2,1,0:T(8,128)(2,1)S(1)}, u32[]{:S(2)}, u32[]{:S(2)}) collective-permute-start(bf16[2,32,1152]{2,1,0:T(8,128)(2,1)S(1)} %get-tuple-element.271), channel_id=1, source_target_pairs={{0,1},{1,0},{2,3},{3,2},{4,5},{5,4},{6,7},{7,6},{8,9},{9,8},{10,11... | collective-permute-start | bytes 442376 | tf_op jit(solution)/shard_map/ppermute | solution.py:716
  316.7 101.5 %reduce-scatter.11.cloned.1.call-start = ((), (), s32[]{:S(2)}) async-start(), calls=%async_computation.16 | async-start | bytes 2211840 | tf_op jit(solution)/shard_map/reduce_scatter | solution.py:747
  320.3 8.0 %collective-permute-start.78 = (bf16[2,32,1152]{2,1,0:T(8,128)(2,1)S(1)}, bf16[2,32,1152]{2,1,0:T(8,128)(2,1)S(1)}, u32[]{:S(2)}, u32[]{:S(2)}) collective-permute-start(bf16[2,32,1152]{2,1,0:T(8,128)(2,1)S(1)} %get-tuple-element.276.refs_1_), channel_id=1, source_target_pairs={{0,4},{1,5},{2,6},{3,7},{4,0},{5,1},{6,2},{7,3},{8,12},{9,13},{10,... | collective-permute-start | bytes 442376 | tf_op jit(solution)/shard_map/ppermute | solution.py:716
  345.8 9.6 %collective-permute-start.85 = (bf16[2,32,1152]{2,1,0:T(8,128)(2,1)S(1)}, bf16[2,32,1152]{2,1,0:T(8,128)(2,1)S(1)}, u32[]{:S(2)}, u32[]{:S(2)}) collective-permute-start(bf16[2,32,1152]{2,1,0:T(8,128)(2,1)S(1)} %get-tuple-element.290), channel_id=1, source_target_pairs={{0,5},{1,4},{2,7},{3,6},{4,1},{5,0},{6,3},{7,2},{8,13},{9,12},{10,... | collective-permute-start | bytes 442376 | tf_op jit(solution)/shard_map/ppermute | solution.py:716
  347.8 8.6 %collective-permute-start.86 = (bf16[2,32,1152]{2,1,0:T(8,128)(2,1)S(1)}, bf16[2,32,1152]{2,1,0:T(8,128)(2,1)S(1)}, u32[]{:S(2)}, u32[]{:S(2)}) collective-permute-start(bf16[2,32,1152]{2,1,0:T(8,128)(2,1)S(1)} %get-tuple-element.291), channel_id=1, source_target_pairs={{0,1},{1,0},{2,3},{3,2},{4,5},{5,4},{6,7},{7,6},{8,9},{9,8},{10,11... | collective-permute-start | bytes 442376 | tf_op jit(solution)/shard_map/ppermute | solution.py:716
  367.0 17.4 %collective-permute-start.88 = (bf16[288,1152]{1,0:T(8,128)(2,1)S(1)}, bf16[288,1152]{1,0:T(8,128)(2,1)S(1)}, u32[]{:S(2)}, u32[]{:S(2)}) collective-permute-start(bf16[288,1152]{1,0:T(8,128)(2,1)S(1)} %copy-done.1), channel_id=1, source_target_pairs={{0,1},{2,3},{4,5},{6,7},{8,9},{10,11},{12,13},{14,15},{16,17},{18,... | collective-permute-start | bytes 1990664 | tf_op jit(solution)/shard_map/ppermute | solution.py:1056
  371.0 9.7 %all-to-all-start.4 = ((f32[4,1,9856]{2,1,0:T(1,128)}), f32[4,1,9856]{2,1,0:T(1,128)S(1)}, u32[]{:S(2)}, u32[]{:S(2)}) async-start(f32[4,1,9856]{2,1,0:T(1,128)} %broadcast_in_dim.101), calls=%async_computation.6 | async-start | bytes 315392 | tf_op jit(solution)/shard_map/all_to_all | solution.py:739
  374.4 37.9 %collective-permute-start.94 = (bf16[2,32,1152]{2,1,0:T(8,128)(2,1)}, bf16[2,32,1152]{2,1,0:T(8,128)(2,1)}, u32[]{:S(2)}, u32[]{:S(2)}) collective-permute-start(bf16[2,32,1152]{2,1,0:T(8,128)(2,1)} %get-tuple-element.317), channel_id=1, source_target_pairs={{1,0},{3,2},{5,4},{7,6},{9,8},{11,10},{13,12},{15,14},{17,16},{19,... | collective-permute-start | bytes 442376 | tf_op jit(solution)/shard_map/ppermute | solution.py:1185
  380.8 7.8 %collective-permute-start.90 = (bf16[4,2,32,1152]{3,2,1,0:T(8,128)(2,1)}, bf16[4,2,32,1152]{3,2,1,0:T(8,128)(2,1)}, u32[]{:S(2)}, u32[]{:S(2)}) collective-permute-start(bf16[4,2,32,1152]{3,2,1,0:T(8,128)(2,1)} %get-tuple-element.322), channel_id=1, source_target_pairs={{0,2},{1,3},{2,0},{3,1},{4,6},{5,7},{6,4},{7,5},{8,10},{9,11},{10,... | collective-permute-start | bytes 1769480 | tf_op jit(solution)/shard_map/ppermute | solution.py:716
  381.0 20.6 %collective-permute-start.89 = (bf16[288,1152]{1,0:T(8,128)(2,1)}, bf16[288,1152]{1,0:T(8,128)(2,1)S(1)}, u32[]{:S(2)}, u32[]{:S(2)}) collective-permute-start(bf16[288,1152]{1,0:T(8,128)(2,1)} %reduce-scatter.9.cloned.1.call-done.refs_1_), channel_id=1, source_target_pairs={{1,0},{3,2},{5,4},{7,6},{9,8},{11,10},{13,12},{15,14},{17,16},{19,... | collective-permute-start | bytes 1990664 | tf_op jit(solution)/shard_map/ppermute | solution.py:1059
  385.1 19.7 %all-to-all-start.5 = ((f32[32,2,288]{2,1,0:T(2,128)}), f32[32,2,288]{2,1,0:T(2,128)}, u32[]{:S(2)}, u32[]{:S(2)}) async-start(f32[32,2,288]{2,1,0:T(2,128)} %bitcast.86), calls=%async_computation.8 | async-start | bytes 196608 | tf_op jit(solution)/shard_map/all_to_all | solution.py:1171
  392.3 13.6 %collective-permute-start.91 = (bf16[2,32,1152]{2,1,0:T(8,128)(2,1)}, bf16[2,32,1152]{2,1,0:T(8,128)(2,1)}, u32[]{:S(2)}, u32[]{:S(2)}) collective-permute-start(bf16[2,32,1152]{2,1,0:T(8,128)(2,1)} %get-tuple-element.324), channel_id=1, source_target_pairs={{0,5},{1,4},{2,7},{3,6},{4,1},{5,0},{6,3},{7,2},{8,13},{9,12},{10,... | collective-permute-start | bytes 442376 | tf_op jit(solution)/shard_map/ppermute | solution.py:716
  394.9 13.0 %collective-permute-start.92 = (bf16[2,32,1152]{2,1,0:T(8,128)(2,1)}, bf16[2,32,1152]{2,1,0:T(8,128)(2,1)}, u32[]{:S(2)}, u32[]{:S(2)}) collective-permute-start(bf16[2,32,1152]{2,1,0:T(8,128)(2,1)} %get-tuple-element.325), channel_id=1, source_target_pairs={{0,1},{1,0},{2,3},{3,2},{4,5},{5,4},{6,7},{7,6},{8,9},{9,8},{10,11... | collective-permute-start | bytes 442376 | tf_op jit(solution)/shard_map/ppermute | solution.py:716
  395.5 12.5 %collective-permute-start.93 = (bf16[2,32,1152]{2,1,0:T(8,128)(2,1)}, bf16[2,32,1152]{2,1,0:T(8,128)(2,1)}, u32[]{:S(2)}, u32[]{:S(2)}) collective-permute-start(bf16[2,32,1152]{2,1,0:T(8,128)(2,1)} %get-tuple-element.326), channel_id=1, source_target_pairs={{0,4},{1,5},{2,6},{3,7},{4,0},{5,1},{6,2},{7,3},{8,12},{9,13},{10,... | collective-permute-start | bytes 442376 | tf_op jit(solution)/shard_map/ppermute | solution.py:716
  402.5 15.7 %collective-permute-start.96 = (bf16[288,768]{1,0:T(8,128)(2,1)}, bf16[288,768]{1,0:T(8,128)(2,1)}, u32[]{:S(2)}, u32[]{:S(2)}) collective-permute-start(bf16[288,768]{1,0:T(8,128)(2,1)} %reduce-scatter.7.cloned.1.call-done.refs_3_), channel_id=1, source_target_pairs={{0,1},{2,3},{4,5},{6,7},{8,9},{10,11},{12,13},{14,15},{16,17},{18,... | collective-permute-start | bytes 1327112 | tf_op jit(solution)/shard_map/ppermute | solution.py:1056
  418.2 12.9 %collective-permute-start.97 = (bf16[288,768]{1,0:T(8,128)(2,1)}, bf16[288,768]{1,0:T(8,128)(2,1)}, u32[]{:S(2)}, u32[]{:S(2)}) collective-permute-start(bf16[288,768]{1,0:T(8,128)(2,1)} %reduce-scatter.11.cloned.1.call-done.refs_1_), channel_id=1, source_target_pairs={{1,0},{3,2},{5,4},{7,6},{9,8},{11,10},{13,12},{15,14},{17,16},{19,... | collective-permute-start | bytes 1327112 | tf_op jit(solution)/shard_map/ppermute | solution.py:1059
  (109 other events, 610.7 us)
Sparse Core Ops, SparseCore 0:
  27.3 40.5 all-gather.3
  70.1 83.5 all-gather.5
  155.2 53.8 all-gather.7
  229.2 50.3 reduce-scatter.4
  282.4 38.0 reduce-scatter.6
  322.8 51.7 reduce-scatter.8
  377.5 39.6 reduce-scatter.10

commit v5 on v4

--- a/solution.py
+++ b/solution.py
@@ -13,7 +13,6 @@
 LANES = 128
 F32 = jnp.float32
 BF16 = jnp.bfloat16
-HIGHEST = lax.Precision.HIGHEST
 PLANE = ("tensor", "section")
 
 
@@ -285,12 +284,22 @@
     ]
 
 
+def three_parts(v):
+    parts = []
+    for _ in range(3):
+        parts.append(v.astype(BF16))
+        v = v - parts[-1].astype(F32)
+    return jnp.concatenate(parts, axis=1)
+
+
+def add_parts(v):
+    return v[:, :LANES] + v[:, LANES : 2 * LANES] + v[:, 2 * LANES :]
+
+
 def decay_parts(logits, mask, gate_lane, heads):
     rates = -(jnp.maximum(logits, 0.0) + jnp.log1p(jnp.exp(-jnp.abs(logits))))
-    ones = jnp.where(mask, 1.0, 0.0)
-    totals = lax.dot_general(
-        ones, rates, (((1,), (0,)), ((), ())), precision=HIGHEST, preferred_element_type=F32
-    )
+    ones = jnp.where(mask, 1.0, 0.0).astype(BF16)
+    totals = add_parts(mm(ones, three_parts(rates)))
     turned = totals.T
     decays = []
     for h in range(heads):
@@ -549,13 +558,7 @@
             g_span = (g_scores * raw + g_mass) * w
             across = jnp.where(gate_sets[h], jnp.sum(g_span, axis=1, keepdims=True), across)
             down = jnp.where(sublane == gate_lane + h, rows_sum(g_span), down)
-        g_rates = lax.dot_general(
-            ones,
-            across - down.T,
-            (((0,), (0,)), ((), ())),
-            precision=HIGHEST,
-            preferred_element_type=F32,
-        )
+        g_rates = add_parts(mm_tn(ones, three_parts(across - down.T)))
         g_logits = (-g_rates * jax.nn.sigmoid(logits)).astype(BF16).astype(F32)
         g_bias = rows_sum(g_logits)
         gtap_ref[9:10, :LANES] = g_bias if m == 0 else gtap_ref[9:10, :LANES] + g_bias

time: 448 us -> 447 us (level)
  no operation moved by 1% of the time
where the time goes in v5:
time: 447 us; the launch traced here: 442 us
  waiting for transfers between devices  188 us (42%)
  starting transfers between devices  94.5 us (21%)
  Pallas kernels  87.4 us (20%)
  local copies, waits for them, and re-layouts  27.6 us (6%)
  blocking collectives  16.8 us (4%)
  between operations  15.8 us (4%)
  other arithmetic  9.11 us (2%)
    ppermute x88, waiting for transfers between devices, swap(): return lax.ppermute(value, PLANE, route)  111 us
    pallas_call x33, Pallas kernels, call(): pl.pallas_call(kernel, out_shape=tuple(shapes), in_specs=specs, out_specs...  87.4 us
    ppermute x88, starting transfers between devices, swap(): return lax.ppermute(value, PLANE, route)  60.8 us
    all_gather x3, waiting for transfers between devices, gather_all(): return lax.all_gather(own, 'dp', axis=0, tiled=True)  37.8 us
    unnamed x104, local copies, waits for them, and re-layouts  18.3 us
    ppermute x2, waiting for transfers between devices, to_first(): return lax.ppermute(value, 'section', [(1, 0)])  10.5 us
  transfers between devices with their start and end apart: 109, of which 64 were waited for; matrix products, arithmetic and copies ran while one was open for 5% of the time, Pallas kernels for 17%

profile of v5, /device:TPU:0, one launch (start us, length us, event | category | flops | bytes accessed | tf_op | source)
XLA Modules:
  0.0 442.0 jit_solution(9322901075844545423)
XLA Ops:
  11.3 3.0 collective-permute-start.2
  15.9 4.9 %all-to-all-start = ((bf16[4,2,288]{2,1,0:T(2,128)(2,1)}), bf16[4,2,288]{2,1,0:T(2,128)(2,1)S(1)}, u32[]{:S(2)}, u32[]{:S(2)}) async-start(bf16[4,2,288]{2,1,0:T(2,128)(2,1)} %bitcast.68), calls=%async_computation | async-start | bytes 12288 | tf_op jit(solution)/shard_map/all_to_all | solution.py:879
  20.8 5.6 %all-to-all-done = bf16[4,2,288]{2,1,0:T(2,128)(2,1)S(1)} async-done(((bf16[4,2,288]{2,1,0:T(2,128)(2,1)}), bf16[4,2,288]{2,1,0:T(2,128)(2,1)S(1)}, u32[]{:S(2)}, u32[]{:S(2)}) %all-to-all-start) | async-done | bytes 4640 | tf_op jit(solution)/shard_map/all_to_all | solution.py:879
  30.1 4.2 all-to-all-start.1
  34.3 6.8 %all-to-all-done.1 = f32[4,2,1728]{2,1,0:T(2,128)S(1)} async-done(((f32[4,2,1728]{2,1,0:T(2,128)}), f32[4,2,1728]{2,1,0:T(2,128)S(1)}, u32[]{:S(2)}, u32[]{:S(2)}) %all-to-all-start.1) | async-done | bytes 55328 | tf_op jit(solution)/shard_map/all_to_all | solution.py:883
  41.2 8.1 %all_to_all.41 = f32[8,2,1728]{2,1,0:T(2,128)} all-to-all(f32[8,2,1728]{2,1,0:T(2,128)S(1)} %broadcast_in_dim.90), channel_id=1, replica_groups=mesh['dp'=4,'tensor'=4,'section'=2] {'section','tensor'}, dimensions={0} | all-to-all | bytes 221184 | tf_op jit(solution)/shard_map/all_to_all | solution.py:742
  53.8 4.6 %collective-permute-done = bf16[2,32,1152]{2,1,0:T(8,128)(2,1)S(1)} collective-permute-done((bf16[2,32,1152]{2,1,0:T(8,128)(2,1)S(1)}, bf16[2,32,1152]{2,1,0:T(8,128)(2,1)S(1)}, u32[]{:S(2)}, u32[]{:S(2)}) %collective-permute-start) | collective-permute-done | bytes 147488 | tf_op jit(solution)/shard_map/ppermute | solution.py:851
  62.2 2.8 collective-permute-done.12.refs_3_
  72.5 3.3 collective-permute-done.5.refs_4_
  75.8 2.7 collective-permute-done.4.refs_3_
  83.9 7.3 %shard_map.224 = (bf16[2,256,1152]{2,1,0:T(8,128)(2,1)}, bf16[2,256,1024]{2,1,0:T(8,128)(2,1)}, f32[2,256,128]{2,1,0:T(8,128)}, f32[2,256,256]{2,1,0:T(8,128)}, ...) custom-call(s32[1]{0:T(128)} %bitcast.refs_0_, ...), custom_call_target="tpu_custom_call" | custom-call | flops 2315255808 | bytes 7422468 | tf_op jit(solution)/shard_map/pallas_call | solution.py:96
  97.0 4.1 collective-permute-done.19.refs_1_
  108.0 4.2 collective-permute-done.24.refs_3_
  115.8 37.8 %all-gather.6.cloned.1.call-done.refs_8_.refs_9_.refs_12_ = bf16[1152,1920]{1,0:T(8,128)(2,1)} async-done(((bf16[288,1920]{1,0:T(8,128)(2,1)}), bf16[1152,1920]{1,0:T(8,128)(2,1)}) %all-gather.6.cloned.1.call-update) | async-done | bytes 4423696 | tf_op jit(solution)/shard_map/all_gather | solution.py:746
  153.6 6.4 %shard_map.227 = (bf16[512,1152]{1,0:T(8,128)(2,1)}, f32[512,640]{1,0:T(8,128)}, bf16[512,640]{1,0:T(8,128)(2,1)}, bf16[4,2,32,1152]{3,2,1,0:T(8,128)(2,1)S(1)},...) custom-call(bf16[2,32,1152]{2,1,0:T(8,128)(2,1)S(1)} %get-tuple-elem, ...), custom_call_target="tpu_custom_call" | custom-call | flops 1358954496 | bytes 8161792 | tf_op jit(solution)/shard_map/pallas_call | solution.py:96
  166.0 4.0 collective-permute-done.30.refs_1_
  176.9 3.4 collective-permute-done.35.refs_4_
  180.3 2.7 collective-permute-done.34.refs_3_
  184.6 6.6 %shard_map.230 = (bf16[2,256,1152]{2,1,0:T(8,128)(2,1)}, bf16[2,256,1024]{2,1,0:T(8,128)(2,1)}, f32[2,256,128]{2,1,0:T(8,128)}, f32[2,256,256]{2,1,0:T(8,128)}, ...) custom-call(s32[1]{0:T(128)} %bitcast.refs_0_, ...), custom_call_target="tpu_custom_call" | custom-call | flops 2315255808 | bytes 7422468 | tf_op jit(solution)/shard_map/pallas_call | solution.py:96
  197.2 4.1 collective-permute-done.41.refs_1_
  201.3 2.7 collective-permute-done.42.refs_2_
  208.5 4.1 collective-permute-done.46.refs_3_
  217.5 9.3 %shard_map.234 = (bf16[1152,1152]{1,0:T(8,128)(2,1)}, f32[1,640]{1,0:T(1,128)S(1)}, f32[2,1,1152]{2,1,0:T(1,128)S(1)}, bf16[4,2,32,1152]{3,2,1,0:T(8,128)(2,1)S(...) custom-call(bf16[512,1152]{1,0:T(8,128)(2,1)} %shard_map.233.refs_0_, ...), custom_call_target="tpu_custom_call" | custom-call | flops 4076863488 | bytes 10096640 | tf_op jit(solution)/shard_map/pallas_call | solution.py:96
  234.5 4.1 collective-permute-done.52.refs_1_
  238.6 2.7 collective-permute-done.53.refs_2_
  246.0 4.0 collective-permute-done.57.refs_4_
  253.8 8.0 %shard_map.237 = (bf16[2,256,1152]{2,1,0:T(8,128)(2,1)S(1)}, bf16[2,256,640]{2,1,0:T(8,128)(2,1)S(1)}, f32[16,256]{1,0:T(8,128)S(1)}, bf16[4,2,32,1152]{3,2,1,0:...) custom-call(s32[1]{0:T(128)} %bitcast.refs_0_, ...), custom_call_target="tpu_custom_call" | custom-call | flops 4630511616 | bytes 7831556 | tf_op jit(solution)/shard_map/pallas_call | solution.py:96
  267.6 4.1 collective-permute-done.63.refs_1_.refs_5_
  271.7 2.7 collective-permute-done.64.refs_2_.refs_6_
  274.4 4.0 shard_map.240.refs_10_
  284.2 3.9 collective-permute-done.68.refs_3_
  292.0 6.0 %shard_map.241 = (bf16[512,1152]{1,0:T(8,128)(2,1)S(1)}, bf16[512,640]{1,0:T(8,128)(2,1)S(1)}, f32[1,640]{1,0:T(1,128)S(1)}, bf16[4,2,32,1152]{3,2,1,0:T(8,128)(...) custom-call(bf16[2,32,1152]{2,1,0:T(8,128)(2,1)S(1)} %get-tuple-elem, ...), custom_call_target="tpu_custom_call" | custom-call | flops 1358954496 | bytes 8161792 | tf_op jit(solution)/shard_map/pallas_call | solution.py:96
  303.7 4.1 collective-permute-done.74.refs_1_.refs_5_
  307.8 2.7 collective-permute-done.75.refs_2_.refs_6_
  310.6 5.0 %shard_map.244.refs_14_ = bf16[1152,1152]{1,0:T(8,128)(2,1)} custom-call(bf16[512,1152]{1,0:T(8,128)(2,1)} %get-tuple-element.280.refs_0_, bf16[512,640]{1,0:T(8,128)(2,1)S(1)} %get-tuple-element.281.refs_1_, bf16[512,1152]{1,0:T(8,128)(2,1)S(1)} %get-tuple-element.282.refs_2_, bf16[512,640]{1,0:T(8,128)(2,1)} %get-tuple-element.283.refs_3_, ...), custom_call_target="tpu_custom_call" | custom-call | flops 1358954496 | bytes 6324224 | tf_op jit(solution)/shard_map/pallas_call | solution.py:96
  321.3 4.0 collective-permute-done.79.refs_4_
  331.7 8.4 %shard_map.245 = (bf16[2,256,1152]{2,1,0:T(8,128)(2,1)S(1)}, bf16[2,256,640]{2,1,0:T(8,128)(2,1)S(1)}, f32[16,256]{1,0:T(8,128)S(1)}, bf16[4,2,32,1152]{3,2,1,0:...) custom-call(s32[1]{0:T(128)} %bitcast.refs_0_, ...), custom_call_target="tpu_custom_call" | custom-call | flops 4630511616 | bytes 7831556 | tf_op jit(solution)/shard_map/pallas_call | solution.py:96
  350.0 4.0 shard_map.247.refs_9_
  356.7 8.7 %all_to_all.42 = f32[8,1,6656]{2,1,0:T(1,128)S(1)} all-to-all(f32[8,1,6656]{2,1,0:T(1,128)S(1)} %copy.101), channel_id=1, replica_groups=mesh['dp'=4,'tensor'=4,'section'=2] {'section','tensor'}, dimensions={0} | all-to-all | bytes 425984 | tf_op jit(solution)/shard_map/all_to_all | solution.py:1151
  365.6 3.2 collective-permute-start.88
  369.6 3.3 all-to-all-start.4
  374.3 5.0 %all-to-all-done.4 = f32[4,1,9856]{2,1,0:T(1,128)S(1)} async-done(((f32[4,1,9856]{2,1,0:T(1,128)}), f32[4,1,9856]{2,1,0:T(1,128)S(1)}, u32[]{:S(2)}, u32[]{:S(2)}) %all-to-all-start.4) | async-done | bytes 157728 | tf_op jit(solution)/shard_map/all_to_all | solution.py:742
  383.7 3.3 all-to-all-start.5
  387.2 3.0 shard_map.249
  395.8 4.5 %collective-permute-done.89.refs_2_ = bf16[288,1152]{1,0:T(8,128)(2,1)S(1)} collective-permute-done((bf16[288,1152]{1,0:T(8,128)(2,1)}, bf16[288,1152]{1,0:T(8,128)(2,1)S(1)}, u32[]{:S(2)}, u32[]{:S(2)}) %collective-permute-start.89) | collective-permute-done | bytes 663584 | tf_op jit(solution)/shard_map/ppermute | solution.py:1062
  410.9 4.1 collective-permute-done.95
  424.1 6.1 %collective-permute-done.97.refs_2_ = bf16[288,768]{1,0:T(8,128)(2,1)} collective-permute-done((bf16[288,768]{1,0:T(8,128)(2,1)}, bf16[288,768]{1,0:T(8,128)(2,1)}, u32[]{:S(2)}, u32[]{:S(2)}) %collective-permute-start.97) | collective-permute-done | bytes 442400 | tf_op jit(solution)/shard_map/ppermute | solution.py:1062
  430.2 2.8 shard_map.251
  (425 shorter events, 171.7 us)
Async XLA Ops:
  11.3 15.1 %collective-permute-start.2 = (bf16[288,768]{1,0:T(8,128)(2,1)S(1)}, bf16[288,768]{1,0:T(8,128)(2,1)S(1)}, u32[]{:S(2)}, u32[]{:S(2)}) collective-permute-start(bf16[288,768]{1,0:T(8,128)(2,1)S(1)} %get-tuple-element.181), channel_id=1, source_target_pairs={{0,1},{1,0},{2,3},{3,2},{4,5},{5,4},{6,7},{7,6},{8,9},{9,8},{10,11... | collective-permute-start | bytes 1327112 | tf_op jit(solution)/shard_map/ppermute | solution.py:825
  15.9 10.5 %all-to-all-start = ((bf16[4,2,288]{2,1,0:T(2,128)(2,1)}), bf16[4,2,288]{2,1,0:T(2,128)(2,1)S(1)}, u32[]{:S(2)}, u32[]{:S(2)}) async-start(bf16[4,2,288]{2,1,0:T(2,128)(2,1)} %bitcast.68), calls=%async_computation | async-start | bytes 12288 | tf_op jit(solution)/shard_map/all_to_all | solution.py:879
  20.8 62.3 %all-gather.4.cloned.1.call-start = ((), (), s32[]{:S(2)}) async-start(), calls=%async_computation.10 | async-start | bytes 2211840 | tf_op jit(solution)/shard_map/all_gather | solution.py:746
  28.6 20.7 %collective-permute-start.1 = (bf16[288,1152]{1,0:T(8,128)(2,1)S(1)}, bf16[288,1152]{1,0:T(8,128)(2,1)}, u32[]{:S(2)}, u32[]{:S(2)}) collective-permute-start(bf16[288,1152]{1,0:T(8,128)(2,1)S(1)} %get-tuple-element.179), channel_id=1, source_target_pairs={{0,1},{1,0},{2,3},{3,2},{4,5},{5,4},{6,7},{7,6},{8,9},{9,8},{10,11... | collective-permute-start | bytes 1990664 | tf_op jit(solution)/shard_map/ppermute | solution.py:835
  30.1 11.0 %all-to-all-start.1 = ((f32[4,2,1728]{2,1,0:T(2,128)}), f32[4,2,1728]{2,1,0:T(2,128)S(1)}, u32[]{:S(2)}, u32[]{:S(2)}) async-start(f32[4,2,1728]{2,1,0:T(2,128)} %fusion), calls=%async_computation.1 | async-start | bytes 114688 | tf_op jit(solution)/shard_map/all_to_all | solution.py:883
  34.3 119.4 %all-gather.6.cloned.1.call-start = ((), (), s32[]{:S(2)}) async-start(), calls=%async_computation.11 | async-start | bytes 5529600 | tf_op jit(solution)/shard_map/all_gather | solution.py:746
  52.5 165.0 %all-gather.8.cloned.1.call-start = ((), (), s32[]{:S(2)}) async-start(), calls=%async_computation.12 | async-start | bytes 3317760 | tf_op jit(solution)/shard_map/all_gather | solution.py:746
  59.3 7.8 %collective-permute-start.11 = (bf16[2,32,1152]{2,1,0:T(8,128)(2,1)S(1)}, bf16[2,32,1152]{2,1,0:T(8,128)(2,1)S(1)}, u32[]{:S(2)}, u32[]{:S(2)}) collective-permute-start(bf16[2,32,1152]{2,1,0:T(8,128)(2,1)S(1)} %get-tuple-element.432.refs_0_.refs_4_), channel_id=1, source_target_pairs={{0,4},{1,5},{2,6},{3,7},{4,0},{5,1},{6,2},{7,3},{8,12},{9,13},{10,... | collective-permute-start | bytes 442376 | tf_op jit(solution)/shard_map/ppermute | solution.py:719
  60.9 8.5 %collective-permute-start.13 = (bf16[2,32,1152]{2,1,0:T(8,128)(2,1)S(1)}, bf16[2,32,1152]{2,1,0:T(8,128)(2,1)S(1)}, u32[]{:S(2)}, u32[]{:S(2)}) collective-permute-start(bf16[2,32,1152]{2,1,0:T(8,128)(2,1)S(1)} %get-tuple-element.432.refs_0_.refs_4_), channel_id=1, source_target_pairs={{0,2},{1,3},{2,0},{3,1},{4,6},{5,7},{6,4},{7,5},{8,10},{9,11},{10,... | collective-permute-start | bytes 442376 | tf_op jit(solution)/shard_map/ppermute | solution.py:719
  61.0 9.9 %collective-permute-start.10 = (bf16[2,32,1152]{2,1,0:T(8,128)(2,1)S(1)}, bf16[2,32,1152]{2,1,0:T(8,128)(2,1)S(1)}, u32[]{:S(2)}, u32[]{:S(2)}) collective-permute-start(bf16[2,32,1152]{2,1,0:T(8,128)(2,1)S(1)} %get-tuple-element.432.refs_0_.refs_4_), channel_id=1, source_target_pairs={{0,1},{1,0},{2,3},{3,2},{4,5},{5,4},{6,7},{7,6},{8,9},{9,8},{10,11... | collective-permute-start | bytes 442376 | tf_op jit(solution)/shard_map/ppermute | solution.py:719
  68.2 7.7 %collective-permute-start.5 = (bf16[2,32,1152]{2,1,0:T(8,128)(2,1)S(1)}, bf16[2,32,1152]{2,1,0:T(8,128)(2,1)S(1)}, u32[]{:S(2)}, u32[]{:S(2)}) collective-permute-start(bf16[2,32,1152]{2,1,0:T(8,128)(2,1)S(1)} %shard_map.222.refs_1_), channel_id=1, source_target_pairs={{0,5},{1,4},{2,7},{3,6},{4,1},{5,0},{6,3},{7,2},{8,13},{9,12},{10,... | collective-permute-start | bytes 442376 | tf_op jit(solution)/shard_map/ppermute | solution.py:719
  69.4 9.1 %collective-permute-start.4 = (bf16[2,32,1152]{2,1,0:T(8,128)(2,1)S(1)}, bf16[2,32,1152]{2,1,0:T(8,128)(2,1)S(1)}, u32[]{:S(2)}, u32[]{:S(2)}) collective-permute-start(bf16[2,32,1152]{2,1,0:T(8,128)(2,1)S(1)} %shard_map.222.refs_1_), channel_id=1, source_target_pairs={{0,4},{1,5},{2,6},{3,7},{4,0},{5,1},{6,2},{7,3},{8,12},{9,13},{10,... | collective-permute-start | bytes 442376 | tf_op jit(solution)/shard_map/ppermute | solution.py:719
  70.9 7.7 %collective-permute-start.3 = (bf16[2,32,1152]{2,1,0:T(8,128)(2,1)S(1)}, bf16[2,32,1152]{2,1,0:T(8,128)(2,1)S(1)}, u32[]{:S(2)}, u32[]{:S(2)}) collective-permute-start(bf16[2,32,1152]{2,1,0:T(8,128)(2,1)S(1)} %shard_map.222.refs_1_), channel_id=1, source_target_pairs={{0,1},{1,0},{2,3},{3,2},{4,5},{5,4},{6,7},{7,6},{8,9},{9,8},{10,11... | collective-permute-start | bytes 442376 | tf_op jit(solution)/shard_map/ppermute | solution.py:719
  72.1 9.4 %collective-permute-start.6 = (bf16[2,32,1152]{2,1,0:T(8,128)(2,1)S(1)}, bf16[2,32,1152]{2,1,0:T(8,128)(2,1)S(1)}, u32[]{:S(2)}, u32[]{:S(2)}) collective-permute-start(bf16[2,32,1152]{2,1,0:T(8,128)(2,1)S(1)} %shard_map.222.refs_1_), channel_id=1, source_target_pairs={{0,2},{1,3},{2,0},{3,1},{4,6},{5,7},{6,4},{7,5},{8,10},{9,11},{10,... | collective-permute-start | bytes 442376 | tf_op jit(solution)/shard_map/ppermute | solution.py:719
  81.5 234.5 %reduce-scatter.5.cloned.1.call-start = ((), (), s32[]{:S(2)}) async-start(), calls=%async_computation.13 | async-start | bytes 3317760 | tf_op jit(solution)/shard_map/reduce_scatter | solution.py:750
  93.5 7.7 %collective-permute-start.19 = (bf16[2,32,1152]{2,1,0:T(8,128)(2,1)S(1)}, bf16[2,32,1152]{2,1,0:T(8,128)(2,1)S(1)}, u32[]{:S(2)}, u32[]{:S(2)}) collective-permute-start(bf16[2,32,1152]{2,1,0:T(8,128)(2,1)S(1)} %get-tuple-element.202), channel_id=1, source_target_pairs={{0,5},{1,4},{2,7},{3,6},{4,1},{5,0},{6,3},{7,2},{8,13},{9,12},{10,... | collective-permute-start | bytes 442376 | tf_op jit(solution)/shard_map/ppermute | solution.py:719
  94.7 8.5 %collective-permute-start.20 = (bf16[2,32,1152]{2,1,0:T(8,128)(2,1)S(1)}, bf16[2,32,1152]{2,1,0:T(8,128)(2,1)S(1)}, u32[]{:S(2)}, u32[]{:S(2)}) collective-permute-start(bf16[2,32,1152]{2,1,0:T(8,128)(2,1)S(1)} %get-tuple-element.203), channel_id=1, source_target_pairs={{0,1},{1,0},{2,3},{3,2},{4,5},{5,4},{6,7},{7,6},{8,9},{9,8},{10,11... | collective-permute-start | bytes 442376 | tf_op jit(solution)/shard_map/ppermute | solution.py:719
  104.4 7.7 %collective-permute-start.24 = (bf16[2,32,1152]{2,1,0:T(8,128)(2,1)S(1)}, bf16[2,32,1152]{2,1,0:T(8,128)(2,1)S(1)}, u32[]{:S(2)}, u32[]{:S(2)}) collective-permute-start(bf16[2,32,1152]{2,1,0:T(8,128)(2,1)S(1)} %get-tuple-element.205.refs_0_), channel_id=1, source_target_pairs={{0,5},{1,4},{2,7},{3,6},{4,1},{5,0},{6,3},{7,2},{8,13},{9,12},{10,... | collective-permute-start | bytes 442376 | tf_op jit(solution)/shard_map/ppermute | solution.py:719
  105.8 8.5 %collective-permute-start.23 = (bf16[2,32,1152]{2,1,0:T(8,128)(2,1)S(1)}, bf16[2,32,1152]{2,1,0:T(8,128)(2,1)S(1)}, u32[]{:S(2)}, u32[]{:S(2)}) collective-permute-start(bf16[2,32,1152]{2,1,0:T(8,128)(2,1)S(1)} %get-tuple-element.205.refs_0_), channel_id=1, source_target_pairs={{0,4},{1,5},{2,6},{3,7},{4,0},{5,1},{6,2},{7,3},{8,12},{9,13},{10,... | collective-permute-start | bytes 442376 | tf_op jit(solution)/shard_map/ppermute | solution.py:719
  162.3 7.7 %collective-permute-start.30 = (bf16[2,32,1152]{2,1,0:T(8,128)(2,1)S(1)}, bf16[2,32,1152]{2,1,0:T(8,128)(2,1)S(1)}, u32[]{:S(2)}, u32[]{:S(2)}) collective-permute-start(bf16[2,32,1152]{2,1,0:T(8,128)(2,1)S(1)} %get-tuple-element.212), channel_id=1, source_target_pairs={{0,5},{1,4},{2,7},{3,6},{4,1},{5,0},{6,3},{7,2},{8,13},{9,12},{10,... | collective-permute-start | bytes 442376 | tf_op jit(solution)/shard_map/ppermute | solution.py:719
  195.4 8.6 %collective-permute-start.42 = (bf16[2,32,1152]{2,1,0:T(8,128)(2,1)S(1)}, bf16[2,32,1152]{2,1,0:T(8,128)(2,1)S(1)}, u32[]{:S(2)}, u32[]{:S(2)}) collective-permute-start(bf16[2,32,1152]{2,1,0:T(8,128)(2,1)S(1)} %get-tuple-element.224), channel_id=1, source_target_pairs={{0,1},{1,0},{2,3},{3,2},{4,5},{5,4},{6,7},{7,6},{8,9},{9,8},{10,11... | collective-permute-start | bytes 442376 | tf_op jit(solution)/shard_map/ppermute | solution.py:719
  205.0 7.7 %collective-permute-start.46 = (bf16[2,32,1152]{2,1,0:T(8,128)(2,1)S(1)}, bf16[2,32,1152]{2,1,0:T(8,128)(2,1)S(1)}, u32[]{:S(2)}, u32[]{:S(2)}) collective-permute-start(bf16[2,32,1152]{2,1,0:T(8,128)(2,1)S(1)} %get-tuple-element.227.refs_0_), channel_id=1, source_target_pairs={{0,5},{1,4},{2,7},{3,6},{4,1},{5,0},{6,3},{7,2},{8,13},{9,12},{10,... | collective-permute-start | bytes 442376 | tf_op jit(solution)/shard_map/ppermute | solution.py:719
  206.6 8.0 %collective-permute-start.45 = (bf16[2,32,1152]{2,1,0:T(8,128)(2,1)S(1)}, bf16[2,32,1152]{2,1,0:T(8,128)(2,1)S(1)}, u32[]{:S(2)}, u32[]{:S(2)}) collective-permute-start(bf16[2,32,1152]{2,1,0:T(8,128)(2,1)S(1)} %get-tuple-element.227.refs_0_), channel_id=1, source_target_pairs={{0,4},{1,5},{2,6},{3,7},{4,0},{5,1},{6,2},{7,3},{8,12},{9,13},{10,... | collective-permute-start | bytes 442376 | tf_op jit(solution)/shard_map/ppermute | solution.py:719
  228.2 137.2 %reduce-scatter.7.cloned.1.call-start = ((), (), s32[]{:S(2)}) async-start(), calls=%async_computation.14 | async-start | bytes 2211840 | tf_op jit(solution)/shard_map/reduce_scatter | solution.py:750
  230.9 7.7 %collective-permute-start.52 = (bf16[2,32,1152]{2,1,0:T(8,128)(2,1)S(1)}, bf16[2,32,1152]{2,1,0:T(8,128)(2,1)S(1)}, u32[]{:S(2)}, u32[]{:S(2)}) collective-permute-start(bf16[2,32,1152]{2,1,0:T(8,128)(2,1)S(1)} %get-tuple-element.236), channel_id=1, source_target_pairs={{0,5},{1,4},{2,7},{3,6},{4,1},{5,0},{6,3},{7,2},{8,13},{9,12},{10,... | collective-permute-start | bytes 442376 | tf_op jit(solution)/shard_map/ppermute | solution.py:719
  232.6 8.7 %collective-permute-start.53 = (bf16[2,32,1152]{2,1,0:T(8,128)(2,1)S(1)}, bf16[2,32,1152]{2,1,0:T(8,128)(2,1)S(1)}, u32[]{:S(2)}, u32[]{:S(2)}) collective-permute-start(bf16[2,32,1152]{2,1,0:T(8,128)(2,1)S(1)} %get-tuple-element.237), channel_id=1, source_target_pairs={{0,1},{1,0},{2,3},{3,2},{4,5},{5,4},{6,7},{7,6},{8,9},{9,8},{10,11... | collective-permute-start | bytes 442376 | tf_op jit(solution)/shard_map/ppermute | solution.py:719
  243.9 8.0 %collective-permute-start.56 = (bf16[2,32,1152]{2,1,0:T(8,128)(2,1)S(1)}, bf16[2,32,1152]{2,1,0:T(8,128)(2,1)S(1)}, u32[]{:S(2)}, u32[]{:S(2)}) collective-permute-start(bf16[2,32,1152]{2,1,0:T(8,128)(2,1)S(1)} %get-tuple-element.241.refs_1_), channel_id=1, source_target_pairs={{0,4},{1,5},{2,6},{3,7},{4,0},{5,1},{6,2},{7,3},{8,12},{9,13},{10,... | collective-permute-start | bytes 442376 | tf_op jit(solution)/shard_map/ppermute | solution.py:719
  264.0 7.7 %collective-permute-start.63 = (bf16[2,32,1152]{2,1,0:T(8,128)(2,1)S(1)}, bf16[2,32,1152]{2,1,0:T(8,128)(2,1)S(1)}, u32[]{:S(2)}, u32[]{:S(2)}) collective-permute-start(bf16[2,32,1152]{2,1,0:T(8,128)(2,1)S(1)} %get-tuple-element.251), channel_id=1, source_target_pairs={{0,5},{1,4},{2,7},{3,6},{4,1},{5,0},{6,3},{7,2},{8,13},{9,12},{10,... | collective-permute-start | bytes 442376 | tf_op jit(solution)/shard_map/ppermute | solution.py:719
  265.7 8.7 %collective-permute-start.64 = (bf16[2,32,1152]{2,1,0:T(8,128)(2,1)S(1)}, bf16[2,32,1152]{2,1,0:T(8,128)(2,1)S(1)}, u32[]{:S(2)}, u32[]{:S(2)}) collective-permute-start(bf16[2,32,1152]{2,1,0:T(8,128)(2,1)S(1)} %get-tuple-element.252), channel_id=1, source_target_pairs={{0,1},{1,0},{2,3},{3,2},{4,5},{5,4},{6,7},{7,6},{8,9},{9,8},{10,11... | collective-permute-start | bytes 442376 | tf_op jit(solution)/shard_map/ppermute | solution.py:719
  278.5 100.9 %reduce-scatter.9.cloned.1.call-start = ((), (), s32[]{:S(2)}) async-start(), calls=%async_computation.15 | async-start | bytes 3317760 | tf_op jit(solution)/shard_map/reduce_scatter | solution.py:750
  282.2 8.0 %collective-permute-start.67 = (bf16[2,32,1152]{2,1,0:T(8,128)(2,1)S(1)}, bf16[2,32,1152]{2,1,0:T(8,128)(2,1)S(1)}, u32[]{:S(2)}, u32[]{:S(2)}) collective-permute-start(bf16[2,32,1152]{2,1,0:T(8,128)(2,1)S(1)} %get-tuple-element.258.refs_0_), channel_id=1, source_target_pairs={{0,4},{1,5},{2,6},{3,7},{4,0},{5,1},{6,2},{7,3},{8,12},{9,13},{10,... | collective-permute-start | bytes 442376 | tf_op jit(solution)/shard_map/ppermute | solution.py:719
  300.2 7.7 %collective-permute-start.74 = (bf16[2,32,1152]{2,1,0:T(8,128)(2,1)S(1)}, bf16[2,32,1152]{2,1,0:T(8,128)(2,1)S(1)}, u32[]{:S(2)}, u32[]{:S(2)}) collective-permute-start(bf16[2,32,1152]{2,1,0:T(8,128)(2,1)S(1)} %get-tuple-element.270), channel_id=1, source_target_pairs={{0,5},{1,4},{2,7},{3,6},{4,1},{5,0},{6,3},{7,2},{8,13},{9,12},{10,... | collective-permute-start | bytes 442376 | tf_op jit(solution)/shard_map/ppermute | solution.py:719
  301.8 8.7 %collective-permute-start.75 = (bf16[2,32,1152]{2,1,0:T(8,128)(2,1)S(1)}, bf16[2,32,1152]{2,1,0:T(8,128)(2,1)S(1)}, u32[]{:S(2)}, u32[]{:S(2)}) collective-permute-start(bf16[2,32,1152]{2,1,0:T(8,128)(2,1)S(1)} %get-tuple-element.271), channel_id=1, source_target_pairs={{0,1},{1,0},{2,3},{3,2},{4,5},{5,4},{6,7},{7,6},{8,9},{9,8},{10,11... | collective-permute-start | bytes 442376 | tf_op jit(solution)/shard_map/ppermute | solution.py:719
  315.7 101.2 %reduce-scatter.11.cloned.1.call-start = ((), (), s32[]{:S(2)}) async-start(), calls=%async_computation.16 | async-start | bytes 2211840 | tf_op jit(solution)/shard_map/reduce_scatter | solution.py:750
  319.2 8.0 %collective-permute-start.78 = (bf16[2,32,1152]{2,1,0:T(8,128)(2,1)S(1)}, bf16[2,32,1152]{2,1,0:T(8,128)(2,1)S(1)}, u32[]{:S(2)}, u32[]{:S(2)}) collective-permute-start(bf16[2,32,1152]{2,1,0:T(8,128)(2,1)S(1)} %get-tuple-element.276.refs_1_), channel_id=1, source_target_pairs={{0,4},{1,5},{2,6},{3,7},{4,0},{5,1},{6,2},{7,3},{8,12},{9,13},{10,... | collective-permute-start | bytes 442376 | tf_op jit(solution)/shard_map/ppermute | solution.py:719
  344.4 9.7 %collective-permute-start.85 = (bf16[2,32,1152]{2,1,0:T(8,128)(2,1)S(1)}, bf16[2,32,1152]{2,1,0:T(8,128)(2,1)S(1)}, u32[]{:S(2)}, u32[]{:S(2)}) collective-permute-start(bf16[2,32,1152]{2,1,0:T(8,128)(2,1)S(1)} %get-tuple-element.290), channel_id=1, source_target_pairs={{0,5},{1,4},{2,7},{3,6},{4,1},{5,0},{6,3},{7,2},{8,13},{9,12},{10,... | collective-permute-start | bytes 442376 | tf_op jit(solution)/shard_map/ppermute | solution.py:719
  346.4 8.6 %collective-permute-start.86 = (bf16[2,32,1152]{2,1,0:T(8,128)(2,1)S(1)}, bf16[2,32,1152]{2,1,0:T(8,128)(2,1)S(1)}, u32[]{:S(2)}, u32[]{:S(2)}) collective-permute-start(bf16[2,32,1152]{2,1,0:T(8,128)(2,1)S(1)} %get-tuple-element.291), channel_id=1, source_target_pairs={{0,1},{1,0},{2,3},{3,2},{4,5},{5,4},{6,7},{7,6},{8,9},{9,8},{10,11... | collective-permute-start | bytes 442376 | tf_op jit(solution)/shard_map/ppermute | solution.py:719
  365.6 17.4 %collective-permute-start.88 = (bf16[288,1152]{1,0:T(8,128)(2,1)S(1)}, bf16[288,1152]{1,0:T(8,128)(2,1)S(1)}, u32[]{:S(2)}, u32[]{:S(2)}) collective-permute-start(bf16[288,1152]{1,0:T(8,128)(2,1)S(1)} %copy-done.1), channel_id=1, source_target_pairs={{0,1},{2,3},{4,5},{6,7},{8,9},{10,11},{12,13},{14,15},{16,17},{18,... | collective-permute-start | bytes 1990664 | tf_op jit(solution)/shard_map/ppermute | solution.py:1059
  369.6 9.7 %all-to-all-start.4 = ((f32[4,1,9856]{2,1,0:T(1,128)}), f32[4,1,9856]{2,1,0:T(1,128)S(1)}, u32[]{:S(2)}, u32[]{:S(2)}) async-start(f32[4,1,9856]{2,1,0:T(1,128)} %broadcast_in_dim.101), calls=%async_computation.6 | async-start | bytes 315392 | tf_op jit(solution)/shard_map/all_to_all | solution.py:742
  373.0 37.9 %collective-permute-start.94 = (bf16[2,32,1152]{2,1,0:T(8,128)(2,1)}, bf16[2,32,1152]{2,1,0:T(8,128)(2,1)}, u32[]{:S(2)}, u32[]{:S(2)}) collective-permute-start(bf16[2,32,1152]{2,1,0:T(8,128)(2,1)} %get-tuple-element.317), channel_id=1, source_target_pairs={{1,0},{3,2},{5,4},{7,6},{9,8},{11,10},{13,12},{15,14},{17,16},{19,... | collective-permute-start | bytes 442376 | tf_op jit(solution)/shard_map/ppermute | solution.py:1188
  379.4 7.8 %collective-permute-start.90 = (bf16[4,2,32,1152]{3,2,1,0:T(8,128)(2,1)}, bf16[4,2,32,1152]{3,2,1,0:T(8,128)(2,1)}, u32[]{:S(2)}, u32[]{:S(2)}) collective-permute-start(bf16[4,2,32,1152]{3,2,1,0:T(8,128)(2,1)} %get-tuple-element.322), channel_id=1, source_target_pairs={{0,2},{1,3},{2,0},{3,1},{4,6},{5,7},{6,4},{7,5},{8,10},{9,11},{10,... | collective-permute-start | bytes 1769480 | tf_op jit(solution)/shard_map/ppermute | solution.py:719
  379.6 20.6 %collective-permute-start.89 = (bf16[288,1152]{1,0:T(8,128)(2,1)}, bf16[288,1152]{1,0:T(8,128)(2,1)S(1)}, u32[]{:S(2)}, u32[]{:S(2)}) collective-permute-start(bf16[288,1152]{1,0:T(8,128)(2,1)} %reduce-scatter.9.cloned.1.call-done.refs_1_), channel_id=1, source_target_pairs={{1,0},{3,2},{5,4},{7,6},{9,8},{11,10},{13,12},{15,14},{17,16},{19,... | collective-permute-start | bytes 1990664 | tf_op jit(solution)/shard_map/ppermute | solution.py:1062
  383.7 19.7 %all-to-all-start.5 = ((f32[32,2,288]{2,1,0:T(2,128)}), f32[32,2,288]{2,1,0:T(2,128)}, u32[]{:S(2)}, u32[]{:S(2)}) async-start(f32[32,2,288]{2,1,0:T(2,128)} %bitcast.86), calls=%async_computation.8 | async-start | bytes 196608 | tf_op jit(solution)/shard_map/all_to_all | solution.py:1174
  390.9 13.6 %collective-permute-start.91 = (bf16[2,32,1152]{2,1,0:T(8,128)(2,1)}, bf16[2,32,1152]{2,1,0:T(8,128)(2,1)}, u32[]{:S(2)}, u32[]{:S(2)}) collective-permute-start(bf16[2,32,1152]{2,1,0:T(8,128)(2,1)} %get-tuple-element.324), channel_id=1, source_target_pairs={{0,5},{1,4},{2,7},{3,6},{4,1},{5,0},{6,3},{7,2},{8,13},{9,12},{10,... | collective-permute-start | bytes 442376 | tf_op jit(solution)/shard_map/ppermute | solution.py:719
  393.4 13.1 %collective-permute-start.92 = (bf16[2,32,1152]{2,1,0:T(8,128)(2,1)}, bf16[2,32,1152]{2,1,0:T(8,128)(2,1)}, u32[]{:S(2)}, u32[]{:S(2)}) collective-permute-start(bf16[2,32,1152]{2,1,0:T(8,128)(2,1)} %get-tuple-element.325), channel_id=1, source_target_pairs={{0,1},{1,0},{2,3},{3,2},{4,5},{5,4},{6,7},{7,6},{8,9},{9,8},{10,11... | collective-permute-start | bytes 442376 | tf_op jit(solution)/shard_map/ppermute | solution.py:719
  394.0 12.6 %collective-permute-start.93 = (bf16[2,32,1152]{2,1,0:T(8,128)(2,1)}, bf16[2,32,1152]{2,1,0:T(8,128)(2,1)}, u32[]{:S(2)}, u32[]{:S(2)}) collective-permute-start(bf16[2,32,1152]{2,1,0:T(8,128)(2,1)} %get-tuple-element.326), channel_id=1, source_target_pairs={{0,4},{1,5},{2,6},{3,7},{4,0},{5,1},{6,2},{7,3},{8,12},{9,13},{10,... | collective-permute-start | bytes 442376 | tf_op jit(solution)/shard_map/ppermute | solution.py:719
  401.1 15.7 %collective-permute-start.96 = (bf16[288,768]{1,0:T(8,128)(2,1)}, bf16[288,768]{1,0:T(8,128)(2,1)}, u32[]{:S(2)}, u32[]{:S(2)}) collective-permute-start(bf16[288,768]{1,0:T(8,128)(2,1)} %reduce-scatter.7.cloned.1.call-done.refs_3_), channel_id=1, source_target_pairs={{0,1},{2,3},{4,5},{6,7},{8,9},{10,11},{12,13},{14,15},{16,17},{18,... | collective-permute-start | bytes 1327112 | tf_op jit(solution)/shard_map/ppermute | solution.py:1059
  416.8 13.3 %collective-permute-start.97 = (bf16[288,768]{1,0:T(8,128)(2,1)}, bf16[288,768]{1,0:T(8,128)(2,1)}, u32[]{:S(2)}, u32[]{:S(2)}) collective-permute-start(bf16[288,768]{1,0:T(8,128)(2,1)} %reduce-scatter.11.cloned.1.call-done.refs_1_), channel_id=1, source_target_pairs={{1,0},{3,2},{5,4},{7,6},{9,8},{11,10},{13,12},{15,14},{17,16},{19,... | collective-permute-start | bytes 1327112 | tf_op jit(solution)/shard_map/ppermute | solution.py:1062
  (109 other events, 611.7 us)
Sparse Core Ops, SparseCore 0:
  27.3 40.5 all-gather.3
  70.1 83.5 all-gather.5
  155.2 53.8 all-gather.7
  228.3 50.2 reduce-scatter.4
  281.4 38.0 reduce-scatter.6
  321.8 51.7 reduce-scatter.8
  376.5 39.6 reduce-scatter.10

commit v6 on v5

--- a/solution.py
+++ b/solution.py
@@ -662,18 +662,20 @@
     put_shards(total, own_refs[0].shape, other_ref, own_refs)
 
 
-def mlp_both_kernel(left, traffic, n_ref, raw_ref, w_ref, ub_ref, mod_ref, *refs):
+def mlp_both_kernel(left, traffic, *refs):
+    shards, (raw_ref, w_ref, ub_ref, mod_ref), refs = refs[:8], refs[8:12], refs[12:]
     gw_ref, gub_ref, gate_ref, other_ref = refs[:4]
     own_refs, end_ref, end_refs = refs[4:8], refs[8], refs[9:13]
-    g_ref = refs[13]
+    g_ref, n_ref = refs[13:15]
     images, rows = own_refs[0].shape[:2]
     main = (w_ref.shape[1] - LANES) // 2
     lane = lax.broadcasted_iota(jnp.int32, (1, LANES), 1)
     spans = [(i % images, slice(i * rows, (i + 1) * rows)) for i in range(8 * images)]
-    traffic.wait(0, 1)
+    stack_shards(shards, n_ref)
+    traffic.wait(8)
     for m, span in spans:
         g_ref[span] = (mod_ref[m, 5:6] * raw_ref[span].astype(F32)).astype(BF16)
-    traffic.wait(2)
+    traffic.wait(9)
     n, g = n_ref[...], g_ref[...]
     value, slope = gelu_terms(mm(n, w_ref[:, :main]) + ub_ref[:, :main])
     hidden = value.astype(BF16)
@@ -989,19 +991,19 @@
     shape_gw = out((width, 2 * main + LANES), BF16)
     shape_gub = out((1, main + LANES), F32)
 
-    def mlp_both(b, gathered, gradient):
+    def mlp_both(b, shards, gradient):
         _, w, _, _, up_row = weights[b]
         found = call(
             functools.partial(mlp_both_kernel, left),
             (shape_gw, shape_gub, vector, *pieces_out, *pieces_out),
-            gathered,
+            *shards,
             gradient,
             w,
             up_row,
             mods[b],
             flops=3 * mlp_flops,
-            scratch=[pltpu.VMEM(flat.shape, flat.dtype)],
-            streamed=(0, 1, 2),
+            scratch=[pltpu.VMEM(flat.shape, flat.dtype)] * 2,
+            streamed=(8, 9),
             saved=(0, 8, 9, 10, 11, 12),
         )
         return scatter_plane(found[3], found[4:8]), found[0], found[1], found[2], found[8:]
@@ -1081,8 +1083,7 @@
     )
 
     three, six = (out((images, n, width), F32) for n in (3, 6))
-    (n_all,) = call(stack_kernel, (flat,), *gather_plane(normed), saved=(0,))
-    terms, mlp_grads1, g_up_bias1, g_gate_two1, end_pieces = mlp_both(1, n_all, g1_all)
+    terms, mlp_grads1, g_up_bias1, g_gate_two1, end_pieces = mlp_both(1, gather_plane(normed), g1_all)
     g_after, g_attn, g_some = call(
         back_mlp_rows_kernel,
         (shard_wide, shard, three),

time: 447 us -> 454 us (1.016)
  local copies, waits for them, and re-layouts: 27.6 us -> 37 us
    unnamed x104 -> x128, local copies, waits for them, and re-layouts: 18.3 us -> 27.8 us
    pallas_call x33 -> x32, Pallas kernels: 87.4 us -> 85.9 us  [call(): pl.pallas_call(kernel, out_shape=tuple(shapes), in_specs=specs, out_specs...]
  transfers between devices with their start and end apart: 109 -> 109, of which waited for: 64 -> 61; matrix products, arithmetic and copies ran while one was open for 5% -> 5% of each run, Pallas kernels for 17% -> 16%
where the time goes in v6:
time: 454 us; the launch traced here: 449 us
  waiting for transfers between devices  187 us (41%)
  starting transfers between devices  94.7 us (21%)
  Pallas kernels  85.9 us (19%)
  local copies, waits for them, and re-layouts  37 us (8%)
  blocking collectives  16.8 us (4%)
  between operations  15.8 us (3%)
  other arithmetic  9.11 us (2%)
    ppermute x88, waiting for transfers between devices, swap(): return lax.ppermute(value, PLANE, route)  109 us
    pallas_call x32, Pallas kernels, call(): pl.pallas_call(kernel, out_shape=tuple(shapes), in_specs=specs, out_specs...  85.9 us
    ppermute x88, starting transfers between devices, swap(): return lax.ppermute(value, PLANE, route)  61.1 us
    all_gather x3, waiting for transfers between devices, gather_all(): return lax.all_gather(own, 'dp', axis=0, tiled=True)  37.8 us
    unnamed x128, local copies, waits for them, and re-layouts  27.8 us
    ppermute x2, waiting for transfers between devices, to_first(): return lax.ppermute(value, 'section', [(1, 0)])  10.8 us
  transfers between devices with their start and end apart: 109, of which 61 were waited for; matrix products, arithmetic and copies ran while one was open for 5% of the time, Pallas kernels for 16%

profile of v6, /device:TPU:0, one launch (start us, length us, event | category | flops | bytes accessed | tf_op | source)
XLA Modules:
  0.0 449.0 jit_solution(8817702681907688464)
XLA Ops:
  11.3 3.0 collective-permute-start.2
  15.9 4.9 %all-to-all-start = ((bf16[4,2,288]{2,1,0:T(2,128)(2,1)}), bf16[4,2,288]{2,1,0:T(2,128)(2,1)S(1)}, u32[]{:S(2)}, u32[]{:S(2)}) async-start(bf16[4,2,288]{2,1,0:T(2,128)(2,1)} %bitcast.68), calls=%async_computation | async-start | bytes 12288 | tf_op jit(solution)/shard_map/all_to_all | solution.py:881
  20.8 5.6 %all-to-all-done = bf16[4,2,288]{2,1,0:T(2,128)(2,1)S(1)} async-done(((bf16[4,2,288]{2,1,0:T(2,128)(2,1)}), bf16[4,2,288]{2,1,0:T(2,128)(2,1)S(1)}, u32[]{:S(2)}, u32[]{:S(2)}) %all-to-all-start) | async-done | bytes 4640 | tf_op jit(solution)/shard_map/all_to_all | solution.py:881
  30.1 4.2 all-to-all-start.1
  34.3 6.8 %all-to-all-done.1 = f32[4,2,1728]{2,1,0:T(2,128)S(1)} async-done(((f32[4,2,1728]{2,1,0:T(2,128)}), f32[4,2,1728]{2,1,0:T(2,128)S(1)}, u32[]{:S(2)}, u32[]{:S(2)}) %all-to-all-start.1) | async-done | bytes 55328 | tf_op jit(solution)/shard_map/all_to_all | solution.py:885
  41.2 8.1 %all_to_all.41 = f32[8,2,1728]{2,1,0:T(2,128)} all-to-all(f32[8,2,1728]{2,1,0:T(2,128)S(1)} %broadcast_in_dim.90), channel_id=1, replica_groups=mesh['dp'=4,'tensor'=4,'section'=2] {'section','tensor'}, dimensions={0} | all-to-all | bytes 221184 | tf_op jit(solution)/shard_map/all_to_all | solution.py:744
  53.8 4.6 %collective-permute-done = bf16[2,32,1152]{2,1,0:T(8,128)(2,1)S(1)} collective-permute-done((bf16[2,32,1152]{2,1,0:T(8,128)(2,1)S(1)}, bf16[2,32,1152]{2,1,0:T(8,128)(2,1)S(1)}, u32[]{:S(2)}, u32[]{:S(2)}) %collective-permute-start) | collective-permute-done | bytes 147488 | tf_op jit(solution)/shard_map/ppermute | solution.py:853
  62.2 2.8 collective-permute-done.12.refs_3_
  72.5 3.3 collective-permute-done.5.refs_4_
  75.8 2.7 collective-permute-done.4.refs_3_
  83.9 7.4 %shard_map.224 = (bf16[2,256,1152]{2,1,0:T(8,128)(2,1)}, bf16[2,256,1024]{2,1,0:T(8,128)(2,1)}, f32[2,256,128]{2,1,0:T(8,128)}, f32[2,256,256]{2,1,0:T(8,128)}, ...) custom-call(s32[1]{0:T(128)} %bitcast.refs_0_, ...), custom_call_target="tpu_custom_call" | custom-call | flops 2315255808 | bytes 7422468 | tf_op jit(solution)/shard_map/pallas_call | solution.py:96
  97.1 4.1 collective-permute-done.19.refs_1_
  108.0 4.2 collective-permute-done.24.refs_3_
  115.9 37.7 %all-gather.6.cloned.1.call-done.refs_8_.refs_9_.refs_12_ = bf16[1152,1920]{1,0:T(8,128)(2,1)} async-done(((bf16[288,1920]{1,0:T(8,128)(2,1)}), bf16[1152,1920]{1,0:T(8,128)(2,1)}) %all-gather.6.cloned.1.call-update) | async-done | bytes 4423696 | tf_op jit(solution)/shard_map/all_gather | solution.py:748
  153.6 6.5 %shard_map.227 = (bf16[512,1152]{1,0:T(8,128)(2,1)}, f32[512,640]{1,0:T(8,128)}, bf16[512,640]{1,0:T(8,128)(2,1)}, bf16[4,2,32,1152]{3,2,1,0:T(8,128)(2,1)S(1)},...) custom-call(bf16[2,32,1152]{2,1,0:T(8,128)(2,1)S(1)} %get-tuple-elem, ...), custom_call_target="tpu_custom_call" | custom-call | flops 1358954496 | bytes 8161792 | tf_op jit(solution)/shard_map/pallas_call | solution.py:96
  166.0 4.0 collective-permute-done.30.refs_1_
  176.9 3.4 collective-permute-done.35.refs_4_
  180.4 2.7 collective-permute-done.34.refs_3_
  184.7 6.6 %shard_map.230 = (bf16[2,256,1152]{2,1,0:T(8,128)(2,1)}, bf16[2,256,1024]{2,1,0:T(8,128)(2,1)}, f32[2,256,128]{2,1,0:T(8,128)}, f32[2,256,256]{2,1,0:T(8,128)}, ...) custom-call(s32[1]{0:T(128)} %bitcast.refs_0_, ...), custom_call_target="tpu_custom_call" | custom-call | flops 2315255808 | bytes 7422468 | tf_op jit(solution)/shard_map/pallas_call | solution.py:96
  197.3 4.1 collective-permute-done.41.refs_1_
  201.4 2.7 collective-permute-done.42.refs_2_
  208.6 4.1 collective-permute-done.46.refs_3_
  224.7 8.8 %shard_map.233 = (bf16[1152,1152]{1,0:T(8,128)(2,1)}, f32[1,640]{1,0:T(1,128)S(1)}, f32[2,1,1152]{2,1,0:T(1,128)S(1)}, bf16[4,2,32,1152]{3,2,1,0:T(8,128)(2,1)S(...) custom-call(bf16[2,32,1152]{2,1,0:T(8,128)(2,1)S(1)} %get-tuple-elem, ...), custom_call_target="tpu_custom_call" | custom-call | flops 4076863488 | bytes 10096640 | tf_op jit(solution)/shard_map/pallas_call | solution.py:96
  241.2 4.1 collective-permute-done.52.refs_1_
  245.3 2.7 collective-permute-done.53.refs_2_
  252.8 3.7 collective-permute-done.57.refs_4_
  260.6 8.0 %shard_map.236 = (bf16[2,256,1152]{2,1,0:T(8,128)(2,1)S(1)}, bf16[2,256,640]{2,1,0:T(8,128)(2,1)S(1)}, f32[16,256]{1,0:T(8,128)S(1)}, bf16[4,2,32,1152]{3,2,1,0:...) custom-call(s32[1]{0:T(128)} %bitcast.refs_0_, ...), custom_call_target="tpu_custom_call" | custom-call | flops 4630511616 | bytes 7831556 | tf_op jit(solution)/shard_map/pallas_call | solution.py:96
  274.3 4.1 collective-permute-done.63.refs_1_.refs_5_
  278.4 2.7 collective-permute-done.64.refs_2_.refs_6_
  281.2 4.0 shard_map.239.refs_10_
  291.0 4.0 collective-permute-done.68.refs_3_
  298.8 5.9 %shard_map.240 = (bf16[512,1152]{1,0:T(8,128)(2,1)S(1)}, bf16[512,640]{1,0:T(8,128)(2,1)S(1)}, f32[1,640]{1,0:T(1,128)S(1)}, bf16[4,2,32,1152]{3,2,1,0:T(8,128)(...) custom-call(bf16[2,32,1152]{2,1,0:T(8,128)(2,1)S(1)} %get-tuple-elem, ...), custom_call_target="tpu_custom_call" | custom-call | flops 1358954496 | bytes 8161792 | tf_op jit(solution)/shard_map/pallas_call | solution.py:96
  310.5 4.1 collective-permute-done.74.refs_1_.refs_5_
  314.6 2.8 collective-permute-done.75.refs_2_.refs_6_
  317.4 5.1 %shard_map.243.refs_14_ = bf16[1152,1152]{1,0:T(8,128)(2,1)} custom-call(bf16[512,1152]{1,0:T(8,128)(2,1)} %get-tuple-element.280.refs_0_, bf16[512,640]{1,0:T(8,128)(2,1)S(1)} %get-tuple-element.281.refs_1_, bf16[512,1152]{1,0:T(8,128)(2,1)S(1)} %get-tuple-element.282.refs_2_, bf16[512,640]{1,0:T(8,128)(2,1)} %get-tuple-element.283.refs_3_, ...), custom_call_target="tpu_custom_call" | custom-call | flops 1358954496 | bytes 6324224 | tf_op jit(solution)/shard_map/pallas_call | solution.py:96
  328.1 4.1 collective-permute-done.79.refs_4_
  338.5 8.4 %shard_map.244 = (bf16[2,256,1152]{2,1,0:T(8,128)(2,1)S(1)}, bf16[2,256,640]{2,1,0:T(8,128)(2,1)S(1)}, f32[16,256]{1,0:T(8,128)S(1)}, bf16[4,2,32,1152]{3,2,1,0:...) custom-call(s32[1]{0:T(128)} %bitcast.refs_0_, ...), custom_call_target="tpu_custom_call" | custom-call | flops 4630511616 | bytes 7831556 | tf_op jit(solution)/shard_map/pallas_call | solution.py:96
  356.8 4.0 shard_map.246.refs_9_
  363.4 8.7 %all_to_all.42 = f32[8,1,6656]{2,1,0:T(1,128)S(1)} all-to-all(f32[8,1,6656]{2,1,0:T(1,128)S(1)} %copy.101), channel_id=1, replica_groups=mesh['dp'=4,'tensor'=4,'section'=2] {'section','tensor'}, dimensions={0} | all-to-all | bytes 425984 | tf_op jit(solution)/shard_map/all_to_all | solution.py:1152
  372.4 3.2 collective-permute-start.88
  376.4 3.3 all-to-all-start.4
  381.0 5.0 %all-to-all-done.4 = f32[4,1,9856]{2,1,0:T(1,128)S(1)} async-done(((f32[4,1,9856]{2,1,0:T(1,128)}), f32[4,1,9856]{2,1,0:T(1,128)S(1)}, u32[]{:S(2)}, u32[]{:S(2)}) %all-to-all-start.4) | async-done | bytes 157728 | tf_op jit(solution)/shard_map/all_to_all | solution.py:744
  390.5 3.3 all-to-all-start.5
  393.9 3.0 shard_map.248
  402.5 4.5 %collective-permute-done.89.refs_2_ = bf16[288,1152]{1,0:T(8,128)(2,1)S(1)} collective-permute-done((bf16[288,1152]{1,0:T(8,128)(2,1)}, bf16[288,1152]{1,0:T(8,128)(2,1)S(1)}, u32[]{:S(2)}, u32[]{:S(2)}) %collective-permute-start.89) | collective-permute-done | bytes 663584 | tf_op jit(solution)/shard_map/ppermute | solution.py:1064
  417.7 4.1 collective-permute-done.95
  430.9 6.3 %collective-permute-done.97.refs_2_ = bf16[288,768]{1,0:T(8,128)(2,1)} collective-permute-done((bf16[288,768]{1,0:T(8,128)(2,1)}, bf16[288,768]{1,0:T(8,128)(2,1)}, u32[]{:S(2)}, u32[]{:S(2)}) %collective-permute-start.97) | collective-permute-done | bytes 442400 | tf_op jit(solution)/shard_map/ppermute | solution.py:1064
  437.1 2.8 shard_map.250
  (448 shorter events, 179.0 us)
Async XLA Ops:
  11.3 15.1 %collective-permute-start.2 = (bf16[288,768]{1,0:T(8,128)(2,1)S(1)}, bf16[288,768]{1,0:T(8,128)(2,1)S(1)}, u32[]{:S(2)}, u32[]{:S(2)}) collective-permute-start(bf16[288,768]{1,0:T(8,128)(2,1)S(1)} %get-tuple-element.181), channel_id=1, source_target_pairs={{0,1},{1,0},{2,3},{3,2},{4,5},{5,4},{6,7},{7,6},{8,9},{9,8},{10,11... | collective-permute-start | bytes 1327112 | tf_op jit(solution)/shard_map/ppermute | solution.py:827
  15.9 10.5 %all-to-all-start = ((bf16[4,2,288]{2,1,0:T(2,128)(2,1)}), bf16[4,2,288]{2,1,0:T(2,128)(2,1)S(1)}, u32[]{:S(2)}, u32[]{:S(2)}) async-start(bf16[4,2,288]{2,1,0:T(2,128)(2,1)} %bitcast.68), calls=%async_computation | async-start | bytes 12288 | tf_op jit(solution)/shard_map/all_to_all | solution.py:881
  20.8 62.2 %all-gather.4.cloned.1.call-start = ((), (), s32[]{:S(2)}) async-start(), calls=%async_computation.10 | async-start | bytes 2211840 | tf_op jit(solution)/shard_map/all_gather | solution.py:748
  28.6 20.7 %collective-permute-start.1 = (bf16[288,1152]{1,0:T(8,128)(2,1)S(1)}, bf16[288,1152]{1,0:T(8,128)(2,1)}, u32[]{:S(2)}, u32[]{:S(2)}) collective-permute-start(bf16[288,1152]{1,0:T(8,128)(2,1)S(1)} %get-tuple-element.179), channel_id=1, source_target_pairs={{0,1},{1,0},{2,3},{3,2},{4,5},{5,4},{6,7},{7,6},{8,9},{9,8},{10,11... | collective-permute-start | bytes 1990664 | tf_op jit(solution)/shard_map/ppermute | solution.py:837
  30.1 11.0 %all-to-all-start.1 = ((f32[4,2,1728]{2,1,0:T(2,128)}), f32[4,2,1728]{2,1,0:T(2,128)S(1)}, u32[]{:S(2)}, u32[]{:S(2)}) async-start(f32[4,2,1728]{2,1,0:T(2,128)} %fusion), calls=%async_computation.1 | async-start | bytes 114688 | tf_op jit(solution)/shard_map/all_to_all | solution.py:885
  34.3 119.4 %all-gather.6.cloned.1.call-start = ((), (), s32[]{:S(2)}) async-start(), calls=%async_computation.11 | async-start | bytes 5529600 | tf_op jit(solution)/shard_map/all_gather | solution.py:748
  52.5 164.0 %all-gather.8.cloned.1.call-start = ((), (), s32[]{:S(2)}) async-start(), calls=%async_computation.12 | async-start | bytes 3317760 | tf_op jit(solution)/shard_map/all_gather | solution.py:748
  59.3 7.8 %collective-permute-start.11 = (bf16[2,32,1152]{2,1,0:T(8,128)(2,1)S(1)}, bf16[2,32,1152]{2,1,0:T(8,128)(2,1)S(1)}, u32[]{:S(2)}, u32[]{:S(2)}) collective-permute-start(bf16[2,32,1152]{2,1,0:T(8,128)(2,1)S(1)} %get-tuple-element.432.refs_0_.refs_4_), channel_id=1, source_target_pairs={{0,4},{1,5},{2,6},{3,7},{4,0},{5,1},{6,2},{7,3},{8,12},{9,13},{10,... | collective-permute-start | bytes 442376 | tf_op jit(solution)/shard_map/ppermute | solution.py:721
  60.9 8.5 %collective-permute-start.13 = (bf16[2,32,1152]{2,1,0:T(8,128)(2,1)S(1)}, bf16[2,32,1152]{2,1,0:T(8,128)(2,1)S(1)}, u32[]{:S(2)}, u32[]{:S(2)}) collective-permute-start(bf16[2,32,1152]{2,1,0:T(8,128)(2,1)S(1)} %get-tuple-element.432.refs_0_.refs_4_), channel_id=1, source_target_pairs={{0,2},{1,3},{2,0},{3,1},{4,6},{5,7},{6,4},{7,5},{8,10},{9,11},{10,... | collective-permute-start | bytes 442376 | tf_op jit(solution)/shard_map/ppermute | solution.py:721
  61.0 9.9 %collective-permute-start.10 = (bf16[2,32,1152]{2,1,0:T(8,128)(2,1)S(1)}, bf16[2,32,1152]{2,1,0:T(8,128)(2,1)S(1)}, u32[]{:S(2)}, u32[]{:S(2)}) collective-permute-start(bf16[2,32,1152]{2,1,0:T(8,128)(2,1)S(1)} %get-tuple-element.432.refs_0_.refs_4_), channel_id=1, source_target_pairs={{0,1},{1,0},{2,3},{3,2},{4,5},{5,4},{6,7},{7,6},{8,9},{9,8},{10,11... | collective-permute-start | bytes 442376 | tf_op jit(solution)/shard_map/ppermute | solution.py:721
  69.4 9.1 %collective-permute-start.4 = (bf16[2,32,1152]{2,1,0:T(8,128)(2,1)S(1)}, bf16[2,32,1152]{2,1,0:T(8,128)(2,1)S(1)}, u32[]{:S(2)}, u32[]{:S(2)}) collective-permute-start(bf16[2,32,1152]{2,1,0:T(8,128)(2,1)S(1)} %shard_map.222.refs_1_), channel_id=1, source_target_pairs={{0,4},{1,5},{2,6},{3,7},{4,0},{5,1},{6,2},{7,3},{8,12},{9,13},{10,... | collective-permute-start | bytes 442376 | tf_op jit(solution)/shard_map/ppermute | solution.py:721
  70.9 7.7 %collective-permute-start.3 = (bf16[2,32,1152]{2,1,0:T(8,128)(2,1)S(1)}, bf16[2,32,1152]{2,1,0:T(8,128)(2,1)S(1)}, u32[]{:S(2)}, u32[]{:S(2)}) collective-permute-start(bf16[2,32,1152]{2,1,0:T(8,128)(2,1)S(1)} %shard_map.222.refs_1_), channel_id=1, source_target_pairs={{0,1},{1,0},{2,3},{3,2},{4,5},{5,4},{6,7},{7,6},{8,9},{9,8},{10,11... | collective-permute-start | bytes 442376 | tf_op jit(solution)/shard_map/ppermute | solution.py:721
  72.0 9.4 %collective-permute-start.6 = (bf16[2,32,1152]{2,1,0:T(8,128)(2,1)S(1)}, bf16[2,32,1152]{2,1,0:T(8,128)(2,1)S(1)}, u32[]{:S(2)}, u32[]{:S(2)}) collective-permute-start(bf16[2,32,1152]{2,1,0:T(8,128)(2,1)S(1)} %shard_map.222.refs_1_), channel_id=1, source_target_pairs={{0,2},{1,3},{2,0},{3,1},{4,6},{5,7},{6,4},{7,5},{8,10},{9,11},{10,... | collective-permute-start | bytes 442376 | tf_op jit(solution)/shard_map/ppermute | solution.py:721
  81.5 241.3 %reduce-scatter.5.cloned.1.call-start = ((), (), s32[]{:S(2)}) async-start(), calls=%async_computation.13 | async-start | bytes 3317760 | tf_op jit(solution)/shard_map/reduce_scatter | solution.py:752
  93.5 7.7 %collective-permute-start.19 = (bf16[2,32,1152]{2,1,0:T(8,128)(2,1)S(1)}, bf16[2,32,1152]{2,1,0:T(8,128)(2,1)S(1)}, u32[]{:S(2)}, u32[]{:S(2)}) collective-permute-start(bf16[2,32,1152]{2,1,0:T(8,128)(2,1)S(1)} %get-tuple-element.202), channel_id=1, source_target_pairs={{0,5},{1,4},{2,7},{3,6},{4,1},{5,0},{6,3},{7,2},{8,13},{9,12},{10,... | collective-permute-start | bytes 442376 | tf_op jit(solution)/shard_map/ppermute | solution.py:721
  94.8 8.5 %collective-permute-start.20 = (bf16[2,32,1152]{2,1,0:T(8,128)(2,1)S(1)}, bf16[2,32,1152]{2,1,0:T(8,128)(2,1)S(1)}, u32[]{:S(2)}, u32[]{:S(2)}) collective-permute-start(bf16[2,32,1152]{2,1,0:T(8,128)(2,1)S(1)} %get-tuple-element.203), channel_id=1, source_target_pairs={{0,1},{1,0},{2,3},{3,2},{4,5},{5,4},{6,7},{7,6},{8,9},{9,8},{10,11... | collective-permute-start | bytes 442376 | tf_op jit(solution)/shard_map/ppermute | solution.py:721
  104.5 7.7 %collective-permute-start.24 = (bf16[2,32,1152]{2,1,0:T(8,128)(2,1)S(1)}, bf16[2,32,1152]{2,1,0:T(8,128)(2,1)S(1)}, u32[]{:S(2)}, u32[]{:S(2)}) collective-permute-start(bf16[2,32,1152]{2,1,0:T(8,128)(2,1)S(1)} %get-tuple-element.205.refs_0_), channel_id=1, source_target_pairs={{0,5},{1,4},{2,7},{3,6},{4,1},{5,0},{6,3},{7,2},{8,13},{9,12},{10,... | collective-permute-start | bytes 442376 | tf_op jit(solution)/shard_map/ppermute | solution.py:721
  105.8 8.5 %collective-permute-start.23 = (bf16[2,32,1152]{2,1,0:T(8,128)(2,1)S(1)}, bf16[2,32,1152]{2,1,0:T(8,128)(2,1)S(1)}, u32[]{:S(2)}, u32[]{:S(2)}) collective-permute-start(bf16[2,32,1152]{2,1,0:T(8,128)(2,1)S(1)} %get-tuple-element.205.refs_0_), channel_id=1, source_target_pairs={{0,4},{1,5},{2,6},{3,7},{4,0},{5,1},{6,2},{7,3},{8,12},{9,13},{10,... | collective-permute-start | bytes 442376 | tf_op jit(solution)/shard_map/ppermute | solution.py:721
  162.3 7.7 %collective-permute-start.30 = (bf16[2,32,1152]{2,1,0:T(8,128)(2,1)S(1)}, bf16[2,32,1152]{2,1,0:T(8,128)(2,1)S(1)}, u32[]{:S(2)}, u32[]{:S(2)}) collective-permute-start(bf16[2,32,1152]{2,1,0:T(8,128)(2,1)S(1)} %get-tuple-element.212), channel_id=1, source_target_pairs={{0,5},{1,4},{2,7},{3,6},{4,1},{5,0},{6,3},{7,2},{8,13},{9,12},{10,... | collective-permute-start | bytes 442376 | tf_op jit(solution)/shard_map/ppermute | solution.py:721
  195.5 8.6 %collective-permute-start.42 = (bf16[2,32,1152]{2,1,0:T(8,128)(2,1)S(1)}, bf16[2,32,1152]{2,1,0:T(8,128)(2,1)S(1)}, u32[]{:S(2)}, u32[]{:S(2)}) collective-permute-start(bf16[2,32,1152]{2,1,0:T(8,128)(2,1)S(1)} %get-tuple-element.224), channel_id=1, source_target_pairs={{0,1},{1,0},{2,3},{3,2},{4,5},{5,4},{6,7},{7,6},{8,9},{9,8},{10,11... | collective-permute-start | bytes 442376 | tf_op jit(solution)/shard_map/ppermute | solution.py:721
  205.0 7.7 %collective-permute-start.46 = (bf16[2,32,1152]{2,1,0:T(8,128)(2,1)S(1)}, bf16[2,32,1152]{2,1,0:T(8,128)(2,1)S(1)}, u32[]{:S(2)}, u32[]{:S(2)}) collective-permute-start(bf16[2,32,1152]{2,1,0:T(8,128)(2,1)S(1)} %get-tuple-element.227.refs_0_), channel_id=1, source_target_pairs={{0,5},{1,4},{2,7},{3,6},{4,1},{5,0},{6,3},{7,2},{8,13},{9,12},{10,... | collective-permute-start | bytes 442376 | tf_op jit(solution)/shard_map/ppermute | solution.py:721
  206.6 8.0 %collective-permute-start.45 = (bf16[2,32,1152]{2,1,0:T(8,128)(2,1)S(1)}, bf16[2,32,1152]{2,1,0:T(8,128)(2,1)S(1)}, u32[]{:S(2)}, u32[]{:S(2)}) collective-permute-start(bf16[2,32,1152]{2,1,0:T(8,128)(2,1)S(1)} %get-tuple-element.227.refs_0_), channel_id=1, source_target_pairs={{0,4},{1,5},{2,6},{3,7},{4,0},{5,1},{6,2},{7,3},{8,12},{9,13},{10,... | collective-permute-start | bytes 442376 | tf_op jit(solution)/shard_map/ppermute | solution.py:721
  208.6 8.0 %collective-permute-start.47 = (bf16[2,32,1152]{2,1,0:T(8,128)(2,1)S(1)}, bf16[2,32,1152]{2,1,0:T(8,128)(2,1)S(1)}, u32[]{:S(2)}, u32[]{:S(2)}) collective-permute-start(bf16[2,32,1152]{2,1,0:T(8,128)(2,1)S(1)} %get-tuple-element.227.refs_0_), channel_id=1, source_target_pairs={{0,2},{1,3},{2,0},{3,1},{4,6},{5,7},{6,4},{7,5},{8,10},{9,11},{10,... | collective-permute-start | bytes 442376 | tf_op jit(solution)/shard_map/ppermute | solution.py:721
  234.9 137.3 %reduce-scatter.7.cloned.1.call-start = ((), (), s32[]{:S(2)}) async-start(), calls=%async_computation.14 | async-start | bytes 2211840 | tf_op jit(solution)/shard_map/reduce_scatter | solution.py:752
  237.6 7.7 %collective-permute-start.52 = (bf16[2,32,1152]{2,1,0:T(8,128)(2,1)S(1)}, bf16[2,32,1152]{2,1,0:T(8,128)(2,1)S(1)}, u32[]{:S(2)}, u32[]{:S(2)}) collective-permute-start(bf16[2,32,1152]{2,1,0:T(8,128)(2,1)S(1)} %get-tuple-element.236), channel_id=1, source_target_pairs={{0,5},{1,4},{2,7},{3,6},{4,1},{5,0},{6,3},{7,2},{8,13},{9,12},{10,... | collective-permute-start | bytes 442376 | tf_op jit(solution)/shard_map/ppermute | solution.py:721
  239.5 8.5 %collective-permute-start.53 = (bf16[2,32,1152]{2,1,0:T(8,128)(2,1)S(1)}, bf16[2,32,1152]{2,1,0:T(8,128)(2,1)S(1)}, u32[]{:S(2)}, u32[]{:S(2)}) collective-permute-start(bf16[2,32,1152]{2,1,0:T(8,128)(2,1)S(1)} %get-tuple-element.237), channel_id=1, source_target_pairs={{0,1},{1,0},{2,3},{3,2},{4,5},{5,4},{6,7},{7,6},{8,9},{9,8},{10,11... | collective-permute-start | bytes 442376 | tf_op jit(solution)/shard_map/ppermute | solution.py:721
  250.7 7.8 %collective-permute-start.56 = (bf16[2,32,1152]{2,1,0:T(8,128)(2,1)S(1)}, bf16[2,32,1152]{2,1,0:T(8,128)(2,1)S(1)}, u32[]{:S(2)}, u32[]{:S(2)}) collective-permute-start(bf16[2,32,1152]{2,1,0:T(8,128)(2,1)S(1)} %get-tuple-element.241.refs_1_), channel_id=1, source_target_pairs={{0,4},{1,5},{2,6},{3,7},{4,0},{5,1},{6,2},{7,3},{8,12},{9,13},{10,... | collective-permute-start | bytes 442376 | tf_op jit(solution)/shard_map/ppermute | solution.py:721
  270.8 7.7 %collective-permute-start.63 = (bf16[2,32,1152]{2,1,0:T(8,128)(2,1)S(1)}, bf16[2,32,1152]{2,1,0:T(8,128)(2,1)S(1)}, u32[]{:S(2)}, u32[]{:S(2)}) collective-permute-start(bf16[2,32,1152]{2,1,0:T(8,128)(2,1)S(1)} %get-tuple-element.251), channel_id=1, source_target_pairs={{0,5},{1,4},{2,7},{3,6},{4,1},{5,0},{6,3},{7,2},{8,13},{9,12},{10,... | collective-permute-start | bytes 442376 | tf_op jit(solution)/shard_map/ppermute | solution.py:721
  272.4 8.8 %collective-permute-start.64 = (bf16[2,32,1152]{2,1,0:T(8,128)(2,1)S(1)}, bf16[2,32,1152]{2,1,0:T(8,128)(2,1)S(1)}, u32[]{:S(2)}, u32[]{:S(2)}) collective-permute-start(bf16[2,32,1152]{2,1,0:T(8,128)(2,1)S(1)} %get-tuple-element.252), channel_id=1, source_target_pairs={{0,1},{1,0},{2,3},{3,2},{4,5},{5,4},{6,7},{7,6},{8,9},{9,8},{10,11... | collective-permute-start | bytes 442376 | tf_op jit(solution)/shard_map/ppermute | solution.py:721
  285.2 100.9 %reduce-scatter.9.cloned.1.call-start = ((), (), s32[]{:S(2)}) async-start(), calls=%async_computation.15 | async-start | bytes 3317760 | tf_op jit(solution)/shard_map/reduce_scatter | solution.py:752
  288.8 8.0 %collective-permute-start.67 = (bf16[2,32,1152]{2,1,0:T(8,128)(2,1)S(1)}, bf16[2,32,1152]{2,1,0:T(8,128)(2,1)S(1)}, u32[]{:S(2)}, u32[]{:S(2)}) collective-permute-start(bf16[2,32,1152]{2,1,0:T(8,128)(2,1)S(1)} %get-tuple-element.258.refs_0_), channel_id=1, source_target_pairs={{0,4},{1,5},{2,6},{3,7},{4,0},{5,1},{6,2},{7,3},{8,12},{9,13},{10,... | collective-permute-start | bytes 442376 | tf_op jit(solution)/shard_map/ppermute | solution.py:721
  306.9 7.7 %collective-permute-start.74 = (bf16[2,32,1152]{2,1,0:T(8,128)(2,1)S(1)}, bf16[2,32,1152]{2,1,0:T(8,128)(2,1)S(1)}, u32[]{:S(2)}, u32[]{:S(2)}) collective-permute-start(bf16[2,32,1152]{2,1,0:T(8,128)(2,1)S(1)} %get-tuple-element.270), channel_id=1, source_target_pairs={{0,5},{1,4},{2,7},{3,6},{4,1},{5,0},{6,3},{7,2},{8,13},{9,12},{10,... | collective-permute-start | bytes 442376 | tf_op jit(solution)/shard_map/ppermute | solution.py:721
  308.6 8.8 %collective-permute-start.75 = (bf16[2,32,1152]{2,1,0:T(8,128)(2,1)S(1)}, bf16[2,32,1152]{2,1,0:T(8,128)(2,1)S(1)}, u32[]{:S(2)}, u32[]{:S(2)}) collective-permute-start(bf16[2,32,1152]{2,1,0:T(8,128)(2,1)S(1)} %get-tuple-element.271), channel_id=1, source_target_pairs={{0,1},{1,0},{2,3},{3,2},{4,5},{5,4},{6,7},{7,6},{8,9},{9,8},{10,11... | collective-permute-start | bytes 442376 | tf_op jit(solution)/shard_map/ppermute | solution.py:721
  322.5 101.1 %reduce-scatter.11.cloned.1.call-start = ((), (), s32[]{:S(2)}) async-start(), calls=%async_computation.16 | async-start | bytes 2211840 | tf_op jit(solution)/shard_map/reduce_scatter | solution.py:752
  325.9 8.1 %collective-permute-start.78 = (bf16[2,32,1152]{2,1,0:T(8,128)(2,1)S(1)}, bf16[2,32,1152]{2,1,0:T(8,128)(2,1)S(1)}, u32[]{:S(2)}, u32[]{:S(2)}) collective-permute-start(bf16[2,32,1152]{2,1,0:T(8,128)(2,1)S(1)} %get-tuple-element.276.refs_1_), channel_id=1, source_target_pairs={{0,4},{1,5},{2,6},{3,7},{4,0},{5,1},{6,2},{7,3},{8,12},{9,13},{10,... | collective-permute-start | bytes 442376 | tf_op jit(solution)/shard_map/ppermute | solution.py:721
  351.2 9.7 %collective-permute-start.85 = (bf16[2,32,1152]{2,1,0:T(8,128)(2,1)S(1)}, bf16[2,32,1152]{2,1,0:T(8,128)(2,1)S(1)}, u32[]{:S(2)}, u32[]{:S(2)}) collective-permute-start(bf16[2,32,1152]{2,1,0:T(8,128)(2,1)S(1)} %get-tuple-element.290), channel_id=1, source_target_pairs={{0,5},{1,4},{2,7},{3,6},{4,1},{5,0},{6,3},{7,2},{8,13},{9,12},{10,... | collective-permute-start | bytes 442376 | tf_op jit(solution)/shard_map/ppermute | solution.py:721
  353.1 8.7 %collective-permute-start.86 = (bf16[2,32,1152]{2,1,0:T(8,128)(2,1)S(1)}, bf16[2,32,1152]{2,1,0:T(8,128)(2,1)S(1)}, u32[]{:S(2)}, u32[]{:S(2)}) collective-permute-start(bf16[2,32,1152]{2,1,0:T(8,128)(2,1)S(1)} %get-tuple-element.291), channel_id=1, source_target_pairs={{0,1},{1,0},{2,3},{3,2},{4,5},{5,4},{6,7},{7,6},{8,9},{9,8},{10,11... | collective-permute-start | bytes 442376 | tf_op jit(solution)/shard_map/ppermute | solution.py:721
  372.4 17.4 %collective-permute-start.88 = (bf16[288,1152]{1,0:T(8,128)(2,1)S(1)}, bf16[288,1152]{1,0:T(8,128)(2,1)S(1)}, u32[]{:S(2)}, u32[]{:S(2)}) collective-permute-start(bf16[288,1152]{1,0:T(8,128)(2,1)S(1)} %copy-done.1), channel_id=1, source_target_pairs={{0,1},{2,3},{4,5},{6,7},{8,9},{10,11},{12,13},{14,15},{16,17},{18,... | collective-permute-start | bytes 1990664 | tf_op jit(solution)/shard_map/ppermute | solution.py:1061
  376.4 9.7 %all-to-all-start.4 = ((f32[4,1,9856]{2,1,0:T(1,128)}), f32[4,1,9856]{2,1,0:T(1,128)S(1)}, u32[]{:S(2)}, u32[]{:S(2)}) async-start(f32[4,1,9856]{2,1,0:T(1,128)} %broadcast_in_dim.101), calls=%async_computation.6 | async-start | bytes 315392 | tf_op jit(solution)/shard_map/all_to_all | solution.py:744
  379.7 37.9 %collective-permute-start.94 = (bf16[2,32,1152]{2,1,0:T(8,128)(2,1)}, bf16[2,32,1152]{2,1,0:T(8,128)(2,1)}, u32[]{:S(2)}, u32[]{:S(2)}) collective-permute-start(bf16[2,32,1152]{2,1,0:T(8,128)(2,1)} %get-tuple-element.317), channel_id=1, source_target_pairs={{1,0},{3,2},{5,4},{7,6},{9,8},{11,10},{13,12},{15,14},{17,16},{19,... | collective-permute-start | bytes 442376 | tf_op jit(solution)/shard_map/ppermute | solution.py:1189
  386.1 7.8 %collective-permute-start.90 = (bf16[4,2,32,1152]{3,2,1,0:T(8,128)(2,1)}, bf16[4,2,32,1152]{3,2,1,0:T(8,128)(2,1)}, u32[]{:S(2)}, u32[]{:S(2)}) collective-permute-start(bf16[4,2,32,1152]{3,2,1,0:T(8,128)(2,1)} %get-tuple-element.322), channel_id=1, source_target_pairs={{0,2},{1,3},{2,0},{3,1},{4,6},{5,7},{6,4},{7,5},{8,10},{9,11},{10,... | collective-permute-start | bytes 1769480 | tf_op jit(solution)/shard_map/ppermute | solution.py:721
  386.4 20.6 %collective-permute-start.89 = (bf16[288,1152]{1,0:T(8,128)(2,1)}, bf16[288,1152]{1,0:T(8,128)(2,1)S(1)}, u32[]{:S(2)}, u32[]{:S(2)}) collective-permute-start(bf16[288,1152]{1,0:T(8,128)(2,1)} %reduce-scatter.9.cloned.1.call-done.refs_1_), channel_id=1, source_target_pairs={{1,0},{3,2},{5,4},{7,6},{9,8},{11,10},{13,12},{15,14},{17,16},{19,... | collective-permute-start | bytes 1990664 | tf_op jit(solution)/shard_map/ppermute | solution.py:1064
  390.5 19.7 %all-to-all-start.5 = ((f32[32,2,288]{2,1,0:T(2,128)}), f32[32,2,288]{2,1,0:T(2,128)}, u32[]{:S(2)}, u32[]{:S(2)}) async-start(f32[32,2,288]{2,1,0:T(2,128)} %bitcast.86), calls=%async_computation.8 | async-start | bytes 196608 | tf_op jit(solution)/shard_map/all_to_all | solution.py:1175
  397.6 13.6 %collective-permute-start.91 = (bf16[2,32,1152]{2,1,0:T(8,128)(2,1)}, bf16[2,32,1152]{2,1,0:T(8,128)(2,1)}, u32[]{:S(2)}, u32[]{:S(2)}) collective-permute-start(bf16[2,32,1152]{2,1,0:T(8,128)(2,1)} %get-tuple-element.324), channel_id=1, source_target_pairs={{0,5},{1,4},{2,7},{3,6},{4,1},{5,0},{6,3},{7,2},{8,13},{9,12},{10,... | collective-permute-start | bytes 442376 | tf_op jit(solution)/shard_map/ppermute | solution.py:721
  400.1 13.2 %collective-permute-start.92 = (bf16[2,32,1152]{2,1,0:T(8,128)(2,1)}, bf16[2,32,1152]{2,1,0:T(8,128)(2,1)}, u32[]{:S(2)}, u32[]{:S(2)}) collective-permute-start(bf16[2,32,1152]{2,1,0:T(8,128)(2,1)} %get-tuple-element.325), channel_id=1, source_target_pairs={{0,1},{1,0},{2,3},{3,2},{4,5},{5,4},{6,7},{7,6},{8,9},{9,8},{10,11... | collective-permute-start | bytes 442376 | tf_op jit(solution)/shard_map/ppermute | solution.py:721
  400.7 12.6 %collective-permute-start.93 = (bf16[2,32,1152]{2,1,0:T(8,128)(2,1)}, bf16[2,32,1152]{2,1,0:T(8,128)(2,1)}, u32[]{:S(2)}, u32[]{:S(2)}) collective-permute-start(bf16[2,32,1152]{2,1,0:T(8,128)(2,1)} %get-tuple-element.326), channel_id=1, source_target_pairs={{0,4},{1,5},{2,6},{3,7},{4,0},{5,1},{6,2},{7,3},{8,12},{9,13},{10,... | collective-permute-start | bytes 442376 | tf_op jit(solution)/shard_map/ppermute | solution.py:721
  407.9 15.7 %collective-permute-start.96 = (bf16[288,768]{1,0:T(8,128)(2,1)}, bf16[288,768]{1,0:T(8,128)(2,1)}, u32[]{:S(2)}, u32[]{:S(2)}) collective-permute-start(bf16[288,768]{1,0:T(8,128)(2,1)} %reduce-scatter.7.cloned.1.call-done.refs_3_), channel_id=1, source_target_pairs={{0,1},{2,3},{4,5},{6,7},{8,9},{10,11},{12,13},{14,15},{16,17},{18,... | collective-permute-start | bytes 1327112 | tf_op jit(solution)/shard_map/ppermute | solution.py:1061
  423.6 13.5 %collective-permute-start.97 = (bf16[288,768]{1,0:T(8,128)(2,1)}, bf16[288,768]{1,0:T(8,128)(2,1)}, u32[]{:S(2)}, u32[]{:S(2)}) collective-permute-start(bf16[288,768]{1,0:T(8,128)(2,1)} %reduce-scatter.11.cloned.1.call-done.refs_1_), channel_id=1, source_target_pairs={{1,0},{3,2},{5,4},{7,6},{9,8},{11,10},{13,12},{15,14},{17,16},{19,... | collective-permute-start | bytes 1327112 | tf_op jit(solution)/shard_map/ppermute | solution.py:1064
  (121 other events, 628.6 us)
Sparse Core Ops, SparseCore 0:
  27.3 40.5 all-gather.3
  70.1 83.5 all-gather.5
  155.2 53.8 all-gather.7
  235.1 50.4 reduce-scatter.4
  288.3 38.0 reduce-scatter.6
  328.7 51.6 reduce-scatter.8
  383.5 39.6 reduce-scatter.10
